TPU v7x, 32 devices: a whole 2x2x4 slice. The times are simulated.
32 devices in a mesh: dp: 8 (over z, x), tensor: 4 (over y, core).
Axes of the slice: x: 2, y: 2, z: 4, core: 2. Of those that a mesh axis runs over, the one named last changes fastest.
Arguments:
- inputs: bfloat16 [16384, 4096], P('tensor', 'dp'), may hold values from -6 to 6
- cotangent: bfloat16 [16384, 4096], P('tensor', 'dp'), may hold values from -6 to 6
- first_left: bfloat16 [128, 128, 128], P('tensor', 'dp'), may hold values from -0.5 to 0.5
- first_right: bfloat16 [128, 128, 128], P('tensor', 'dp'), may hold values from -0.5 to 0.5
- second_left: bfloat16 [128, 128, 128], P('tensor', 'dp'), may hold values from -0.5 to 0.5
- second_right: bfloat16 [128, 128, 128], P('tensor', 'dp'), may hold values from -0.5 to 0.5
Outputs:
- mixed: bfloat16 [16384, 4096], P('tensor', 'dp')
- input_grad: bfloat16 [16384, 4096], P('tensor', 'dp')
- first_left_grad: float32 [128, 128, 128], P('tensor', 'dp')
- first_right_grad: float32 [128, 128, 128], P('tensor', 'dp')
- second_left_grad: float32 [128, 128, 128], P('tensor', 'dp')
- second_right_grad: float32 [128, 128, 128], P('tensor', 'dp')
All inputs are finite; a program needn't handle non-finite values.
Results may differ from a plain program's by a relative error of at most 0.0068.
Values may be sent and summed in bfloat16 or wider, within the bound.
No kernel may reach another device: no remote copies, remote signals or barrier semaphores. Data moves between devices by JAX's collectives and lax.ppermute only.
A program may use at most 128 MiB of HBM per device.

v0:
```python
import jax
import jax.numpy as jnp
from jax import lax
from jax.sharding import PartitionSpec as P


def gelu_value(values):
    return jax.nn.gelu(values, approximate=True)


def gelu_back(values, upstream):
    return jax.vjp(gelu_value, values)[1](upstream)[0]


def spread(values):
    return values.reshape(values.shape[0], lax.axis_size("tensor"), -1, values.shape[2])


def settle(moved):
    return moved.reshape(moved.shape[0], moved.shape[2], moved.shape[3])


def inner_move(values):
    return settle(lax.all_to_all(spread(values), "tensor", split_axis=1, concat_axis=0, tiled=True))


def block_move(values):
    return settle(lax.all_to_all(spread(values), "tensor", split_axis=1, concat_axis=0, tiled=True))


def outer_back(values):
    return settle(lax.all_to_all(spread(values), "tensor", split_axis=1, concat_axis=0, tiled=True))


def inner_back(values):
    return settle(lax.all_to_all(spread(values), "tensor", split_axis=1, concat_axis=0, tiled=True))


def product(form, left, right):
    return jnp.einsum(form, left, right, preferred_element_type=jnp.float32)


def per_device(inputs, cotangent, first_left, first_right, second_left, second_right):
    bf16 = jnp.bfloat16
    f32 = jnp.float32
    left_one, right_one, left_two, right_two = (
        lax.all_gather(first_left, "dp", axis=1, tiled=True),
        lax.all_gather(first_right, "dp", axis=1, tiled=True),
        lax.all_gather(second_left, "dp", axis=1, tiled=True),
        lax.all_gather(second_right, "dp", axis=1, tiled=True),
    )
    blocks = first_left.shape[0]
    width = left_one.shape[1]
    tok_rows = inputs.shape[1]
    x_three = inputs.reshape(blocks, width, tok_rows)
    g_three = cotangent.reshape(blocks, width, tok_rows)
    first_out = product("bjt,bjo->bot", x_three, left_one).astype(bf16)
    moved_one = inner_move(first_out)
    second_out = product("ibt,bip->bpt", moved_one, right_one).astype(bf16)
    hidden_pre = inner_move(second_out)
    activated = gelu_value(hidden_pre.astype(f32)).astype(bf16)
    third_out = product("jbt,bjo->bot", activated, left_two).astype(bf16)
    moved_three = block_move(third_out)
    fourth_out = product("ibt,bio->bot", moved_three, right_two).astype(bf16)
    returned = block_move(fourth_out)
    mixed = (x_three.astype(f32) + jnp.swapaxes(returned, 0, 1).astype(f32)).astype(bf16)
    cot_four = outer_back(g_three)
    back_three = product("obt,bio->bit", cot_four, right_two).astype(bf16)
    cot_three = outer_back(back_three)
    grad_rtwo = product("ibt,obt->bio", moved_three, cot_four)
    grad_ltwo = product("jbt,obt->bjo", activated, cot_three)
    back_act = product("obt,bjo->bjt", cot_three, left_two)
    hidden_cot = gelu_back(jnp.swapaxes(hidden_pre, 0, 1).astype(f32), back_act).astype(bf16)
    cot_two = inner_back(hidden_cot)
    grad_rone = product("ibt,pbt->bip", moved_one, cot_two)
    back_one = product("pbt,bip->bit", cot_two, right_one).astype(bf16)
    cot_one = inner_back(back_one)
    grad_lone = product("bjt,obt->bjo", x_three, cot_one)
    input_grad = (g_three.astype(f32) + product("obt,bjo->bjt", cot_one, left_one)).astype(bf16)
    grad_lone, grad_rone, grad_ltwo, grad_rtwo = (
        lax.psum_scatter(grad_lone, "dp", scatter_dimension=1, tiled=True),
        lax.psum_scatter(grad_rone, "dp", scatter_dimension=1, tiled=True),
        lax.psum_scatter(grad_ltwo, "dp", scatter_dimension=1, tiled=True),
        lax.psum_scatter(grad_rtwo, "dp", scatter_dimension=1, tiled=True),
    )
    return (
        mixed.reshape(blocks * width, tok_rows),
        input_grad.reshape(blocks * width, tok_rows),
        grad_lone,
        grad_rone,
        grad_ltwo,
        grad_rtwo,
    )


def solution(mesh):
    return jax.shard_map(
        per_device,
        mesh=mesh,
        in_specs=(
            P("tensor", "dp"),
            P("tensor", "dp"),
            P("tensor", "dp", None),
            P("tensor", "dp", None),
            P("tensor", "dp", None),
            P("tensor", "dp", None),
        ),
        out_specs=(
            P("tensor", "dp"),
            P("tensor", "dp"),
            P("tensor", "dp", None),
            P("tensor", "dp", None),
            P("tensor", "dp", None),
            P("tensor", "dp", None),
        ),
        check_vma=False,
    )
```

profile of v0, /device:TPU:0, one launch (start us, length us, event | category | flops | bytes accessed | tf_op | source)
XLA Modules:
  0.0 652.4 jit_solution(14788380351703544463)
XLA Ops:
  7.2 6.6 %copy.46 = bf16[32,4,32,512]{3,0,2,1:T(8,128)(2,1)} copy(bf16[32,4,32,512]{3,2,1,0:T(8,128)(2,1)} %bitcast.116) | data formatting | bytes 8388608 | tf_op jit(solution)/shard_map/reshape;reshape | solution.py:16
  13.8 4.9 all-to-all-start.4
  19.4 44.9 %all-gather.5.cloned.1.call-done = bf16[32,128,128]{2,1,0:T(8,128)(2,1)} async-done(((bf16[32,16,128]{2,1,0:T(8,128)(2,1)}), bf16[32,128,128]{2,1,0:T(8,128)(2,1)}) %all-gather.5.cloned.1.call-update) | async-done | bytes 1048592 | tf_op jit(solution)/shard_map/all_gather | solution.py:47
  70.6 4.9 all-to-all-start
  81.0 36.4 %all-gather.11.cloned.1.call-done = bf16[32,128,128]{2,1,0:T(8,128)(2,1)} async-done(((bf16[32,16,128]{2,1,0:T(8,128)(2,1)}), bf16[32,128,128]{2,1,0:T(8,128)(2,1)}) %all-gather.11.cloned.1.call-update) | async-done | bytes 1048592 | tf_op jit(solution)/shard_map/all_gather | solution.py:50
  123.7 4.9 all-to-all-start.5
  129.3 6.5 %copy.39 = bf16[4,32,1,32,512]{4,1,0,3,2:T(8,128)(2,1)} copy(bf16[4,32,1,32,512]{4,3,1,0,2:T(8,128)(2,1)} %bitcast.3) | data formatting | bytes 8388608 | tf_op jit(solution)/shard_map/all_to_all | solution.py:24
  135.9 34.6 %all-gather.7.cloned.1.call-done = bf16[32,128,128]{2,1,0:T(8,128)(2,1)} async-done(((bf16[32,16,128]{2,1,0:T(8,128)(2,1)}), bf16[32,128,128]{2,1,0:T(8,128)(2,1)}) %all-gather.7.cloned.1.call-update) | async-done | bytes 1048592 | tf_op jit(solution)/shard_map/all_gather | solution.py:48
  176.8 4.9 all-to-all-start.1
  182.8 6.6 %copy.49 = bf16[4,32,1,32,512]{4,1,0,3,2:T(8,128)(2,1)} copy(bf16[4,32,1,32,512]{4,3,1,0,2:T(8,128)(2,1)} %bitcast.29) | data formatting | bytes 8388608 | tf_op jit(solution)/shard_map/all_to_all | solution.py:32
  189.3 40.6 %all-to-all-done.1 = bf16[32,4,32,512]{3,2,0,1:T(8,128)(2,1)} async-done(((bf16[32,4,32,512]{3,2,0,1:T(8,128)(2,1)}), bf16[32,4,32,512]{3,2,0,1:T(8,128)(2,1)}, u32[]{:S(2)}, u32[]{:S(2)}) %all-to-all-start.1) | async-done | bytes 4194336 | tf_op jit(solution)/shard_map/all_to_all | solution.py:24
  233.3 8.1 %copy.41 = f32[4,32,1,32,512]{4,1,0,3,2:T(8,128)} copy(f32[4,32,1,32,512]{4,3,1,0,2:T(8,128)S(1)} %convert_bitcast_fusion) | data formatting | bytes 16777216 | tf_op jit(solution)/shard_map/convert_element_type | solution.py:61
  241.5 9.2 %fusion.6 = bf16[32,128,512]{2,1,0:T(8,128)(2,1)S(1)} fusion(f32[32,128,512]{2,1,0:T(8,128)} %bitcast.126, bf16[32,128,128]{2,1,0:T(8,128)(2,1)} %all-gather.9.cloned.1.call-done, bf16[128,32,512]{2,0,1:T(8,128)(2,1)} %bitcast.129), kind=kOutput, calls=%fused_computation.9 | convolution fusion | flops 578813952 | bytes 17825792 | tf_op jit(solution)/shard_map/obt,bjo->bjt/dot_general | solution.py:40
  251.2 50.9 %all_to_all.108 = bf16[32,4,32,512]{3,2,0,1:T(8,128)(2,1)S(1)} all-to-all(bf16[32,4,32,512]{3,2,0,1:T(8,128)(2,1)S(1)} %copy.50), channel_id=1, replica_groups=mesh['dp'=8,'tensor'=4] {'tensor'}, dimensions={1} | all-to-all | bytes 8388608 | tf_op jit(solution)/shard_map/all_to_all | solution.py:36
  307.0 50.7 %all_to_all.109 = bf16[32,4,32,512]{3,2,0,1:T(8,128)(2,1)S(1)} all-to-all(bf16[32,4,32,512]{3,2,0,1:T(8,128)(2,1)S(1)} %copy.52), channel_id=1, replica_groups=mesh['dp'=8,'tensor'=4] {'tensor'}, dimensions={1} | all-to-all | bytes 8388608 | tf_op jit(solution)/shard_map/all_to_all | solution.py:36
  365.5 8.7 %fusion.20 = f32[32,128,128]{2,1,0:T(8,128)} fusion(bf16[128,32,512]{2,0,1:T(8,128)(2,1)} %bitcast.130, f32[128,32,512]{2,0,1:T(8,128)} %bitcast.127), kind=kOutput, calls=%fused_computation.36 | convolution fusion | flops 555745280 | bytes 14680064 | tf_op jit(solution)/shard_map/jbt,obt->bjo/dot_general | solution.py:40
  374.5 5.7 convolution_convert_fusion.3
  380.7 50.7 %all_to_all.110 = bf16[32,4,32,512]{3,2,0,1:T(8,128)(2,1)S(1)} all-to-all(bf16[32,4,32,512]{3,2,0,1:T(8,128)(2,1)S(1)} %copy.42), channel_id=1, replica_groups=mesh['dp'=8,'tensor'=4] {'tensor'}, dimensions={1} | all-to-all | bytes 8388608 | tf_op jit(solution)/shard_map/all_to_all | solution.py:28
  444.4 4.9 all-to-all-start.3
  449.5 6.2 fusion.23
  455.8 41.7 %all-to-all-done.3 = bf16[32,4,32,512]{3,2,0,1:T(8,128)(2,1)} async-done(((bf16[32,4,32,512]{3,2,0,1:T(8,128)(2,1)}), bf16[32,4,32,512]{3,2,0,1:T(8,128)(2,1)}, u32[]{:S(2)}, u32[]{:S(2)}) %all-to-all-start.3) | async-done | bytes 4194336 | tf_op jit(solution)/shard_map/all_to_all | solution.py:28
  505.5 6.8 %fusion.19 = bf16[32,128,512]{2,1,0:T(8,128)(2,1)} fusion(f32[128,32,512]{2,1,0:T(8,128)S(1)} %bitcast.115, bf16[32,128,512]{2,1,0:T(8,128)(2,1)S(1)} %bitcast.114), kind=kLoop, calls=%fused_computation.27 | loop fusion | flops 6291456 | bytes 16777216 | tf_op jit(solution)/shard_map/convert_element_type | solution.py:66
  514.2 59.7 %reduce-scatter.11.cloned.1.call-done = f32[32,16,128]{2,1,0:T(8,128)} async-done(((f32[32,128,128]{2,1,0:T(8,128)}), f32[32,16,128]{2,1,0:T(8,128)}) %reduce-scatter.11.cloned.1.call-update) | async-done | bytes 262160 | tf_op jit(solution)/shard_map/reduce_scatter | solution.py:84
  573.9 71.3 %reduce-scatter.7.cloned.1.call-done = f32[32,16,128]{2,1,0:T(8,128)} async-done(((f32[32,128,128]{2,1,0:T(8,128)}), f32[32,16,128]{2,1,0:T(8,128)}) %reduce-scatter.7.cloned.1.call-update) | async-done | bytes 262160 | tf_op jit(solution)/shard_map/reduce_scatter | solution.py:82
  (69 shorter events, 67.4 us)
Async XLA Ops:
  13.8 56.8 %all-to-all-start.4 = ((bf16[32,4,32,512]{3,0,2,1:T(8,128)(2,1)}), bf16[32,4,32,512]{3,0,2,1:T(8,128)(2,1)}, u32[]{:S(2)}, u32[]{:S(2)}) async-start(bf16[32,4,32,512]{3,0,2,1:T(8,128)(2,1)} %copy.46), calls=%async_computation.4 | async-start | bytes 8388608 | tf_op jit(solution)/shard_map/all_to_all | solution.py:32
  18.7 45.6 %all-gather.5.cloned.1.call-start = ((), (), s32[]{:S(2)}) async-start(), calls=%async_computation.12 | async-start | bytes 1179648 | tf_op jit(solution)/shard_map/all_gather | solution.py:47
  70.6 53.1 %all-to-all-start = ((bf16[32,4,32,512]{3,2,0,1:T(8,128)(2,1)}), bf16[32,4,32,512]{3,2,0,1:T(8,128)(2,1)}, u32[]{:S(2)}, u32[]{:S(2)}) async-start(bf16[32,4,32,512]{3,2,0,1:T(8,128)(2,1)} %copy.38), calls=%async_computation | async-start | bytes 8388608 | tf_op jit(solution)/shard_map/all_to_all | solution.py:24
  75.5 41.9 %all-gather.11.cloned.1.call-start = ((), (), s32[]{:S(2)}) async-start(), calls=%async_computation.15 | async-start | bytes 1179648 | tf_op jit(solution)/shard_map/all_gather | solution.py:50
  123.7 53.1 %all-to-all-start.5 = ((bf16[32,4,32,512]{3,2,0,1:T(8,128)(2,1)}), bf16[32,4,32,512]{3,2,0,1:T(8,128)(2,1)}, u32[]{:S(2)}, u32[]{:S(2)}) async-start(bf16[32,4,32,512]{3,2,0,1:T(8,128)(2,1)} %copy.48), calls=%async_computation.5 | async-start | bytes 8388608 | tf_op jit(solution)/shard_map/all_to_all | solution.py:32
  128.6 41.9 %all-gather.7.cloned.1.call-start = ((), (), s32[]{:S(2)}) async-start(), calls=%async_computation.13 | async-start | bytes 1179648 | tf_op jit(solution)/shard_map/all_gather | solution.py:48
  176.8 53.1 %all-to-all-start.1 = ((bf16[32,4,32,512]{3,2,0,1:T(8,128)(2,1)}), bf16[32,4,32,512]{3,2,0,1:T(8,128)(2,1)}, u32[]{:S(2)}, u32[]{:S(2)}) async-start(bf16[32,4,32,512]{3,2,0,1:T(8,128)(2,1)} %copy.40), calls=%async_computation.1 | async-start | bytes 8388608 | tf_op jit(solution)/shard_map/all_to_all | solution.py:24
  181.7 59.8 %all-gather.9.cloned.1.call-start = ((), (), s32[]{:S(2)}) async-start(), calls=%async_computation.14 | async-start | bytes 1179648 | tf_op jit(solution)/shard_map/all_gather | solution.py:49
  182.3 330.1 %reduce-scatter.5.cloned.1.call-start = ((), (), s32[]{:S(2)}) async-start(), calls=%async_computation.16 | async-start | bytes 2359296 | tf_op jit(solution)/shard_map/reduce_scatter | solution.py:81
  302.1 2.4 copy-start.9
  304.5 2.0 copy-start.3
  357.8 4.3 copy-start.5
  365.4 148.8 %reduce-scatter.9.cloned.1.call-start = ((), (), s32[]{:S(2)}) async-start(), calls=%async_computation.18 | async-start | bytes 2359296 | tf_op jit(solution)/shard_map/reduce_scatter | solution.py:83
  365.5 9.0 %copy-start.11 = (bf16[32,128,128]{2,1,0:T(8,128)(2,1)S(1)}, bf16[32,128,128]{2,1,0:T(8,128)(2,1)}, u32[]{:S(2)}) copy-start(bf16[32,128,128]{2,1,0:T(8,128)(2,1)} %all-gather.9.cloned.1.call-done) | copy-start | bytes 3145732
  374.2 199.6 %reduce-scatter.11.cloned.1.call-start = ((), (), s32[]{:S(2)}) async-start(), calls=%async_computation.19 | async-start | bytes 2359296 | tf_op jit(solution)/shard_map/reduce_scatter | solution.py:84
  431.5 4.4 copy-start
  433.9 2.0 copy-start.4
  435.9 2.7 copy-start.8
  444.4 53.1 %all-to-all-start.3 = ((bf16[32,4,32,512]{3,2,0,1:T(8,128)(2,1)}), bf16[32,4,32,512]{3,2,0,1:T(8,128)(2,1)}, u32[]{:S(2)}, u32[]{:S(2)}) async-start(bf16[32,4,32,512]{3,2,0,1:T(8,128)(2,1)} %copy.44), calls=%async_computation.3 | async-start | bytes 8388608 | tf_op jit(solution)/shard_map/all_to_all | solution.py:28
  449.2 195.9 %reduce-scatter.7.cloned.1.call-start = ((), (), s32[]{:S(2)}) async-start(), calls=%async_computation.17 | async-start | bytes 2359296 | tf_op jit(solution)/shard_map/reduce_scatter | solution.py:82
  455.8 45.3 %copy-start.10 = (bf16[32,128,128]{2,1,0:T(8,128)(2,1)S(1)}, bf16[32,128,128]{2,1,0:T(8,128)(2,1)}, u32[]{:S(2)}) copy-start(bf16[32,128,128]{2,1,0:T(8,128)(2,1)} %all-gather.5.cloned.1.call-done) | copy-start | bytes 3145732
  497.5 3.6 copy-start.2
  497.5 4.8 copy-start.7
  502.3 3.3 copy-start.6
  (1 other events, 1.9 us)
Sparse Core Ops, SparseCore 0:
  21.6 42.6 all-gather.4
  78.3 38.9 all-gather.10
  131.5 38.9 all-gather.6
  184.3 38.9 all-gather.8
  365.5 65.8 reduce-scatter.4
  435.4 67.1 reduce-scatter.8
  506.7 67.1 reduce-scatter.10
  578.0 67.1 reduce-scatter.6
where the time goes:
time: 661 us; the launch traced here: 652 us
  waiting for transfers between devices  332 us (50%)
  blocking collectives  152 us (23%)
  local copies, waits for them, and re-layouts  60.8 us (9%)
  matrix products  52.9 us (8%)
  starting transfers between devices  25.7 us (4%)
  between operations  14.8 us (2%)
  other arithmetic  13.8 us (2%)
    all_to_all x2, blocking collectives, inner_back(): lax.all_to_all(spread(values), 'tensor', split_axis=1, concat_axis=0, til...  102 us
    reduce_scatter x1, waiting for transfers between devices, per_device(): lax.psum_scatter(grad_rone, 'dp', scatter_dimension=1, tiled=True)  71.3 us
    reduce_scatter x1, waiting for transfers between devices, per_device(): lax.psum_scatter(grad_rtwo, 'dp', scatter_dimension=1, tiled=True)  59.7 us
    dot_general x12, matrix products, product(): return jnp.einsum(form, left, right, preferred_element_type=jnp.float32)  52.9 us
    all_to_all x1, blocking collectives, block_move(): lax.all_to_all(spread(values), 'tensor', split_axis=1, concat_axis=0, til...  50.7 us
    all_gather x1, waiting for transfers between devices, per_device(): lax.all_gather(first_left, 'dp', axis=1, tiled=True)  44.9 us
    all_to_all x1, waiting for transfers between devices, block_move(): lax.all_to_all(spread(values), 'tensor', split_axis=1, concat_axis=0, til...  41.7 us
    all_to_all x2, waiting for transfers between devices, inner_move(): lax.all_to_all(spread(values), 'tensor', split_axis=1, concat_axis=0, til...  40.7 us
  transfers between devices with their start and end apart: 13, of which 9 were waited for; matrix products, arithmetic and copies ran while one was open for 15% of the time, Pallas kernels for 0%

commit v1 on v0

v1 whole, which is shorter than its diff:
```python
import math

import jax
import jax.numpy as jnp
from jax import lax
from jax.sharding import PartitionSpec as P

BF16 = jnp.bfloat16
F32 = jnp.float32
LANES = 128


def gelu_value(values):
    return jax.nn.gelu(values, approximate=True)


def gelu_back(values, upstream):
    return jax.vjp(gelu_value, values)[1](upstream)[0]


def product(form, left, right):
    return jnp.einsum(form, left, right, preferred_element_type=F32)


class Ring:
    def __init__(self, axis, stride, size):
        self.axis, self.stride, self.size = axis, stride, size

    def here(self):
        return lax.rem(lax.axis_index(self.axis) // self.stride, self.size)

    def send(self, value, step):
        pairs = []
        for src in range(lax.axis_size(self.axis)):
            own = src // self.stride % self.size
            pairs.append((src, src + ((own + step) % self.size - own) * self.stride))
        return lax.ppermute(value, self.axis, pairs)

    def gather(self, value):
        if self.size == 1:
            return value[None]
        here = self.here()
        out = jnp.zeros((self.size,) + value.shape, value.dtype)
        out = lax.dynamic_update_index_in_dim(out, value, here, 0)
        for step in range(1, self.size):
            got = self.send(value, step)
            out = lax.dynamic_update_index_in_dim(out, got, lax.rem(here - step + self.size, self.size), 0)
        return out

    def scatter(self, value, dim):
        here = self.here()
        if self.size == 1:
            return lax.index_in_dim(value, 0, dim, keepdims=False)
        total = lax.dynamic_index_in_dim(value, here, dim, keepdims=False).astype(F32)
        for step in range(1, self.size):
            there = lax.rem(here + step, self.size)
            term = lax.dynamic_index_in_dim(value, there, dim, keepdims=False).astype(BF16)
            total = total + self.send(term, step).astype(F32)
        return total


def halves(size):
    low = 2 if size % 2 == 0 else 1
    return size // low, low


def per_device(inputs, cotangent, first_left, first_right, second_left, second_right):
    n_dp, n_tensor = lax.axis_size("dp"), lax.axis_size("tensor")
    home, rows, size = first_left.shape
    tokens = inputs.shape[1]
    share = math.gcd(n_tensor, max(1, tokens // LANES))
    groups = n_tensor // share
    held = home * share
    cut = tokens // share

    far, near = halves(share)
    ring_y, ring_core = Ring("tensor", near, far), Ring("tensor", 1, near)
    far, near = halves(n_dp)
    ring_z, ring_x = Ring("dp", near, far), Ring("dp", 1, near)

    same_tokens = [[group * share + part for group in range(groups)] for part in range(share)]

    def cross(pieces):
        return lax.all_to_all(pieces, "tensor", split_axis=0, concat_axis=0, tiled=True)

    def go(values):
        pieces = values.reshape(home, groups, held, share, cut).transpose(1, 3, 2, 0, 4)
        got = cross(pieces.reshape(n_tensor, held, home, cut))
        return got.transpose(1, 0, 2, 3).reshape(held, size, cut)

    def back(values):
        pieces = values.reshape(held, n_tensor, home, cut).transpose(1, 0, 2, 3)
        got = cross(pieces).reshape(groups, share, held, home, cut)
        return got.transpose(3, 0, 2, 1, 4).reshape(home, size, tokens)

    def turn(values):
        if groups == 1:
            return jnp.swapaxes(values, 0, 1)
        moved = lax.all_to_all(
            values.reshape(held, groups, held, cut), "tensor", split_axis=1, concat_axis=0, tiled=True, axis_index_groups=same_tokens
        )
        return jnp.swapaxes(moved.reshape(size, held, cut), 0, 1)

    def whole(factor):
        one = ring_z.gather(ring_y.gather(factor))
        all_rows = ring_core.gather(ring_x.gather(one))
        return all_rows.transpose(3, 0, 4, 2, 1, 5, 6).reshape(held, size, size)

    def own_sum(partial):
        split = partial.reshape(ring_y.size, ring_core.size, home, ring_z.size, ring_x.size, rows, size)
        split = ring_core.scatter(split, 1)
        split = ring_x.scatter(split, 3)
        split = ring_z.scatter(split, 2)
        return ring_y.scatter(split, 0)

    x_home = inputs.reshape(home, size, tokens)
    g_home = cotangent.reshape(home, size, tokens)
    g_mid = go(g_home)

    left_one = ring_x.gather(ring_z.gather(first_left)).transpose(2, 1, 0, 3, 4).reshape(home, size, size)
    right_one, left_two, right_two = whole(first_right), whole(second_left), whole(second_right)

    s_one = go(product("bjt,bjo->bot", x_home, left_one).astype(BF16))
    s_two = turn(product("bit,bip->bpt", s_one, right_one).astype(BF16))
    act = gelu_value(s_two.astype(F32)).astype(BF16)
    e_three = turn(product("bot,bio->bit", g_mid, right_two).astype(BF16))
    hidden = gelu_back(s_two.astype(F32), product("bot,bjo->bjt", e_three, left_two)).astype(BF16)
    h_mid = turn(hidden)
    e_one = back(product("bpt,bip->bit", h_mid, right_one).astype(BF16))
    s_three = turn(product("bjt,bjo->bot", act, left_two).astype(BF16))
    s_four = back(product("bit,bio->bot", s_three, right_two).astype(BF16))
    mixed = (x_home.astype(F32) + s_four.astype(F32)).astype(BF16)

    grad_rtwo = own_sum(product("bit,bot->bio", s_three, g_mid))
    grad_ltwo = own_sum(product("bjt,bot->bjo", act, e_three))
    grad_rone = own_sum(product("bit,bpt->bip", s_one, h_mid))
    grad_lone = product("bjt,bot->bjo", x_home, e_one).reshape(home, ring_z.size, ring_x.size, rows, size)
    grad_lone = ring_z.scatter(ring_x.scatter(grad_lone, 2), 1)
    input_grad = (g_home.astype(F32) + product("bot,bjo->bjt", e_one, left_one)).astype(BF16)
    return (
        mixed.reshape(home * size, tokens),
        input_grad.reshape(home * size, tokens),
        grad_lone,
        grad_rone,
        grad_ltwo,
        grad_rtwo,
    )


def solution(mesh):
    wide, factor = P("tensor", "dp"), P("tensor", "dp", None)
    return jax.shard_map(
        per_device,
        mesh=mesh,
        in_specs=(wide, wide, factor, factor, factor, factor),
        out_specs=(wide, wide, factor, factor, factor, factor),
        check_vma=False,
    )
```

time: 661 us -> 547 us (0.83)
  waiting for transfers between devices: 332 us -> 165 us
  blocking collectives: 152 us -> 0 us
  local copies, waits for them, and re-layouts: 60.8 us -> 157 us
  starting transfers between devices: 25.7 us -> 91.5 us
  matrix products: 52.9 us -> 80.5 us
  other arithmetic: 13.8 us -> 40.5 us
  between operations: 14.8 us -> 2.04 us
    ppermute x0 -> x44, waiting for transfers between devices: none -> 155 us  [send(): return lax.ppermute(value, self.axis, pairs)]
    all_to_all x3 -> x0, blocking collectives: 152 us -> none  [the longest x2 102 us: inner_back(): lax.all_to_all(spread(values), 'tensor', split_axis=1, concat_axis=0, til...]
    reduce_scatter x4 -> x0, waiting for transfers between devices: 131 us -> none  [the longest x1 71.3 us: per_device(): lax.psum_scatter(grad_rone, 'dp', scatter_dimension=1, tiled=True)]
    all_gather x4 -> x0, waiting for transfers between devices: 116 us -> none  [the longest x1 44.9 us: per_device(): lax.all_gather(first_left, 'dp', axis=1, tiled=True)]
    all_to_all x5 -> x4, waiting for transfers between devices: 82.6 us -> 10.5 us  [cross(): lax.all_to_all(pieces, 'tensor', split_axis=0, concat_axis=0, tiled=True)]
    ppermute x0 -> x44, starting transfers between devices: none -> 71.3 us  [send(): return lax.ppermute(value, self.axis, pairs)]
    transpose x0 -> x3, local copies, waits for them, and re-layouts: none -> 28.5 us  [the longest x2 21 us: go(): return got.transpose(1, 0, 2, 3).reshape(held, size, cut)]
    dot_general x12, matrix products: 52.9 us -> 80.5 us  [product(): return jnp.einsum(form, left, right, preferred_element_type=F32)]
  transfers between devices with their start and end apart: 13 -> 48, of which waited for: 9 -> 15; matrix products, arithmetic and copies ran while one was open for 15% -> 39% of each run, Pallas kernels for 0% -> 0%
where the time goes in v1:
time: 547 us; the launch traced here: 537 us
  waiting for transfers between devices  165 us (30%)
  local copies, waits for them, and re-layouts  157 us (29%)
  starting transfers between devices  91.5 us (17%)
  matrix products  80.5 us (15%)
  other arithmetic  40.5 us (7%)
    ppermute x44, waiting for transfers between devices, send(): return lax.ppermute(value, self.axis, pairs)  155 us
    dot_general x12, matrix products, product(): return jnp.einsum(form, left, right, preferred_element_type=F32)  80.5 us
    ppermute x44, starting transfers between devices, send(): return lax.ppermute(value, self.axis, pairs)  71.3 us
    unnamed x66, local copies, waits for them, and re-layouts  26.4 us
    add x13, other arithmetic, scatter(): total = total + self.send(term, step).astype(F32)  21.9 us
    transpose x2, local copies, waits for them, and re-layouts, go(): return got.transpose(1, 0, 2, 3).reshape(held, size, cut)  21 us
    all_to_all x4, starting transfers between devices, cross(): lax.all_to_all(pieces, 'tensor', split_axis=0, concat_axis=0, tiled=True)  20.2 us
    convert_element_type x2, other arithmetic, per_device(): mixed = (x_home.astype(F32) + s_four.astype(F32)).astype(BF16)  18.6 us
  transfers between devices with their start and end apart: 48, of which 15 were waited for; matrix products, arithmetic and copies ran while one was open for 39% of the time, Pallas kernels for 0%

profile of v1, /device:TPU:0, one launch (start us, length us, event | category | flops | bytes accessed | tf_op | source)
XLA Modules:
  0.0 536.6 jit_solution(4744936071792086389)
XLA Ops:
  9.7 6.9 %reshape.124 = bf16[32,1,128,4,128]{4,3,2,0,1:T(4,128)(2,1)} reshape(bf16[4096,512]{1,0:T(8,128)(2,1)} %param.7) | data formatting | bytes 8388608 | tf_op jit(solution)/shard_map/reshape;reshape | solution.py:87
  16.6 6.9 %copy.235 = bf16[32,1,128,4,128]{4,0,2,3,1:T(8,128)(2,1)} copy(bf16[32,1,128,4,128]{4,3,2,0,1:T(4,128)(2,1)} %reshape.124) | data formatting | bytes 8388608 | tf_op jit(solution)/shard_map/reshape | solution.py:88
  37.6 41.8 %collective-permute-done = bf16[32,16,128]{2,1,0:T(8,128)(2,1)S(1)} collective-permute-done((bf16[32,16,128]{2,1,0:T(8,128)(2,1)S(1)}, bf16[32,16,128]{2,1,0:T(8,128)(2,1)S(1)}, u32[]{:S(2)}, u32[]{:S(2)}) %collective-permute-start) | collective-permute-done | bytes 131104 | tf_op jit(solution)/shard_map/ppermute | solution.py:37
  90.6 11.2 %collective-permute-done.8 = bf16[2,32,16,128]{3,2,1,0:T(8,128)(2,1)S(1)} collective-permute-done((bf16[2,32,16,128]{3,2,1,0:T(8,128)(2,1)S(1)}, bf16[2,32,16,128]{3,2,1,0:T(8,128)(2,1)S(1)}, u32[]{:S(2)}, u32[]{:S(2)}) %collective-permute-start.8) | collective-permute-done | bytes 262176 | tf_op jit(solution)/shard_map/ppermute | solution.py:37
  110.2 12.7 %collective-permute-done.2 = bf16[2,32,16,128]{3,2,1,0:T(8,128)(2,1)S(1)} collective-permute-done((bf16[2,32,16,128]{3,2,1,0:T(8,128)(2,1)S(1)}, bf16[2,32,16,128]{3,2,1,0:T(8,128)(2,1)S(1)}, u32[]{:S(2)}, u32[]{:S(2)}) %collective-permute-start.2) | collective-permute-done | bytes 262176 | tf_op jit(solution)/shard_map/ppermute | solution.py:37
  135.3 21.3 %collective-permute-done.10 = bf16[4,2,32,16,128]{4,3,0,2,1:T(8,128)(2,1)S(1)} collective-permute-done((bf16[4,2,32,16,128]{4,3,0,2,1:T(8,128)(2,1)S(1)}, bf16[4,2,32,16,128]{4,3,0,2,1:T(8,128)(2,1)S(1)}, u32[]{:S(2)}, u32[]{:S(2)}) %collective-permute-start.10) | collective-permute-done | bytes 1048608 | tf_op jit(solution)/shard_map/ppermute | solution.py:37
  157.9 16.4 %collective-permute-done.4 = bf16[4,2,32,16,128]{4,3,0,2,1:T(8,128)(2,1)S(1)} collective-permute-done((bf16[4,2,32,16,128]{4,3,0,2,1:T(8,128)(2,1)S(1)}, bf16[4,2,32,16,128]{4,3,0,2,1:T(8,128)(2,1)S(1)}, u32[]{:S(2)}, u32[]{:S(2)}) %collective-permute-start.4) | collective-permute-done | bytes 1048608 | tf_op jit(solution)/shard_map/ppermute | solution.py:37
  178.8 6.9 %reshape.107 = bf16[32,1,128,4,128]{4,3,2,0,1:T(4,128)(2,1)} reshape(bf16[32,128,512]{2,1,0:T(8,128)(2,1)} %convolution_convert_fusion) | data formatting | bytes 8388608 | tf_op jit(solution)/shard_map/reshape | solution.py:87
  225.6 7.9 %fusion.22 = f32[128,128,128]{2,1,0:T(8,128)} fusion(bf16[128,128,128]{2,1,0:T(8,128)(2,1)S(1)} %bitcast.321, bf16[128,128,128]{2,0,1:T(8,128)(2,1)S(1)} %convert_bitcast_fusion.1), kind=kOutput, calls=%fused_computation.43 | convolution fusion | flops 536870912 | bytes 16777216 | tf_op jit(solution)/shard_map/bot,bjo->bjt/dot_general | solution.py:22
  233.5 10.5 %all-to-all-done = bf16[4,128,32,128]{3,1,2,0:T(8,128)(2,1)} async-done(((bf16[4,128,32,128]{3,1,2,0:T(8,128)(2,1)}), bf16[4,128,32,128]{3,1,2,0:T(8,128)(2,1)}, u32[]{:S(2)}, u32[]{:S(2)}) %all-to-all-start) | async-done | bytes 4194336 | tf_op jit(solution)/shard_map/all_to_all | solution.py:84
  244.0 17.7 %copy.161 = bf16[128,4,32,128]{3,2,1,0:T(8,128)(2,1)S(1)} copy(bf16[128,4,32,128]{3,0,2,1:T(8,128)(2,1)} %bitcast.65) | data formatting | bytes 8388608 | tf_op jit(solution)/shard_map/transpose | solution.py:89
  261.7 14.8 %fusion.6 = (bf16[128,128,128]{2,1,0:T(8,128)(2,1)S(1)}, f32[128,128,128]{2,1,0:T(8,128)}) fusion(f32[128,128,128]{2,1,0:T(8,128)} %fusion.22, bf16[128,128,128]{2,1,0:T(8,128)(2,1)S(1)} %bitcast.312, bf16[128,128,128]{2,1,0:T(8,128)(2,1)S(1)} %bitcast.319), kind=kOutput, calls=%fused_computation.9 | convolution fusion | flops 583008256 | bytes 29360128 | tf_op jit(solution)/shard_map/bit,bip->bpt/dot_general | solution.py:22
  276.5 17.2 %fusion.20 = f32[128,128,128]{2,1,0:T(8,128)} fusion(bf16[128,128,128]{2,0,1:T(8,128)(2,1)S(1)} %copy-done.15, f32[128,128,128]{2,1,0:T(8,128)} %get-tuple-element.25), kind=kOutput, calls=%fused_computation.41 | convolution fusion | flops 555745280 | bytes 20971520 | tf_op jit(solution)/shard_map/bjt,bot->bjo/dot_general | solution.py:22
  303.2 11.7 %convert_bitcast_fusion.2 = bf16[128,128,128]{2,0,1:T(8,128)(2,1)S(1)} fusion(bf16[128,128,128]{2,1,0:T(8,128)(2,1)} %bitcast.322, f32[128,128,128]{2,1,0:T(8,128)} %get-tuple-element.25), kind=kOutput, calls=%fused_computation.39 | convolution fusion | flops 557842432 | bytes 16777216 | tf_op jit(solution)/shard_map/bjt,bjo->bot/dot_general | solution.py:22
  338.6 6.5 %fusion.28 = bf16[128,128,128]{2,1,0:T(8,128)(2,1)S(1)} fusion(bf16[128,128,128]{2,1,0:T(8,128)(2,1)S(1)} %bitcast.300, bf16[128,128,128]{2,0,1:T(8,128)(2,1)} %copy-done.13), kind=kOutput, calls=%fused_computation.50 | convolution fusion | flops 538968064 | bytes 12582912 | tf_op jit(solution)/shard_map/bit,bio->bot/dot_general | solution.py:22
  380.8 22.5 %collective-permute-done.39 = bf16[2,32,4,16,128]{4,3,1,0,2:T(8,128)(2,1)} collective-permute-done((bf16[2,32,4,16,128]{4,3,1,0,2:T(8,128)(2,1)}, bf16[2,32,4,16,128]{4,3,1,0,2:T(8,128)(2,1)}, u32[]{:S(2)}, u32[]{:S(2)}) %collective-permute-start.39) | collective-permute-done | bytes 1048608 | tf_op jit(solution)/shard_map/ppermute | solution.py:37
  406.4 13.3 %collective-permute-start.40 = (bf16[2,32,16,128]{3,2,1,0:T(8,128)(2,1)}, bf16[2,32,16,128]{3,2,1,0:T(8,128)(2,1)}, u32[]{:S(2)}, u32[]{:S(2)}) collective-permute-start(bf16[2,32,16,128]{3,2,1,0:T(8,128)(2,1)} %get-tuple-element.12), channel_id=1, source_target_pairs={{0,8},{4,12},{8,16},{12,20},{16,24},{20,28},{24,0},{28,4},{1,9},{5... | collective-permute-start | bytes 786440 | tf_op jit(solution)/shard_map/ppermute | solution.py:37
  422.9 7.4 %copy.175 = bf16[32,1,128,4,128]{4,3,2,0,1:T(4,128)(2,1)} copy(bf16[32,1,128,4,128]{4,0,2,3,1:T(8,128)(2,1)} %bitcast.88) | data formatting | bytes 8388608 | tf_op jit(solution)/shard_map/transpose | solution.py:94
  430.4 7.4 %reshape.115 = bf16[32,128,512]{2,1,0:T(8,128)(2,1)} reshape(bf16[32,1,128,4,128]{4,3,2,0,1:T(4,128)(2,1)} %copy.175) | data formatting | bytes 8388608 | tf_op jit(solution)/shard_map/reshape | solution.py:94
  447.3 6.6 %convert_bitcast_fusion = f32[32,1,128,4,128]{4,0,2,3,1:T(8,128)} fusion(bf16[4,128,32,128]{3,2,1,0:T(8,128)(2,1)} %all-to-all-done.1), kind=kLoop, calls=%fused_computation.22 | loop fusion | flops 2097152 | bytes 12582912 | tf_op jit(solution)/shard_map/convert_element_type | solution.py:132
  453.9 10.9 %copy.168 = f32[32,1,128,4,128]{2,0,4,3,1:T(8,128)} copy(f32[32,1,128,4,128]{4,0,2,3,1:T(8,128)} %convert_bitcast_fusion) | data formatting | bytes 16777216 | tf_op jit(solution)/shard_map/convert_element_type | solution.py:132
  464.8 12.0 %fusion.15 = bf16[4096,512]{0,1:T(8,128)(2,1)} fusion(f32[64,8,32,128]{3,2,1,0:T(8,128)} %bitcast.305, bf16[4096,512]{0,1:T(8,128)(2,1)} %copy.138), kind=kLoop, calls=%fused_computation.19 | loop fusion | flops 6291456 | bytes 16777216 | tf_op jit(solution)/shard_map/convert_element_type | solution.py:132
  482.1 6.5 %copy.186 = bf16[4096,512]{1,0:T(8,128)(2,1)} copy(bf16[4096,512]{0,1:T(8,128)(2,1)} %fusion.15) | data formatting | bytes 8388608
  508.5 8.3 %collective-permute-done.29 = bf16[2,32,16,128]{3,2,1,0:T(8,128)(2,1)S(1)} collective-permute-done((bf16[2,32,16,128]{3,2,1,0:T(8,128)(2,1)S(1)}, bf16[2,32,16,128]{3,2,1,0:T(8,128)(2,1)S(1)}, u32[]{:S(2)}, u32[]{:S(2)}) %collective-permute-start.29) | collective-permute-done | bytes 262176 | tf_op jit(solution)/shard_map/ppermute | solution.py:37
  (240 shorter events, 229.2 us)
Async XLA Ops:
  0.6 30.4 %collective-permute-start.18 = (bf16[32,16,128]{2,1,0:T(8,128)(2,1)}, bf16[32,16,128]{2,1,0:T(8,128)(2,1)S(1)}, u32[]{:S(2)}, u32[]{:S(2)}) collective-permute-start(bf16[32,16,128]{2,1,0:T(8,128)(2,1)} %param.8), channel_id=1, source_target_pairs={{0,8},{4,12},{8,16},{12,20},{16,24},{20,28},{24,0},{28,4},{1,9},{5... | collective-permute-start | bytes 393224 | tf_op jit(solution)/shard_map/ppermute | solution.py:37
  23.5 167.5 %all-to-all-start.2 = ((bf16[4,128,32,128]{3,2,1,0:T(8,128)(2,1)}), bf16[4,128,32,128]{3,2,1,0:T(8,128)(2,1)}, u32[]{:S(2)}, u32[]{:S(2)}) async-start(bf16[4,128,32,128]{3,2,1,0:T(8,128)(2,1)} %bitcast.315), calls=%async_computation.2 | async-start | bytes 8388608 | tf_op jit(solution)/shard_map/all_to_all | solution.py:84
  29.0 50.4 %collective-permute-start = (bf16[32,16,128]{2,1,0:T(8,128)(2,1)S(1)}, bf16[32,16,128]{2,1,0:T(8,128)(2,1)S(1)}, u32[]{:S(2)}, u32[]{:S(2)}) collective-permute-start(bf16[32,16,128]{2,1,0:T(8,128)(2,1)S(1)} %copy-done.31), channel_id=1, source_target_pairs={{0,2},{1,3},{2,0},{3,1},{4,6},{5,7},{6,4},{7,5},{8,10},{9,11},{10,... | collective-permute-start | bytes 393224 | tf_op jit(solution)/shard_map/ppermute | solution.py:37
  31.0 49.4 %collective-permute-start.13 = (bf16[2,32,16,128]{3,2,1,0:T(8,128)(2,1)S(1)}, bf16[2,32,16,128]{3,2,1,0:T(8,128)(2,1)S(1)}, u32[]{:S(2)}, u32[]{:S(2)}) collective-permute-start(bf16[2,32,16,128]{3,2,1,0:T(8,128)(2,1)S(1)} %bitcast_dynamic-update-slice_fusion.28), channel_id=1, source_target_pairs={{0,8},{4,12},{8,16},{12,20},{16,24},{20,28},{24,0},{28,4},{1,9},{5... | collective-permute-start | bytes 786440 | tf_op jit(solution)/shard_map/ppermute | solution.py:37
  31.8 49.1 %collective-permute-start.14 = (bf16[2,32,16,128]{3,2,1,0:T(8,128)(2,1)S(1)}, bf16[2,32,16,128]{3,2,1,0:T(8,128)(2,1)S(1)}, u32[]{:S(2)}, u32[]{:S(2)}) collective-permute-start(bf16[2,32,16,128]{3,2,1,0:T(8,128)(2,1)S(1)} %bitcast_dynamic-update-slice_fusion.28), channel_id=1, source_target_pairs={{0,16},{4,20},{8,24},{12,28},{16,0},{20,4},{24,8},{28,12},{1,17},{... | collective-permute-start | bytes 786440 | tf_op jit(solution)/shard_map/ppermute | solution.py:37
  32.2 51.6 %collective-permute-start.15 = (bf16[2,32,16,128]{3,2,1,0:T(8,128)(2,1)S(1)}, bf16[2,32,16,128]{3,2,1,0:T(8,128)(2,1)S(1)}, u32[]{:S(2)}, u32[]{:S(2)}) collective-permute-start(bf16[2,32,16,128]{3,2,1,0:T(8,128)(2,1)S(1)} %bitcast_dynamic-update-slice_fusion.28), channel_id=1, source_target_pairs={{0,24},{4,28},{8,0},{12,4},{16,8},{20,12},{24,16},{28,20},{1,25},{... | collective-permute-start | bytes 786440 | tf_op jit(solution)/shard_map/ppermute | solution.py:37
  35.8 122.0 %collective-permute-start.21 = (bf16[4,32,16,128]{3,2,1,0:T(8,128)(2,1)S(1)}, bf16[4,32,16,128]{3,2,1,0:T(8,128)(2,1)S(1)}, u32[]{:S(2)}, u32[]{:S(2)}) collective-permute-start(bf16[4,32,16,128]{3,2,1,0:T(8,128)(2,1)S(1)} %bitcast_dynamic-update-slice_fusion.24), channel_id=1, source_target_pairs={{0,4},{4,0},{8,12},{12,8},{16,20},{20,16},{24,28},{28,24},{1,5},{5... | collective-permute-start | bytes 1572872 | tf_op jit(solution)/shard_map/ppermute | solution.py:37
  90.5 32.4 %collective-permute-start.2 = (bf16[2,32,16,128]{3,2,1,0:T(8,128)(2,1)S(1)}, bf16[2,32,16,128]{3,2,1,0:T(8,128)(2,1)S(1)}, u32[]{:S(2)}, u32[]{:S(2)}) collective-permute-start(bf16[2,32,16,128]{3,2,1,0:T(8,128)(2,1)S(1)} %bitcast_dynamic-update-slice_fusion.32), channel_id=1, source_target_pairs={{0,16},{4,20},{8,24},{12,28},{16,0},{20,4},{24,8},{28,12},{1,17},{... | collective-permute-start | bytes 786440 | tf_op jit(solution)/shard_map/ppermute | solution.py:37
  109.8 46.7 %collective-permute-start.10 = (bf16[4,2,32,16,128]{4,3,0,2,1:T(8,128)(2,1)S(1)}, bf16[4,2,32,16,128]{4,3,0,2,1:T(8,128)(2,1)S(1)}, u32[]{:S(2)}, u32[]{:S(2)}) collective-permute-start(bf16[4,2,32,16,128]{4,3,0,2,1:T(8,128)(2,1)S(1)} %bitcast_dynamic-update-slice_fusion.16), channel_id=1, source_target_pairs={{0,4},{4,0},{8,12},{12,8},{16,20},{20,16},{24,28},{28,24},{1,5},{5... | collective-permute-start | bytes 3145736 | tf_op jit(solution)/shard_map/ppermute | solution.py:37
  123.0 51.2 %collective-permute-start.4 = (bf16[4,2,32,16,128]{4,3,0,2,1:T(8,128)(2,1)S(1)}, bf16[4,2,32,16,128]{4,3,0,2,1:T(8,128)(2,1)S(1)}, u32[]{:S(2)}, u32[]{:S(2)}) collective-permute-start(bf16[4,2,32,16,128]{4,3,0,2,1:T(8,128)(2,1)S(1)} %bitcast_dynamic-update-slice_fusion.20), channel_id=1, source_target_pairs={{0,4},{4,0},{8,12},{12,8},{16,20},{20,16},{24,28},{28,24},{1,5},{5... | collective-permute-start | bytes 3145736 | tf_op jit(solution)/shard_map/ppermute | solution.py:37
  135.3 74.5 %collective-permute-start.17 = (bf16[2,4,2,32,16,128]{5,4,0,1,3,2:T(8,128)(2,1)}, bf16[2,4,2,32,16,128]{5,4,0,1,3,2:T(8,128)(2,1)}, u32[]{:S(2)}, u32[]{:S(2)}) collective-permute-start(bf16[2,4,2,32,16,128]{5,4,0,1,3,2:T(8,128)(2,1)} %bitcast_dynamic-update-slice_fusion.11), channel_id=1, source_target_pairs={{0,1},{1,0},{2,3},{3,2},{4,5},{5,4},{6,7},{7,6},{8,9},{9,8},{10,11... | collective-permute-start | bytes 6291464 | tf_op jit(solution)/shard_map/ppermute | solution.py:37
  157.7 55.9 %collective-permute-start.11 = (bf16[2,4,2,32,16,128]{5,4,0,1,3,2:T(8,128)(2,1)}, bf16[2,4,2,32,16,128]{5,4,0,1,3,2:T(8,128)(2,1)}, u32[]{:S(2)}, u32[]{:S(2)}) collective-permute-start(bf16[2,4,2,32,16,128]{5,4,0,1,3,2:T(8,128)(2,1)} %bitcast_dynamic-update-slice_fusion.7), channel_id=1, source_target_pairs={{0,1},{1,0},{2,3},{3,2},{4,5},{5,4},{6,7},{7,6},{8,9},{9,8},{10,11... | collective-permute-start | bytes 6291464 | tf_op jit(solution)/shard_map/ppermute | solution.py:37
  175.4 42.2 %collective-permute-start.5 = (bf16[2,4,2,32,16,128]{5,4,0,1,3,2:T(8,128)(2,1)}, bf16[2,4,2,32,16,128]{5,4,0,1,3,2:T(8,128)(2,1)}, u32[]{:S(2)}, u32[]{:S(2)}) collective-permute-start(bf16[2,4,2,32,16,128]{5,4,0,1,3,2:T(8,128)(2,1)} %bitcast_dynamic-update-slice_fusion.9), channel_id=1, source_target_pairs={{0,1},{1,0},{2,3},{3,2},{4,5},{5,4},{6,7},{7,6},{8,9},{9,8},{10,11... | collective-permute-start | bytes 6291464 | tf_op jit(solution)/shard_map/ppermute | solution.py:37
  190.9 53.1 %all-to-all-start = ((bf16[4,128,32,128]{3,1,2,0:T(8,128)(2,1)}), bf16[4,128,32,128]{3,1,2,0:T(8,128)(2,1)}, u32[]{:S(2)}, u32[]{:S(2)}) async-start(bf16[4,128,32,128]{3,1,2,0:T(8,128)(2,1)} %bitcast.318), calls=%async_computation | async-start | bytes 8388608 | tf_op jit(solution)/shard_map/all_to_all | solution.py:84
  297.9 57.9 %all-to-all-start.3 = ((bf16[4,128,32,128]{3,2,1,0:T(8,128)(2,1)}), bf16[4,128,32,128]{3,2,1,0:T(8,128)(2,1)}, u32[]{:S(2)}, u32[]{:S(2)}) async-start(bf16[4,128,32,128]{3,2,1,0:T(8,128)(2,1)} %bitcast.317), calls=%async_computation.3 | async-start | bytes 8388608 | tf_op jit(solution)/shard_map/all_to_all | solution.py:84
  329.7 30.9 %collective-permute-start.38 = (bf16[2,32,4,2,16,128]{5,4,1,0,2,3:T(8,128)(2,1)}, bf16[2,32,4,2,16,128]{5,4,1,0,2,3:T(8,128)(2,1)}, u32[]{:S(2)}, u32[]{:S(2)}) collective-permute-start(bf16[2,32,4,2,16,128]{5,4,1,0,2,3:T(8,128)(2,1)} %fusion.33), channel_id=1, source_target_pairs={{0,1},{1,0},{2,3},{3,2},{4,5},{5,4},{6,7},{7,6},{8,9},{9,8},{10,11... | collective-permute-start | bytes 6291464 | tf_op jit(solution)/shard_map/ppermute | solution.py:37
  335.2 39.1 %collective-permute-start.26 = (bf16[2,32,4,2,16,128]{5,4,1,0,2,3:T(8,128)(2,1)}, bf16[2,32,4,2,16,128]{5,4,1,0,2,3:T(8,128)(2,1)}, u32[]{:S(2)}, u32[]{:S(2)}) collective-permute-start(bf16[2,32,4,2,16,128]{5,4,1,0,2,3:T(8,128)(2,1)} %fusion.31), channel_id=1, source_target_pairs={{0,1},{1,0},{2,3},{3,2},{4,5},{5,4},{6,7},{7,6},{8,9},{9,8},{10,11... | collective-permute-start | bytes 6291464 | tf_op jit(solution)/shard_map/ppermute | solution.py:37
  355.8 91.5 %all-to-all-start.1 = ((bf16[4,128,32,128]{3,2,1,0:T(8,128)(2,1)}), bf16[4,128,32,128]{3,2,1,0:T(8,128)(2,1)}, u32[]{:S(2)}, u32[]{:S(2)}) async-start(bf16[4,128,32,128]{3,2,1,0:T(8,128)(2,1)} %bitcast.316), calls=%async_computation.1 | async-start | bytes 8388608 | tf_op jit(solution)/shard_map/all_to_all | solution.py:84
  367.1 36.1 %collective-permute-start.39 = (bf16[2,32,4,16,128]{4,3,1,0,2:T(8,128)(2,1)}, bf16[2,32,4,16,128]{4,3,1,0,2:T(8,128)(2,1)}, u32[]{:S(2)}, u32[]{:S(2)}) collective-permute-start(bf16[2,32,4,16,128]{4,3,1,0,2:T(8,128)(2,1)} %fusion.36), channel_id=1, source_target_pairs={{0,4},{4,0},{8,12},{12,8},{16,20},{20,16},{24,28},{28,24},{1,5},{5... | collective-permute-start | bytes 3145736 | tf_op jit(solution)/shard_map/ppermute | solution.py:37
  377.9 98.8 %collective-permute-start.27 = (bf16[2,32,4,16,128]{4,3,1,0,2:T(8,128)(2,1)S(1)}, bf16[2,32,4,16,128]{4,3,1,0,2:T(8,128)(2,1)}, u32[]{:S(2)}, u32[]{:S(2)}) collective-permute-start(bf16[2,32,4,16,128]{4,3,1,0,2:T(8,128)(2,1)S(1)} %fusion.34), channel_id=1, source_target_pairs={{0,4},{4,0},{8,12},{12,8},{16,20},{20,16},{24,28},{28,24},{1,5},{5... | collective-permute-start | bytes 3145736 | tf_op jit(solution)/shard_map/ppermute | solution.py:37
  406.4 83.9 %collective-permute-start.40 = (bf16[2,32,16,128]{3,2,1,0:T(8,128)(2,1)}, bf16[2,32,16,128]{3,2,1,0:T(8,128)(2,1)}, u32[]{:S(2)}, u32[]{:S(2)}) collective-permute-start(bf16[2,32,16,128]{3,2,1,0:T(8,128)(2,1)} %get-tuple-element.12), channel_id=1, source_target_pairs={{0,8},{4,12},{8,16},{12,20},{16,24},{20,28},{24,0},{28,4},{1,9},{5... | collective-permute-start | bytes 786440 | tf_op jit(solution)/shard_map/ppermute | solution.py:37
  419.7 71.8 %collective-permute-start.41 = (bf16[2,32,16,128]{3,2,1,0:T(8,128)(2,1)}, bf16[2,32,16,128]{3,2,1,0:T(8,128)(2,1)}, u32[]{:S(2)}, u32[]{:S(2)}) collective-permute-start(bf16[2,32,16,128]{3,2,1,0:T(8,128)(2,1)} %get-tuple-element.14), channel_id=1, source_target_pairs={{0,16},{4,20},{8,24},{12,28},{16,0},{20,4},{24,8},{28,12},{1,17},{... | collective-permute-start | bytes 786440 | tf_op jit(solution)/shard_map/ppermute | solution.py:37
  419.7 72.6 %collective-permute-start.42 = (bf16[2,32,16,128]{3,2,1,0:T(8,128)(2,1)}, bf16[2,32,16,128]{3,2,1,0:T(8,128)(2,1)}, u32[]{:S(2)}, u32[]{:S(2)}) collective-permute-start(bf16[2,32,16,128]{3,2,1,0:T(8,128)(2,1)} %get-tuple-element.13), channel_id=1, source_target_pairs={{0,24},{4,28},{8,0},{12,4},{16,8},{20,12},{24,16},{28,20},{1,25},{... | collective-permute-start | bytes 786440 | tf_op jit(solution)/shard_map/ppermute | solution.py:37
  422.9 72.2 %collective-permute-start.34 = (bf16[2,32,16,128]{3,2,1,0:T(8,128)(2,1)}, bf16[2,32,16,128]{3,2,1,0:T(8,128)(2,1)}, u32[]{:S(2)}, u32[]{:S(2)}) collective-permute-start(bf16[2,32,16,128]{3,2,1,0:T(8,128)(2,1)} %get-tuple-element.15), channel_id=1, source_target_pairs={{0,8},{4,12},{8,16},{12,20},{16,24},{20,28},{24,0},{28,4},{1,9},{5... | collective-permute-start | bytes 786440 | tf_op jit(solution)/shard_map/ppermute | solution.py:37
  (56 other events, 842.3 us)

commit v2 on v1

--- a/solution.py
+++ b/solution.py
@@ -1,13 +1,18 @@
+import functools
 import math
 
 import jax
 import jax.numpy as jnp
 from jax import lax
+from jax.experimental import pallas as pl
+from jax.experimental.pallas import tpu as pltpu
 from jax.sharding import PartitionSpec as P
 
 BF16 = jnp.bfloat16
 F32 = jnp.float32
 LANES = 128
+PAD = 8
+VMEM_BYTES = 48 * 1024 * 1024
 
 
 def gelu_value(values):
@@ -18,8 +23,472 @@
     return jax.vjp(gelu_value, values)[1](upstream)[0]
 
 
+def gelu_both(v):
+    root, cubic = 0.7978845608028654, 0.044715
+    square = v * v
+    t = jnp.tanh(root * (v + cubic * (v * square)))
+    half = 0.5 * (1.0 + t)
+    slope = half + (0.5 * v) * (1.0 - t * t) * (root + (3.0 * cubic * root) * square)
+    return v * half, slope
+
+
 def product(form, left, right):
     return jnp.einsum(form, left, right, preferred_element_type=F32)
+
+
+def dot_nn(left, right):
+    return lax.dot_general(left, right, (((1,), (0,)), ((), ())), preferred_element_type=F32)
+
+
+def dot_tn(left, right):
+    return lax.dot_general(left, right, (((0,), (0,)), ((), ())), preferred_element_type=F32)
+
+
+def dot_nt(left, right):
+    return lax.dot_general(left, right, (((1,), (1,)), ((), ())), preferred_element_type=F32)
+
+
+def call(body, out, grid, in_specs, out_specs, scratch, args, scalars=None, dots=0):
+    moved = sum(math.prod(a.shape) * a.dtype.itemsize for a in args)
+    moved += sum(math.prod(o.shape) * o.dtype.itemsize for o in jax.tree.leaves(out))
+    spec = pltpu.PrefetchScalarGridSpec(
+        num_scalar_prefetch=0 if scalars is None else 1,
+        grid=grid,
+        in_specs=in_specs,
+        out_specs=out_specs,
+        scratch_shapes=scratch,
+    )
+    return pl.pallas_call(
+        body,
+        out_shape=out,
+        grid_spec=spec,
+        compiler_params=pltpu.CompilerParams(
+            dimension_semantics=("arbitrary",) * len(grid), vmem_limit_bytes=VMEM_BYTES
+        ),
+        cost_estimate=pl.CostEstimate(flops=dots, bytes_accessed=moved, transcendentals=0),
+    )(*(() if scalars is None else (scalars,)), *args)
+
+
+def shape(dims, dtype=BF16):
+    return jax.ShapeDtypeStruct(dims, dtype)
+
+
+def each(count, body, unroll=4):
+    def step(k, carry):
+        body(k)
+        return carry
+
+    lax.fori_loop(0, count, step, 0, unroll=math.gcd(count, unroll))
+
+
+def during(phase, steps):
+    return lambda p, j: jnp.where(p == phase, j, jnp.where(p < phase, 0, steps - 1))
+
+
+def stacked(ref, k):
+    return jnp.concatenate([ref[c, k] for c in range(ref.shape[0])], axis=0)
+
+
+def deal_kernel(g_ref, out_ref, turned):
+    home, size, _ = g_ref.shape
+    pitch = home + PAD
+
+    def store(o):
+        turned[pl.ds(o, size, stride=pitch), :] = g_ref[o].astype(F32)
+
+    def load(b):
+        out_ref[0, b] = turned[pl.ds(pl.multiple_of(b * pitch, 8), home), :].astype(BF16)
+
+    each(home, store)
+    each(size, load, 8)
+
+
+def deal(g_home, share, cut):
+    home, size, _ = g_home.shape
+    return call(
+        deal_kernel,
+        shape((share, size, home, cut)),
+        (share,),
+        [pl.BlockSpec((home, size, cut), lambda s: (0, 0, s))],
+        pl.BlockSpec((1, size, home, cut), lambda s: (s, 0, 0, 0)),
+        [pltpu.VMEM((size * (home + PAD), cut), F32)],
+        (g_home,),
+    )
+
+
+def first_kernel(x_ref, w_ref, out_ref, turned):
+    home, size, _ = x_ref.shape
+    pitch = home + PAD
+
+    def store(b):
+        turned[pl.ds(b, size, stride=pitch), :] = dot_tn(w_ref[b], x_ref[b])
+
+    def load(o):
+        out_ref[0, o] = turned[pl.ds(pl.multiple_of(o * pitch, 8), home), :].astype(BF16)
+
+    each(home, store)
+    each(size, load, 8)
+
+
+def first_stage(x_home, left_one, share, cut):
+    home, size, _ = x_home.shape
+    return call(
+        first_kernel,
+        shape((share, size, home, cut)),
+        (share,),
+        [
+            pl.BlockSpec((home, size, cut), lambda s: (0, 0, s)),
+            pl.BlockSpec((home, size, size), lambda s: (0, 0, 0)),
+        ],
+        pl.BlockSpec((1, size, home, cut), lambda s: (s, 0, 0, 0)),
+        [pltpu.VMEM((size * (home + PAD), cut), F32)],
+        (x_home, left_one),
+        dots=2 * home * size * size * share * cut,
+    )
+
+
+def last_kernel(e_ref, x_ref, g_ref, w_ref, out_ref, grad_ref, turned):
+    _, blocks, home, _ = e_ref.shape
+    pitch = blocks + PAD
+    first = pl.program_id(0) == 0
+
+    def store(o):
+        turned[pl.ds(o, home, stride=pitch), :] = e_ref[0, o].astype(F32)
+
+    def load(b):
+        e_b = turned[pl.ds(pl.multiple_of(b * pitch, 8), blocks), :].astype(BF16)
+        out_ref[b] = (g_ref[b].astype(F32) + dot_nn(w_ref[b], e_b)).astype(BF16)
+        before = jnp.where(first, 0.0, grad_ref[b])
+        grad_ref[b] = before + dot_nt(x_ref[b], e_b)
+
+    each(blocks, store, 8)
+    each(home, load)
+
+
+def last_stage(e_got, x_home, g_home, left_one):
+    share, blocks, home, cut = e_got.shape
+    size = x_home.shape[1]
+    wide = pl.BlockSpec((home, size, cut), lambda s: (0, 0, s))
+    fixed = pl.BlockSpec((home, size, size), lambda s: (0, 0, 0))
+    return call(
+        last_kernel,
+        (shape(g_home.shape), shape((home, size, size), F32)),
+        (share,),
+        [pl.BlockSpec((1, blocks, home, cut), lambda s: (s, 0, 0, 0)), wide, wide, fixed],
+        (wide, fixed),
+        [pltpu.VMEM((home * (blocks + PAD), cut), F32)],
+        (e_got, x_home, g_home, left_one),
+        dots=4 * home * size * size * share * cut,
+    )
+
+
+def mixed_kernel(s_ref, x_ref, out_ref):
+    out_ref[...] = (x_ref[...].astype(F32) + s_ref[0].astype(F32)).astype(BF16)
+
+
+def add_home(s_got, x_home):
+    share, home, blocks, cut = s_got.shape
+    per = math.gcd(home, 16)
+    wide = pl.BlockSpec((per, blocks, cut), lambda s, h: (h, 0, s))
+    return call(
+        mixed_kernel,
+        shape(x_home.shape),
+        (share, home // per),
+        [pl.BlockSpec((1, per, blocks, cut), lambda s, h: (s, h, 0, 0)), wide],
+        wide,
+        [],
+        (s_got, x_home),
+    )
+
+
+def back_two_kernel(g_ref, w_ref, out_ref, turned):
+    per, size, _ = out_ref.shape
+    pitch = size + PAD
+    phase, j = pl.program_id(0), pl.program_id(1)
+
+    @pl.when(phase == 0)
+    def _():
+        def body(k):
+            turned[pl.ds(j * per + k, size, stride=pitch), :] = dot_nn(w_ref[k], stacked(g_ref, k))
+
+        each(per, body)
+
+    @pl.when(phase == 1)
+    def _():
+        def body(k):
+            out_ref[k] = turned[pl.ds(pl.multiple_of((j * per + k) * pitch, 8), size), :].astype(BF16)
+
+        each(per, body, 8)
+
+
+def middle_sizes(weights):
+    blocks, size, _ = weights.shape
+    per = math.gcd(blocks, 32)
+    return blocks, size, per, blocks // per
+
+
+def back_two(g_mid, right_two):
+    blocks, size, per, steps = middle_sizes(right_two)
+    n, _, home, cut = g_mid.shape
+    at = [during(phase, steps) for phase in range(2)]
+    return call(
+        back_two_kernel,
+        shape((blocks, size, cut)),
+        (2, steps),
+        [
+            pl.BlockSpec((n, per, home, cut), lambda p, j: (0, at[0](p, j), 0, 0)),
+            pl.BlockSpec((per, size, size), lambda p, j: (at[0](p, j), 0, 0)),
+        ],
+        pl.BlockSpec((per, size, cut), lambda p, j: (at[1](p, j), 0, 0)),
+        [pltpu.VMEM((blocks * (size + PAD), cut), F32)],
+        (g_mid, right_two),
+        dots=2 * blocks * size * size * cut,
+    )
+
+
+def middle_kernel(s_ref, one_ref, two_ref, e_ref, act_ref, h_ref, out_ref, turned, hidden):
+    per, size, _ = act_ref.shape
+    pitch = size + PAD
+    n, _, home, _ = s_ref.shape
+    phase, j = pl.program_id(0), pl.program_id(1)
+
+    def rows(k):
+        return pl.ds(pl.multiple_of((j * per + k) * pitch, 8), size)
+
+    def column(k):
+        return pl.ds(j * per + k, size, stride=pitch)
+
+    @pl.when(phase == 0)
+    def _():
+        def body(k):
+            turned[column(k), :] = dot_tn(one_ref[k], stacked(s_ref, k))
+
+        each(per, body)
+
+    @pl.when(phase == 1)
+    def _():
+        def body(k):
+            v = turned[rows(k), :].astype(BF16).astype(F32)
+            value, slope = gelu_both(v)
+            act_ref[k] = value.astype(BF16)
+            hidden[column(k), :] = slope * dot_nn(two_ref[k], e_ref[k])
+
+        each(per, body)
+
+    @pl.when(phase == 2)
+    def _():
+        def body(k):
+            h = hidden[rows(k), :].astype(BF16)
+            h_ref[k] = h
+            e = dot_nn(one_ref[k], h).astype(BF16)
+            for c in range(n):
+                out_ref[c, k] = e[c * home : (c + 1) * home]
+
+        each(per, body)
+
+
+def middle(s_mid, e_mid, right_one, left_two):
+    blocks, size, per, steps = middle_sizes(right_one)
+    n, _, home, cut = s_mid.shape
+    at = [during(phase, steps) for phase in range(3)]
+    block = (per, size, cut)
+    pieces = (n, per, home, cut)
+
+    def one(p, j):
+        return (jnp.where(p == 1, 0, j), 0, 0)
+
+    return call(
+        middle_kernel,
+        (shape((blocks, size, cut)), shape((blocks, size, cut)), shape(s_mid.shape)),
+        (3, steps),
+        [
+            pl.BlockSpec(pieces, lambda p, j: (0, at[0](p, j), 0, 0)),
+            pl.BlockSpec((per, size, size), one),
+            pl.BlockSpec((per, size, size), lambda p, j: (at[1](p, j), 0, 0)),
+            pl.BlockSpec(block, lambda p, j: (at[1](p, j), 0, 0)),
+        ],
+        (
+            pl.BlockSpec(block, lambda p, j: (at[1](p, j), 0, 0)),
+            pl.BlockSpec(block, lambda p, j: (at[2](p, j), 0, 0)),
+            pl.BlockSpec(pieces, lambda p, j: (0, at[2](p, j), 0, 0)),
+        ),
+        [pltpu.VMEM((blocks * (size + PAD), cut), F32)] * 2,
+        (s_mid, right_one, left_two, e_mid),
+        dots=6 * blocks * size * size * cut,
+    )
+
+
+def forward_two_kernel(act_ref, left_ref, right_ref, third_ref, out_ref, turned, fourth):
+    per, size, _ = third_ref.shape
+    pitch = size + PAD
+    phase, j = pl.program_id(0), pl.program_id(1)
+
+    def rows(k):
+        return pl.ds(pl.multiple_of((j * per + k) * pitch, 8), size)
+
+    def column(k):
+        return pl.ds(j * per + k, size, stride=pitch)
+
+    @pl.when(phase == 0)
+    def _():
+        def body(k):
+            turned[column(k), :] = dot_tn(left_ref[k], act_ref[k])
+
+        each(per, body)
+
+    @pl.when(phase == 1)
+    def _():
+        def body(k):
+            third = turned[rows(k), :].astype(BF16)
+            third_ref[k] = third
+            fourth[column(k), :] = dot_tn(right_ref[k], third)
+
+        each(per, body)
+
+    @pl.when(phase == 2)
+    def _():
+        def body(k):
+            out_ref[k] = fourth[rows(k), :].astype(BF16)
+
+        each(per, body, 8)
+
+
+def forward_two(act, left_two, right_two):
+    blocks, size, per, steps = middle_sizes(left_two)
+    cut = act.shape[2]
+    at = [during(phase, steps) for phase in range(3)]
+    block = (per, size, cut)
+    return call(
+        forward_two_kernel,
+        (shape(act.shape), shape(act.shape)),
+        (3, steps),
+        [
+            pl.BlockSpec(block, lambda p, j: (at[0](p, j), 0, 0)),
+            pl.BlockSpec((per, size, size), lambda p, j: (at[0](p, j), 0, 0)),
+            pl.BlockSpec((per, size, size), lambda p, j: (at[1](p, j), 0, 0)),
+        ],
+        (
+            pl.BlockSpec(block, lambda p, j: (at[1](p, j), 0, 0)),
+            pl.BlockSpec(block, lambda p, j: (at[2](p, j), 0, 0)),
+        ),
+        [pltpu.VMEM((blocks * (size + PAD), cut), F32)] * 2,
+        (act, left_two, right_two),
+        dots=4 * blocks * size * size * cut,
+    )
+
+
+def grads_kernel(near, split, pos_ref, *refs):
+    pairs = len(split)
+    keep_ref, send_ref = refs[2 * pairs :]
+    rc = pl.program_id(0)
+    per = keep_ref.shape[2]
+
+    def fill(out_ref):
+        def body(k):
+            for n in range(pairs):
+                sides = [stacked(refs[2 * n + m], k) if split[n][m] else refs[2 * n + m][k] for m in range(2)]
+                out_ref[n, 0, k] = dot_nt(*sides).astype(out_ref.dtype)
+
+        each(per, body)
+
+    @pl.when(rc == 0)
+    def _():
+        fill(keep_ref)
+
+    if near > 1:
+
+        @pl.when(rc > 0)
+        def _():
+            fill(send_ref)
+
+
+def grads(pairs, home, size, far, near, pos):
+    per = math.gcd(home, 16)
+    subs = home // per
+    split = tuple(tuple(a.ndim == 4 for a in pair) for pair in pairs)
+
+    def block(rc, y, s, pos):
+        return (y * near + lax.rem(pos[1] + rc, near)) * subs + s
+
+    specs, args = [], []
+    for pair in pairs:
+        for a in pair:
+            args.append(a)
+            if a.ndim == 4:
+                specs.append(pl.BlockSpec((a.shape[0], per) + a.shape[2:], lambda rc, y, s, pos: (0, block(rc, y, s, pos), 0, 0)))
+            else:
+                specs.append(pl.BlockSpec((per,) + a.shape[1:], lambda rc, y, s, pos: (block(rc, y, s, pos), 0, 0)))
+    n = len(pairs)
+    dims = (n, far, home, size, size)
+
+    def kept(rc, y, s, pos):
+        return (0, jnp.where(rc == 0, y, far - 1), jnp.where(rc == 0, s, subs - 1), 0, 0)
+
+    def sent(rc, y, s, pos):
+        return (0, jnp.where(rc == 0, 0, y), jnp.where(rc == 0, 0, s), 0, 0)
+
+    cut = args[0].shape[-1]
+    return call(
+        functools.partial(grads_kernel, near, split),
+        (shape(dims, F32), shape(dims)),
+        (near, far, subs),
+        specs,
+        (pl.BlockSpec((n, 1, per, size, size), kept), pl.BlockSpec((n, 1, per, size, size), sent)),
+        [],
+        tuple(args),
+        scalars=pos,
+        dots=2 * n * far * near * home * size * size * cut,
+    )
+
+
+def join_kernel(near, n_x, pos_ref, *refs):
+    out_ref = refs[-1]
+    rc = pl.program_id(0)
+    n_z, _, _, rows, _ = refs[0].shape
+
+    for c in range(near):
+
+        @pl.when(rc == c)
+        def _():
+            for rx in range(n_x):
+                for rz in range(n_z):
+                    z = lax.rem(pos_ref[2] - rz + n_z, n_z)
+                    x = lax.rem(pos_ref[3] - rx + n_x, n_x)
+                    at = pl.multiple_of((z * n_x + x) * rows, rows)
+                    out_ref[:, pl.ds(at, rows), :] = refs[c * n_x + rx][rz, 0]
+
+
+def join(pieces, pos):
+    near, n_x = len(pieces), len(pieces[0])
+    n_z, far, home, rows, size = pieces[0][0].shape
+    per = math.gcd(home, 16)
+    subs = home // per
+    specs = []
+    for c in range(near):
+        for _ in range(n_x):
+
+            def index(rc, ry, s, pos, c=c):
+                y = jnp.where(rc == c, ry, jnp.where(rc < c, 0, far - 1))
+                return (0, y, jnp.where(rc == c, s, jnp.where(rc < c, 0, subs - 1)), 0, 0)
+
+            specs.append(pl.BlockSpec((n_z, 1, per, rows, size), index))
+
+    def out_index(rc, ry, s, pos):
+        y = lax.rem(pos[0] - ry + far, far)
+        core = lax.rem(pos[1] - rc + near, near)
+        return ((y * near + core) * subs + s, 0, 0)
+
+    full = n_z * n_x * rows
+    return call(
+        functools.partial(join_kernel, near, n_x),
+        shape((near * far * home, full, size)),
+        (near, far, subs),
+        specs,
+        pl.BlockSpec((per, full, size), out_index),
+        [],
+        tuple(p for row in pieces for p in row),
+        scalars=pos,
+    )
 
 
 class Ring:
@@ -35,6 +504,9 @@
             own = src // self.stride % self.size
             pairs.append((src, src + ((own + step) % self.size - own) * self.stride))
         return lax.ppermute(value, self.axis, pairs)
+
+    def sends(self, value):
+        return [self.send(value, step) for step in range(1, self.size)]
 
     def gather(self, value):
         if self.size == 1:
@@ -64,24 +536,78 @@
     return size // low, low
 
 
-def per_device(inputs, cotangent, first_left, first_right, second_left, second_right):
-    n_dp, n_tensor = lax.axis_size("dp"), lax.axis_size("tensor")
-    home, rows, size = first_left.shape
-    tokens = inputs.shape[1]
-    share = math.gcd(n_tensor, max(1, tokens // LANES))
+def cross(pieces):
+    return lax.all_to_all(pieces, "tensor", split_axis=0, concat_axis=0, tiled=True)
+
+
+def after(value, *others):
+    return lax.optimization_barrier((value,) + others)[0]
+
+
+def whole_tokens(x_home, g_home, factors, rings, share, cut):
+    home, size, tokens = x_home.shape
+    ring_y, ring_core, ring_z, ring_x = rings
+    first_left = factors[0]
+    rows = first_left.shape[1]
+    pos = jnp.stack([ring.here() for ring in rings]).astype(jnp.int32)
+
+    mine = jnp.stack([factors[3], factors[1], factors[2]])
+    from_y = [mine] + ring_y.sends(mine)
+    one = [first_left] + ring_z.sends(first_left)
+    one = jnp.stack(one)
+    zero = jnp.zeros_like(pos[:1])
+    one = join([[p[:, None] for p in [one] + ring_x.sends(one)]], jnp.concatenate([zero, zero, pos[2:]]))
+
+    g_mid = cross(deal(g_home, share, cut))
+
+    wholes, before = [], None
+    for n in range(3):
+        start = jnp.stack([part[n] for part in from_y])
+        if before is not None:
+            start = after(start, before)
+        from_z = jnp.stack([start] + ring_z.sends(start))
+        before = from_z
+        from_x = [from_z] + ring_x.sends(from_z)
+        from_core = [[p] + ring_core.sends(p) for p in from_x]
+        wholes.append(join([[p[c] for p in from_core] for c in range(ring_core.size)], pos))
+    right_two, right_one, left_two = wholes
+
+    s_mid = cross(first_stage(x_home, one, share, cut))
+    e_mid = back_two(g_mid, right_two)
+    act, hidden, e_out = middle(s_mid, e_mid, right_one, left_two)
+    e_got = cross(e_out)
+    third, s_out = forward_two(act, left_two, right_two)
+    s_out = s_out.reshape(share, home, size, cut)
+    s_got = cross(after(s_out, e_got))
+
+    def own_sum(pairs):
+        keep, send = grads(pairs, home, size, ring_y.size, ring_core.size, pos)
+        total = keep
+        if ring_core.size > 1:
+            total = total + ring_core.send(send, 1).astype(F32)
+        split = total.reshape(len(pairs), ring_y.size, home, ring_z.size, ring_x.size, rows, size)
+        split = ring_x.scatter(split, 4)
+        split = ring_z.scatter(split, 3)
+        return ring_y.scatter(split, 1)
+
+    grad_ltwo, grad_rone = own_sum([(act, e_mid), (s_mid, hidden)])
+    grad_rtwo = own_sum([(third, g_mid)])[0]
+
+    input_grad, grad_lone = last_stage(e_got, x_home, g_home, one)
+    grad_lone = grad_lone.reshape(home, ring_z.size, ring_x.size, rows, size)
+    grad_lone = ring_z.scatter(ring_x.scatter(grad_lone, 2), 1)
+    mixed = add_home(s_got, x_home)
+    return mixed, input_grad, grad_lone, grad_rone, grad_ltwo, grad_rtwo
+
+
+def split_blocks(x_home, g_home, factors, rings, share, cut):
+    home, size, tokens = x_home.shape
+    ring_y, ring_core, ring_z, ring_x = rings
+    rows = factors[0].shape[1]
+    n_tensor = lax.axis_size("tensor")
     groups = n_tensor // share
     held = home * share
-    cut = tokens // share
-
-    far, near = halves(share)
-    ring_y, ring_core = Ring("tensor", near, far), Ring("tensor", 1, near)
-    far, near = halves(n_dp)
-    ring_z, ring_x = Ring("dp", near, far), Ring("dp", 1, near)
-
     same_tokens = [[group * share + part for group in range(groups)] for part in range(share)]
-
-    def cross(pieces):
-        return lax.all_to_all(pieces, "tensor", split_axis=0, concat_axis=0, tiled=True)
 
     def go(values):
         pieces = values.reshape(home, groups, held, share, cut).transpose(1, 3, 2, 0, 4)
@@ -94,8 +620,6 @@
         return got.transpose(3, 0, 2, 1, 4).reshape(home, size, tokens)
 
     def turn(values):
-        if groups == 1:
-            return jnp.swapaxes(values, 0, 1)
         moved = lax.all_to_all(
             values.reshape(held, groups, held, cut), "tensor", split_axis=1, concat_axis=0, tiled=True, axis_index_groups=same_tokens
         )
@@ -113,10 +637,8 @@
         split = ring_z.scatter(split, 2)
         return ring_y.scatter(split, 0)
 
-    x_home = inputs.reshape(home, size, tokens)
-    g_home = cotangent.reshape(home, size, tokens)
+    first_left, first_right, second_left, second_right = factors
     g_mid = go(g_home)
-
     left_one = ring_x.gather(ring_z.gather(first_left)).transpose(2, 1, 0, 3, 4).reshape(home, size, size)
     right_one, left_two, right_two = whole(first_right), whole(second_left), whole(second_right)
 
@@ -124,8 +646,7 @@
     s_two = turn(product("bit,bip->bpt", s_one, right_one).astype(BF16))
     act = gelu_value(s_two.astype(F32)).astype(BF16)
     e_three = turn(product("bot,bio->bit", g_mid, right_two).astype(BF16))
-    hidden = gelu_back(s_two.astype(F32), product("bot,bjo->bjt", e_three, left_two)).astype(BF16)
-    h_mid = turn(hidden)
+    h_mid = turn(gelu_back(s_two.astype(F32), product("bot,bjo->bjt", e_three, left_two)).astype(BF16))
     e_one = back(product("bpt,bip->bit", h_mid, right_one).astype(BF16))
     s_three = turn(product("bjt,bjo->bot", act, left_two).astype(BF16))
     s_four = back(product("bit,bio->bot", s_three, right_two).astype(BF16))
@@ -137,14 +658,28 @@
     grad_lone = product("bjt,bot->bjo", x_home, e_one).reshape(home, ring_z.size, ring_x.size, rows, size)
     grad_lone = ring_z.scatter(ring_x.scatter(grad_lone, 2), 1)
     input_grad = (g_home.astype(F32) + product("bot,bjo->bjt", e_one, left_one)).astype(BF16)
-    return (
-        mixed.reshape(home * size, tokens),
-        input_grad.reshape(home * size, tokens),
-        grad_lone,
-        grad_rone,
-        grad_ltwo,
-        grad_rtwo,
-    )
+    return mixed, input_grad, grad_lone, grad_rone, grad_ltwo, grad_rtwo
+
+
+def per_device(inputs, cotangent, first_left, first_right, second_left, second_right):
+    n_dp, n_tensor = lax.axis_size("dp"), lax.axis_size("tensor")
+    home, _, size = first_left.shape
+    tokens = inputs.shape[1]
+    share = math.gcd(n_tensor, max(1, tokens // LANES))
+    cut = tokens // share
+    far, near = halves(share)
+    outer, inner = halves(n_dp)
+    rings = (Ring("tensor", near, far), Ring("tensor", 1, near), Ring("dp", inner, outer), Ring("dp", 1, inner))
+    plan = whole_tokens if share == n_tensor else split_blocks
+    mixed, input_grad, *weight_grads = plan(
+        inputs.reshape(home, size, tokens),
+        cotangent.reshape(home, size, tokens),
+        (first_left, first_right, second_left, second_right),
+        rings,
+        share,
+        cut,
+    )
+    return (mixed.reshape(inputs.shape), input_grad.reshape(inputs.shape), *weight_grads)
 
 
 def solution(mesh):

time: 547 us -> 484 us (0.88); the launches traced: 537 us -> 481 us
  Pallas kernels: 0 us -> 138 us
  local copies, waits for them, and re-layouts: 157 us -> 19.9 us
  matrix products: 80.5 us -> 0 us
  starting transfers between devices: 91.5 us -> 119 us
  other arithmetic: 40.5 us -> 17.6 us
  waiting for transfers between devices: 165 us -> 185 us
    pallas_call x0 -> x13, Pallas kernels: none -> 138 us  [call(): pl.pallas_call(body, out_shape=out, grid_spec=spec, compiler_params=pltpu...]
    dot_general x12 -> x0, matrix products: 80.5 us -> none  [product(): return jnp.einsum(form, left, right, preferred_element_type=F32)]
    reshape x6 -> x0, local copies, waits for them, and re-layouts: 32.3 us -> none  [the longest x2 12.2 us: go(): values.reshape(home, groups, held, share, cut).transpose(1, 3, 2, 0, 4)]
    transpose x3 -> x0, local copies, waits for them, and re-layouts: 28.5 us -> none  [the longest x2 21 us: go(): return got.transpose(1, 0, 2, 3).reshape(held, size, cut)]
    ppermute x44 -> x39, starting transfers between devices: 71.3 us -> 99.7 us  [send(): return lax.ppermute(value, self.axis, pairs)]
    dynamic_update_slice x36 -> x0, local copies, waits for them, and re-layouts: 27 us -> none  [the longest x22 15.9 us: gather(): lax.dynamic_update_index_in_dim(out, got, lax.rem(here - step + self.size...]
    all_to_all x4, waiting for transfers between devices: 10.5 us -> 30.5 us  [cross(): lax.all_to_all(pieces, 'tensor', split_axis=0, concat_axis=0, tiled=True)]
    convert_element_type x2 -> x0, other arithmetic: 18.6 us -> none  [per_device(): mixed = (x_home.astype(F32) + s_four.astype(F32)).astype(BF16)]
  transfers between devices with their start and end apart: 48 -> 43, of which waited for: 15 -> 14; matrix products, arithmetic and copies ran while one was open for 39% -> 4% of each run, Pallas kernels for 0% -> 19%
where the time goes in v2:
time: 484 us; the launch traced here: 481 us
  waiting for transfers between devices  185 us (38%)
  Pallas kernels  138 us (29%)
  starting transfers between devices  119 us (25%)
  local copies, waits for them, and re-layouts  19.9 us (4%)
  other arithmetic  17.6 us (4%)
    ppermute x39, waiting for transfers between devices, send(): return lax.ppermute(value, self.axis, pairs)  155 us
    pallas_call x13, Pallas kernels, call(): pl.pallas_call(body, out_shape=out, grid_spec=spec, compiler_params=pltpu...  138 us
    ppermute x39, starting transfers between devices, send(): return lax.ppermute(value, self.axis, pairs)  99.7 us
    all_to_all x4, waiting for transfers between devices, cross(): lax.all_to_all(pieces, 'tensor', split_axis=0, concat_axis=0, tiled=True)  30.5 us
    all_to_all x4, starting transfers between devices, cross(): lax.all_to_all(pieces, 'tensor', split_axis=0, concat_axis=0, tiled=True)  19.5 us
    unnamed x32, local copies, waits for them, and re-layouts  16.1 us
  transfers between devices with their start and end apart: 43, of which 14 were waited for; matrix products, arithmetic and copies ran while one was open for 4% of the time, Pallas kernels for 19%

profile of v2, /device:TPU:0, one launch (start us, length us, event | category | flops | bytes accessed | tf_op | source)
XLA Modules:
  0.0 481.5 jit_solution(16880703983066057025)
XLA Ops:
  30.3 39.2 %collective-permute-done.4 = bf16[3,32,16,128]{3,2,1,0:T(8,128)(2,1)S(1)} collective-permute-done((bf16[3,32,16,128]{3,2,1,0:T(8,128)(2,1)S(1)}, bf16[3,32,16,128]{3,2,1,0:T(8,128)(2,1)S(1)}, u32[]{:S(2)}, u32[]{:S(2)}) %collective-permute-start.4) | collective-permute-done | bytes 393248 | tf_op jit(solution)/shard_map/ppermute | solution.py:506
  76.9 8.9 %shard_map.110 = bf16[4,128,32,128]{3,2,1,0:T(8,128)(2,1)S(1)} custom-call(bf16[32,128,512]{2,1,0:T(8,128)(2,1)} %bitcast.104, bf16[32,128,128]{2,1,0:T(8,128)(2,1)S(1)} %shard_map.109.w_ref), custom_call_target="tpu_custom_call" | custom-call | flops 536870912 | bytes 9437184 | tf_op jit(solution)/shard_map/pallas_call | solution.py:61
  107.3 9.2 %collective-permute-done.9 = bf16[2,32,16,128]{3,2,1,0:T(8,128)(2,1)S(1)} collective-permute-done((bf16[2,32,16,128]{3,2,1,0:T(8,128)(2,1)S(1)}, bf16[2,32,16,128]{3,2,1,0:T(8,128)(2,1)S(1)}, u32[]{:S(2)}, u32[]{:S(2)}) %collective-permute-start.9) | collective-permute-done | bytes 262176 | tf_op jit(solution)/shard_map/ppermute | solution.py:506
  116.6 6.1 %collective-permute-start.14 = (bf16[2,32,16,128]{3,2,1,0:T(8,128)(2,1)S(1)}, bf16[2,32,16,128]{3,2,1,0:T(8,128)(2,1)S(1)}, u32[]{:S(2)}, u32[]{:S(2)}) collective-permute-start(bf16[2,32,16,128]{3,2,1,0:T(8,128)(2,1)S(1)} %pad_maximum_fusion.7), channel_id=1, source_target_pairs={{0,8},{4,12},{8,16},{12,20},{16,24},{20,28},{24,0},{28,4},{1,9},{5... | collective-permute-start | bytes 786440 | tf_op jit(solution)/shard_map/ppermute | solution.py:506
  133.6 8.5 %collective-permute-done.15 = bf16[2,32,16,128]{3,2,1,0:T(8,128)(2,1)S(1)} collective-permute-done((bf16[2,32,16,128]{3,2,1,0:T(8,128)(2,1)S(1)}, bf16[2,32,16,128]{3,2,1,0:T(8,128)(2,1)S(1)}, u32[]{:S(2)}, u32[]{:S(2)}) %collective-permute-start.15) | collective-permute-done | bytes 262176 | tf_op jit(solution)/shard_map/ppermute | solution.py:506
  144.7 6.8 %collective-permute-done.20.refs_1_ = bf16[4,2,32,16,128]{4,3,2,1,0:T(8,128)(2,1)} collective-permute-done((bf16[4,2,32,16,128]{4,3,2,1,0:T(8,128)(2,1)S(1)}, bf16[4,2,32,16,128]{4,3,2,1,0:T(8,128)(2,1)}, u32[]{:S(2)}, u32[]{:S(2)}) %collective-permute-start.20) | collective-permute-done | bytes 1048608 | tf_op jit(solution)/shard_map/ppermute | solution.py:506
  152.1 22.0 %collective-permute-done.11.refs_1_ = bf16[4,2,32,16,128]{4,3,2,1,0:T(8,128)(2,1)} collective-permute-done((bf16[4,2,32,16,128]{4,3,2,1,0:T(8,128)(2,1)S(1)}, bf16[4,2,32,16,128]{4,3,2,1,0:T(8,128)(2,1)}, u32[]{:S(2)}, u32[]{:S(2)}) %collective-permute-start.11) | collective-permute-done | bytes 1048608 | tf_op jit(solution)/shard_map/ppermute | solution.py:506
  175.5 19.4 %collective-permute-done.17.refs_1_ = bf16[4,2,32,16,128]{4,3,2,1,0:T(8,128)(2,1)} collective-permute-done((bf16[4,2,32,16,128]{4,3,2,1,0:T(8,128)(2,1)}, bf16[4,2,32,16,128]{4,3,2,1,0:T(8,128)(2,1)}, u32[]{:S(2)}, u32[]{:S(2)}) %collective-permute-start.17) | collective-permute-done | bytes 1048608 | tf_op jit(solution)/shard_map/ppermute | solution.py:506
  196.2 6.9 %shard_map.114.w_ref.right_ref = bf16[128,128,128]{2,1,0:T(8,128)(2,1)} custom-call(s32[4]{0:T(128)S(1)} %pad_add_fusion.1.pos_ref, bf16[4,2,32,16,128]{4,3,2,1,0:T(8,128)(2,1)S(1)} %pad_maximum_fusion.refs_0_, bf16[4,2,32,16,128]{4,3,2,1,0:T(8,128)(2,1)} %collective-permute-done.20.refs_1_, bf16[4,2,32,16,128]{4,3,2,1,0:T(8,128)(2,1)S(1)} %copy-done.6, ...), custom_call_target="tpu_custom_call" | custom-call | bytes 8388608 | tf_op jit(solution)/shard_map/pallas_call | solution.py:61
  203.1 7.3 %shard_map.111.one_ref = bf16[128,128,128]{2,1,0:T(8,128)(2,1)} custom-call(s32[4]{0:T(128)S(1)} %pad_add_fusion.1.pos_ref, bf16[4,2,32,16,128]{4,3,2,1,0:T(8,128)(2,1)S(1)} %pad_maximum_fusion.1.refs_0_, bf16[4,2,32,16,128]{4,3,2,1,0:T(8,128)(2,1)} %collective-permute-done.11.refs_1_, bf16[4,2,32,16,128]{4,3,2,1,0:T(8,128)(2,1)} %collective-permute-done.12.refs_2_, ...), custom_call_target="tpu_custom_call" | custom-call | bytes 8388608 | tf_op jit(solution)/shard_map/pallas_call | solution.py:61
  210.4 8.1 %shard_map.115.e_ref.refs_1_ = bf16[128,128,128]{2,1,0:T(8,128)(2,1)S(1)} custom-call(bf16[4,128,32,128]{3,2,1,0:T(8,128)(2,1)} %all-to-all-done.1.g_ref.refs_1_, bf16[128,128,128]{2,1,0:T(8,128)(2,1)} %shard_map.114.w_ref.right_ref), custom_call_target="tpu_custom_call" | custom-call | flops 536870912 | bytes 12582912 | tf_op jit(solution)/shard_map/pallas_call | solution.py:61
  220.6 7.7 %shard_map.112.two_ref.left_ref = bf16[128,128,128]{2,1,0:T(8,128)(2,1)} custom-call(s32[4]{0:T(128)S(1)} %pad_add_fusion.1.pos_ref, bf16[4,2,32,16,128]{4,3,2,1,0:T(8,128)(2,1)} %pad_maximum_fusion.2.refs_0_, bf16[4,2,32,16,128]{4,3,2,1,0:T(8,128)(2,1)} %collective-permute-done.17.refs_1_, bf16[4,2,32,16,128]{4,3,2,1,0:T(8,128)(2,1)} %collective-permute-done.18.refs_2_, ...), custom_call_target="tpu_custom_call" | custom-call | bytes 8388608 | tf_op jit(solution)/shard_map/pallas_call | solution.py:61
  228.3 25.8 %shard_map.116 = (bf16[128,128,128]{2,1,0:T(8,128)(2,1)S(1)}, bf16[128,128,128]{2,1,0:T(8,128)(2,1)}, bf16[4,128,32,128]{3,2,1,0:T(8,128)(2,1)}) custom-call(bf16[4,128,32,128]{3,2,1,0:T(8,128)(2,1)} %all-to-all-done.s_ref.refs_2_, bf16[128,128,128]{2,1,0:T(8,128)(2,1)} %shard_map.111.one_ref, bf16[128,128,128]{2,1,0:T(8,128)(2,1)} %shard_map.112.two_ref.left_ref, ...), custom_call_target="tpu_custom_call" | custom-call | flops 1610612736 | bytes 29360128 | tf_op jit(solution)/shard_map/pallas_call | solution.py:61
  256.2 16.7 %shard_map.120 = (f32[2,2,32,128,128]{4,3,2,1,0:T(8,128)}, bf16[2,2,32,128,128]{4,3,2,1,0:T(8,128)(2,1)}) custom-call(s32[4]{0:T(128)S(1)} %pad_add_fusion.1.pos_ref, bf16[128,128,128]{2,1,0:T(8,128)(2,1)} %copy-done.1, bf16[128,128,128]{2,1,0:T(8,128)(2,1)} %copy-done, bf16[4,128,32,128]{3,2,1,0:T(8,128)(2,1)} %all-to-all-done.s_ref.refs_2_, ...), custom_call_target="tpu_custom_call" | custom-call | flops 1073741824 | bytes 29360128 | tf_op jit(solution)/shard_map/pallas_call | solution.py:61
  273.3 19.1 %shard_map.117 = (bf16[128,128,128]{2,1,0:T(8,128)(2,1)S(1)}, bf16[128,128,128]{2,1,0:T(8,128)(2,1)}) custom-call(bf16[128,128,128]{2,1,0:T(8,128)(2,1)} %copy-done.1, bf16[128,128,128]{2,1,0:T(8,128)(2,1)} %shard_map.112.two_ref.left_ref, bf16[128,128,128]{2,1,0:T(8,128)(2,1)} %shard_map.114.w_ref.right_ref), custom_call_target="tpu_custom_call" | custom-call | flops 1073741824 | bytes 20971520 | tf_op jit(solution)/shard_map/pallas_call | solution.py:61
  294.5 11.6 %shard_map.121 = (f32[1,2,32,128,128]{4,3,2,1,0:T(8,128)}, bf16[1,2,32,128,128]{4,3,2,1,0:T(8,128)(2,1)S(1)}) custom-call(s32[4]{0:T(128)S(1)} %pad_add_fusion.1.pos_ref, bf16[128,128,128]{2,1,0:T(8,128)(2,1)} %copy-done.4, bf16[4,128,32,128]{3,2,1,0:T(8,128)(2,1)} %all-to-all-done.1.g_ref.refs_1_), custom_call_target="tpu_custom_call" | custom-call | flops 536870912 | bytes 14680064 | tf_op jit(solution)/shard_map/pallas_call | solution.py:61
  310.9 6.1 %convert_add_fusion = f32[2,2,32,128,128]{4,3,2,1,0:T(8,128)S(1)} fusion(f32[2,2,32,128,128]{4,3,2,1,0:T(8,128)} %get-tuple-element.29, bf16[2,2,32,128,128]{4,3,2,1,0:T(8,128)(2,1)} %collective-permute-done.27), kind=kLoop, calls=%fused_computation | loop fusion | flops 4194304 | bytes 20971520 | tf_op jit(solution)/shard_map/add | solution.py:587
  328.6 30.5 %all-to-all-done.2.e_ref = bf16[4,128,32,128]{3,2,1,0:T(8,128)(2,1)} async-done(((bf16[4,128,32,128]{3,2,1,0:T(8,128)(2,1)}), bf16[4,128,32,128]{3,2,1,0:T(8,128)(2,1)}, u32[]{:S(2)}, u32[]{:S(2)}) %all-to-all-start.2) | async-done | bytes 4194336 | tf_op jit(solution)/shard_map/all_to_all | solution.py:540
  364.1 25.7 %collective-permute-done.34 = bf16[1,2,32,4,16,128]{5,4,2,1,3,0:T(8,128)(2,1)S(1)} collective-permute-done((bf16[1,2,32,4,16,128]{5,4,2,1,3,0:T(8,128)(2,1)S(1)}, bf16[1,2,32,4,16,128]{5,4,2,1,3,0:T(8,128)(2,1)S(1)}, u32[]{:S(2)}, u32[]{:S(2)}) %collective-permute-start.34) | collective-permute-done | bytes 1048608 | tf_op jit(solution)/shard_map/ppermute | solution.py:506
  395.8 12.8 %shard_map.119 = (bf16[32,128,512]{2,1,0:T(8,128)(2,1)}, f32[32,128,128]{2,1,0:T(8,128)S(1)}) custom-call(bf16[4,128,32,128]{3,2,1,0:T(8,128)(2,1)} %all-to-all-done.2.e_ref, bf16[32,128,512]{2,1,0:T(8,128)(2,1)} %bitcast.105, bf16[32,128,512]{2,1,0:T(8,128)(2,1)} %bitcast.112, bf16[32,128,128]{2,1,0:T(8,128)(2,1)S(1)} %shard_map.109.w_ref), custom_call_target="tpu_custom_call" | custom-call | flops 1073741824 | bytes 19922944 | tf_op jit(solution)/shard_map/pallas_call | solution.py:61
  422.0 21.3 %collective-permute-start.24 = (bf16[32,16,128]{2,1,0:T(8,128)(2,1)S(1)}, bf16[32,16,128]{2,1,0:T(8,128)(2,1)S(1)}, u32[]{:S(2)}, u32[]{:S(2)}) collective-permute-start(bf16[32,16,128]{2,1,0:T(8,128)(2,1)S(1)} %get-tuple-element.40), channel_id=1, source_target_pairs={{0,8},{4,12},{8,16},{12,20},{16,24},{20,28},{24,0},{28,4},{1,9},{5... | collective-permute-start | bytes 393224 | tf_op jit(solution)/shard_map/ppermute | solution.py:506
  443.3 10.7 %collective-permute-start.25 = (bf16[32,16,128]{2,1,0:T(8,128)(2,1)S(1)}, bf16[32,16,128]{2,1,0:T(8,128)(2,1)S(1)}, u32[]{:S(2)}, u32[]{:S(2)}) collective-permute-start(bf16[32,16,128]{2,1,0:T(8,128)(2,1)S(1)} %get-tuple-element.42), channel_id=1, source_target_pairs={{0,16},{4,20},{8,24},{12,28},{16,0},{20,4},{24,8},{28,12},{1,17},{... | collective-permute-start | bytes 393224 | tf_op jit(solution)/shard_map/ppermute | solution.py:506
  457.9 9.7 %collective-permute-start.26 = (bf16[32,16,128]{2,1,0:T(8,128)(2,1)S(1)}, bf16[32,16,128]{2,1,0:T(8,128)(2,1)S(1)}, u32[]{:S(2)}, u32[]{:S(2)}) collective-permute-start(bf16[32,16,128]{2,1,0:T(8,128)(2,1)S(1)} %get-tuple-element.41), channel_id=1, source_target_pairs={{0,24},{4,28},{8,0},{12,4},{16,8},{20,12},{24,16},{28,20},{1,25},{... | collective-permute-start | bytes 393224 | tf_op jit(solution)/shard_map/ppermute | solution.py:506
  472.7 7.8 %shard_map.118 = bf16[32,128,512]{2,1,0:T(8,128)(2,1)} custom-call(bf16[4,32,128,128]{3,2,1,0:T(8,128)(2,1)} %all-to-all-done.3.s_ref, bf16[32,128,512]{2,1,0:T(8,128)(2,1)} %bitcast.106), custom_call_target="tpu_custom_call" | custom-call | bytes 12582912 | tf_op jit(solution)/shard_map/pallas_call | solution.py:61
  (139 shorter events, 132.2 us)
Async XLA Ops:
  7.3 80.5 %all-to-all-start.1 = ((bf16[4,128,32,128]{3,2,1,0:T(8,128)(2,1)}), bf16[4,128,32,128]{3,2,1,0:T(8,128)(2,1)}, u32[]{:S(2)}, u32[]{:S(2)}) async-start(bf16[4,128,32,128]{3,2,1,0:T(8,128)(2,1)} %copy-done.3), calls=%async_computation.1 | async-start | bytes 8388608 | tf_op jit(solution)/shard_map/all_to_all | solution.py:540
  12.3 57.2 %collective-permute-start.4 = (bf16[3,32,16,128]{3,2,1,0:T(8,128)(2,1)S(1)}, bf16[3,32,16,128]{3,2,1,0:T(8,128)(2,1)S(1)}, u32[]{:S(2)}, u32[]{:S(2)}) collective-permute-start(bf16[3,32,16,128]{3,2,1,0:T(8,128)(2,1)S(1)} %pad_maximum_fusion.4), channel_id=1, source_target_pairs={{0,2},{1,3},{2,0},{3,1},{4,6},{5,7},{6,4},{7,5},{8,10},{9,11},{10,... | collective-permute-start | bytes 1179656 | tf_op jit(solution)/shard_map/ppermute | solution.py:506
  28.7 47.3 %collective-permute-start.3 = (bf16[4,32,16,128]{3,2,1,0:T(8,128)(2,1)S(1)}, bf16[4,32,16,128]{3,2,1,0:T(8,128)(2,1)S(1)}, u32[]{:S(2)}, u32[]{:S(2)}) collective-permute-start(bf16[4,32,16,128]{3,2,1,0:T(8,128)(2,1)S(1)} %get-tuple-element.45), channel_id=1, source_target_pairs={{0,4},{4,0},{8,12},{12,8},{16,20},{20,16},{24,28},{28,24},{1,5},{5... | collective-permute-start | bytes 1572872 | tf_op jit(solution)/shard_map/ppermute | solution.py:506
  87.8 140.5 %all-to-all-start = ((bf16[4,128,32,128]{3,2,1,0:T(8,128)(2,1)}), bf16[4,128,32,128]{3,2,1,0:T(8,128)(2,1)}, u32[]{:S(2)}, u32[]{:S(2)}) async-start(bf16[4,128,32,128]{3,2,1,0:T(8,128)(2,1)} %copy-done.2), calls=%async_computation | async-start | bytes 8388608 | tf_op jit(solution)/shard_map/all_to_all | solution.py:540
  125.3 26.2 %collective-permute-start.20 = (bf16[4,2,32,16,128]{4,3,2,1,0:T(8,128)(2,1)S(1)}, bf16[4,2,32,16,128]{4,3,2,1,0:T(8,128)(2,1)}, u32[]{:S(2)}, u32[]{:S(2)}) collective-permute-start(bf16[4,2,32,16,128]{4,3,2,1,0:T(8,128)(2,1)S(1)} %pad_maximum_fusion.refs_0_), channel_id=1, source_target_pairs={{0,4},{4,0},{8,12},{12,8},{16,20},{20,16},{24,28},{28,24},{1,5},{5... | collective-permute-start | bytes 3145736 | tf_op jit(solution)/shard_map/ppermute | solution.py:506
  126.8 47.2 %collective-permute-start.21 = (bf16[4,2,32,16,128]{4,3,2,1,0:T(8,128)(2,1)S(1)}, bf16[4,2,32,16,128]{4,3,2,1,0:T(8,128)(2,1)S(1)}, u32[]{:S(2)}, u32[]{:S(2)}) collective-permute-start(bf16[4,2,32,16,128]{4,3,2,1,0:T(8,128)(2,1)S(1)} %pad_maximum_fusion.refs_0_), channel_id=1, source_target_pairs={{0,1},{1,0},{2,3},{3,2},{4,5},{5,4},{6,7},{7,6},{8,9},{9,8},{10,11... | collective-permute-start | bytes 3145736 | tf_op jit(solution)/shard_map/ppermute | solution.py:506
  132.1 41.9 %collective-permute-start.11 = (bf16[4,2,32,16,128]{4,3,2,1,0:T(8,128)(2,1)S(1)}, bf16[4,2,32,16,128]{4,3,2,1,0:T(8,128)(2,1)}, u32[]{:S(2)}, u32[]{:S(2)}) collective-permute-start(bf16[4,2,32,16,128]{4,3,2,1,0:T(8,128)(2,1)S(1)} %pad_maximum_fusion.1.refs_0_), channel_id=1, source_target_pairs={{0,4},{4,0},{8,12},{12,8},{16,20},{20,16},{24,28},{28,24},{1,5},{5... | collective-permute-start | bytes 3145736 | tf_op jit(solution)/shard_map/ppermute | solution.py:506
  143.2 51.6 %collective-permute-start.17 = (bf16[4,2,32,16,128]{4,3,2,1,0:T(8,128)(2,1)}, bf16[4,2,32,16,128]{4,3,2,1,0:T(8,128)(2,1)}, u32[]{:S(2)}, u32[]{:S(2)}) collective-permute-start(bf16[4,2,32,16,128]{4,3,2,1,0:T(8,128)(2,1)} %pad_maximum_fusion.2.refs_0_), channel_id=1, source_target_pairs={{0,4},{4,0},{8,12},{12,8},{16,20},{20,16},{24,28},{28,24},{1,5},{5... | collective-permute-start | bytes 3145736 | tf_op jit(solution)/shard_map/ppermute | solution.py:506
  151.5 43.4 %collective-permute-start.22 = (bf16[4,2,32,16,128]{4,3,2,1,0:T(8,128)(2,1)}, bf16[4,2,32,16,128]{4,3,2,1,0:T(8,128)(2,1)}, u32[]{:S(2)}, u32[]{:S(2)}) collective-permute-start(bf16[4,2,32,16,128]{4,3,2,1,0:T(8,128)(2,1)} %collective-permute-done.20.refs_1_), channel_id=1, source_target_pairs={{0,1},{1,0},{2,3},{3,2},{4,5},{5,4},{6,7},{7,6},{8,9},{9,8},{10,11... | collective-permute-start | bytes 3145736 | tf_op jit(solution)/shard_map/ppermute | solution.py:506
  151.5 51.6 %collective-permute-start.12 = (bf16[4,2,32,16,128]{4,3,2,1,0:T(8,128)(2,1)S(1)}, bf16[4,2,32,16,128]{4,3,2,1,0:T(8,128)(2,1)}, u32[]{:S(2)}, u32[]{:S(2)}) collective-permute-start(bf16[4,2,32,16,128]{4,3,2,1,0:T(8,128)(2,1)S(1)} %pad_maximum_fusion.1.refs_0_), channel_id=1, source_target_pairs={{0,1},{1,0},{2,3},{3,2},{4,5},{5,4},{6,7},{7,6},{8,9},{9,8},{10,11... | collective-permute-start | bytes 3145736 | tf_op jit(solution)/shard_map/ppermute | solution.py:506
  174.0 29.1 %collective-permute-start.13 = (bf16[4,2,32,16,128]{4,3,2,1,0:T(8,128)(2,1)}, bf16[4,2,32,16,128]{4,3,2,1,0:T(8,128)(2,1)}, u32[]{:S(2)}, u32[]{:S(2)}) collective-permute-start(bf16[4,2,32,16,128]{4,3,2,1,0:T(8,128)(2,1)} %collective-permute-done.11.refs_1_), channel_id=1, source_target_pairs={{0,1},{1,0},{2,3},{3,2},{4,5},{5,4},{6,7},{7,6},{8,9},{9,8},{10,11... | collective-permute-start | bytes 3145736 | tf_op jit(solution)/shard_map/ppermute | solution.py:506
  175.0 45.6 %collective-permute-start.18 = (bf16[4,2,32,16,128]{4,3,2,1,0:T(8,128)(2,1)}, bf16[4,2,32,16,128]{4,3,2,1,0:T(8,128)(2,1)}, u32[]{:S(2)}, u32[]{:S(2)}) collective-permute-start(bf16[4,2,32,16,128]{4,3,2,1,0:T(8,128)(2,1)} %pad_maximum_fusion.2.refs_0_), channel_id=1, source_target_pairs={{0,1},{1,0},{2,3},{3,2},{4,5},{5,4},{6,7},{7,6},{8,9},{9,8},{10,11... | collective-permute-start | bytes 3145736 | tf_op jit(solution)/shard_map/ppermute | solution.py:506
  272.9 38.1 %collective-permute-start.27 = (bf16[2,2,32,128,128]{4,3,2,1,0:T(8,128)(2,1)}, bf16[2,2,32,128,128]{4,3,2,1,0:T(8,128)(2,1)}, u32[]{:S(2)}, u32[]{:S(2)}) collective-permute-start(bf16[2,2,32,128,128]{4,3,2,1,0:T(8,128)(2,1)} %get-tuple-element.30), channel_id=1, source_target_pairs={{0,1},{1,0},{2,3},{3,2},{4,5},{5,4},{6,7},{7,6},{8,9},{9,8},{10,11... | collective-permute-start | bytes 12582920 | tf_op jit(solution)/shard_map/ppermute | solution.py:506
  306.1 53.1 %all-to-all-start.2 = ((bf16[4,128,32,128]{3,2,1,0:T(8,128)(2,1)}), bf16[4,128,32,128]{3,2,1,0:T(8,128)(2,1)}, u32[]{:S(2)}, u32[]{:S(2)}) async-start(bf16[4,128,32,128]{3,2,1,0:T(8,128)(2,1)} %get-tuple-element.24), calls=%async_computation.2 | async-start | bytes 8388608 | tf_op jit(solution)/shard_map/all_to_all | solution.py:540
  319.1 91.2 %collective-permute-start.28 = (bf16[2,2,32,4,16,128]{5,4,2,0,1,3:T(8,128)(2,1)}, bf16[2,2,32,4,16,128]{5,4,2,0,1,3:T(8,128)(2,1)}, u32[]{:S(2)}, u32[]{:S(2)}) collective-permute-start(bf16[2,2,32,4,16,128]{5,4,2,0,1,3:T(8,128)(2,1)} %fusion), channel_id=1, source_target_pairs={{0,4},{4,0},{8,12},{12,8},{16,20},{20,16},{24,28},{28,24},{1,5},{5... | collective-permute-start | bytes 6291464 | tf_op jit(solution)/shard_map/ppermute | solution.py:506
  327.1 62.7 %collective-permute-start.34 = (bf16[1,2,32,4,16,128]{5,4,2,1,3,0:T(8,128)(2,1)S(1)}, bf16[1,2,32,4,16,128]{5,4,2,1,3,0:T(8,128)(2,1)S(1)}, u32[]{:S(2)}, u32[]{:S(2)}) collective-permute-start(bf16[1,2,32,4,16,128]{5,4,2,1,3,0:T(8,128)(2,1)S(1)} %fusion.1), channel_id=1, source_target_pairs={{0,4},{4,0},{8,12},{12,8},{16,20},{20,16},{24,28},{28,24},{1,5},{5... | collective-permute-start | bytes 3145736 | tf_op jit(solution)/shard_map/ppermute | solution.py:506
  359.1 113.6 %all-to-all-start.3 = ((bf16[4,32,128,128]{3,2,1,0:T(8,128)(2,1)}), bf16[4,32,128,128]{3,2,1,0:T(8,128)(2,1)}, u32[]{:S(2)}, u32[]{:S(2)}) async-start(bf16[4,32,128,128]{3,2,1,0:T(8,128)(2,1)} %bitcast.116), calls=%async_computation.3 | async-start | bytes 8388608 | tf_op jit(solution)/shard_map/all_to_all | solution.py:540
  394.1 25.8 %collective-permute-start.37 = (bf16[1,2,32,16,128]{4,3,2,1,0:T(8,128)(2,1)S(1)}, bf16[1,2,32,16,128]{4,3,2,1,0:T(8,128)(2,1)S(1)}, u32[]{:S(2)}, u32[]{:S(2)}) collective-permute-start(bf16[1,2,32,16,128]{4,3,2,1,0:T(8,128)(2,1)S(1)} %get-tuple-element.38), channel_id=1, source_target_pairs={{0,24},{4,28},{8,0},{12,4},{16,8},{20,12},{24,16},{28,20},{1,25},{... | collective-permute-start | bytes 786440 | tf_op jit(solution)/shard_map/ppermute | solution.py:506
  412.8 30.5 %collective-permute-start.29 = (bf16[2,2,32,16,128]{4,3,2,0,1:T(8,128)(2,1)S(1)}, bf16[2,2,32,16,128]{4,3,2,0,1:T(8,128)(2,1)S(1)}, u32[]{:S(2)}, u32[]{:S(2)}) collective-permute-start(bf16[2,2,32,16,128]{4,3,2,0,1:T(8,128)(2,1)S(1)} %get-tuple-element.34), channel_id=1, source_target_pairs={{0,8},{4,12},{8,16},{12,20},{16,24},{20,28},{24,0},{28,4},{1,9},{5... | collective-permute-start | bytes 1572872 | tf_op jit(solution)/shard_map/ppermute | solution.py:506
  413.4 44.5 %collective-permute-start.30 = (bf16[2,2,32,16,128]{4,3,2,0,1:T(8,128)(2,1)S(1)}, bf16[2,2,32,16,128]{4,3,2,0,1:T(8,128)(2,1)S(1)}, u32[]{:S(2)}, u32[]{:S(2)}) collective-permute-start(bf16[2,2,32,16,128]{4,3,2,0,1:T(8,128)(2,1)S(1)} %get-tuple-element.36), channel_id=1, source_target_pairs={{0,16},{4,20},{8,24},{12,28},{16,0},{20,4},{24,8},{28,12},{1,17},{... | collective-permute-start | bytes 1572872 | tf_op jit(solution)/shard_map/ppermute | solution.py:506
  415.2 52.4 %collective-permute-start.31 = (bf16[2,2,32,16,128]{4,3,2,0,1:T(8,128)(2,1)S(1)}, bf16[2,2,32,16,128]{4,3,2,0,1:T(8,128)(2,1)S(1)}, u32[]{:S(2)}, u32[]{:S(2)}) collective-permute-start(bf16[2,2,32,16,128]{4,3,2,0,1:T(8,128)(2,1)S(1)} %get-tuple-element.35), channel_id=1, source_target_pairs={{0,24},{4,28},{8,0},{12,4},{16,8},{20,12},{24,16},{28,20},{1,25},{... | collective-permute-start | bytes 1572872 | tf_op jit(solution)/shard_map/ppermute | solution.py:506
  420.0 49.6 %collective-permute-start.38 = (bf16[1,32,16,128]{3,2,1,0:T(8,128)(2,1)S(1)}, bf16[1,32,16,128]{3,2,1,0:T(8,128)(2,1)S(1)}, u32[]{:S(2)}, u32[]{:S(2)}) collective-permute-start(bf16[1,32,16,128]{3,2,1,0:T(8,128)(2,1)S(1)} %fusion.20), channel_id=1, source_target_pairs={{0,2},{1,3},{2,0},{3,1},{4,6},{5,7},{6,4},{7,5},{8,10},{9,11},{10,... | collective-permute-start | bytes 393224 | tf_op jit(solution)/shard_map/ppermute | solution.py:506
  422.0 48.4 %collective-permute-start.24 = (bf16[32,16,128]{2,1,0:T(8,128)(2,1)S(1)}, bf16[32,16,128]{2,1,0:T(8,128)(2,1)S(1)}, u32[]{:S(2)}, u32[]{:S(2)}) collective-permute-start(bf16[32,16,128]{2,1,0:T(8,128)(2,1)S(1)} %get-tuple-element.40), channel_id=1, source_target_pairs={{0,8},{4,12},{8,16},{12,20},{16,24},{20,28},{24,0},{28,4},{1,9},{5... | collective-permute-start | bytes 393224 | tf_op jit(solution)/shard_map/ppermute | solution.py:506
  443.3 28.6 %collective-permute-start.25 = (bf16[32,16,128]{2,1,0:T(8,128)(2,1)S(1)}, bf16[32,16,128]{2,1,0:T(8,128)(2,1)S(1)}, u32[]{:S(2)}, u32[]{:S(2)}) collective-permute-start(bf16[32,16,128]{2,1,0:T(8,128)(2,1)S(1)} %get-tuple-element.42), channel_id=1, source_target_pairs={{0,16},{4,20},{8,24},{12,28},{16,0},{20,4},{24,8},{28,12},{1,17},{... | collective-permute-start | bytes 393224 | tf_op jit(solution)/shard_map/ppermute | solution.py:506
  (35 other events, 398.1 us)

commit v3 on v2

--- a/solution.py
+++ b/solution.py
@@ -12,7 +12,7 @@
 F32 = jnp.float32
 LANES = 128
 PAD = 8
-VMEM_BYTES = 48 * 1024 * 1024
+VMEM_BYTES = 60 * 1024 * 1024
 
 
 def gelu_value(values):
@@ -48,9 +48,7 @@
     return lax.dot_general(left, right, (((1,), (1,)), ((), ())), preferred_element_type=F32)
 
 
-def call(body, out, grid, in_specs, out_specs, scratch, args, scalars=None, dots=0):
-    moved = sum(math.prod(a.shape) * a.dtype.itemsize for a in args)
-    moved += sum(math.prod(o.shape) * o.dtype.itemsize for o in jax.tree.leaves(out))
+def call(body, out, grid, in_specs, out_specs, scratch, args, scalars=None):
     spec = pltpu.PrefetchScalarGridSpec(
         num_scalar_prefetch=0 if scalars is None else 1,
         grid=grid,
@@ -65,7 +63,7 @@
         compiler_params=pltpu.CompilerParams(
             dimension_semantics=("arbitrary",) * len(grid), vmem_limit_bytes=VMEM_BYTES
         ),
-        cost_estimate=pl.CostEstimate(flops=dots, bytes_accessed=moved, transcendentals=0),
+        cost_estimate=pl.CostEstimate(flops=0, bytes_accessed=1024, transcendentals=0),
     )(*(() if scalars is None else (scalars,)), *args)
 
 
@@ -73,7 +71,7 @@
     return jax.ShapeDtypeStruct(dims, dtype)
 
 
-def each(count, body, unroll=4):
+def each(count, body, unroll=16):
     def step(k, carry):
         body(k)
         return carry
@@ -91,25 +89,27 @@
 
 def deal_kernel(g_ref, out_ref, turned):
     home, size, _ = g_ref.shape
+    cut = out_ref.shape[3]
     pitch = home + PAD
+    lanes = pl.ds(pl.multiple_of(pl.program_id(0) * cut, cut), cut)
 
     def store(o):
-        turned[pl.ds(o, size, stride=pitch), :] = g_ref[o].astype(F32)
+        turned[pl.ds(o, size, stride=pitch), :] = g_ref[o, :, lanes].astype(F32)
 
     def load(b):
         out_ref[0, b] = turned[pl.ds(pl.multiple_of(b * pitch, 8), home), :].astype(BF16)
 
     each(home, store)
-    each(size, load, 8)
+    each(size, load)
 
 
 def deal(g_home, share, cut):
-    home, size, _ = g_home.shape
+    home, size, tokens = g_home.shape
     return call(
         deal_kernel,
         shape((share, size, home, cut)),
         (share,),
-        [pl.BlockSpec((home, size, cut), lambda s: (0, 0, s))],
+        [pl.BlockSpec((home, size, tokens), lambda s: (0, 0, 0))],
         pl.BlockSpec((1, size, home, cut), lambda s: (s, 0, 0, 0)),
         [pltpu.VMEM((size * (home + PAD), cut), F32)],
         (g_home,),
@@ -118,83 +118,89 @@
 
 def first_kernel(x_ref, w_ref, out_ref, turned):
     home, size, _ = x_ref.shape
+    cut = out_ref.shape[3]
     pitch = home + PAD
+    lanes = pl.ds(pl.multiple_of(pl.program_id(0) * cut, cut), cut)
 
     def store(b):
-        turned[pl.ds(b, size, stride=pitch), :] = dot_tn(w_ref[b], x_ref[b])
+        turned[pl.ds(b, size, stride=pitch), :] = dot_tn(w_ref[b], x_ref[b, :, lanes])
 
     def load(o):
         out_ref[0, o] = turned[pl.ds(pl.multiple_of(o * pitch, 8), home), :].astype(BF16)
 
     each(home, store)
-    each(size, load, 8)
+    each(size, load)
 
 
 def first_stage(x_home, left_one, share, cut):
-    home, size, _ = x_home.shape
+    home, size, tokens = x_home.shape
     return call(
         first_kernel,
         shape((share, size, home, cut)),
         (share,),
         [
-            pl.BlockSpec((home, size, cut), lambda s: (0, 0, s)),
+            pl.BlockSpec((home, size, tokens), lambda s: (0, 0, 0)),
             pl.BlockSpec((home, size, size), lambda s: (0, 0, 0)),
         ],
         pl.BlockSpec((1, size, home, cut), lambda s: (s, 0, 0, 0)),
         [pltpu.VMEM((size * (home + PAD), cut), F32)],
         (x_home, left_one),
-        dots=2 * home * size * size * share * cut,
     )
 
 
 def last_kernel(e_ref, x_ref, g_ref, w_ref, out_ref, grad_ref, turned):
-    _, blocks, home, _ = e_ref.shape
+    share, blocks, per, cut = e_ref.shape
     pitch = blocks + PAD
-    first = pl.program_id(0) == 0
-
-    def store(o):
-        turned[pl.ds(o, home, stride=pitch), :] = e_ref[0, o].astype(F32)
+
+    for s in range(share):
+
+        def store(o):
+            turned[s, pl.ds(o, per, stride=pitch), :] = e_ref[s, o].astype(F32)
+
+        each(blocks, store)
 
     def load(b):
-        e_b = turned[pl.ds(pl.multiple_of(b * pitch, 8), blocks), :].astype(BF16)
+        rows = pl.ds(pl.multiple_of(b * pitch, 8), blocks)
+        e_b = jnp.concatenate([turned[s, rows, :].astype(BF16) for s in range(share)], axis=1)
         out_ref[b] = (g_ref[b].astype(F32) + dot_nn(w_ref[b], e_b)).astype(BF16)
-        before = jnp.where(first, 0.0, grad_ref[b])
-        grad_ref[b] = before + dot_nt(x_ref[b], e_b)
-
-    each(blocks, store, 8)
-    each(home, load)
+        grad_ref[b] = dot_nt(x_ref[b], e_b).astype(BF16)
+
+    each(per, load, 4)
 
 
 def last_stage(e_got, x_home, g_home, left_one):
     share, blocks, home, cut = e_got.shape
-    size = x_home.shape[1]
-    wide = pl.BlockSpec((home, size, cut), lambda s: (0, 0, s))
-    fixed = pl.BlockSpec((home, size, size), lambda s: (0, 0, 0))
+    _, size, tokens = x_home.shape
+    per = math.gcd(home, 16)
+    wide = pl.BlockSpec((per, size, tokens), lambda h: (h, 0, 0))
+    factor = pl.BlockSpec((per, size, size), lambda h: (h, 0, 0))
     return call(
         last_kernel,
-        (shape(g_home.shape), shape((home, size, size), F32)),
-        (share,),
-        [pl.BlockSpec((1, blocks, home, cut), lambda s: (s, 0, 0, 0)), wide, wide, fixed],
-        (wide, fixed),
-        [pltpu.VMEM((home * (blocks + PAD), cut), F32)],
+        (shape(g_home.shape), shape((home, size, size))),
+        (home // per,),
+        [pl.BlockSpec((share, blocks, per, cut), lambda h: (0, 0, h, 0)), wide, wide, factor],
+        (wide, factor),
+        [pltpu.VMEM((share, per * (blocks + PAD), cut), F32)],
         (e_got, x_home, g_home, left_one),
-        dots=4 * home * size * size * share * cut,
     )
 
 
 def mixed_kernel(s_ref, x_ref, out_ref):
-    out_ref[...] = (x_ref[...].astype(F32) + s_ref[0].astype(F32)).astype(BF16)
+    cut = s_ref.shape[3]
+    for s in range(s_ref.shape[0]):
+        lanes = slice(s * cut, (s + 1) * cut)
+        out_ref[:, :, lanes] = (x_ref[:, :, lanes].astype(F32) + s_ref[s].astype(F32)).astype(BF16)
 
 
 def add_home(s_got, x_home):
     share, home, blocks, cut = s_got.shape
-    per = math.gcd(home, 16)
-    wide = pl.BlockSpec((per, blocks, cut), lambda s, h: (h, 0, s))
+    per = math.gcd(home, 8)
+    wide = pl.BlockSpec((per,) + x_home.shape[1:], lambda h: (h, 0, 0))
     return call(
         mixed_kernel,
         shape(x_home.shape),
-        (share, home // per),
-        [pl.BlockSpec((1, per, blocks, cut), lambda s, h: (s, h, 0, 0)), wide],
+        (home // per,),
+        [pl.BlockSpec((share, per, blocks, cut), lambda h: (0, h, 0, 0)), wide],
         wide,
         [],
         (s_got, x_home),
@@ -218,7 +224,7 @@
         def body(k):
             out_ref[k] = turned[pl.ds(pl.multiple_of((j * per + k) * pitch, 8), size), :].astype(BF16)
 
-        each(per, body, 8)
+        each(per, body)
 
 
 def middle_sizes(weights):
@@ -242,7 +248,6 @@
         pl.BlockSpec((per, size, cut), lambda p, j: (at[1](p, j), 0, 0)),
         [pltpu.VMEM((blocks * (size + PAD), cut), F32)],
         (g_mid, right_two),
-        dots=2 * blocks * size * size * cut,
     )
 
 
@@ -314,7 +319,6 @@
         ),
         [pltpu.VMEM((blocks * (size + PAD), cut), F32)] * 2,
         (s_mid, right_one, left_two, e_mid),
-        dots=6 * blocks * size * size * cut,
     )
 
 
@@ -350,7 +354,7 @@
         def body(k):
             out_ref[k] = fourth[rows(k), :].astype(BF16)
 
-        each(per, body, 8)
+        each(per, body)
 
 
 def forward_two(act, left_two, right_two):
@@ -373,7 +377,6 @@
         ),
         [pltpu.VMEM((blocks * (size + PAD), cut), F32)] * 2,
         (act, left_two, right_two),
-        dots=4 * blocks * size * size * cut,
     )
 
 
@@ -427,17 +430,15 @@
     def sent(rc, y, s, pos):
         return (0, jnp.where(rc == 0, 0, y), jnp.where(rc == 0, 0, s), 0, 0)
 
-    cut = args[0].shape[-1]
     return call(
         functools.partial(grads_kernel, near, split),
-        (shape(dims, F32), shape(dims)),
+        (shape(dims), shape(dims)),
         (near, far, subs),
         specs,
         (pl.BlockSpec((n, 1, per, size, size), kept), pl.BlockSpec((n, 1, per, size, size), sent)),
         [],
         tuple(args),
         scalars=pos,
-        dots=2 * n * far * near * home * size * size * cut,
     )
 
 
@@ -461,7 +462,7 @@
 def join(pieces, pos):
     near, n_x = len(pieces), len(pieces[0])
     n_z, far, home, rows, size = pieces[0][0].shape
-    per = math.gcd(home, 16)
+    per = math.gcd(home, 32)
     subs = home // per
     specs = []
     for c in range(near):
@@ -519,16 +520,19 @@
             out = lax.dynamic_update_index_in_dim(out, got, lax.rem(here - step + self.size, self.size), 0)
         return out
 
-    def scatter(self, value, dim):
+    def scatter(self, terms, dim):
         here = self.here()
         if self.size == 1:
-            return lax.index_in_dim(value, 0, dim, keepdims=False)
-        total = lax.dynamic_index_in_dim(value, here, dim, keepdims=False).astype(F32)
+            return [lax.index_in_dim(t, 0, dim, keepdims=False) for t in terms]
+        out = [lax.dynamic_index_in_dim(t, here, dim, keepdims=False) for t in terms]
         for step in range(1, self.size):
             there = lax.rem(here + step, self.size)
-            term = lax.dynamic_index_in_dim(value, there, dim, keepdims=False).astype(BF16)
-            total = total + self.send(term, step).astype(F32)
-        return total
+            out.append(self.send(total([lax.dynamic_index_in_dim(t, there, dim, keepdims=False) for t in terms]).astype(BF16), step))
+        return out
+
+
+def total(terms):
+    return functools.reduce(jnp.add, [t.astype(F32) for t in terms])
 
 
 def halves(size):
@@ -558,7 +562,7 @@
     zero = jnp.zeros_like(pos[:1])
     one = join([[p[:, None] for p in [one] + ring_x.sends(one)]], jnp.concatenate([zero, zero, pos[2:]]))
 
-    g_mid = cross(deal(g_home, share, cut))
+    g_mid = cross(after(deal(g_home, share, cut), *from_y[1:]))
 
     wholes, before = [], None
     for n in range(3):
@@ -581,21 +585,17 @@
     s_got = cross(after(s_out, e_got))
 
     def own_sum(pairs):
-        keep, send = grads(pairs, home, size, ring_y.size, ring_core.size, pos)
-        total = keep
-        if ring_core.size > 1:
-            total = total + ring_core.send(send, 1).astype(F32)
-        split = total.reshape(len(pairs), ring_y.size, home, ring_z.size, ring_x.size, rows, size)
-        split = ring_x.scatter(split, 4)
-        split = ring_z.scatter(split, 3)
-        return ring_y.scatter(split, 1)
+        terms = grads(pairs, home, size, ring_y.size, ring_core.size, pos)
+        terms = [terms[0], ring_core.send(terms[1], 1)] if ring_core.size > 1 else terms[:1]
+        terms = [t.reshape(len(pairs), ring_y.size, home, ring_z.size, ring_x.size, rows, size) for t in terms]
+        return total(ring_y.scatter(ring_z.scatter(ring_x.scatter(terms, 4), 3), 1))
 
     grad_ltwo, grad_rone = own_sum([(act, e_mid), (s_mid, hidden)])
     grad_rtwo = own_sum([(third, g_mid)])[0]
 
     input_grad, grad_lone = last_stage(e_got, x_home, g_home, one)
     grad_lone = grad_lone.reshape(home, ring_z.size, ring_x.size, rows, size)
-    grad_lone = ring_z.scatter(ring_x.scatter(grad_lone, 2), 1)
+    grad_lone = total(ring_z.scatter(ring_x.scatter([grad_lone], 2), 1))
     mixed = add_home(s_got, x_home)
     return mixed, input_grad, grad_lone, grad_rone, grad_ltwo, grad_rtwo
 
@@ -632,10 +632,8 @@
 
     def own_sum(partial):
         split = partial.reshape(ring_y.size, ring_core.size, home, ring_z.size, ring_x.size, rows, size)
-        split = ring_core.scatter(split, 1)
-        split = ring_x.scatter(split, 3)
-        split = ring_z.scatter(split, 2)
-        return ring_y.scatter(split, 0)
+        terms = ring_core.scatter([split], 1)
+        return total(ring_y.scatter(ring_z.scatter(ring_x.scatter(terms, 3), 2), 0))
 
     first_left, first_right, second_left, second_right = factors
     g_mid = go(g_home)
@@ -656,7 +654,7 @@
     grad_ltwo = own_sum(product("bjt,bot->bjo", act, e_three))
     grad_rone = own_sum(product("bit,bpt->bip", s_one, h_mid))
     grad_lone = product("bjt,bot->bjo", x_home, e_one).reshape(home, ring_z.size, ring_x.size, rows, size)
-    grad_lone = ring_z.scatter(ring_x.scatter(grad_lone, 2), 1)
+    grad_lone = total(ring_z.scatter(ring_x.scatter([grad_lone], 2), 1))
     input_grad = (g_home.astype(F32) + product("bot,bjo->bjt", e_one, left_one)).astype(BF16)
     return mixed, input_grad, grad_lone, grad_rone, grad_ltwo, grad_rtwo
 

time: 484 us -> 442 us (0.913)
  starting transfers between devices: 119 us -> 88.8 us
  Pallas kernels: 138 us -> 115 us
  waiting for transfers between devices: 185 us -> 203 us
  local copies, waits for them, and re-layouts: 19.9 us -> 7.51 us
  other arithmetic: 17.6 us -> 25 us
    ppermute x39, starting transfers between devices: 99.7 us -> 69.2 us  [send(): return lax.ppermute(value, self.axis, pairs)]
    pallas_call x13, Pallas kernels: 138 us -> 115 us  [call(): pl.pallas_call(body, out_shape=out, grid_spec=spec, compiler_params=pltpu...]
    ppermute x39, waiting for transfers between devices: 155 us -> 174 us  [send(): return lax.ppermute(value, self.axis, pairs)]
    convert_element_type x0 -> x7, other arithmetic: none -> 16.7 us  [scatter(): total([lax.dynamic_index_in_dim(t, there, dim, keepdims=False) for t in t...]
    unnamed x32 -> x20, local copies, waits for them, and re-layouts: 16.1 us -> 0.84 us
    add x9 -> x2, other arithmetic: 14.1 us -> 3.26 us  [total(): return functools.reduce(jnp.add, [t.astype(F32) for t in terms])]
  transfers between devices with their start and end apart: 43 -> 43, of which waited for: 14 -> 16; matrix products, arithmetic and copies ran while one was open for 4% -> 6% of each run, Pallas kernels for 19% -> 18%
where the time goes in v3:
time: 442 us; the launch traced here: 440 us
  waiting for transfers between devices  203 us (46%)
  Pallas kernels  115 us (26%)
  starting transfers between devices  88.8 us (20%)
  other arithmetic  25 us (6%)
  local copies, waits for them, and re-layouts  7.51 us (2%)
    ppermute x39, waiting for transfers between devices, send(): return lax.ppermute(value, self.axis, pairs)  174 us
    pallas_call x13, Pallas kernels, call(): pl.pallas_call(body, out_shape=out, grid_spec=spec, compiler_params=pltpu...  115 us
    ppermute x39, starting transfers between devices, send(): return lax.ppermute(value, self.axis, pairs)  69.2 us
    all_to_all x4, waiting for transfers between devices, cross(): lax.all_to_all(pieces, 'tensor', split_axis=0, concat_axis=0, tiled=True)  28.1 us
    all_to_all x4, starting transfers between devices, cross(): lax.all_to_all(pieces, 'tensor', split_axis=0, concat_axis=0, tiled=True)  19.6 us
    convert_element_type x7, other arithmetic, scatter(): total([lax.dynamic_index_in_dim(t, there, dim, keepdims=False) for t in t...  16.7 us
  transfers between devices with their start and end apart: 43, of which 16 were waited for; matrix products, arithmetic and copies ran while one was open for 6% of the time, Pallas kernels for 18%

profile of v3, /device:TPU:0, one launch (start us, length us, event | category | flops | bytes accessed | tf_op | source)
XLA Modules:
  0.0 439.8 jit_solution(809317897559802507)
XLA Ops:
  4.7 6.1 %shard_map.113 = bf16[4,128,32,128]{3,2,1,0:T(8,128)(2,1)} custom-call(bf16[32,128,512]{2,1,0:T(8,128)(2,1)} %bitcast.200), custom_call_target="tpu_custom_call" | custom-call | bytes 1024 | tf_op jit(solution)/shard_map/pallas_call | solution.py:59
  41.3 5.8 %collective-permute-done.3 = bf16[4,32,16,128]{3,2,1,0:T(8,128)(2,1)S(1)} collective-permute-done((bf16[4,32,16,128]{3,2,1,0:T(8,128)(2,1)S(1)}, bf16[4,32,16,128]{3,2,1,0:T(8,128)(2,1)S(1)}, u32[]{:S(2)}, u32[]{:S(2)}) %collective-permute-start.3) | collective-permute-done | bytes 524320 | tf_op jit(solution)/shard_map/ppermute | solution.py:507
  50.8 7.1 %shard_map.110 = bf16[4,128,32,128]{3,2,1,0:T(8,128)(2,1)} custom-call(bf16[32,128,512]{2,1,0:T(8,128)(2,1)} %bitcast.197, bf16[32,128,128]{2,1,0:T(8,128)(2,1)} %shard_map.109.w_ref), custom_call_target="tpu_custom_call" | custom-call | bytes 1024 | tf_op jit(solution)/shard_map/pallas_call | solution.py:59
  57.9 9.1 %all-to-all-done.1.g_ref.refs_1_ = bf16[4,128,32,128]{3,2,1,0:T(8,128)(2,1)} async-done(((bf16[4,128,32,128]{3,2,1,0:T(8,128)(2,1)}), bf16[4,128,32,128]{3,2,1,0:T(8,128)(2,1)}, u32[]{:S(2)}, u32[]{:S(2)}) %all-to-all-start.1) | async-done | bytes 4194336 | tf_op jit(solution)/shard_map/all_to_all | solution.py:544
  83.3 11.0 %collective-permute-done.9 = bf16[2,32,16,128]{3,2,1,0:T(8,128)(2,1)S(1)} collective-permute-done((bf16[2,32,16,128]{3,2,1,0:T(8,128)(2,1)S(1)}, bf16[2,32,16,128]{3,2,1,0:T(8,128)(2,1)S(1)}, u32[]{:S(2)}, u32[]{:S(2)}) %collective-permute-start.9) | collective-permute-done | bytes 262176 | tf_op jit(solution)/shard_map/ppermute | solution.py:507
  94.4 6.2 %collective-permute-start.14 = (bf16[2,32,16,128]{3,2,1,0:T(8,128)(2,1)S(1)}, bf16[2,32,16,128]{3,2,1,0:T(8,128)(2,1)S(1)}, u32[]{:S(2)}, u32[]{:S(2)}) collective-permute-start(bf16[2,32,16,128]{3,2,1,0:T(8,128)(2,1)S(1)} %pad_maximum_fusion.7), channel_id=1, source_target_pairs={{0,8},{4,12},{8,16},{12,20},{16,24},{20,28},{24,0},{28,4},{1,9},{5... | collective-permute-start | bytes 786440 | tf_op jit(solution)/shard_map/ppermute | solution.py:507
  110.3 8.7 %collective-permute-done.15 = bf16[2,32,16,128]{3,2,1,0:T(8,128)(2,1)S(1)} collective-permute-done((bf16[2,32,16,128]{3,2,1,0:T(8,128)(2,1)S(1)}, bf16[2,32,16,128]{3,2,1,0:T(8,128)(2,1)S(1)}, u32[]{:S(2)}, u32[]{:S(2)}) %collective-permute-start.15) | collective-permute-done | bytes 262176 | tf_op jit(solution)/shard_map/ppermute | solution.py:507
  120.8 8.4 %collective-permute-done.20.refs_1_ = bf16[4,2,32,16,128]{4,3,2,1,0:T(8,128)(2,1)} collective-permute-done((bf16[4,2,32,16,128]{4,3,2,1,0:T(8,128)(2,1)S(1)}, bf16[4,2,32,16,128]{4,3,2,1,0:T(8,128)(2,1)}, u32[]{:S(2)}, u32[]{:S(2)}) %collective-permute-start.20) | collective-permute-done | bytes 1048608 | tf_op jit(solution)/shard_map/ppermute | solution.py:507
  129.2 22.5 %collective-permute-done.11.refs_1_ = bf16[4,2,32,16,128]{4,3,2,1,0:T(8,128)(2,1)} collective-permute-done((bf16[4,2,32,16,128]{4,3,2,1,0:T(8,128)(2,1)S(1)}, bf16[4,2,32,16,128]{4,3,2,1,0:T(8,128)(2,1)}, u32[]{:S(2)}, u32[]{:S(2)}) %collective-permute-start.11) | collective-permute-done | bytes 1048608 | tf_op jit(solution)/shard_map/ppermute | solution.py:507
  152.1 20.5 %collective-permute-done.17.refs_1_ = bf16[4,2,32,16,128]{4,3,2,1,0:T(8,128)(2,1)} collective-permute-done((bf16[4,2,32,16,128]{4,3,2,1,0:T(8,128)(2,1)S(1)}, bf16[4,2,32,16,128]{4,3,2,1,0:T(8,128)(2,1)}, u32[]{:S(2)}, u32[]{:S(2)}) %collective-permute-start.17) | collective-permute-done | bytes 1048608 | tf_op jit(solution)/shard_map/ppermute | solution.py:507
  173.3 6.1 %shard_map.114.w_ref.right_ref = bf16[128,128,128]{2,1,0:T(8,128)(2,1)} custom-call(s32[4]{0:T(128)} %pad_add_fusion.1.pos_ref, bf16[4,2,32,16,128]{4,3,2,1,0:T(8,128)(2,1)} %copy-done, bf16[4,2,32,16,128]{4,3,2,1,0:T(8,128)(2,1)} %collective-permute-done.20.refs_1_, bf16[4,2,32,16,128]{4,3,2,1,0:T(8,128)(2,1)} %copy-done.4, ...), custom_call_target="tpu_custom_call" | custom-call | bytes 1024 | tf_op jit(solution)/shard_map/pallas_call | solution.py:59
  179.4 6.0 %shard_map.111.one_ref = bf16[128,128,128]{2,1,0:T(8,128)(2,1)} custom-call(s32[4]{0:T(128)} %pad_add_fusion.1.pos_ref, bf16[4,2,32,16,128]{4,3,2,1,0:T(8,128)(2,1)} %copy-done.1, bf16[4,2,32,16,128]{4,3,2,1,0:T(8,128)(2,1)} %collective-permute-done.11.refs_1_, bf16[4,2,32,16,128]{4,3,2,1,0:T(8,128)(2,1)} %collective-permute-done.12.refs_2_, ...), custom_call_target="tpu_custom_call" | custom-call | bytes 1024 | tf_op jit(solution)/shard_map/pallas_call | solution.py:59
  185.4 6.1 %shard_map.112.two_ref.left_ref = bf16[128,128,128]{2,1,0:T(8,128)(2,1)} custom-call(s32[4]{0:T(128)} %pad_add_fusion.1.pos_ref, bf16[4,2,32,16,128]{4,3,2,1,0:T(8,128)(2,1)} %copy-done.2, bf16[4,2,32,16,128]{4,3,2,1,0:T(8,128)(2,1)} %collective-permute-done.17.refs_1_, bf16[4,2,32,16,128]{4,3,2,1,0:T(8,128)(2,1)} %collective-permute-done.18.refs_2_, ...), custom_call_target="tpu_custom_call" | custom-call | bytes 1024 | tf_op jit(solution)/shard_map/pallas_call | solution.py:59
  191.6 7.9 %shard_map.115.e_ref.refs_1_ = bf16[128,128,128]{2,1,0:T(8,128)(2,1)} custom-call(bf16[4,128,32,128]{3,2,1,0:T(8,128)(2,1)} %all-to-all-done.1.g_ref.refs_1_, bf16[128,128,128]{2,1,0:T(8,128)(2,1)} %shard_map.114.w_ref.right_ref), custom_call_target="tpu_custom_call" | custom-call | bytes 1024 | tf_op jit(solution)/shard_map/pallas_call | solution.py:59
  199.4 20.2 %shard_map.116 = (bf16[128,128,128]{2,1,0:T(8,128)(2,1)}, bf16[128,128,128]{2,1,0:T(8,128)(2,1)}, bf16[4,128,32,128]{3,2,1,0:T(8,128)(2,1)}) custom-call(bf16[4,128,32,128]{3,2,1,0:T(8,128)(2,1)} %all-to-all-done.s_ref.refs_2_, bf16[128,128,128]{2,1,0:T(8,128)(2,1)} %shard_map.111.one_ref, bf16[128,128,128]{2,1,0:T(8,128)(2,1)} %shard_map.112.two_ref.left_ref, ...), custom_call_target="tpu_custom_call" | custom-call | bytes 1024 | tf_op jit(solution)/shard_map/pallas_call | solution.py:59
  219.6 14.0 %shard_map.120 = (bf16[2,2,32,128,128]{4,3,2,1,0:T(8,128)(2,1)}, bf16[2,2,32,128,128]{4,3,2,1,0:T(8,128)(2,1)}) custom-call(s32[4]{0:T(128)} %pad_add_fusion.1.pos_ref, bf16[128,128,128]{2,1,0:T(8,128)(2,1)} %get-tuple-element.24.act_ref.refs_0_, bf16[128,128,128]{2,1,0:T(8,128)(2,1)} %shard_map.115.e_ref.refs_1_, ...), custom_call_target="tpu_custom_call" | custom-call | bytes 1024 | tf_op jit(solution)/shard_map/pallas_call | solution.py:59
  238.9 13.4 %shard_map.117 = (bf16[128,128,128]{2,1,0:T(8,128)(2,1)}, bf16[128,128,128]{2,1,0:T(8,128)(2,1)}) custom-call(bf16[128,128,128]{2,1,0:T(8,128)(2,1)} %get-tuple-element.24.act_ref.refs_0_, bf16[128,128,128]{2,1,0:T(8,128)(2,1)} %shard_map.112.two_ref.left_ref, bf16[128,128,128]{2,1,0:T(8,128)(2,1)} %shard_map.114.w_ref.right_ref), custom_call_target="tpu_custom_call" | custom-call | bytes 1024 | tf_op jit(solution)/shard_map/pallas_call | solution.py:59
  252.3 9.8 %shard_map.121 = (bf16[1,2,32,128,128]{4,3,2,1,0:T(8,128)(2,1)}, bf16[1,2,32,128,128]{4,3,2,1,0:T(8,128)(2,1)}) custom-call(s32[4]{0:T(128)} %pad_add_fusion.1.pos_ref, bf16[128,128,128]{2,1,0:T(8,128)(2,1)} %get-tuple-element.33.refs_0_, bf16[4,128,32,128]{3,2,1,0:T(8,128)(2,1)} %all-to-all-done.1.g_ref.refs_1_), custom_call_target="tpu_custom_call" | custom-call | bytes 1024 | tf_op jit(solution)/shard_map/pallas_call | solution.py:59
  268.1 19.0 %all-to-all-done.2.e_ref = bf16[4,128,32,128]{3,2,1,0:T(8,128)(2,1)} async-done(((bf16[4,128,32,128]{3,2,1,0:T(8,128)(2,1)}), bf16[4,128,32,128]{3,2,1,0:T(8,128)(2,1)}, u32[]{:S(2)}, u32[]{:S(2)}) %all-to-all-start.2) | async-done | bytes 4194336 | tf_op jit(solution)/shard_map/all_to_all | solution.py:544
  297.8 39.2 %collective-permute-done.34 = bf16[1,2,32,4,16,128]{5,4,2,3,1,0:T(8,128)(2,1)} collective-permute-done((bf16[1,2,32,4,16,128]{5,4,2,3,1,0:T(8,128)(2,1)}, bf16[1,2,32,4,16,128]{5,4,2,3,1,0:T(8,128)(2,1)}, u32[]{:S(2)}, u32[]{:S(2)}) %collective-permute-start.34) | collective-permute-done | bytes 1048608 | tf_op jit(solution)/shard_map/ppermute | solution.py:507
  341.7 9.4 %shard_map.119 = (bf16[32,128,512]{2,1,0:T(8,128)(2,1)}, bf16[32,128,128]{2,1,0:T(8,128)(2,1)}) custom-call(bf16[4,128,32,128]{3,2,1,0:T(8,128)(2,1)} %all-to-all-done.2.e_ref, bf16[32,128,512]{2,1,0:T(8,128)(2,1)} %bitcast.198, bf16[32,128,512]{2,1,0:T(8,128)(2,1)} %bitcast.201, bf16[32,128,128]{2,1,0:T(8,128)(2,1)} %shard_map.109.w_ref), custom_call_target="tpu_custom_call" | custom-call | bytes 1024 | tf_op jit(solution)/shard_map/pallas_call | solution.py:59
  365.7 35.9 %collective-permute-done.37 = bf16[1,2,32,16,128]{4,3,2,1,0:T(8,128)(2,1)} collective-permute-done((bf16[1,2,32,16,128]{4,3,2,1,0:T(8,128)(2,1)}, bf16[1,2,32,16,128]{4,3,2,1,0:T(8,128)(2,1)}, u32[]{:S(2)}, u32[]{:S(2)}) %collective-permute-start.37) | collective-permute-done | bytes 262176 | tf_op jit(solution)/shard_map/ppermute | solution.py:507
  406.4 14.8 %collective-permute-start.24 = (bf16[32,16,128]{2,1,0:T(8,128)(2,1)S(1)}, bf16[32,16,128]{2,1,0:T(8,128)(2,1)S(1)}, u32[]{:S(2)}, u32[]{:S(2)}) collective-permute-start(bf16[32,16,128]{2,1,0:T(8,128)(2,1)S(1)} %get-tuple-element.48), channel_id=1, source_target_pairs={{0,8},{4,12},{8,16},{12,20},{16,24},{20,28},{24,0},{28,4},{1,9},{5... | collective-permute-start | bytes 393224 | tf_op jit(solution)/shard_map/ppermute | solution.py:507
  431.4 6.1 %shard_map.118 = bf16[32,128,512]{2,1,0:T(8,128)(2,1)} custom-call(bf16[4,32,128,128]{3,2,1,0:T(8,128)(2,1)} %all-to-all-done.3.s_ref, bf16[32,128,512]{2,1,0:T(8,128)(2,1)} %bitcast.199), custom_call_target="tpu_custom_call" | custom-call | bytes 1024 | tf_op jit(solution)/shard_map/pallas_call | solution.py:59
  (121 shorter events, 125.8 us)
Async XLA Ops:
  13.9 53.1 %all-to-all-start.1 = ((bf16[4,128,32,128]{3,2,1,0:T(8,128)(2,1)}), bf16[4,128,32,128]{3,2,1,0:T(8,128)(2,1)}, u32[]{:S(2)}, u32[]{:S(2)}) async-start(bf16[4,128,32,128]{3,2,1,0:T(8,128)(2,1)} %shard_map.113), calls=%async_computation.1 | async-start | bytes 8388608 | tf_op jit(solution)/shard_map/all_to_all | solution.py:544
  34.9 37.0 %collective-permute-start.5 = (bf16[2,32,16,128]{3,2,1,0:T(8,128)(2,1)S(1)}, bf16[2,32,16,128]{3,2,1,0:T(8,128)(2,1)S(1)}, u32[]{:S(2)}, u32[]{:S(2)}) collective-permute-start(bf16[2,32,16,128]{3,2,1,0:T(8,128)(2,1)S(1)} %get-tuple-element.59), channel_id=1, source_target_pairs={{0,8},{4,12},{8,16},{12,20},{16,24},{20,28},{24,0},{28,4},{1,9},{5... | collective-permute-start | bytes 786440 | tf_op jit(solution)/shard_map/ppermute | solution.py:507
  38.2 33.7 %collective-permute-start.6 = (bf16[2,32,16,128]{3,2,1,0:T(8,128)(2,1)S(1)}, bf16[2,32,16,128]{3,2,1,0:T(8,128)(2,1)S(1)}, u32[]{:S(2)}, u32[]{:S(2)}) collective-permute-start(bf16[2,32,16,128]{3,2,1,0:T(8,128)(2,1)S(1)} %get-tuple-element.59), channel_id=1, source_target_pairs={{0,16},{4,20},{8,24},{12,28},{16,0},{20,4},{24,8},{28,12},{1,17},{... | collective-permute-start | bytes 786440 | tf_op jit(solution)/shard_map/ppermute | solution.py:507
  39.9 32.0 %collective-permute-start.7 = (bf16[2,32,16,128]{3,2,1,0:T(8,128)(2,1)S(1)}, bf16[2,32,16,128]{3,2,1,0:T(8,128)(2,1)S(1)}, u32[]{:S(2)}, u32[]{:S(2)}) collective-permute-start(bf16[2,32,16,128]{3,2,1,0:T(8,128)(2,1)S(1)} %get-tuple-element.59), channel_id=1, source_target_pairs={{0,24},{4,28},{8,0},{12,4},{16,8},{20,12},{24,16},{28,20},{1,25},{... | collective-permute-start | bytes 786440 | tf_op jit(solution)/shard_map/ppermute | solution.py:507
  67.0 132.4 %all-to-all-start = ((bf16[4,128,32,128]{3,2,1,0:T(8,128)(2,1)}), bf16[4,128,32,128]{3,2,1,0:T(8,128)(2,1)}, u32[]{:S(2)}, u32[]{:S(2)}) async-start(bf16[4,128,32,128]{3,2,1,0:T(8,128)(2,1)} %shard_map.110), calls=%async_computation | async-start | bytes 8388608 | tf_op jit(solution)/shard_map/all_to_all | solution.py:544
  103.0 26.2 %collective-permute-start.20 = (bf16[4,2,32,16,128]{4,3,2,1,0:T(8,128)(2,1)S(1)}, bf16[4,2,32,16,128]{4,3,2,1,0:T(8,128)(2,1)}, u32[]{:S(2)}, u32[]{:S(2)}) collective-permute-start(bf16[4,2,32,16,128]{4,3,2,1,0:T(8,128)(2,1)S(1)} %pad_maximum_fusion.refs_0_), channel_id=1, source_target_pairs={{0,4},{4,0},{8,12},{12,8},{16,20},{20,16},{24,28},{28,24},{1,5},{5... | collective-permute-start | bytes 3145736 | tf_op jit(solution)/shard_map/ppermute | solution.py:507
  104.5 47.2 %collective-permute-start.21 = (bf16[4,2,32,16,128]{4,3,2,1,0:T(8,128)(2,1)S(1)}, bf16[4,2,32,16,128]{4,3,2,1,0:T(8,128)(2,1)S(1)}, u32[]{:S(2)}, u32[]{:S(2)}) collective-permute-start(bf16[4,2,32,16,128]{4,3,2,1,0:T(8,128)(2,1)S(1)} %pad_maximum_fusion.refs_0_), channel_id=1, source_target_pairs={{0,1},{1,0},{2,3},{3,2},{4,5},{5,4},{6,7},{7,6},{8,9},{9,8},{10,11... | collective-permute-start | bytes 3145736 | tf_op jit(solution)/shard_map/ppermute | solution.py:507
  108.9 42.8 %collective-permute-start.11 = (bf16[4,2,32,16,128]{4,3,2,1,0:T(8,128)(2,1)S(1)}, bf16[4,2,32,16,128]{4,3,2,1,0:T(8,128)(2,1)}, u32[]{:S(2)}, u32[]{:S(2)}) collective-permute-start(bf16[4,2,32,16,128]{4,3,2,1,0:T(8,128)(2,1)S(1)} %pad_maximum_fusion.1.refs_0_), channel_id=1, source_target_pairs={{0,4},{4,0},{8,12},{12,8},{16,20},{20,16},{24,28},{28,24},{1,5},{5... | collective-permute-start | bytes 3145736 | tf_op jit(solution)/shard_map/ppermute | solution.py:507
  119.2 53.5 %collective-permute-start.17 = (bf16[4,2,32,16,128]{4,3,2,1,0:T(8,128)(2,1)S(1)}, bf16[4,2,32,16,128]{4,3,2,1,0:T(8,128)(2,1)}, u32[]{:S(2)}, u32[]{:S(2)}) collective-permute-start(bf16[4,2,32,16,128]{4,3,2,1,0:T(8,128)(2,1)S(1)} %pad_maximum_fusion.2.refs_0_), channel_id=1, source_target_pairs={{0,4},{4,0},{8,12},{12,8},{16,20},{20,16},{24,28},{28,24},{1,5},{5... | collective-permute-start | bytes 3145736 | tf_op jit(solution)/shard_map/ppermute | solution.py:507
  120.8 58.6 %collective-permute-start.12 = (bf16[4,2,32,16,128]{4,3,2,1,0:T(8,128)(2,1)S(1)}, bf16[4,2,32,16,128]{4,3,2,1,0:T(8,128)(2,1)}, u32[]{:S(2)}, u32[]{:S(2)}) collective-permute-start(bf16[4,2,32,16,128]{4,3,2,1,0:T(8,128)(2,1)S(1)} %pad_maximum_fusion.1.refs_0_), channel_id=1, source_target_pairs={{0,1},{1,0},{2,3},{3,2},{4,5},{5,4},{6,7},{7,6},{8,9},{9,8},{10,11... | collective-permute-start | bytes 3145736 | tf_op jit(solution)/shard_map/ppermute | solution.py:507
  129.2 44.1 %collective-permute-start.22 = (bf16[4,2,32,16,128]{4,3,2,1,0:T(8,128)(2,1)}, bf16[4,2,32,16,128]{4,3,2,1,0:T(8,128)(2,1)}, u32[]{:S(2)}, u32[]{:S(2)}) collective-permute-start(bf16[4,2,32,16,128]{4,3,2,1,0:T(8,128)(2,1)} %collective-permute-done.20.refs_1_), channel_id=1, source_target_pairs={{0,1},{1,0},{2,3},{3,2},{4,5},{5,4},{6,7},{7,6},{8,9},{9,8},{10,11... | collective-permute-start | bytes 3145736 | tf_op jit(solution)/shard_map/ppermute | solution.py:507
  151.6 27.8 %collective-permute-start.13 = (bf16[4,2,32,16,128]{4,3,2,1,0:T(8,128)(2,1)}, bf16[4,2,32,16,128]{4,3,2,1,0:T(8,128)(2,1)}, u32[]{:S(2)}, u32[]{:S(2)}) collective-permute-start(bf16[4,2,32,16,128]{4,3,2,1,0:T(8,128)(2,1)} %collective-permute-done.11.refs_1_), channel_id=1, source_target_pairs={{0,1},{1,0},{2,3},{3,2},{4,5},{5,4},{6,7},{7,6},{8,9},{9,8},{10,11... | collective-permute-start | bytes 3145736 | tf_op jit(solution)/shard_map/ppermute | solution.py:507
  151.6 33.8 %collective-permute-start.18 = (bf16[4,2,32,16,128]{4,3,2,1,0:T(8,128)(2,1)S(1)}, bf16[4,2,32,16,128]{4,3,2,1,0:T(8,128)(2,1)}, u32[]{:S(2)}, u32[]{:S(2)}) collective-permute-start(bf16[4,2,32,16,128]{4,3,2,1,0:T(8,128)(2,1)S(1)} %pad_maximum_fusion.2.refs_0_), channel_id=1, source_target_pairs={{0,1},{1,0},{2,3},{3,2},{4,5},{5,4},{6,7},{7,6},{8,9},{9,8},{10,11... | collective-permute-start | bytes 3145736 | tf_op jit(solution)/shard_map/ppermute | solution.py:507
  233.6 28.9 %collective-permute-start.27 = (bf16[2,2,32,128,128]{4,3,2,1,0:T(8,128)(2,1)}, bf16[2,2,32,128,128]{4,3,2,1,0:T(8,128)(2,1)}, u32[]{:S(2)}, u32[]{:S(2)}) collective-permute-start(bf16[2,2,32,128,128]{4,3,2,1,0:T(8,128)(2,1)} %get-tuple-element.32), channel_id=1, source_target_pairs={{0,1},{1,0},{2,3},{3,2},{4,5},{5,4},{6,7},{7,6},{8,9},{9,8},{10,11... | collective-permute-start | bytes 12582920 | tf_op jit(solution)/shard_map/ppermute | solution.py:507
  234.0 53.1 %all-to-all-start.2 = ((bf16[4,128,32,128]{3,2,1,0:T(8,128)(2,1)}), bf16[4,128,32,128]{3,2,1,0:T(8,128)(2,1)}, u32[]{:S(2)}, u32[]{:S(2)}) async-start(bf16[4,128,32,128]{3,2,1,0:T(8,128)(2,1)} %get-tuple-element.26), calls=%async_computation.2 | async-start | bytes 8388608 | tf_op jit(solution)/shard_map/all_to_all | solution.py:544
  262.1 30.1 %collective-permute-start.33 = (bf16[1,2,32,128,128]{4,3,2,1,0:T(8,128)(2,1)}, bf16[1,2,32,128,128]{4,3,2,1,0:T(8,128)(2,1)}, u32[]{:S(2)}, u32[]{:S(2)}) collective-permute-start(bf16[1,2,32,128,128]{4,3,2,1,0:T(8,128)(2,1)} %get-tuple-element.35), channel_id=1, source_target_pairs={{0,1},{1,0},{2,3},{3,2},{4,5},{5,4},{6,7},{7,6},{8,9},{9,8},{10,11... | collective-permute-start | bytes 6291464 | tf_op jit(solution)/shard_map/ppermute | solution.py:507
  266.6 89.6 %collective-permute-start.28 = (bf16[2,2,32,4,16,128]{5,4,2,0,3,1:T(8,128)(2,1)}, bf16[2,2,32,4,16,128]{5,4,2,0,3,1:T(8,128)(2,1)}, u32[]{:S(2)}, u32[]{:S(2)}) collective-permute-start(bf16[2,2,32,4,16,128]{5,4,2,0,3,1:T(8,128)(2,1)} %fusion), channel_id=1, source_target_pairs={{0,4},{4,0},{8,12},{12,8},{16,20},{20,16},{24,28},{28,24},{1,5},{5... | collective-permute-start | bytes 6291464 | tf_op jit(solution)/shard_map/ppermute | solution.py:507
  287.1 144.3 %all-to-all-start.3 = ((bf16[4,32,128,128]{3,2,1,0:T(8,128)(2,1)}), bf16[4,32,128,128]{3,2,1,0:T(8,128)(2,1)}, u32[]{:S(2)}, u32[]{:S(2)}) async-start(bf16[4,32,128,128]{3,2,1,0:T(8,128)(2,1)} %bitcast.203), calls=%async_computation.3 | async-start | bytes 8388608 | tf_op jit(solution)/shard_map/all_to_all | solution.py:544
  294.6 42.3 %collective-permute-start.34 = (bf16[1,2,32,4,16,128]{5,4,2,3,1,0:T(8,128)(2,1)}, bf16[1,2,32,4,16,128]{5,4,2,3,1,0:T(8,128)(2,1)}, u32[]{:S(2)}, u32[]{:S(2)}) collective-permute-start(bf16[1,2,32,4,16,128]{5,4,2,3,1,0:T(8,128)(2,1)} %fusion.1), channel_id=1, source_target_pairs={{0,4},{4,0},{8,12},{12,8},{16,20},{20,16},{24,28},{28,24},{1,5},{5... | collective-permute-start | bytes 3145736 | tf_op jit(solution)/shard_map/ppermute | solution.py:507
  353.0 52.1 %collective-permute-start.23 = (bf16[32,4,16,128]{3,2,0,1:T(8,128)(2,1)}, bf16[32,4,16,128]{3,2,0,1:T(8,128)(2,1)}, u32[]{:S(2)}, u32[]{:S(2)}) collective-permute-start(bf16[32,4,16,128]{3,2,0,1:T(8,128)(2,1)} %copy_bitcast_fusion), channel_id=1, source_target_pairs={{0,4},{4,0},{8,12},{12,8},{16,20},{20,16},{24,28},{28,24},{1,5},{5... | collective-permute-start | bytes 1572872 | tf_op jit(solution)/shard_map/ppermute | solution.py:507
  359.2 62.0 %collective-permute-start.29 = (bf16[2,2,32,16,128]{4,3,2,0,1:T(8,128)(2,1)}, bf16[2,2,32,16,128]{4,3,2,0,1:T(8,128)(2,1)S(1)}, u32[]{:S(2)}, u32[]{:S(2)}) collective-permute-start(bf16[2,2,32,16,128]{4,3,2,0,1:T(8,128)(2,1)} %get-tuple-element.45), channel_id=1, source_target_pairs={{0,8},{4,12},{8,16},{12,20},{16,24},{20,28},{24,0},{28,4},{1,9},{5... | collective-permute-start | bytes 1572872 | tf_op jit(solution)/shard_map/ppermute | solution.py:507
  361.3 59.9 %collective-permute-start.30 = (bf16[2,2,32,16,128]{4,3,2,0,1:T(8,128)(2,1)}, bf16[2,2,32,16,128]{4,3,2,0,1:T(8,128)(2,1)S(1)}, u32[]{:S(2)}, u32[]{:S(2)}) collective-permute-start(bf16[2,2,32,16,128]{4,3,2,0,1:T(8,128)(2,1)} %get-tuple-element.47), channel_id=1, source_target_pairs={{0,16},{4,20},{8,24},{12,28},{16,0},{20,4},{24,8},{28,12},{1,17},{... | collective-permute-start | bytes 1572872 | tf_op jit(solution)/shard_map/ppermute | solution.py:507
  361.4 62.3 %collective-permute-start.31 = (bf16[2,2,32,16,128]{4,3,2,0,1:T(8,128)(2,1)}, bf16[2,2,32,16,128]{4,3,2,0,1:T(8,128)(2,1)}, u32[]{:S(2)}, u32[]{:S(2)}) collective-permute-start(bf16[2,2,32,16,128]{4,3,2,0,1:T(8,128)(2,1)} %get-tuple-element.46), channel_id=1, source_target_pairs={{0,24},{4,28},{8,0},{12,4},{16,8},{20,12},{24,16},{28,20},{1,25},{... | collective-permute-start | bytes 1572872 | tf_op jit(solution)/shard_map/ppermute | solution.py:507
  363.7 37.9 %collective-permute-start.37 = (bf16[1,2,32,16,128]{4,3,2,1,0:T(8,128)(2,1)}, bf16[1,2,32,16,128]{4,3,2,1,0:T(8,128)(2,1)}, u32[]{:S(2)}, u32[]{:S(2)}) collective-permute-start(bf16[1,2,32,16,128]{4,3,2,1,0:T(8,128)(2,1)} %get-tuple-element.37), channel_id=1, source_target_pairs={{0,24},{4,28},{8,0},{12,4},{16,8},{20,12},{24,16},{28,20},{1,25},{... | collective-permute-start | bytes 786440 | tf_op jit(solution)/shard_map/ppermute | solution.py:507
  (29 other events, 624.7 us)

commit v4 on v1

v4 whole, which is shorter than its diff:
```python
import functools
import itertools
import math

import jax
import jax.numpy as jnp
from jax import lax
from jax.experimental import pallas as pl
from jax.experimental.pallas import tpu as pltpu
from jax.sharding import PartitionSpec as P

BF16 = jnp.bfloat16
F32 = jnp.float32
LANES = 128
PAD = 8
VMEM_BYTES = 60 * 1024 * 1024


def gelu_value(values):
    return jax.nn.gelu(values, approximate=True)


def gelu_back(values, upstream):
    return jax.vjp(gelu_value, values)[1](upstream)[0]


def gelu_both(v):
    root, cubic = 0.7978845608028654, 0.044715
    square = v * v
    t = jnp.tanh(root * (v + cubic * (v * square)))
    half = 0.5 * (1.0 + t)
    slope = half + (0.5 * v) * (1.0 - t * t) * (root + (3.0 * cubic * root) * square)
    return v * half, slope


def product(form, left, right):
    return jnp.einsum(form, left, right, preferred_element_type=F32)


def dot_nn(left, right):
    return lax.dot_general(left, right, (((1,), (0,)), ((), ())), preferred_element_type=F32)


def dot_tn(left, right):
    return lax.dot_general(left, right, (((0,), (0,)), ((), ())), preferred_element_type=F32)


def dot_nt(left, right):
    return lax.dot_general(left, right, (((1,), (1,)), ((), ())), preferred_element_type=F32)


def call(body, out, grid, in_specs, out_specs, scratch, args, scalars=None):
    spec = pltpu.PrefetchScalarGridSpec(
        num_scalar_prefetch=0 if scalars is None else 1,
        grid=grid,
        in_specs=in_specs,
        out_specs=out_specs,
        scratch_shapes=scratch,
    )
    return pl.pallas_call(
        body,
        out_shape=out,
        grid_spec=spec,
        compiler_params=pltpu.CompilerParams(
            dimension_semantics=("arbitrary",) * len(grid), vmem_limit_bytes=VMEM_BYTES
        ),
        cost_estimate=pl.CostEstimate(flops=0, bytes_accessed=1024, transcendentals=0),
    )(*(() if scalars is None else (scalars,)), *args)


def shape(dims, dtype=BF16):
    return jax.ShapeDtypeStruct(dims, dtype)


def each(count, body, unroll=16):
    def step(k, carry):
        body(k)
        return carry

    lax.fori_loop(0, count, step, 0, unroll=math.gcd(count, unroll))


def during(phase, steps):
    return lambda p, j: jnp.where(p == phase, j, jnp.where(p < phase, 0, steps - 1))


def stacked(ref, k):
    return jnp.concatenate([ref[c, k] for c in range(ref.shape[0])], axis=0)


class Ring:
    def __init__(self, axis, *digits):
        self.axis, self.digits, self.last = axis, digits, None
        self.stride, self.size = digits[0]

    def here(self):
        return lax.rem(lax.axis_index(self.axis) // self.stride, self.size)

    def send(self, value, *steps):
        pairs = []
        for src in range(lax.axis_size(self.axis)):
            dst = src
            for (stride, size), step in zip(self.digits, steps):
                own = src // stride % size
                dst += ((own + step) % size - own) * stride
            pairs.append((src, dst))
        if self.last is not None:
            value = after(value, self.last)
        self.last = lax.ppermute(value, self.axis, pairs)
        return self.last

    def sends(self, value):
        return [self.send(value, step) for step in range(1, self.size)]

    def gather(self, value):
        if self.size == 1:
            return value[None]
        here = self.here()
        out = jnp.zeros((self.size,) + value.shape, value.dtype)
        out = lax.dynamic_update_index_in_dim(out, value, here, 0)
        for step in range(1, self.size):
            got = self.send(value, step)
            out = lax.dynamic_update_index_in_dim(out, got, lax.rem(here - step + self.size, self.size), 0)
        return out

    def scatter(self, terms, dim):
        here = self.here()
        if self.size == 1:
            return [lax.index_in_dim(t, 0, dim, keepdims=False) for t in terms]
        out = [lax.dynamic_index_in_dim(t, here, dim, keepdims=False) for t in terms]
        for step in range(1, self.size):
            there = lax.rem(here + step, self.size)
            out.append(self.send(total([lax.dynamic_index_in_dim(t, there, dim, keepdims=False) for t in terms]).astype(BF16), step))
        return out


def total(terms):
    return functools.reduce(jnp.add, [t.astype(F32) for t in terms])


def after(value, *others):
    return lax.optimization_barrier((value,) + others)[0]


def turned_back(here, step, size):
    return lax.rem(here - step + size, size)


class Place:
    def __init__(self, share, n_dp):
        self.far, self.near = halves(share)
        self.y, self.core = Ring("tensor", (self.near, self.far)), Ring("tensor", (1, self.near))
        self.dp, stride = [], 1
        while stride < n_dp:
            size = next(p for p in range(2, n_dp + 1) if n_dp // stride % p == 0)
            self.dp.append(Ring("dp", (stride, size)))
            stride *= size
        self.steps = [(y, c) for y in range(self.far) for c in range(self.near)]
        self.links = {step: Ring("tensor", (self.near, self.far), (1, self.near)) for step in self.steps[1:]}
        self.links[(1, 0)] = self.y if self.far > 1 else None
        if self.near > 1:
            self.links[(0, 1)] = self.core
        self.rows = [ring.size for ring in self.dp]

    def position(self):
        return jnp.stack([ring.here() for ring in [self.y, self.core] + self.dp]).astype(jnp.int32)

    def onward(self, pos, n):
        y, c = self.steps[n]
        return lax.rem(pos[0] + y, self.far) * self.near + lax.rem(pos[1] + c, self.near)

    def source(self, pos, n):
        y, c = self.steps[n]
        return turned_back(pos[0], y, self.far) * self.near + turned_back(pos[1], c, self.near)

    def exchange(self, pieces):
        got = [pieces[0]] + [None] * (len(pieces) - 1)
        for n in reversed(range(1, len(pieces))):
            y, c = self.steps[n]
            if y == 0:
                got[n] = self.core.send(pieces[n], c)
            elif c == 0:
                got[n] = self.y.send(pieces[n], y)
            else:
                got[n] = self.links[(y, c)].send(pieces[n], y, c)
        return got


def piece_copies(place, pos_ref, pieces, whole, sems):
    copies = []
    home, rows, _ = pieces[0][0].shape[-3:]
    inner = [range(ring.size) for ring in place.dp[1:]]
    strides = [ring.stride for ring in place.dp]
    for c, row in enumerate(pieces):
        for d, ref in enumerate(row):
            lead = ref.shape[:-3]
            for back in itertools.product(*inner, range(lead[-1])):
                steps = (d,) + back[:-1]
                at = sum(turned_back(pos_ref[2 + n], steps[n], place.rows[n]) * strides[n] for n in range(len(steps))) if place.dp else 0
                group = 0
                if len(pieces) > 1 or lead[-1] > 1:
                    group = turned_back(pos_ref[0], back[-1], place.far) * place.near + turned_back(pos_ref[1], c, place.near)
                dst = whole.at[pl.ds(group * home, home), pl.ds(pl.multiple_of(at * rows, rows), rows), :]
                copies.append(pltpu.make_async_copy(ref.at[back], dst, sems.at[len(copies)]))
    return copies


def share_copies(place, pos_ref, parts, whole, sems):
    return [pltpu.make_async_copy(ref, whole.at[place.source(pos_ref, n)], sems.at[n]) for n, ref in enumerate(parts)]


def run(copies):
    for copy in copies:
        copy.start()


def finish(copies):
    for copy in copies:
        copy.wait()


def n_copies(place):
    return place.far * place.near * math.prod(place.rows)


def anywhere(count):
    return [pl.BlockSpec(memory_space=pl.ANY)] * count


def flat(pieces):
    return tuple(p for row in pieces for p in row)


def unflat(place, refs):
    wide = len(refs) // place.near
    return [refs[c * wide : (c + 1) * wide] for c in range(place.near)]


def deal_kernel(pos_ref, g_ref, out_ref, turned):
    home, size, _ = g_ref.shape
    pitch = home + PAD

    def store(o):
        turned[pl.ds(o, size, stride=pitch), :] = g_ref[o].astype(F32)

    def load(b):
        out_ref[b] = turned[pl.ds(pl.multiple_of(b * pitch, 8), home), :].astype(BF16)

    each(home, store)
    each(size, load)


def deal(place, pos, g_home, cut, n):
    home, size, _ = g_home.shape
    return call(
        deal_kernel,
        shape((size, home, cut)),
        (1,),
        [pl.BlockSpec((home, size, cut), lambda i, pos: (0, 0, place.onward(pos, n)))],
        pl.BlockSpec((size, home, cut), lambda i, pos: (0, 0, 0)),
        [pltpu.VMEM((size * (home + PAD), cut), F32)],
        (g_home,),
        scalars=pos,
    )


def first_kernel(place, pos_ref, x_ref, w_ref, *refs):
    *out_refs, turned = refs
    home, size, _ = x_ref.shape
    cut = out_refs[0].shape[2]
    pitch = home + PAD

    for n, out_ref in enumerate(out_refs):

        @pl.when(pl.program_id(0) == n)
        def _():
            lanes = pl.ds(pl.multiple_of(place.onward(pos_ref, n) * cut, cut), cut)

            def store(b):
                turned[pl.ds(b, size, stride=pitch), :] = dot_tn(w_ref[b], x_ref[b, :, lanes])

            def load(o):
                out_ref[o] = turned[pl.ds(pl.multiple_of(o * pitch, 8), home), :].astype(BF16)

            each(home, store)
            each(size, load)


def first_stage(place, pos, x_home, left_one, cut):
    home, size, tokens = x_home.shape
    share = tokens // cut
    return call(
        functools.partial(first_kernel, place),
        (shape((size, home, cut)),) * share,
        (share,),
        [
            pl.BlockSpec((home, size, tokens), lambda s, pos: (0, 0, 0)),
            pl.BlockSpec((home, size, size), lambda s, pos: (0, 0, 0)),
        ],
        (pl.BlockSpec((size, home, cut), lambda s, pos: (0, 0, 0)),) * share,
        [pltpu.VMEM((size * (home + PAD), cut), F32)],
        (x_home, left_one),
        scalars=pos,
    )


def last_kernel(place, pos_ref, *refs):
    share = place.far * place.near
    e_refs = refs[:share]
    x_ref, g_ref, w_ref, out_ref, grad_ref, turned = refs[share:]
    blocks, per, cut = e_refs[0].shape
    pitch = blocks + PAD

    for n in range(share):
        s = place.source(pos_ref, n)

        def store(o):
            turned[s, pl.ds(o, per, stride=pitch), :] = e_refs[n][o].astype(F32)

        each(blocks, store)

    def load(b):
        rows = pl.ds(pl.multiple_of(b * pitch, 8), blocks)
        e_b = jnp.concatenate([turned[s, rows, :].astype(BF16) for s in range(share)], axis=1)
        out_ref[b] = (g_ref[b].astype(F32) + dot_nn(w_ref[b], e_b)).astype(BF16)
        grad_ref[b] = dot_nt(x_ref[b], e_b).astype(BF16)

    each(per, load, 4)


def last_stage(place, pos, e_got, x_home, g_home, left_one):
    share = len(e_got)
    blocks, home, cut = e_got[0].shape
    _, size, tokens = x_home.shape
    per = math.gcd(home, 16)
    wide = pl.BlockSpec((per, size, tokens), lambda h, pos: (h, 0, 0))
    factor = pl.BlockSpec((per, size, size), lambda h, pos: (h, 0, 0))
    return call(
        functools.partial(last_kernel, place),
        (shape(g_home.shape), shape((home, size, size))),
        (home // per,),
        [pl.BlockSpec((blocks, per, cut), lambda h, pos: (0, h, 0))] * share + [wide, wide, factor],
        (wide, factor),
        [pltpu.VMEM((share, per * (blocks + PAD), cut), F32)],
        (*e_got, x_home, g_home, left_one),
        scalars=pos,
    )


def mixed_kernel(place, pos_ref, *refs):
    *s_refs, x_ref, out_ref = refs
    cut = s_refs[0].shape[2]
    for n, s_ref in enumerate(s_refs):
        lanes = pl.ds(pl.multiple_of(place.source(pos_ref, n) * cut, cut), cut)
        out_ref[:, :, lanes] = (x_ref[:, :, lanes].astype(F32) + s_ref[...].astype(F32)).astype(BF16)


def add_home(place, pos, s_got, x_home):
    home, blocks, cut = s_got[0].shape
    per = math.gcd(home, 8)
    wide = pl.BlockSpec((per,) + x_home.shape[1:], lambda h, pos: (h, 0, 0))
    return call(
        functools.partial(mixed_kernel, place),
        shape(x_home.shape),
        (home // per,),
        [pl.BlockSpec((per, blocks, cut), lambda h, pos: (h, 0, 0))] * len(s_got) + [wide],
        wide,
        [],
        (*s_got, x_home),
        scalars=pos,
    )


def join_kernel(place, pos_ref, *refs):
    *pieces, out_ref, sems = refs
    copies = piece_copies(place, pos_ref, [pieces], out_ref, sems)
    run(copies)
    finish(copies)


def join(place, pos, pieces):
    home, rows, size = pieces[0].shape[-3:]
    return call(
        functools.partial(join_kernel, place),
        shape((home, rows * math.prod(place.rows), size)),
        (1,),
        anywhere(len(pieces)),
        pl.BlockSpec(memory_space=pl.ANY),
        [pltpu.SemaphoreType.DMA((math.prod(place.rows),))],
        tuple(pieces),
        scalars=pos,
    )


def back_two_kernel(place, pos_ref, *refs):
    share = place.far * place.near
    g_parts, factor = refs[:share], unflat(place, refs[share:-6])
    out_ref, turned, g_all, w_all, g_sems, w_sems = refs[-6:]
    per, size, _ = out_ref.shape
    pitch = size + PAD
    phase, j = pl.program_id(0), pl.program_id(1)

    @pl.when((phase == 0) & (j == 0))
    def _():
        copies = share_copies(place, pos_ref, g_parts, g_all, g_sems) + piece_copies(place, pos_ref, factor, w_all, w_sems)
        run(copies)
        finish(copies)

    @pl.when(phase == 0)
    def _():
        def body(k):
            b = j * per + k
            turned[pl.ds(b, size, stride=pitch), :] = dot_nn(w_all[b], stacked(g_all, b))

        each(per, body)

    @pl.when(phase == 1)
    def _():
        def body(k):
            out_ref[k] = turned[pl.ds(pl.multiple_of((j * per + k) * pitch, 8), size), :].astype(BF16)

        each(per, body)


def middle_sizes(place, parts):
    blocks, home, cut = parts[0].shape
    return blocks, home, cut, len(parts), (blocks, blocks, blocks)


def back_two(place, pos, g_mid, right_two):
    blocks, home, cut, share, whole = middle_sizes(place, g_mid)
    at = during(1, share)
    return call(
        functools.partial(back_two_kernel, place),
        shape((blocks, blocks, cut)),
        (2, share),
        anywhere(share + len(flat(right_two))),
        pl.BlockSpec((home, blocks, cut), lambda p, j, pos: (at(p, j), 0, 0)),
        [
            pltpu.VMEM((blocks * (blocks + PAD), cut), F32),
            pltpu.VMEM((share, blocks, home, cut), BF16),
            pltpu.VMEM(whole, BF16),
            pltpu.SemaphoreType.DMA((share,)),
            pltpu.SemaphoreType.DMA((n_copies(place),)),
        ],
        (*g_mid, *flat(right_two)),
        scalars=pos,
    )


def either(place, pos_ref, j, keep_ref, send_ref, body):
    mine = lax.rem(j, place.near) == pos_ref[1]

    @pl.when(mine)
    def _():
        body(keep_ref)

    @pl.when(jnp.logical_not(mine))
    def _():
        body(send_ref)


def middle_kernel(place, pos_ref, *refs):
    share = place.far * place.near
    wide = (len(refs) - (2 * share + 15)) // 2
    s_parts, rest = refs[:share], refs[share:]
    one, two, rest = unflat(place, rest[:wide]), unflat(place, rest[wide : 2 * wide]), rest[2 * wide :]
    e_ref, act_ref, keep_two, send_two, keep_one, send_one, *rest = rest
    out_refs, rest = rest[:share], rest[share:]
    turned, hidden, e_one, s_all, one_all, two_all, s_sems, one_sems, two_sems = rest
    per, size, cut = act_ref.shape
    home = s_all.shape[2]
    pitch = size + PAD
    phase, j = pl.program_id(0), pl.program_id(1)

    def rows(k):
        return pl.ds(pl.multiple_of((j * per + k) * pitch, 8), size)

    def column(k):
        return pl.ds(j * per + k, size, stride=pitch)

    def second():
        return piece_copies(place, pos_ref, two, two_all, two_sems)

    @pl.when((phase == 0) & (j == 0))
    def _():
        copies = share_copies(place, pos_ref, s_parts, s_all, s_sems) + piece_copies(place, pos_ref, one, one_all, one_sems)
        run(copies)
        run(second())
        finish(copies)

    @pl.when(phase == 0)
    def _():
        def body(k):
            b = j * per + k
            turned[column(k), :] = dot_tn(one_all[b], stacked(s_all, b))

        each(per, body)

    @pl.when((phase == 1) & (j == 0))
    def _():
        finish(second())

    @pl.when(phase == 1)
    def _():
        def with_out(grad_ref):
            def body(k):
                v = turned[rows(k), :].astype(BF16).astype(F32)
                value, slope = gelu_both(v)
                act = value.astype(BF16)
                act_ref[k] = act
                e = e_ref[k]
                hidden[column(k), :] = slope * dot_nn(two_all[j * per + k], e)
                grad_ref[0, k] = dot_nt(act, e).astype(BF16)

            each(per, body, 8)

        either(place, pos_ref, j, keep_two, send_two, with_out)

    @pl.when(phase == 2)
    def _():
        def with_out(grad_ref):
            def body(k):
                b = j * per + k
                h = hidden[rows(k), :].astype(BF16)
                e_one[k] = dot_nn(one_all[b], h).astype(BF16)
                grad_ref[0, k] = dot_nt(stacked(s_all, b), h).astype(BF16)

            each(per, body)

        either(place, pos_ref, j, keep_one, send_one, with_out)
        for n in range(share):
            at = pl.ds(pl.multiple_of(place.onward(pos_ref, n) * home, home), home)
            out_refs[n][...] = e_one[:, at, :]


def grad_specs(place, phase, home, size, share):
    at = during(phase, share)
    dims = shape((place.far, home, size, size))
    spec = pl.BlockSpec((1, home, size, size), lambda p, j, pos: (at(p, j) // place.near, 0, 0, 0))
    return [dims] * 2, [spec] * 2


def middle(place, pos, s_mid, e_mid, right_one, left_two):
    blocks, home, cut, share, whole = middle_sizes(place, s_mid)
    at = [during(phase, share) for phase in range(3)]
    block = pl.BlockSpec((home, blocks, cut), lambda p, j, pos: (at[1](p, j), 0, 0))
    two, two_specs = grad_specs(place, 1, home, blocks, share)
    one, one_specs = grad_specs(place, 2, home, blocks, share)
    piece = pl.BlockSpec((home, home, cut), lambda p, j, pos: (at[2](p, j), 0, 0))
    out = call(
        functools.partial(middle_kernel, place),
        (shape((blocks, blocks, cut)), *two, *one) + (shape((blocks, home, cut)),) * share,
        (3, share),
        anywhere(share + 2 * len(flat(right_one))) + [block],
        (block, *two_specs, *one_specs) + (piece,) * share,
        [pltpu.VMEM((blocks * (blocks + PAD), cut), F32)] * 2
        + [
            pltpu.VMEM((home, blocks, cut), BF16),
            pltpu.VMEM((share, blocks, home, cut), BF16),
            pltpu.VMEM(whole, BF16),
            pltpu.VMEM(whole, BF16),
            pltpu.SemaphoreType.DMA((share,)),
            pltpu.SemaphoreType.DMA((n_copies(place),)),
            pltpu.SemaphoreType.DMA((n_copies(place),)),
        ],
        (*s_mid, *flat(right_one), *flat(left_two), e_mid),
        scalars=pos,
    )
    return out[0], out[1:3], out[3:5], list(out[5:])


def forward_two_kernel(place, pos_ref, *refs):
    share = place.far * place.near
    wide = (len(refs) - (2 * share + 11)) // 2
    g_parts, rest = refs[:share], refs[share:]
    left, right, rest = unflat(place, rest[:wide]), unflat(place, rest[wide : 2 * wide]), rest[2 * wide :]
    act_ref, keep_ref, send_ref, *rest = rest
    out_refs, rest = rest[:share], rest[share:]
    turned, fourth, g_all, left_all, right_all, g_sems, left_sems, right_sems = rest
    per, size, _ = act_ref.shape
    pitch = size + PAD
    phase, j = pl.program_id(0), pl.program_id(1)

    def rows(k):
        return pl.ds(pl.multiple_of((j * per + k) * pitch, 8), size)

    def column(k):
        return pl.ds(j * per + k, size, stride=pitch)

    def second():
        return piece_copies(place, pos_ref, right, right_all, right_sems) + share_copies(place, pos_ref, g_parts, g_all, g_sems)

    @pl.when((phase == 0) & (j == 0))
    def _():
        copies = piece_copies(place, pos_ref, left, left_all, left_sems)
        run(copies)
        run(second())
        finish(copies)

    @pl.when(phase == 0)
    def _():
        def body(k):
            turned[column(k), :] = dot_tn(left_all[j * per + k], act_ref[k])

        each(per, body)

    @pl.when((phase == 1) & (j == 0))
    def _():
        finish(second())

    @pl.when(phase == 1)
    def _():
        def with_out(grad_ref):
            def body(k):
                b = j * per + k
                third = turned[rows(k), :].astype(BF16)
                fourth[column(k), :] = dot_tn(right_all[b], third)
                grad_ref[0, k] = dot_nt(third, stacked(g_all, b)).astype(BF16)

            each(per, body)

        either(place, pos_ref, j, keep_ref, send_ref, with_out)

    for n in range(share):

        @pl.when((phase == 2) & (j == n))
        def _():
            base = place.onward(pos_ref, n) * per

            def body(k):
                out_refs[n][k] = fourth[pl.ds(pl.multiple_of((base + k) * pitch, 8), size), :].astype(BF16)

            each(per, body)


def forward_two(place, pos, act, g_mid, left_two, right_two):
    blocks, home, cut, share, whole = middle_sizes(place, g_mid)
    at = during(0, share)
    grad, grad_spec = grad_specs(place, 1, home, blocks, share)
    out = call(
        functools.partial(forward_two_kernel, place),
        (*grad,) + (shape((home, blocks, cut)),) * share,
        (3, share),
        anywhere(share + 2 * len(flat(left_two))) + [pl.BlockSpec((home, blocks, cut), lambda p, j, pos: (at(p, j), 0, 0))],
        (*grad_spec,) + (pl.BlockSpec((home, blocks, cut), lambda p, j, pos: (0, 0, 0)),) * share,
        [pltpu.VMEM((blocks * (blocks + PAD), cut), F32)] * 2
        + [
            pltpu.VMEM((share, blocks, home, cut), BF16),
            pltpu.VMEM(whole, BF16),
            pltpu.VMEM(whole, BF16),
            pltpu.SemaphoreType.DMA((share,)),
            pltpu.SemaphoreType.DMA((n_copies(place),)),
            pltpu.SemaphoreType.DMA((n_copies(place),)),
        ],
        (*g_mid, *flat(left_two), *flat(right_two), act),
        scalars=pos,
    )
    return out[:2], list(out[2:])


def halves(size):
    low = 2 if size % 2 == 0 else 1
    return size // low, low


def cross(pieces):
    return lax.all_to_all(pieces, "tensor", split_axis=0, concat_axis=0, tiled=True)


def whole_tokens(x_home, g_home, factors, share, cut):
    home, size, tokens = x_home.shape
    first_left = factors[0]
    rows = first_left.shape[1]
    place = Place(share, lax.axis_size("dp"))
    pos = place.position()

    def spread(start):
        for ring in reversed(place.dp[1:]):
            start = jnp.stack([start] + ring.sends(start))
        return [start] + (place.dp[0].sends(start) if place.dp else [])

    mine = jnp.stack([factors[3], factors[1], factors[2]])
    from_y = [mine] + place.y.sends(mine)
    one = join(place, pos, [p[..., None, :, :, :] for p in spread(first_left)])
    order = list(reversed(range(share)))
    g_pieces = {n: deal(place, pos, g_home, cut, n) for n in order}
    g_mid = place.exchange([g_pieces[n] for n in range(share)])

    def whole(n, *before):
        pieces = spread(jnp.stack([part[n] for part in from_y]))
        pieces = [after(p, *before) for p in pieces] if before else pieces
        by_core = [[p] + place.core.sends(p) for p in pieces]
        return [[p[c] for p in by_core] for c in range(place.near)]

    right_two = whole(0)
    s_mid = place.exchange(list(first_stage(place, pos, x_home, one, cut)))
    e_mid = back_two(place, pos, g_mid, right_two)
    right_one = whole(1)
    left_two = whole(2)
    act, grad_two, grad_one, e_out = middle(place, pos, s_mid, e_mid, right_one, left_two)
    e_got = place.exchange(e_out)

    def own_sum(terms):
        terms = [terms[0], place.core.send(terms[1], 1)] if place.near > 1 else terms[:1]
        terms = [t.reshape([place.far, home] + place.rows[::-1] + [rows, size]) for t in terms]
        return total(place.y.scatter(own_rows(terms, 2), 0))

    def own_rows(terms, dim):
        for n, ring in enumerate(place.dp):
            terms = ring.scatter(terms, dim + len(place.dp) - 1 - n)
        return terms

    grad_ltwo = own_sum(grad_two)
    grad_rone = own_sum(grad_one)
    grad_rtwo, s_out = forward_two(place, pos, act, g_mid, left_two, right_two)
    s_got = place.exchange(s_out)
    grad_rtwo = own_sum(grad_rtwo)

    input_grad, grad_lone = last_stage(place, pos, e_got, x_home, g_home, one)
    grad_lone = total(own_rows([grad_lone.reshape([home] + place.rows[::-1] + [rows, size])], 1))
    mixed = add_home(place, pos, s_got, x_home)
    return mixed, input_grad, grad_lone, grad_rone, grad_ltwo, grad_rtwo


def split_blocks(x_home, g_home, factors, share, cut):
    home, size, tokens = x_home.shape
    far, near = halves(share)
    outer, inner = halves(lax.axis_size("dp"))
    ring_y, ring_core = Ring("tensor", (near, far)), Ring("tensor", (1, near))
    ring_z, ring_x = Ring("dp", (inner, outer)), Ring("dp", (1, inner))
    rows = factors[0].shape[1]
    n_tensor = lax.axis_size("tensor")
    groups = n_tensor // share
    held = home * share
    same_tokens = [[group * share + part for group in range(groups)] for part in range(share)]

    def go(values):
        pieces = values.reshape(home, groups, held, share, cut).transpose(1, 3, 2, 0, 4)
        got = cross(pieces.reshape(n_tensor, held, home, cut))
        return got.transpose(1, 0, 2, 3).reshape(held, size, cut)

    def back(values):
        pieces = values.reshape(held, n_tensor, home, cut).transpose(1, 0, 2, 3)
        got = cross(pieces).reshape(groups, share, held, home, cut)
        return got.transpose(3, 0, 2, 1, 4).reshape(home, size, tokens)

    def turn(values):
        moved = lax.all_to_all(
            values.reshape(held, groups, held, cut), "tensor", split_axis=1, concat_axis=0, tiled=True, axis_index_groups=same_tokens
        )
        return jnp.swapaxes(moved.reshape(size, held, cut), 0, 1)

    def whole(factor):
        one = ring_z.gather(ring_y.gather(factor))
        all_rows = ring_core.gather(ring_x.gather(one))
        return all_rows.transpose(3, 0, 4, 2, 1, 5, 6).reshape(held, size, size)

    def own_sum(partial):
        split = partial.reshape(ring_y.size, ring_core.size, home, ring_z.size, ring_x.size, rows, size)
        terms = ring_core.scatter([split], 1)
        return total(ring_y.scatter(ring_z.scatter(ring_x.scatter(terms, 3), 2), 0))

    first_left, first_right, second_left, second_right = factors
    g_mid = go(g_home)
    left_one = ring_x.gather(ring_z.gather(first_left)).transpose(2, 1, 0, 3, 4).reshape(home, size, size)
    right_one, left_two, right_two = whole(first_right), whole(second_left), whole(second_right)

    s_one = go(product("bjt,bjo->bot", x_home, left_one).astype(BF16))
    s_two = turn(product("bit,bip->bpt", s_one, right_one).astype(BF16))
    act = gelu_value(s_two.astype(F32)).astype(BF16)
    e_three = turn(product("bot,bio->bit", g_mid, right_two).astype(BF16))
    h_mid = turn(gelu_back(s_two.astype(F32), product("bot,bjo->bjt", e_three, left_two)).astype(BF16))
    e_one = back(product("bpt,bip->bit", h_mid, right_one).astype(BF16))
    s_three = turn(product("bjt,bjo->bot", act, left_two).astype(BF16))
    s_four = back(product("bit,bio->bot", s_three, right_two).astype(BF16))
    mixed = (x_home.astype(F32) + s_four.astype(F32)).astype(BF16)

    grad_rtwo = own_sum(product("bit,bot->bio", s_three, g_mid))
    grad_ltwo = own_sum(product("bjt,bot->bjo", act, e_three))
    grad_rone = own_sum(product("bit,bpt->bip", s_one, h_mid))
    grad_lone = product("bjt,bot->bjo", x_home, e_one).reshape(home, ring_z.size, ring_x.size, rows, size)
    grad_lone = total(ring_z.scatter(ring_x.scatter([grad_lone], 2), 1))
    input_grad = (g_home.astype(F32) + product("bot,bjo->bjt", e_one, left_one)).astype(BF16)
    return mixed, input_grad, grad_lone, grad_rone, grad_ltwo, grad_rtwo


def per_device(inputs, cotangent, first_left, first_right, second_left, second_right):
    n_tensor = lax.axis_size("tensor")
    home, _, size = first_left.shape
    tokens = inputs.shape[1]
    share = math.gcd(n_tensor, max(1, tokens // LANES))
    cut = tokens // share
    plan = whole_tokens if share == n_tensor else split_blocks
    mixed, input_grad, *weight_grads = plan(
        inputs.reshape(home, size, tokens),
        cotangent.reshape(home, size, tokens),
        (first_left, first_right, second_left, second_right),
        share,
        cut,
    )
    return (mixed.reshape(inputs.shape), input_grad.reshape(inputs.shape), *weight_grads)


def solution(mesh):
    wide, factor = P("tensor", "dp"), P("tensor", "dp", None)
    return jax.shard_map(
        per_device,
        mesh=mesh,
        in_specs=(wide, wide, factor, factor, factor, factor),
        out_specs=(wide, wide, factor, factor, factor, factor),
        check_vma=False,
    )
```

time: 547 us -> 481 us (0.88); the launches traced: 537 us -> 479 us
  local copies, waits for them, and re-layouts: 157 us -> 9.27 us
  Pallas kernels: 0 us -> 133 us
  waiting for transfers between devices: 165 us -> 259 us
  matrix products: 80.5 us -> 0 us
  starting transfers between devices: 91.5 us -> 42.2 us
  other arithmetic: 40.5 us -> 34.9 us
    pallas_call x0 -> x11, Pallas kernels: none -> 133 us  [call(): pl.pallas_call(body, out_shape=out, grid_spec=spec, compiler_params=pltpu...]
    ppermute x44 -> x49, waiting for transfers between devices: 155 us -> 259 us  [send(): self.last = lax.ppermute(value, self.axis, pairs)]
    dot_general x12 -> x0, matrix products: 80.5 us -> none  [product(): return jnp.einsum(form, left, right, preferred_element_type=F32)]
    reshape x6 -> x0, local copies, waits for them, and re-layouts: 32.3 us -> none  [the longest x2 12.2 us: go(): values.reshape(home, groups, held, share, cut).transpose(1, 3, 2, 0, 4)]
    ppermute x44 -> x49, starting transfers between devices: 71.3 us -> 42.2 us  [send(): self.last = lax.ppermute(value, self.axis, pairs)]
    transpose x3 -> x0, local copies, waits for them, and re-layouts: 28.5 us -> none  [the longest x2 21 us: go(): return got.transpose(1, 0, 2, 3).reshape(held, size, cut)]
    dynamic_update_slice x36 -> x0, local copies, waits for them, and re-layouts: 27 us -> none  [the longest x22 15.9 us: gather(): lax.dynamic_update_index_in_dim(out, got, lax.rem(here - step + self.size...]
    convert_element_type x15 -> x0, local copies, waits for them, and re-layouts: 26.2 us -> none  [the longest x14 15.3 us: scatter(): lax.dynamic_index_in_dim(value, there, dim, keepdims=False).astype(BF16)]
  transfers between devices with their start and end apart: 48 -> 49, of which waited for: 15 -> 25; matrix products, arithmetic and copies ran while one was open for 39% -> 8% of each run, Pallas kernels for 0% -> 22%
where the time goes in v4:
time: 481 us; the launch traced here: 479 us
  waiting for transfers between devices  259 us (54%)
  Pallas kernels  133 us (28%)
  starting transfers between devices  42.2 us (9%)
  other arithmetic  34.9 us (7%)
  local copies, waits for them, and re-layouts  9.27 us (2%)
    ppermute x49, waiting for transfers between devices, send(): self.last = lax.ppermute(value, self.axis, pairs)  259 us
    pallas_call x11, Pallas kernels, call(): pl.pallas_call(body, out_shape=out, grid_spec=spec, compiler_params=pltpu...  133 us
    ppermute x49, starting transfers between devices, send(): self.last = lax.ppermute(value, self.axis, pairs)  42.2 us
    convert_element_type x14, other arithmetic, scatter(): total([lax.dynamic_index_in_dim(t, there, dim, keepdims=False) for t in t...  21.2 us
  transfers between devices with their start and end apart: 49, of which 25 were waited for; matrix products, arithmetic and copies ran while one was open for 8% of the time, Pallas kernels for 22%

profile of v4, /device:TPU:0, one launch (start us, length us, event | category | flops | bytes accessed | tf_op | source)
XLA Modules:
  0.0 479.2 jit_solution(8781988268286711748)
XLA Ops:
  7.3 6.5 %collective-permute-done.1 = bf16[3,32,16,128]{3,2,1,0:T(8,128)(2,1)S(1)} collective-permute-done((bf16[3,32,16,128]{3,2,1,0:T(8,128)(2,1)S(1)}, bf16[3,32,16,128]{3,2,1,0:T(8,128)(2,1)S(1)}, u32[]{:S(2)}, u32[]{:S(2)}) %collective-permute-start.1) | collective-permute-done | bytes 393248 | tf_op jit(solution)/shard_map/ppermute | solution.py:109
  24.3 5.3 %collective-permute-done.5 = bf16[2,32,16,128]{3,2,1,0:T(8,128)(2,1)S(1)} collective-permute-done((bf16[2,32,16,128]{3,2,1,0:T(8,128)(2,1)S(1)}, bf16[2,32,16,128]{3,2,1,0:T(8,128)(2,1)S(1)}, u32[]{:S(2)}, u32[]{:S(2)}) %collective-permute-start.5) | collective-permute-done | bytes 262176 | tf_op jit(solution)/shard_map/ppermute | solution.py:109
  29.8 5.4 %collective-permute-done.8 = bf16[2,32,16,128]{3,2,1,0:T(8,128)(2,1)S(1)} collective-permute-done((bf16[2,32,16,128]{3,2,1,0:T(8,128)(2,1)S(1)}, bf16[2,32,16,128]{3,2,1,0:T(8,128)(2,1)S(1)}, u32[]{:S(2)}, u32[]{:S(2)}) %collective-permute-start.8) | collective-permute-done | bytes 262176 | tf_op jit(solution)/shard_map/ppermute | solution.py:109
  37.4 11.6 %collective-permute-done.9 = bf16[2,2,32,16,128]{4,3,2,1,0:T(8,128)(2,1)S(1)} collective-permute-done((bf16[2,2,32,16,128]{4,3,2,1,0:T(8,128)(2,1)S(1)}, bf16[2,2,32,16,128]{4,3,2,1,0:T(8,128)(2,1)S(1)}, u32[]{:S(2)}, u32[]{:S(2)}) %collective-permute-start.9) | collective-permute-done | bytes 524320 | tf_op jit(solution)/shard_map/ppermute | solution.py:109
  51.9 23.0 %collective-permute-done.13.refs_5_.refs_9_ = bf16[2,2,2,32,16,128]{5,4,3,2,1,0:T(8,128)(2,1)} collective-permute-done((bf16[2,2,2,32,16,128]{5,4,3,2,1,0:T(8,128)(2,1)S(1)}, bf16[2,2,2,32,16,128]{5,4,3,2,1,0:T(8,128)(2,1)}, u32[]{:S(2)}, u32[]{:S(2)}) %collective-permute-start.13) | collective-permute-done | bytes 1048608 | tf_op jit(solution)/shard_map/ppermute | solution.py:109
  77.6 33.6 %shard_map.113.w_ref.refs_6_ = bf16[32,128,128]{2,1,0:T(8,128)(2,1)} custom-call(s32[5]{0:T(128)} %stack.116.pos_ref, bf16[2,2,1,32,16,128]{5,4,3,2,1,0:T(8,128)(2,1)} %get-tuple-element.134.refs_0_, bf16[2,2,1,32,16,128]{5,4,3,2,1,0:T(8,128)(2,1)} %bitcast.258), custom_call_target="tpu_custom_call" | custom-call | bytes 1024 | tf_op jit(solution)/shard_map/pallas_call | solution.py:60
  111.2 8.8 %shard_map.114 = (bf16[128,32,128]{2,1,0:T(8,128)(2,1)}, bf16[128,32,128]{2,1,0:T(8,128)(2,1)}, bf16[128,32,128]{2,1,0:T(8,128)(2,1)}, bf16[128,32,128]{2,1,0:T(8,128)(2,1)}) custom-call(s32[5]{0:T(128)} %stack.116.pos_ref, bf16[32,128,512]{2,1,0:T(8,128)(2,1)} %bitcast.235, bf16[32,128,128]{2,1,0:T(8,128)(2,1)} %shard_map.113.w_ref.refs_6_), custom_call_target="tpu_custom_call" | custom-call | bytes 1024 | tf_op jit(solution)/shard_map/pallas_call | solution.py:60
  123.0 12.6 %collective-permute-done.10 = bf16[2,2,32,16,128]{4,3,2,1,0:T(8,128)(2,1)S(1)} collective-permute-done((bf16[2,2,32,16,128]{4,3,2,1,0:T(8,128)(2,1)S(1)}, bf16[2,2,32,16,128]{4,3,2,1,0:T(8,128)(2,1)S(1)}, u32[]{:S(2)}, u32[]{:S(2)}) %collective-permute-start.10) | collective-permute-done | bytes 524320 | tf_op jit(solution)/shard_map/ppermute | solution.py:109
  138.3 22.0 %collective-permute-done.14.refs_5_ = bf16[2,2,2,32,16,128]{5,4,3,2,1,0:T(8,128)(2,1)} collective-permute-done((bf16[2,2,2,32,16,128]{5,4,3,2,1,0:T(8,128)(2,1)S(1)}, bf16[2,2,2,32,16,128]{5,4,3,2,1,0:T(8,128)(2,1)}, u32[]{:S(2)}, u32[]{:S(2)}) %collective-permute-start.14) | collective-permute-done | bytes 1048608 | tf_op jit(solution)/shard_map/ppermute | solution.py:109
  178.4 13.8 %collective-permute-done.3.refs_3_ = bf16[128,32,128]{2,1,0:T(8,128)(2,1)S(1)} collective-permute-done((bf16[128,32,128]{2,1,0:T(8,128)(2,1)}, bf16[128,32,128]{2,1,0:T(8,128)(2,1)S(1)}, u32[]{:S(2)}, u32[]{:S(2)}) %collective-permute-start.3) | collective-permute-done | bytes 1048608 | tf_op jit(solution)/shard_map/ppermute | solution.py:109
  192.5 22.2 %collective-permute-done.2.refs_2_ = bf16[128,32,128]{2,1,0:T(8,128)(2,1)S(1)} collective-permute-done((bf16[128,32,128]{2,1,0:T(8,128)(2,1)}, bf16[128,32,128]{2,1,0:T(8,128)(2,1)S(1)}, u32[]{:S(2)}, u32[]{:S(2)}) %collective-permute-start.2) | collective-permute-done | bytes 1048608 | tf_op jit(solution)/shard_map/ppermute | solution.py:109
  220.2 10.0 %shard_map.115.refs_12_ = bf16[128,128,128]{2,1,0:T(8,128)(2,1)} custom-call(s32[5]{0:T(128)} %stack.116.pos_ref, bf16[128,32,128]{2,1,0:T(8,128)(2,1)} %shard_map.109.refs_0_, bf16[128,32,128]{2,1,0:T(8,128)(2,1)} %copy-done.2, bf16[128,32,128]{2,1,0:T(8,128)(2,1)} %copy-done.5, bf16[128,32,128]{2,1,0:T(8,128)(2,1)} %copy-done.4, ...), custom_call_target="tpu_custom_call" | custom-call | bytes 1024 | tf_op jit(solution)/shard_map/pallas_call | solution.py:60
  230.2 7.0 %collective-permute-done.24.refs_3_ = bf16[128,32,128]{2,1,0:T(8,128)(2,1)} collective-permute-done((bf16[128,32,128]{2,1,0:T(8,128)(2,1)}, bf16[128,32,128]{2,1,0:T(8,128)(2,1)}, u32[]{:S(2)}, u32[]{:S(2)}) %collective-permute-start.24) | collective-permute-done | bytes 1048608 | tf_op jit(solution)/shard_map/ppermute | solution.py:109
  237.2 22.5 %collective-permute-done.23.refs_2_ = bf16[128,32,128]{2,1,0:T(8,128)(2,1)} collective-permute-done((bf16[128,32,128]{2,1,0:T(8,128)(2,1)}, bf16[128,32,128]{2,1,0:T(8,128)(2,1)}, u32[]{:S(2)}, u32[]{:S(2)}) %collective-permute-start.23) | collective-permute-done | bytes 1048608 | tf_op jit(solution)/shard_map/ppermute | solution.py:109
  259.7 28.7 %shard_map.116 = (bf16[128,128,128]{2,1,0:T(8,128)(2,1)}, bf16[2,32,128,128]{3,2,1,0:T(8,128)(2,1)}, bf16[2,32,128,128]{3,2,1,0:T(8,128)(2,1)}, bf16[2,32,128,12...) custom-call(s32[5]{0:T(128)} %stack.116.pos_ref, ...), custom_call_target="tpu_custom_call" | custom-call | bytes 1024 | tf_op jit(solution)/shard_map/pallas_call | solution.py:60
  296.1 20.8 %shard_map.117 = (bf16[2,32,128,128]{3,2,1,0:T(8,128)(2,1)}, bf16[2,32,128,128]{3,2,1,0:T(8,128)(2,1)}, bf16[32,128,128]{2,1,0:T(8,128)(2,1)}, bf16[32,128,128]{...) custom-call(s32[5]{0:T(128)} %stack.116.pos_ref, ...), custom_call_target="tpu_custom_call" | custom-call | bytes 1024 | tf_op jit(solution)/shard_map/pallas_call | solution.py:60
  326.2 21.4 %collective-permute-done.29 = bf16[2,32,2,2,16,128]{5,4,1,3,2,0:T(8,128)(2,1)S(1)} collective-permute-done((bf16[2,32,2,2,16,128]{5,4,1,3,2,0:T(8,128)(2,1)S(1)}, bf16[2,32,2,2,16,128]{5,4,1,3,2,0:T(8,128)(2,1)S(1)}, u32[]{:S(2)}, u32[]{:S(2)}) %collective-permute-start.29) | collective-permute-done | bytes 1048608 | tf_op jit(solution)/shard_map/ppermute | solution.py:109
  354.4 19.2 %collective-permute-done.30 = bf16[2,32,2,2,16,128]{5,4,1,0,3,2:T(8,128)(2,1)} collective-permute-done((bf16[2,32,2,2,16,128]{5,4,1,0,3,2:T(8,128)(2,1)}, bf16[2,32,2,2,16,128]{5,4,1,0,3,2:T(8,128)(2,1)}, u32[]{:S(2)}, u32[]{:S(2)}) %collective-permute-start.30) | collective-permute-done | bytes 1048608 | tf_op jit(solution)/shard_map/ppermute | solution.py:109
  380.3 15.3 %collective-permute-done.32 = bf16[2,32,2,16,128]{4,3,1,2,0:T(8,128)(2,1)} collective-permute-done((bf16[2,32,2,16,128]{4,3,1,2,0:T(8,128)(2,1)}, bf16[2,32,2,16,128]{4,3,1,2,0:T(8,128)(2,1)}, u32[]{:S(2)}, u32[]{:S(2)}) %collective-permute-start.32) | collective-permute-done | bytes 524320 | tf_op jit(solution)/shard_map/ppermute | solution.py:109
  398.9 9.9 %collective-permute-done.34 = bf16[2,32,16,128]{3,2,1,0:T(8,128)(2,1)} collective-permute-done((bf16[2,32,16,128]{3,2,1,0:T(8,128)(2,1)S(1)}, bf16[2,32,16,128]{3,2,1,0:T(8,128)(2,1)}, u32[]{:S(2)}, u32[]{:S(2)}) %collective-permute-start.34) | collective-permute-done | bytes 262176 | tf_op jit(solution)/shard_map/ppermute | solution.py:109
  415.1 10.1 %shard_map.119 = (bf16[32,128,512]{2,1,0:T(8,128)(2,1)}, bf16[32,128,128]{2,1,0:T(8,128)(2,1)}) custom-call(s32[5]{0:T(128)} %stack.116.pos_ref, bf16[128,32,128]{2,1,0:T(8,128)(2,1)} %get-tuple-element.121.refs_0_, bf16[128,32,128]{2,1,0:T(8,128)(2,1)} %collective-permute-done.25.refs_1_, bf16[128,32,128]{2,1,0:T(8,128)(2,1)} %collective-permute-done.35.refs_2_, ...), custom_call_target="tpu_custom_call" | custom-call | bytes 1024 | tf_op jit(solution)/shard_map/pallas_call | solution.py:60
  433.1 8.1 %collective-permute-done.43 = bf16[32,2,2,16,128]{4,3,0,2,1:T(8,128)(2,1)} collective-permute-done((bf16[32,2,2,16,128]{4,3,0,2,1:T(8,128)(2,1)}, bf16[32,2,2,16,128]{4,3,0,2,1:T(8,128)(2,1)}, u32[]{:S(2)}, u32[]{:S(2)}) %collective-permute-start.43) | collective-permute-done | bytes 524320 | tf_op jit(solution)/shard_map/ppermute | solution.py:109
  449.0 11.3 %collective-permute-done.40.refs_3_ = bf16[32,128,128]{2,1,0:T(8,128)(2,1)} collective-permute-done((bf16[32,128,128]{2,1,0:T(8,128)(2,1)}, bf16[32,128,128]{2,1,0:T(8,128)(2,1)}, u32[]{:S(2)}, u32[]{:S(2)}) %collective-permute-start.40) | collective-permute-done | bytes 1048608 | tf_op jit(solution)/shard_map/ppermute | solution.py:109
  460.3 6.9 %shard_map.118 = bf16[32,128,512]{2,1,0:T(8,128)(2,1)} custom-call(s32[5]{0:T(128)} %stack.116.pos_ref, bf16[32,128,128]{2,1,0:T(8,128)(2,1)} %get-tuple-element.94.refs_0_, bf16[32,128,128]{2,1,0:T(8,128)(2,1)} %copy-done.10, bf16[32,128,128]{2,1,0:T(8,128)(2,1)} %copy-done.13, bf16[32,128,128]{2,1,0:T(8,128)(2,1)} %collective-permute-done.40.refs_3_, ...), custom_call_target="tpu_custom_call" | custom-call | bytes 1024 | tf_op jit(solution)/shard_map/pallas_call | solution.py:60
  (173 shorter events, 121.9 us)
Async XLA Ops:
  22.6 26.6 %collective-permute-start = (bf16[128,32,128]{2,1,0:T(8,128)(2,1)}, bf16[128,32,128]{2,1,0:T(8,128)(2,1)S(1)}, u32[]{:S(2)}, u32[]{:S(2)}) collective-permute-start(bf16[128,32,128]{2,1,0:T(8,128)(2,1)} %shard_map.110), channel_id=1, source_target_pairs={{0,1},{1,0},{2,3},{3,2},{4,5},{5,4},{6,7},{7,6},{8,9},{9,8},{10,11... | collective-permute-start | bytes 3145736 | tf_op jit(solution)/shard_map/ppermute | solution.py:109
  50.0 25.0 %collective-permute-start.13 = (bf16[2,2,2,32,16,128]{5,4,3,2,1,0:T(8,128)(2,1)S(1)}, bf16[2,2,2,32,16,128]{5,4,3,2,1,0:T(8,128)(2,1)}, u32[]{:S(2)}, u32[]{:S(2)}) collective-permute-start(bf16[2,2,2,32,16,128]{5,4,3,2,1,0:T(8,128)(2,1)S(1)} %pad_maximum_fusion.2.refs_4_.refs_8_), channel_id=1, source_target_pairs={{0,4},{4,0},{8,12},{12,8},{16,20},{20,16},{24,28},{28,24},{1,5},{5... | collective-permute-start | bytes 3145736 | tf_op jit(solution)/shard_map/ppermute | solution.py:109
  75.0 45.1 %collective-permute-start.17 = (bf16[2,2,2,32,16,128]{5,4,3,2,1,0:T(8,128)(2,1)}, bf16[2,2,2,32,16,128]{5,4,3,2,1,0:T(8,128)(2,1)}, u32[]{:S(2)}, u32[]{:S(2)}) collective-permute-start(bf16[2,2,2,32,16,128]{5,4,3,2,1,0:T(8,128)(2,1)} %collective-permute-done.13.refs_5_.refs_9_), channel_id=1, source_target_pairs={{0,1},{1,0},{2,3},{3,2},{4,5},{5,4},{6,7},{7,6},{8,9},{9,8},{10,11... | collective-permute-start | bytes 3145736 | tf_op jit(solution)/shard_map/ppermute | solution.py:109
  75.7 44.6 %collective-permute-start.6 = (bf16[2,32,16,128]{3,2,1,0:T(8,128)(2,1)}, bf16[2,32,16,128]{3,2,1,0:T(8,128)(2,1)}, u32[]{:S(2)}, u32[]{:S(2)}) collective-permute-start(bf16[2,32,16,128]{3,2,1,0:T(8,128)(2,1)} %get-tuple-element.72), channel_id=1, source_target_pairs={{0,16},{4,20},{8,24},{12,28},{16,0},{20,4},{24,8},{28,12},{1,17},{... | collective-permute-start | bytes 786440 | tf_op jit(solution)/shard_map/ppermute | solution.py:109
  135.6 24.7 %collective-permute-start.14 = (bf16[2,2,2,32,16,128]{5,4,3,2,1,0:T(8,128)(2,1)S(1)}, bf16[2,2,2,32,16,128]{5,4,3,2,1,0:T(8,128)(2,1)}, u32[]{:S(2)}, u32[]{:S(2)}) collective-permute-start(bf16[2,2,2,32,16,128]{5,4,3,2,1,0:T(8,128)(2,1)S(1)} %pad_maximum_fusion.1.refs_4_), channel_id=1, source_target_pairs={{0,4},{4,0},{8,12},{12,8},{16,20},{20,16},{24,28},{28,24},{1,5},{5... | collective-permute-start | bytes 3145736 | tf_op jit(solution)/shard_map/ppermute | solution.py:109
  137.2 23.1 %collective-permute-start.19 = (bf16[2,2,2,32,16,128]{5,4,3,2,1,0:T(8,128)(2,1)S(1)}, bf16[2,2,2,32,16,128]{5,4,3,2,1,0:T(8,128)(2,1)S(1)}, u32[]{:S(2)}, u32[]{:S(2)}) collective-permute-start(bf16[2,2,2,32,16,128]{5,4,3,2,1,0:T(8,128)(2,1)S(1)} %pad_maximum_fusion.1.refs_4_), channel_id=1, source_target_pairs={{0,1},{1,0},{2,3},{3,2},{4,5},{5,4},{6,7},{7,6},{8,9},{9,8},{10,11... | collective-permute-start | bytes 3145736 | tf_op jit(solution)/shard_map/ppermute | solution.py:109
  166.5 25.6 %collective-permute-start.3 = (bf16[128,32,128]{2,1,0:T(8,128)(2,1)}, bf16[128,32,128]{2,1,0:T(8,128)(2,1)S(1)}, u32[]{:S(2)}, u32[]{:S(2)}) collective-permute-start(bf16[128,32,128]{2,1,0:T(8,128)(2,1)} %shard_map.112), channel_id=1, source_target_pairs={{0,3},{1,2},{2,1},{3,0},{4,7},{5,6},{6,5},{7,4},{8,11},{9,10},{10,... | collective-permute-start | bytes 3145736 | tf_op jit(solution)/shard_map/ppermute | solution.py:109
  170.4 44.3 %collective-permute-start.2 = (bf16[128,32,128]{2,1,0:T(8,128)(2,1)}, bf16[128,32,128]{2,1,0:T(8,128)(2,1)S(1)}, u32[]{:S(2)}, u32[]{:S(2)}) collective-permute-start(bf16[128,32,128]{2,1,0:T(8,128)(2,1)} %shard_map.111), channel_id=1, source_target_pairs={{0,2},{1,3},{2,0},{3,1},{4,6},{5,7},{6,4},{7,5},{8,10},{9,11},{10,... | collective-permute-start | bytes 3145736 | tf_op jit(solution)/shard_map/ppermute | solution.py:109
  176.8 38.4 %collective-permute-start.15 = (bf16[2,2,2,32,16,128]{5,4,3,2,1,0:T(8,128)(2,1)S(1)}, bf16[2,2,2,32,16,128]{5,4,3,2,1,0:T(8,128)(2,1)}, u32[]{:S(2)}, u32[]{:S(2)}) collective-permute-start(bf16[2,2,2,32,16,128]{5,4,3,2,1,0:T(8,128)(2,1)S(1)} %pad_maximum_fusion.refs_8_.refs_4_), channel_id=1, source_target_pairs={{0,4},{4,0},{8,12},{12,8},{16,20},{20,16},{24,28},{28,24},{1,5},{5... | collective-permute-start | bytes 3145736 | tf_op jit(solution)/shard_map/ppermute | solution.py:109
  178.4 36.8 %collective-permute-start.21 = (bf16[2,2,2,32,16,128]{5,4,3,2,1,0:T(8,128)(2,1)S(1)}, bf16[2,2,2,32,16,128]{5,4,3,2,1,0:T(8,128)(2,1)S(1)}, u32[]{:S(2)}, u32[]{:S(2)}) collective-permute-start(bf16[2,2,2,32,16,128]{5,4,3,2,1,0:T(8,128)(2,1)S(1)} %pad_maximum_fusion.refs_8_.refs_4_), channel_id=1, source_target_pairs={{0,1},{1,0},{2,3},{3,2},{4,5},{5,4},{6,7},{7,6},{8,9},{9,8},{10,11... | collective-permute-start | bytes 3145736 | tf_op jit(solution)/shard_map/ppermute | solution.py:109
  192.2 45.0 %collective-permute-start.24 = (bf16[128,32,128]{2,1,0:T(8,128)(2,1)}, bf16[128,32,128]{2,1,0:T(8,128)(2,1)}, u32[]{:S(2)}, u32[]{:S(2)}) collective-permute-start(bf16[128,32,128]{2,1,0:T(8,128)(2,1)} %get-tuple-element.92), channel_id=1, source_target_pairs={{0,3},{1,2},{2,1},{3,0},{4,7},{5,6},{6,5},{7,4},{8,11},{9,10},{10,... | collective-permute-start | bytes 3145736 | tf_op jit(solution)/shard_map/ppermute | solution.py:109
  214.8 45.0 %collective-permute-start.23 = (bf16[128,32,128]{2,1,0:T(8,128)(2,1)}, bf16[128,32,128]{2,1,0:T(8,128)(2,1)}, u32[]{:S(2)}, u32[]{:S(2)}) collective-permute-start(bf16[128,32,128]{2,1,0:T(8,128)(2,1)} %get-tuple-element.90), channel_id=1, source_target_pairs={{0,2},{1,3},{2,0},{3,1},{4,6},{5,7},{6,4},{7,5},{8,10},{9,11},{10,... | collective-permute-start | bytes 3145736 | tf_op jit(solution)/shard_map/ppermute | solution.py:109
  216.2 43.6 %collective-permute-start.22 = (bf16[2,2,2,32,16,128]{5,4,3,2,1,0:T(8,128)(2,1)}, bf16[2,2,2,32,16,128]{5,4,3,2,1,0:T(8,128)(2,1)}, u32[]{:S(2)}, u32[]{:S(2)}) collective-permute-start(bf16[2,2,2,32,16,128]{5,4,3,2,1,0:T(8,128)(2,1)} %collective-permute-done.15.refs_9_.refs_5_), channel_id=1, source_target_pairs={{0,1},{1,0},{2,3},{3,2},{4,5},{5,4},{6,7},{7,6},{8,9},{9,8},{10,11... | collective-permute-start | bytes 3145736 | tf_op jit(solution)/shard_map/ppermute | solution.py:109
  319.9 32.9 %collective-permute-start.41 = (bf16[2,32,128,128]{3,2,1,0:T(8,128)(2,1)}, bf16[2,32,128,128]{3,2,1,0:T(8,128)(2,1)}, u32[]{:S(2)}, u32[]{:S(2)}) collective-permute-start(bf16[2,32,128,128]{3,2,1,0:T(8,128)(2,1)} %get-tuple-element.126), channel_id=1, source_target_pairs={{0,1},{1,0},{2,3},{3,2},{4,5},{5,4},{6,7},{7,6},{8,9},{9,8},{10,11... | collective-permute-start | bytes 6291464 | tf_op jit(solution)/shard_map/ppermute | solution.py:109
  322.1 25.5 %collective-permute-start.29 = (bf16[2,32,2,2,16,128]{5,4,1,3,2,0:T(8,128)(2,1)S(1)}, bf16[2,32,2,2,16,128]{5,4,1,3,2,0:T(8,128)(2,1)S(1)}, u32[]{:S(2)}, u32[]{:S(2)}) collective-permute-start(bf16[2,32,2,2,16,128]{5,4,1,3,2,0:T(8,128)(2,1)S(1)} %fusion.1), channel_id=1, source_target_pairs={{0,4},{4,0},{8,12},{12,8},{16,20},{20,16},{24,28},{28,24},{1,5},{5... | collective-permute-start | bytes 3145736 | tf_op jit(solution)/shard_map/ppermute | solution.py:109
  348.6 24.9 %collective-permute-start.30 = (bf16[2,32,2,2,16,128]{5,4,1,0,3,2:T(8,128)(2,1)}, bf16[2,32,2,2,16,128]{5,4,1,0,3,2:T(8,128)(2,1)}, u32[]{:S(2)}, u32[]{:S(2)}) collective-permute-start(bf16[2,32,2,2,16,128]{5,4,1,0,3,2:T(8,128)(2,1)} %fusion), channel_id=1, source_target_pairs={{0,4},{4,0},{8,12},{12,8},{16,20},{20,16},{24,28},{28,24},{1,5},{5... | collective-permute-start | bytes 3145736 | tf_op jit(solution)/shard_map/ppermute | solution.py:109
  351.8 24.7 %collective-permute-start.31 = (bf16[2,32,2,16,128]{4,3,1,2,0:T(8,128)(2,1)S(1)}, bf16[2,32,2,16,128]{4,3,1,2,0:T(8,128)(2,1)S(1)}, u32[]{:S(2)}, u32[]{:S(2)}) collective-permute-start(bf16[2,32,2,16,128]{4,3,1,2,0:T(8,128)(2,1)S(1)} %fusion.4), channel_id=1, source_target_pairs={{0,8},{4,12},{8,0},{12,4},{16,24},{20,28},{24,16},{28,20},{1,9},{5... | collective-permute-start | bytes 1572872 | tf_op jit(solution)/shard_map/ppermute | solution.py:109
  352.4 46.5 %collective-permute-start.35 = (bf16[128,32,128]{2,1,0:T(8,128)(2,1)}, bf16[128,32,128]{2,1,0:T(8,128)(2,1)}, u32[]{:S(2)}, u32[]{:S(2)}) collective-permute-start(bf16[128,32,128]{2,1,0:T(8,128)(2,1)} %get-tuple-element.113), channel_id=1, source_target_pairs={{0,2},{1,3},{2,0},{3,1},{4,6},{5,7},{6,4},{7,5},{8,10},{9,11},{10,... | collective-permute-start | bytes 3145736 | tf_op jit(solution)/shard_map/ppermute | solution.py:109
  373.5 37.2 %collective-permute-start.42 = (bf16[2,32,2,2,16,128]{5,4,1,3,2,0:T(8,128)(2,1)S(1)}, bf16[2,32,2,2,16,128]{5,4,1,3,2,0:T(8,128)(2,1)}, u32[]{:S(2)}, u32[]{:S(2)}) collective-permute-start(bf16[2,32,2,2,16,128]{5,4,1,3,2,0:T(8,128)(2,1)S(1)} %fusion.2), channel_id=1, source_target_pairs={{0,4},{4,0},{8,12},{12,8},{16,20},{20,16},{24,28},{28,24},{1,5},{5... | collective-permute-start | bytes 3145736 | tf_op jit(solution)/shard_map/ppermute | solution.py:109
  377.9 37.2 %collective-permute-start.39 = (bf16[128,32,128]{2,1,0:T(8,128)(2,1)}, bf16[128,32,128]{2,1,0:T(8,128)(2,1)}, u32[]{:S(2)}, u32[]{:S(2)}) collective-permute-start(bf16[128,32,128]{2,1,0:T(8,128)(2,1)} %get-tuple-element.119), channel_id=1, source_target_pairs={{0,3},{1,2},{2,1},{3,0},{4,7},{5,6},{6,5},{7,4},{8,11},{9,10},{10,... | collective-permute-start | bytes 3145736 | tf_op jit(solution)/shard_map/ppermute | solution.py:109
  415.1 30.8 %collective-permute-start.38 = (bf16[32,128,128]{2,1,0:T(8,128)(2,1)}, bf16[32,128,128]{2,1,0:T(8,128)(2,1)S(1)}, u32[]{:S(2)}, u32[]{:S(2)}) collective-permute-start(bf16[32,128,128]{2,1,0:T(8,128)(2,1)} %get-tuple-element.116), channel_id=1, source_target_pairs={{0,2},{1,3},{2,0},{3,1},{4,6},{5,7},{6,4},{7,5},{8,10},{9,11},{10,... | collective-permute-start | bytes 3145736 | tf_op jit(solution)/shard_map/ppermute | solution.py:109
  415.1 45.2 %collective-permute-start.40 = (bf16[32,128,128]{2,1,0:T(8,128)(2,1)}, bf16[32,128,128]{2,1,0:T(8,128)(2,1)}, u32[]{:S(2)}, u32[]{:S(2)}) collective-permute-start(bf16[32,128,128]{2,1,0:T(8,128)(2,1)} %get-tuple-element.120), channel_id=1, source_target_pairs={{0,3},{1,2},{2,1},{3,0},{4,7},{5,6},{6,5},{7,4},{8,11},{9,10},{10,... | collective-permute-start | bytes 3145736 | tf_op jit(solution)/shard_map/ppermute | solution.py:109
  442.3 25.0 %collective-permute-start.45 = (bf16[32,2,16,128]{3,2,0,1:T(8,128)(2,1)S(1)}, bf16[32,2,16,128]{3,2,0,1:T(8,128)(2,1)S(1)}, u32[]{:S(2)}, u32[]{:S(2)}) collective-permute-start(bf16[32,2,16,128]{3,2,0,1:T(8,128)(2,1)S(1)} %fusion.7), channel_id=1, source_target_pairs={{0,8},{4,12},{8,0},{12,4},{16,24},{20,28},{24,16},{28,20},{1,9},{5... | collective-permute-start | bytes 786440 | tf_op jit(solution)/shard_map/ppermute | solution.py:109
  446.0 24.6 %collective-permute-start.48 = (bf16[32,16,128]{2,1,0:T(8,128)(2,1)S(1)}, bf16[32,16,128]{2,1,0:T(8,128)(2,1)S(1)}, u32[]{:S(2)}, u32[]{:S(2)}) collective-permute-start(bf16[32,16,128]{2,1,0:T(8,128)(2,1)S(1)} %fusion.10), channel_id=1, source_target_pairs={{0,2},{1,3},{2,0},{3,1},{4,6},{5,7},{6,4},{7,5},{8,10},{9,11},{10,... | collective-permute-start | bytes 393224 | tf_op jit(solution)/shard_map/ppermute | solution.py:109
  (52 other events, 821.0 us)

commit v5 on v4

--- a/solution.py
+++ b/solution.py
@@ -14,6 +14,7 @@
 LANES = 128
 PAD = 8
 VMEM_BYTES = 60 * 1024 * 1024
+BYTES_PER_US = 1_200_000
 
 
 def gelu_value(values):
@@ -49,7 +50,7 @@
     return lax.dot_general(left, right, (((1,), (1,)), ((), ())), preferred_element_type=F32)
 
 
-def call(body, out, grid, in_specs, out_specs, scratch, args, scalars=None):
+def call(body, out, grid, in_specs, out_specs, scratch, args, us, scalars=None):
     spec = pltpu.PrefetchScalarGridSpec(
         num_scalar_prefetch=0 if scalars is None else 1,
         grid=grid,
@@ -64,7 +65,7 @@
         compiler_params=pltpu.CompilerParams(
             dimension_semantics=("arbitrary",) * len(grid), vmem_limit_bytes=VMEM_BYTES
         ),
-        cost_estimate=pl.CostEstimate(flops=0, bytes_accessed=1024, transcendentals=0),
+        cost_estimate=pl.CostEstimate(flops=0, bytes_accessed=int(us * BYTES_PER_US), transcendentals=0),
     )(*(() if scalars is None else (scalars,)), *args)
 
 
@@ -89,8 +90,8 @@
 
 
 class Ring:
-    def __init__(self, axis, *digits):
-        self.axis, self.digits, self.last = axis, digits, None
+    def __init__(self, axis, *digits, tied=True):
+        self.axis, self.digits, self.last, self.tied = axis, digits, None, tied
         self.stride, self.size = digits[0]
 
     def here(self):
@@ -104,7 +105,7 @@
                 own = src // stride % size
                 dst += ((own + step) % size - own) * stride
             pairs.append((src, dst))
-        if self.last is not None:
+        if self.tied and self.last is not None:
             value = after(value, self.last)
         self.last = lax.ppermute(value, self.axis, pairs)
         return self.last
@@ -123,15 +124,57 @@
             out = lax.dynamic_update_index_in_dim(out, got, lax.rem(here - step + self.size, self.size), 0)
         return out
 
-    def scatter(self, terms, dim):
+    def scatter(self, terms, dim, before=()):
         here = self.here()
         if self.size == 1:
             return [lax.index_in_dim(t, 0, dim, keepdims=False) for t in terms]
         out = [lax.dynamic_index_in_dim(t, here, dim, keepdims=False) for t in terms]
         for step in range(1, self.size):
             there = lax.rem(here + step, self.size)
-            out.append(self.send(total([lax.dynamic_index_in_dim(t, there, dim, keepdims=False) for t in terms]).astype(BF16), step))
+            term = total([lax.dynamic_index_in_dim(t, there, dim, keepdims=False) for t in terms]).astype(BF16)
+            out.append(self.send(after(term, *before), step))
         return out
+
+
+def slot(place, values):
+    values = lax.optimization_barrier(values)
+    place.crossed = None
+    for ring in [place.y, place.core] + place.dp + list(place.links.values()):
+        ring.last = None
+    return values
+
+
+class Sum:
+    def __init__(self, arrays, rings, tail):
+        self.left = rings
+        dims = [ring.size if isinstance(ring, Ring) else ring for ring in rings]
+        self.arrays = [a.reshape(dims + list(tail)) for a in arrays]
+        self.rings = [rings] * len(arrays)
+
+    def cut(self, ring=None, index=None):
+        out = []
+        for array, rings in zip(self.arrays, self.rings):
+            dim = 0
+            for r in rings:
+                if isinstance(r, Ring) and (r is ring or r not in self.left):
+                    array = lax.dynamic_index_in_dim(array, index if r is ring else r.here(), dim, keepdims=False)
+                else:
+                    dim += 1
+            out.append(array)
+        return total(out)
+
+    def step(self, ring):
+        if ring not in self.left:
+            return
+        rest = [r for r in self.left if r is not ring]
+        parts = [self.cut(ring, lax.rem(ring.here() + step, ring.size)).astype(BF16) for step in range(1, ring.size)]
+        got = [ring.send(part, step + 1) for step, part in enumerate(parts)]
+        self.arrays, self.rings, self.left = self.arrays + got, self.rings + [rest] * len(got), rest
+
+    def finish(self):
+        for ring in [r for r in self.left[::-1] if isinstance(r, Ring)]:
+            self.step(ring)
+        return self.cut()
 
 
 def total(terms):
@@ -139,6 +182,8 @@
 
 
 def after(value, *others):
+    if not others:
+        return value
     return lax.optimization_barrier((value,) + others)[0]
 
 
@@ -149,17 +194,15 @@
 class Place:
     def __init__(self, share, n_dp):
         self.far, self.near = halves(share)
-        self.y, self.core = Ring("tensor", (self.near, self.far)), Ring("tensor", (1, self.near))
+        self.y, self.core = Ring("tensor", (self.near, self.far)), Ring("tensor", (1, self.near), tied=False)
         self.dp, stride = [], 1
         while stride < n_dp:
             size = next(p for p in range(2, n_dp + 1) if n_dp // stride % p == 0)
             self.dp.append(Ring("dp", (stride, size)))
             stride *= size
         self.steps = [(y, c) for y in range(self.far) for c in range(self.near)]
+        self.crossed = None
         self.links = {step: Ring("tensor", (self.near, self.far), (1, self.near)) for step in self.steps[1:]}
-        self.links[(1, 0)] = self.y if self.far > 1 else None
-        if self.near > 1:
-            self.links[(0, 1)] = self.core
         self.rows = [ring.size for ring in self.dp]
 
     def position(self):
@@ -173,30 +216,29 @@
         y, c = self.steps[n]
         return turned_back(pos[0], y, self.far) * self.near + turned_back(pos[1], c, self.near)
 
-    def exchange(self, pieces):
-        got = [pieces[0]] + [None] * (len(pieces) - 1)
-        for n in reversed(range(1, len(pieces))):
-            y, c = self.steps[n]
-            if y == 0:
-                got[n] = self.core.send(pieces[n], c)
-            elif c == 0:
-                got[n] = self.y.send(pieces[n], y)
-            else:
-                got[n] = self.links[(y, c)].send(pieces[n], y, c)
-        return got
+    def exchange(self, pieces, n):
+        y, c = self.steps[n]
+        piece = pieces[n]
+        if y == 0:
+            return self.core.send(piece, c)
+        if self.crossed is not None:
+            piece = after(piece, self.crossed)
+        self.crossed = self.y.send(piece, y) if c == 0 else self.links[(y, c)].send(piece, y, c)
+        return self.crossed
 
 
 def piece_copies(place, pos_ref, pieces, whole, sems):
     copies = []
+    order = range(len(place.dp))
     home, rows, _ = pieces[0][0].shape[-3:]
-    inner = [range(ring.size) for ring in place.dp[1:]]
-    strides = [ring.stride for ring in place.dp]
+    inner = [range(place.rows[n]) for n in order[1:]]
     for c, row in enumerate(pieces):
         for d, ref in enumerate(row):
             lead = ref.shape[:-3]
             for back in itertools.product(*inner, range(lead[-1])):
-                steps = (d,) + back[:-1]
-                at = sum(turned_back(pos_ref[2 + n], steps[n], place.rows[n]) * strides[n] for n in range(len(steps))) if place.dp else 0
+                at = 0
+                for n, step in zip(order, (d,) + back[:-1]):
+                    at += turned_back(pos_ref[2 + n], step, place.rows[n]) * place.dp[n].stride
                 group = 0
                 if len(pieces) > 1 or lead[-1] > 1:
                     group = turned_back(pos_ref[0], back[-1], place.far) * place.near + turned_back(pos_ref[1], c, place.near)
@@ -260,6 +302,7 @@
         pl.BlockSpec((size, home, cut), lambda i, pos: (0, 0, 0)),
         [pltpu.VMEM((size * (home + PAD), cut), F32)],
         (g_home,),
+        us=3.5,
         scalars=pos,
     )
 
@@ -300,6 +343,7 @@
         (pl.BlockSpec((size, home, cut), lambda s, pos: (0, 0, 0)),) * share,
         [pltpu.VMEM((size * (home + PAD), cut), F32)],
         (x_home, left_one),
+        us=8,
         scalars=pos,
     )
 
@@ -343,6 +387,7 @@
         (wide, factor),
         [pltpu.VMEM((share, per * (blocks + PAD), cut), F32)],
         (*e_got, x_home, g_home, left_one),
+        us=10,
         scalars=pos,
     )
 
@@ -367,6 +412,7 @@
         wide,
         [],
         (*s_got, x_home),
+        us=6,
         scalars=pos,
     )
 
@@ -385,9 +431,10 @@
         shape((home, rows * math.prod(place.rows), size)),
         (1,),
         anywhere(len(pieces)),
-        pl.BlockSpec(memory_space=pl.ANY),
+        pl.BlockSpec((home, rows * math.prod(place.rows), size), lambda i, pos: (0, 0, 0)),
         [pltpu.SemaphoreType.DMA((math.prod(place.rows),))],
         tuple(pieces),
+        us=3,
         scalars=pos,
     )
 
@@ -444,6 +491,7 @@
             pltpu.SemaphoreType.DMA((n_copies(place),)),
         ],
         (*g_mid, *flat(right_two)),
+        us=10,
         scalars=pos,
     )
 
@@ -565,6 +613,7 @@
             pltpu.SemaphoreType.DMA((n_copies(place),)),
         ],
         (*s_mid, *flat(right_one), *flat(left_two), e_mid),
+        us=26,
         scalars=pos,
     )
     return out[0], out[1:3], out[3:5], list(out[5:])
@@ -654,6 +703,7 @@
             pltpu.SemaphoreType.DMA((n_copies(place),)),
         ],
         (*g_mid, *flat(left_two), *flat(right_two), act),
+        us=20,
         scalars=pos,
     )
     return out[:2], list(out[2:])
@@ -675,50 +725,117 @@
     place = Place(share, lax.axis_size("dp"))
     pos = place.position()
 
-    def spread(start):
-        for ring in reversed(place.dp[1:]):
-            start = jnp.stack([start] + ring.sends(start))
-        return [start] + (place.dp[0].sends(start) if place.dp else [])
-
+    def gather(start, skip, *before):
+        ring = place.dp[skip]
+        got = [start] + ring.sends(after(start, *before))
+        return got if skip == 0 else jnp.stack(got)
+
+    def gathers(start):
+        for n in reversed(range(1, len(place.dp))):
+            start = gather(start, n)
+        return start
+
+    last_dp = (lambda start: gather(start, 0)) if place.dp else (lambda start: [start])
+
+    def cores(piece):
+        return [piece] + place.core.sends(piece)
+
+    def by_core(own):
+        return [[p[c] for p in own] for c in range(place.near)]
+
+    def cross(pieces, n):
+        return place.exchange(pieces, n) if n < share else None
+
+    n_one, n_two, n_three = (place.steps.index(step) if step in place.steps else share for step in [(0, 1), (1, 0), (1, 1)])
     mine = jnp.stack([factors[3], factors[1], factors[2]])
     from_y = [mine] + place.y.sends(mine)
-    one = join(place, pos, [p[..., None, :, :, :] for p in spread(first_left)])
-    order = list(reversed(range(share)))
-    g_pieces = {n: deal(place, pos, g_home, cut, n) for n in order}
-    g_mid = place.exchange([g_pieces[n] for n in range(share)])
-
-    def whole(n, *before):
-        pieces = spread(jnp.stack([part[n] for part in from_y]))
-        pieces = [after(p, *before) for p in pieces] if before else pieces
-        by_core = [[p] + place.core.sends(p) for p in pieces]
-        return [[p[c] for p in by_core] for c in range(place.near)]
-
-    right_two = whole(0)
-    s_mid = place.exchange(list(first_stage(place, pos, x_home, one, cut)))
+    one = first_left
+    g = {n: deal(place, pos, g_home, cut, n) for n in range(share) if n >= 2}
+    from_y, g = slot(place, (from_y, g))
+
+    wholes = [jnp.stack([part[n] for part in from_y]) for n in range(3)]
+    got_three = cross(g, n_three)
+    one = last_dp(gathers(one))
+    wholes[0] = gathers(wholes[0])
+    g |= {n: deal(place, pos, g_home, cut, n) for n in range(share) if n < 2}
+    got_one = cross(g, n_one)
+    got_three, got_one, one, wholes, g = slot(place, (got_three, got_one, one, wholes, g))
+
+    got_two = cross(g, n_two)
+    right_two = last_dp(wholes[0])
+    wholes[1] = gathers(wholes[1])
+    one = join(place, pos, [p[..., None, :, :, :] for p in one])
+    s = first_stage(place, pos, x_home, one, cut)
+    got_two, right_two, wholes, one, s = slot(place, (got_two, right_two, wholes, one, list(s)))
+    g_mid = [g[0], got_one, got_two, got_three][:share]
+
+    got_three = cross(s, n_three)
+    got_one = cross(s, n_one)
+    right_one = last_dp(wholes[1])
+    wholes[2] = gathers(wholes[2])
+    right_two = by_core([cores(p) for p in right_two])
+    got_three, got_one, right_one, wholes, right_two = slot(place, (got_three, got_one, right_one, wholes, right_two))
+
+    got_two = cross(s, n_two)
+    left_two = last_dp(wholes[2])
+    left_core = cores(left_two[0])
+    right_one = by_core([cores(p) for p in right_one])
     e_mid = back_two(place, pos, g_mid, right_two)
-    right_one = whole(1)
-    left_two = whole(2)
-    act, grad_two, grad_one, e_out = middle(place, pos, s_mid, e_mid, right_one, left_two)
-    e_got = place.exchange(e_out)
-
-    def own_sum(terms):
-        terms = [terms[0], place.core.send(terms[1], 1)] if place.near > 1 else terms[:1]
-        terms = [t.reshape([place.far, home] + place.rows[::-1] + [rows, size]) for t in terms]
-        return total(place.y.scatter(own_rows(terms, 2), 0))
-
-    def own_rows(terms, dim):
-        for n, ring in enumerate(place.dp):
-            terms = ring.scatter(terms, dim + len(place.dp) - 1 - n)
-        return terms
-
-    grad_ltwo = own_sum(grad_two)
-    grad_rone = own_sum(grad_one)
-    grad_rtwo, s_out = forward_two(place, pos, act, g_mid, left_two, right_two)
-    s_got = place.exchange(s_out)
-    grad_rtwo = own_sum(grad_rtwo)
-
-    input_grad, grad_lone = last_stage(place, pos, e_got, x_home, g_home, one)
-    grad_lone = total(own_rows([grad_lone.reshape([home] + place.rows[::-1] + [rows, size])], 1))
+    got_two, left_two, left_core, right_one, e_mid = slot(place, (got_two, left_two, left_core, right_one, e_mid))
+    s_mid = [s[0], got_one, got_two, got_three][:share]
+    left_two = by_core([left_core] + [cores(p) for p in left_two[1:]])
+
+    act, grad_two, grad_one, e = middle(place, pos, s_mid, e_mid, right_one, left_two)
+
+    def start_sum(keep, send):
+        arrays = [keep, place.core.send(send, 1)] if place.near > 1 else [keep]
+        return Sum(arrays, [place.y, home] + place.dp[::-1], (rows, size))
+
+    def hold(parts, arrays):
+        for part, kept in zip(parts, arrays):
+            part.arrays = kept
+
+    def arrays_of(*parts):
+        return [part.arrays for part in parts]
+
+    x_step, near_step, far_step = (place.dp + [None] * 3)[:3]
+
+    e_three = cross(e, n_three)
+    two = start_sum(*grad_two)
+    grad_three, s = forward_two(place, pos, act, g_mid, left_two, right_two)
+    e_three, kept, grad_three, s, e, grad_one = slot(place, (e_three, arrays_of(two), grad_three, s, e, grad_one))
+    hold([two], kept)
+
+    e_two = cross(e, n_two)
+    two.step(x_step)
+    one_part, three = start_sum(*grad_one), start_sum(*grad_three)
+    e_one = cross(e, n_one)
+    e_two, e_one, kept, s = slot(place, (e_two, e_one, arrays_of(two, one_part, three), s))
+    hold([two, one_part, three], kept)
+    e_got = [e[0], e_one, e_two, e_three][:share]
+
+    s_three = cross(s, n_three)
+    three.step(x_step)
+    one_part.step(near_step)
+    input_grad, lone = last_stage(place, pos, e_got, x_home, g_home, one)
+    s_three, kept, lone, input_grad, s = slot(place, (s_three, arrays_of(two, one_part, three), lone, input_grad, s))
+    hold([two, one_part, three], kept)
+    lone = Sum([lone], [home] + place.dp[::-1], (rows, size))
+
+    s_two, s_one = cross(s, n_two), cross(s, n_one)
+    one_part.step(x_step)
+    two.step(near_step)
+    three.step(near_step)
+    lone.step(x_step)
+    one_part.step(far_step)
+    two.step(far_step)
+    s_got = [s[0], s_one, s_two, s_three][:share]
+    grad_rone = one_part.finish()
+    lone.step(near_step)
+    grad_ltwo = two.finish()
+    three.step(far_step)
+    grad_lone = lone.finish()
+    grad_rtwo = three.finish()
     mixed = add_home(place, pos, s_got, x_home)
     return mixed, input_grad, grad_lone, grad_rone, grad_ltwo, grad_rtwo
 

time: 481 us -> 342 us (0.71)
  waiting for transfers between devices: 259 us -> 147 us
  Pallas kernels: 133 us -> 103 us
    ppermute x49, waiting for transfers between devices: 259 us -> 147 us  [send(): self.last = lax.ppermute(value, self.axis, pairs)]
    pallas_call x11, Pallas kernels: 133 us -> 103 us  [call(): pl.pallas_call(body, out_shape=out, grid_spec=spec, compiler_params=pltpu...]
  transfers between devices with their start and end apart: 49 -> 49, of which waited for: 25 -> 26; matrix products, arithmetic and copies ran while one was open for 8% -> 10% of each run, Pallas kernels for 22% -> 22%
where the time goes in v5:
time: 342 us; the launch traced here: 341 us
  waiting for transfers between devices  147 us (43%)
  Pallas kernels  103 us (30%)
  starting transfers between devices  47 us (14%)
  other arithmetic  38 us (11%)
  local copies, waits for them, and re-layouts  6.01 us (2%)
    ppermute x49, waiting for transfers between devices, send(): self.last = lax.ppermute(value, self.axis, pairs)  147 us
    pallas_call x11, Pallas kernels, call(): pl.pallas_call(body, out_shape=out, grid_spec=spec, compiler_params=pltpu...  103 us
    ppermute x49, starting transfers between devices, send(): self.last = lax.ppermute(value, self.axis, pairs)  47 us
    convert_element_type x14, other arithmetic, step(): self.cut(ring, lax.rem(ring.here() + step, ring.size)).astype(BF16)  23.9 us
    add x4, other arithmetic, total(): return functools.reduce(jnp.add, [t.astype(F32) for t in terms])  7.49 us
  transfers between devices with their start and end apart: 49, of which 26 were waited for; matrix products, arithmetic and copies ran while one was open for 10% of the time, Pallas kernels for 22%

profile of v5, /device:TPU:0, one launch (start us, length us, event | category | flops | bytes accessed | tf_op | source)
XLA Modules:
  0.0 341.3 jit_solution(15287146270358151390)
XLA Ops:
  8.0 3.5 %shard_map.109 = bf16[128,32,128]{2,1,0:T(8,128)(2,1)} custom-call(s32[5]{0:T(128)} %stack.116.pos_ref, bf16[32,128,512]{2,1,0:T(8,128)(2,1)} %bitcast.193), custom_call_target="tpu_custom_call" | custom-call | bytes 4200000 | tf_op jit(solution)/shard_map/pallas_call | solution.py:61
  11.5 3.5 %shard_map.110 = bf16[128,32,128]{2,1,0:T(8,128)(2,1)} custom-call(s32[5]{0:T(128)} %stack.116.pos_ref, bf16[32,128,512]{2,1,0:T(8,128)(2,1)} %bitcast.194), custom_call_target="tpu_custom_call" | custom-call | bytes 4200000 | tf_op jit(solution)/shard_map/pallas_call | solution.py:61
  17.6 3.5 %shard_map.111 = bf16[128,32,128]{2,1,0:T(8,128)(2,1)} custom-call(s32[5]{0:T(128)} %stack.116.pos_ref, bf16[32,128,512]{2,1,0:T(8,128)(2,1)} %bitcast.195), custom_call_target="tpu_custom_call" | custom-call | bytes 4200000 | tf_op jit(solution)/shard_map/pallas_call | solution.py:61
  24.4 5.6 %collective-permute-done.6 = bf16[2,32,16,128]{3,2,1,0:T(8,128)(2,1)S(1)} collective-permute-done((bf16[2,32,16,128]{3,2,1,0:T(8,128)(2,1)S(1)}, bf16[2,32,16,128]{3,2,1,0:T(8,128)(2,1)S(1)}, u32[]{:S(2)}, u32[]{:S(2)}) %collective-permute-start.6) | collective-permute-done | bytes 262176 | tf_op jit(solution)/shard_map/ppermute | solution.py:110
  30.9 4.6 %collective-permute-done.4 = bf16[2,32,16,128]{3,2,1,0:T(8,128)(2,1)S(1)} collective-permute-done((bf16[2,32,16,128]{3,2,1,0:T(8,128)(2,1)S(1)}, bf16[2,32,16,128]{3,2,1,0:T(8,128)(2,1)S(1)}, u32[]{:S(2)}, u32[]{:S(2)}) %collective-permute-start.4) | collective-permute-done | bytes 262176 | tf_op jit(solution)/shard_map/ppermute | solution.py:110
  37.2 3.5 %shard_map.112.refs_0_ = bf16[128,32,128]{2,1,0:T(8,128)(2,1)} custom-call(s32[5]{0:T(128)} %stack.116.pos_ref, bf16[32,128,512]{2,1,0:T(8,128)(2,1)} %bitcast.196), custom_call_target="tpu_custom_call" | custom-call | bytes 4200000 | tf_op jit(solution)/shard_map/pallas_call | solution.py:61
  40.8 8.7 %collective-permute-done.7 = bf16[2,2,32,16,128]{4,3,2,1,0:T(8,128)(2,1)} collective-permute-done((bf16[2,2,32,16,128]{4,3,2,1,0:T(8,128)(2,1)S(1)}, bf16[2,2,32,16,128]{4,3,2,1,0:T(8,128)(2,1)}, u32[]{:S(2)}, u32[]{:S(2)}) %collective-permute-start.7) | collective-permute-done | bytes 524320 | tf_op jit(solution)/shard_map/ppermute | solution.py:110
  55.3 9.5 %collective-permute-done.10 = bf16[2,32,16,128]{3,2,1,0:T(8,128)(2,1)S(1)} collective-permute-done((bf16[2,32,16,128]{3,2,1,0:T(8,128)(2,1)S(1)}, bf16[2,32,16,128]{3,2,1,0:T(8,128)(2,1)S(1)}, u32[]{:S(2)}, u32[]{:S(2)}) %collective-permute-start.10) | collective-permute-done | bytes 262176 | tf_op jit(solution)/shard_map/ppermute | solution.py:110
  68.7 8.8 %shard_map.114 = (bf16[128,32,128]{2,1,0:T(8,128)(2,1)}, bf16[128,32,128]{2,1,0:T(8,128)(2,1)}, bf16[128,32,128]{2,1,0:T(8,128)(2,1)}, bf16[128,32,128]{2,1,0:T(8,128)(2,1)}) custom-call(s32[5]{0:T(128)} %stack.116.pos_ref, bf16[32,128,512]{2,1,0:T(8,128)(2,1)} %bitcast.198, bf16[32,128,128]{2,1,0:T(8,128)(2,1)} %shard_map.113.w_ref.refs_6_), custom_call_target="tpu_custom_call" | custom-call | bytes 9600000 | tf_op jit(solution)/shard_map/pallas_call | solution.py:61
  83.1 12.6 %collective-permute-done.15 = bf16[2,32,16,128]{3,2,1,0:T(8,128)(2,1)S(1)} collective-permute-done((bf16[2,32,16,128]{3,2,1,0:T(8,128)(2,1)S(1)}, bf16[2,32,16,128]{3,2,1,0:T(8,128)(2,1)S(1)}, u32[]{:S(2)}, u32[]{:S(2)}) %collective-permute-start.15) | collective-permute-done | bytes 262176 | tf_op jit(solution)/shard_map/ppermute | solution.py:110
  98.5 11.0 %collective-permute-done.16 = bf16[2,2,32,16,128]{4,3,2,1,0:T(8,128)(2,1)S(1)} collective-permute-done((bf16[2,2,32,16,128]{4,3,2,1,0:T(8,128)(2,1)S(1)}, bf16[2,2,32,16,128]{4,3,2,1,0:T(8,128)(2,1)S(1)}, u32[]{:S(2)}, u32[]{:S(2)}) %collective-permute-start.16) | collective-permute-done | bytes 524320 | tf_op jit(solution)/shard_map/ppermute | solution.py:110
  109.7 11.8 %collective-permute-done.12.refs_3_ = bf16[128,32,128]{2,1,0:T(8,128)(2,1)S(1)} collective-permute-done((bf16[128,32,128]{2,1,0:T(8,128)(2,1)S(1)}, bf16[128,32,128]{2,1,0:T(8,128)(2,1)S(1)}, u32[]{:S(2)}, u32[]{:S(2)}) %collective-permute-start.12) | collective-permute-done | bytes 1048608 | tf_op jit(solution)/shard_map/ppermute | solution.py:110
  125.6 10.0 %shard_map.115.refs_12_ = bf16[128,128,128]{2,1,0:T(8,128)(2,1)} custom-call(s32[5]{0:T(128)} %stack.116.pos_ref, bf16[128,32,128]{2,1,0:T(8,128)(2,1)} %shard_map.112.refs_0_, bf16[128,32,128]{2,1,0:T(8,128)(2,1)} %copy-done.2, bf16[128,32,128]{2,1,0:T(8,128)(2,1)} %collective-permute-done.8.refs_2_, bf16[128,32,128]{2,1,0:T(8,128)(2,1)} %copy-done.3, ...), custom_call_target="tpu_custom_call" | custom-call | bytes 12000000 | tf_op jit(solution)/shard_map/pallas_call | solution.py:61
  135.5 11.5 %collective-permute-done.19.refs_2_ = bf16[128,32,128]{2,1,0:T(8,128)(2,1)} collective-permute-done((bf16[128,32,128]{2,1,0:T(8,128)(2,1)}, bf16[128,32,128]{2,1,0:T(8,128)(2,1)}, u32[]{:S(2)}, u32[]{:S(2)}) %collective-permute-start.19) | collective-permute-done | bytes 1048608 | tf_op jit(solution)/shard_map/ppermute | solution.py:110
  151.7 28.7 %shard_map.116 = (bf16[128,128,128]{2,1,0:T(8,128)(2,1)}, bf16[2,32,128,128]{3,2,1,0:T(8,128)(2,1)}, bf16[2,32,128,128]{3,2,1,0:T(8,128)(2,1)}, bf16[2,32,128,12...) custom-call(s32[5]{0:T(128)} %stack.116.pos_ref, ...), custom_call_target="tpu_custom_call" | custom-call | bytes 31200000 | tf_op jit(solution)/shard_map/pallas_call | solution.py:61
  182.2 21.0 %shard_map.117 = (bf16[2,32,128,128]{3,2,1,0:T(8,128)(2,1)}, bf16[2,32,128,128]{3,2,1,0:T(8,128)(2,1)}, bf16[32,128,128]{2,1,0:T(8,128)(2,1)}, bf16[32,128,128]{...) custom-call(s32[5]{0:T(128)} %stack.116.pos_ref, ...), custom_call_target="tpu_custom_call" | custom-call | bytes 24000000 | tf_op jit(solution)/shard_map/pallas_call | solution.py:61
  211.6 22.4 %collective-permute-done.29 = bf16[2,32,2,2,16,128]{5,4,1,3,2,0:T(8,128)(2,1)} collective-permute-done((bf16[2,32,2,2,16,128]{5,4,1,3,2,0:T(8,128)(2,1)S(1)}, bf16[2,32,2,2,16,128]{5,4,1,3,2,0:T(8,128)(2,1)}, u32[]{:S(2)}, u32[]{:S(2)}) %collective-permute-start.29) | collective-permute-done | bytes 1048608 | tf_op jit(solution)/shard_map/ppermute | solution.py:110
  243.2 10.1 %shard_map.118 = (bf16[32,128,512]{2,1,0:T(8,128)(2,1)}, bf16[32,128,128]{2,1,0:T(8,128)(2,1)}) custom-call(s32[5]{0:T(128)} %stack.116.pos_ref, bf16[128,32,128]{2,1,0:T(8,128)(2,1)} %get-tuple-element.202.refs_0_, bf16[128,32,128]{2,1,0:T(8,128)(2,1)} %collective-permute-done.28.refs_1_, bf16[128,32,128]{2,1,0:T(8,128)(2,1)} %collective-permute-done.27.refs_2_, ...), custom_call_target="tpu_custom_call" | custom-call | bytes 12000000 | tf_op jit(solution)/shard_map/pallas_call | solution.py:61
  253.3 9.3 %collective-permute-done.34 = bf16[2,32,2,2,16,128]{5,4,1,3,2,0:T(8,128)(2,1)} collective-permute-done((bf16[2,32,2,2,16,128]{5,4,1,3,2,0:T(8,128)(2,1)}, bf16[2,32,2,2,16,128]{5,4,1,3,2,0:T(8,128)(2,1)}, u32[]{:S(2)}, u32[]{:S(2)}) %collective-permute-start.34) | collective-permute-done | bytes 1048608 | tf_op jit(solution)/shard_map/ppermute | solution.py:110
  278.4 6.8 %collective-permute-done.37 = bf16[2,32,2,16,128]{4,3,1,2,0:T(8,128)(2,1)} collective-permute-done((bf16[2,32,2,16,128]{4,3,1,2,0:T(8,128)(2,1)}, bf16[2,32,2,16,128]{4,3,1,2,0:T(8,128)(2,1)}, u32[]{:S(2)}, u32[]{:S(2)}) %collective-permute-start.37) | collective-permute-done | bytes 524320 | tf_op jit(solution)/shard_map/ppermute | solution.py:110
  294.6 5.7 %collective-permute-done.42 = bf16[2,32,16,128]{3,2,1,0:T(8,128)(2,1)S(1)} collective-permute-done((bf16[2,32,16,128]{3,2,1,0:T(8,128)(2,1)S(1)}, bf16[2,32,16,128]{3,2,1,0:T(8,128)(2,1)S(1)}, u32[]{:S(2)}, u32[]{:S(2)}) %collective-permute-start.42) | collective-permute-done | bytes 262176 | tf_op jit(solution)/shard_map/ppermute | solution.py:110
  302.6 6.8 %shard_map.119 = bf16[32,128,512]{2,1,0:T(8,128)(2,1)} custom-call(s32[5]{0:T(128)} %stack.116.pos_ref, bf16[32,128,128]{2,1,0:T(8,128)(2,1)} %get-tuple-element.212.refs_0_, bf16[32,128,128]{2,1,0:T(8,128)(2,1)} %collective-permute-done.35.refs_1_, bf16[32,128,128]{2,1,0:T(8,128)(2,1)} %copy-done.14, bf16[32,128,128]{2,1,0:T(8,128)(2,1)} %copy-done.11, ...), custom_call_target="tpu_custom_call" | custom-call | bytes 7200000 | tf_op jit(solution)/shard_map/pallas_call | solution.py:61
  319.8 4.7 %collective-permute-start.47 = (bf16[32,16,128]{2,1,0:T(8,128)(2,1)S(1)}, bf16[32,16,128]{2,1,0:T(8,128)(2,1)S(1)}, u32[]{:S(2)}, u32[]{:S(2)}) collective-permute-start(bf16[32,16,128]{2,1,0:T(8,128)(2,1)S(1)} %fusion.12), channel_id=1, source_target_pairs={{0,2},{1,3},{2,0},{3,1},{4,6},{5,7},{6,4},{7,5},{8,10},{9,11},{10,... | collective-permute-start | bytes 393224 | tf_op jit(solution)/shard_map/ppermute | solution.py:110
  335.9 3.7 %collective-permute-done.45 = bf16[32,16,128]{2,1,0:T(8,128)(2,1)S(1)} collective-permute-done((bf16[32,16,128]{2,1,0:T(8,128)(2,1)S(1)}, bf16[32,16,128]{2,1,0:T(8,128)(2,1)S(1)}, u32[]{:S(2)}, u32[]{:S(2)}) %collective-permute-start.45) | collective-permute-done | bytes 131104 | tf_op jit(solution)/shard_map/ppermute | solution.py:110
  (166 shorter events, 112.8 us)
Async XLA Ops:
  21.1 29.7 %collective-permute-start.2 = (bf16[128,32,128]{2,1,0:T(8,128)(2,1)}, bf16[128,32,128]{2,1,0:T(8,128)(2,1)S(1)}, u32[]{:S(2)}, u32[]{:S(2)}) collective-permute-start(bf16[128,32,128]{2,1,0:T(8,128)(2,1)} %shard_map.111), channel_id=1, source_target_pairs={{0,1},{1,0},{2,3},{3,2},{4,5},{5,4},{6,7},{7,6},{8,9},{9,8},{10,11... | collective-permute-start | bytes 3145736 | tf_op jit(solution)/shard_map/ppermute | solution.py:110
  21.1 29.7 %collective-permute-start.1 = (bf16[128,32,128]{2,1,0:T(8,128)(2,1)}, bf16[128,32,128]{2,1,0:T(8,128)(2,1)S(1)}, u32[]{:S(2)}, u32[]{:S(2)}) collective-permute-start(bf16[128,32,128]{2,1,0:T(8,128)(2,1)} %shard_map.110), channel_id=1, source_target_pairs={{0,3},{1,2},{2,1},{3,0},{4,7},{5,6},{6,5},{7,4},{8,11},{9,10},{10,... | collective-permute-start | bytes 3145736 | tf_op jit(solution)/shard_map/ppermute | solution.py:110
  52.3 29.6 %collective-permute-start.8 = (bf16[128,32,128]{2,1,0:T(8,128)(2,1)}, bf16[128,32,128]{2,1,0:T(8,128)(2,1)}, u32[]{:S(2)}, u32[]{:S(2)}) collective-permute-start(bf16[128,32,128]{2,1,0:T(8,128)(2,1)} %shard_map.109), channel_id=1, source_target_pairs={{0,2},{1,3},{2,0},{3,1},{4,6},{5,7},{6,4},{7,5},{8,10},{9,11},{10,... | collective-permute-start | bytes 3145736 | tf_op jit(solution)/shard_map/ppermute | solution.py:110
  53.8 28.1 %collective-permute-start.9 = (bf16[2,2,2,32,16,128]{5,4,3,2,1,0:T(8,128)(2,1)S(1)}, bf16[2,2,2,32,16,128]{5,4,3,2,1,0:T(8,128)(2,1)}, u32[]{:S(2)}, u32[]{:S(2)}) collective-permute-start(bf16[2,2,2,32,16,128]{5,4,3,2,1,0:T(8,128)(2,1)S(1)} %pad_maximum_fusion.refs_4_.refs_8_), channel_id=1, source_target_pairs={{0,4},{4,0},{8,12},{12,8},{16,20},{20,16},{24,28},{28,24},{1,5},{5... | collective-permute-start | bytes 3145736 | tf_op jit(solution)/shard_map/ppermute | solution.py:110
  95.9 25.5 %collective-permute-start.12 = (bf16[128,32,128]{2,1,0:T(8,128)(2,1)S(1)}, bf16[128,32,128]{2,1,0:T(8,128)(2,1)S(1)}, u32[]{:S(2)}, u32[]{:S(2)}) collective-permute-start(bf16[128,32,128]{2,1,0:T(8,128)(2,1)S(1)} %copy-done.23), channel_id=1, source_target_pairs={{0,3},{1,2},{2,1},{3,0},{4,7},{5,6},{6,5},{7,4},{8,11},{9,10},{10,... | collective-permute-start | bytes 3145736 | tf_op jit(solution)/shard_map/ppermute | solution.py:110
  96.1 26.0 %collective-permute-start.13 = (bf16[128,32,128]{2,1,0:T(8,128)(2,1)S(1)}, bf16[128,32,128]{2,1,0:T(8,128)(2,1)S(1)}, u32[]{:S(2)}, u32[]{:S(2)}) collective-permute-start(bf16[128,32,128]{2,1,0:T(8,128)(2,1)S(1)} %copy-done.22), channel_id=1, source_target_pairs={{0,1},{1,0},{2,3},{3,2},{4,5},{5,4},{6,7},{7,6},{8,9},{9,8},{10,11... | collective-permute-start | bytes 3145736 | tf_op jit(solution)/shard_map/ppermute | solution.py:110
  97.0 25.4 %collective-permute-start.14 = (bf16[2,2,2,32,16,128]{5,4,3,2,1,0:T(8,128)(2,1)}, bf16[2,2,2,32,16,128]{5,4,3,2,1,0:T(8,128)(2,1)}, u32[]{:S(2)}, u32[]{:S(2)}) collective-permute-start(bf16[2,2,2,32,16,128]{5,4,3,2,1,0:T(8,128)(2,1)} %pad_maximum_fusion.1.refs_4_), channel_id=1, source_target_pairs={{0,4},{4,0},{8,12},{12,8},{16,20},{20,16},{24,28},{28,24},{1,5},{5... | collective-permute-start | bytes 3145736 | tf_op jit(solution)/shard_map/ppermute | solution.py:110
  98.5 23.9 %collective-permute-start.17 = (bf16[2,2,2,32,16,128]{5,4,3,2,1,0:T(8,128)(2,1)S(1)}, bf16[2,2,2,32,16,128]{5,4,3,2,1,0:T(8,128)(2,1)S(1)}, u32[]{:S(2)}, u32[]{:S(2)}) collective-permute-start(bf16[2,2,2,32,16,128]{5,4,3,2,1,0:T(8,128)(2,1)S(1)} %pad_maximum_fusion.refs_4_.refs_8_), channel_id=1, source_target_pairs={{0,1},{1,0},{2,3},{3,2},{4,5},{5,4},{6,7},{7,6},{8,9},{9,8},{10,11... | collective-permute-start | bytes 3145736 | tf_op jit(solution)/shard_map/ppermute | solution.py:110
  121.5 25.6 %collective-permute-start.19 = (bf16[128,32,128]{2,1,0:T(8,128)(2,1)}, bf16[128,32,128]{2,1,0:T(8,128)(2,1)}, u32[]{:S(2)}, u32[]{:S(2)}) collective-permute-start(bf16[128,32,128]{2,1,0:T(8,128)(2,1)} %get-tuple-element.145), channel_id=1, source_target_pairs={{0,2},{1,3},{2,0},{3,1},{4,6},{5,7},{6,4},{7,5},{8,10},{9,11},{10,... | collective-permute-start | bytes 3145736 | tf_op jit(solution)/shard_map/ppermute | solution.py:110
  123.5 24.5 %collective-permute-start.20 = (bf16[2,2,2,32,16,128]{5,4,3,2,1,0:T(8,128)(2,1)S(1)}, bf16[2,2,2,32,16,128]{5,4,3,2,1,0:T(8,128)(2,1)S(1)}, u32[]{:S(2)}, u32[]{:S(2)}) collective-permute-start(bf16[2,2,2,32,16,128]{5,4,3,2,1,0:T(8,128)(2,1)S(1)} %pad_maximum_fusion.2.refs_8_.refs_4_), channel_id=1, source_target_pairs={{0,4},{4,0},{8,12},{12,8},{16,20},{20,16},{24,28},{28,24},{1,5},{5... | collective-permute-start | bytes 3145736 | tf_op jit(solution)/shard_map/ppermute | solution.py:110
  125.0 23.0 %collective-permute-start.21 = (bf16[2,2,2,32,16,128]{5,4,3,2,1,0:T(8,128)(2,1)S(1)}, bf16[2,2,2,32,16,128]{5,4,3,2,1,0:T(8,128)(2,1)}, u32[]{:S(2)}, u32[]{:S(2)}) collective-permute-start(bf16[2,2,2,32,16,128]{5,4,3,2,1,0:T(8,128)(2,1)S(1)} %pad_maximum_fusion.2.refs_8_.refs_4_), channel_id=1, source_target_pairs={{0,1},{1,0},{2,3},{3,2},{4,5},{5,4},{6,7},{7,6},{8,9},{9,8},{10,11... | collective-permute-start | bytes 3145736 | tf_op jit(solution)/shard_map/ppermute | solution.py:110
  125.0 23.0 %collective-permute-start.22 = (bf16[2,2,2,32,16,128]{5,4,3,2,1,0:T(8,128)(2,1)}, bf16[2,2,2,32,16,128]{5,4,3,2,1,0:T(8,128)(2,1)}, u32[]{:S(2)}, u32[]{:S(2)}) collective-permute-start(bf16[2,2,2,32,16,128]{5,4,3,2,1,0:T(8,128)(2,1)} %pad_maximum_fusion.1.refs_4_), channel_id=1, source_target_pairs={{0,1},{1,0},{2,3},{3,2},{4,5},{5,4},{6,7},{7,6},{8,9},{9,8},{10,11... | collective-permute-start | bytes 3145736 | tf_op jit(solution)/shard_map/ppermute | solution.py:110
  180.5 25.4 %collective-permute-start.26 = (bf16[2,32,128,128]{3,2,1,0:T(8,128)(2,1)}, bf16[2,32,128,128]{3,2,1,0:T(8,128)(2,1)}, u32[]{:S(2)}, u32[]{:S(2)}) collective-permute-start(bf16[2,32,128,128]{3,2,1,0:T(8,128)(2,1)} %get-tuple-element.169), channel_id=1, source_target_pairs={{0,1},{1,0},{2,3},{3,2},{4,5},{5,4},{6,7},{7,6},{8,9},{9,8},{10,11... | collective-permute-start | bytes 6291464 | tf_op jit(solution)/shard_map/ppermute | solution.py:110
  180.7 25.2 %collective-permute-start.25 = (bf16[128,32,128]{2,1,0:T(8,128)(2,1)}, bf16[128,32,128]{2,1,0:T(8,128)(2,1)S(1)}, u32[]{:S(2)}, u32[]{:S(2)}) collective-permute-start(bf16[128,32,128]{2,1,0:T(8,128)(2,1)} %get-tuple-element.167), channel_id=1, source_target_pairs={{0,3},{1,2},{2,1},{3,0},{4,7},{5,6},{6,5},{7,4},{8,11},{9,10},{10,... | collective-permute-start | bytes 3145736 | tf_op jit(solution)/shard_map/ppermute | solution.py:110
  205.9 29.4 %collective-permute-start.30 = (bf16[2,32,128,128]{3,2,1,0:T(8,128)(2,1)}, bf16[2,32,128,128]{3,2,1,0:T(8,128)(2,1)}, u32[]{:S(2)}, u32[]{:S(2)}) collective-permute-start(bf16[2,32,128,128]{3,2,1,0:T(8,128)(2,1)} %get-tuple-element.187), channel_id=1, source_target_pairs={{0,1},{1,0},{2,3},{3,2},{4,5},{5,4},{6,7},{7,6},{8,9},{9,8},{10,11... | collective-permute-start | bytes 6291464 | tf_op jit(solution)/shard_map/ppermute | solution.py:110
  206.2 29.1 %collective-permute-start.31 = (bf16[2,32,128,128]{3,2,1,0:T(8,128)(2,1)}, bf16[2,32,128,128]{3,2,1,0:T(8,128)(2,1)}, u32[]{:S(2)}, u32[]{:S(2)}) collective-permute-start(bf16[2,32,128,128]{3,2,1,0:T(8,128)(2,1)} %get-tuple-element.189), channel_id=1, source_target_pairs={{0,1},{1,0},{2,3},{3,2},{4,5},{5,4},{6,7},{7,6},{8,9},{9,8},{10,11... | collective-permute-start | bytes 6291464 | tf_op jit(solution)/shard_map/ppermute | solution.py:110
  208.4 25.5 %collective-permute-start.29 = (bf16[2,32,2,2,16,128]{5,4,1,3,2,0:T(8,128)(2,1)S(1)}, bf16[2,32,2,2,16,128]{5,4,1,3,2,0:T(8,128)(2,1)}, u32[]{:S(2)}, u32[]{:S(2)}) collective-permute-start(bf16[2,32,2,2,16,128]{5,4,1,3,2,0:T(8,128)(2,1)S(1)} %fusion), channel_id=1, source_target_pairs={{0,4},{4,0},{8,12},{12,8},{16,20},{20,16},{24,28},{28,24},{1,5},{5... | collective-permute-start | bytes 3145736 | tf_op jit(solution)/shard_map/ppermute | solution.py:110
  209.9 25.4 %collective-permute-start.27 = (bf16[128,32,128]{2,1,0:T(8,128)(2,1)}, bf16[128,32,128]{2,1,0:T(8,128)(2,1)}, u32[]{:S(2)}, u32[]{:S(2)}) collective-permute-start(bf16[128,32,128]{2,1,0:T(8,128)(2,1)} %get-tuple-element.182), channel_id=1, source_target_pairs={{0,2},{1,3},{2,0},{3,1},{4,6},{5,7},{6,4},{7,5},{8,10},{9,11},{10,... | collective-permute-start | bytes 3145736 | tf_op jit(solution)/shard_map/ppermute | solution.py:110
  211.6 23.7 %collective-permute-start.28 = (bf16[128,32,128]{2,1,0:T(8,128)(2,1)}, bf16[128,32,128]{2,1,0:T(8,128)(2,1)}, u32[]{:S(2)}, u32[]{:S(2)}) collective-permute-start(bf16[128,32,128]{2,1,0:T(8,128)(2,1)} %get-tuple-element.183), channel_id=1, source_target_pairs={{0,1},{1,0},{2,3},{3,2},{4,5},{5,4},{6,7},{7,6},{8,9},{9,8},{10,11... | collective-permute-start | bytes 3145736 | tf_op jit(solution)/shard_map/ppermute | solution.py:110
  238.1 24.5 %collective-permute-start.34 = (bf16[2,32,2,2,16,128]{5,4,1,3,2,0:T(8,128)(2,1)}, bf16[2,32,2,2,16,128]{5,4,1,3,2,0:T(8,128)(2,1)}, u32[]{:S(2)}, u32[]{:S(2)}) collective-permute-start(bf16[2,32,2,2,16,128]{5,4,1,3,2,0:T(8,128)(2,1)} %fusion.2), channel_id=1, source_target_pairs={{0,4},{4,0},{8,12},{12,8},{16,20},{20,16},{24,28},{28,24},{1,5},{5... | collective-permute-start | bytes 3145736 | tf_op jit(solution)/shard_map/ppermute | solution.py:110
  241.2 24.5 %collective-permute-start.33 = (bf16[2,32,2,2,16,128]{5,4,1,3,2,0:T(8,128)(2,1)}, bf16[2,32,2,2,16,128]{5,4,1,3,2,0:T(8,128)(2,1)}, u32[]{:S(2)}, u32[]{:S(2)}) collective-permute-start(bf16[2,32,2,2,16,128]{5,4,1,3,2,0:T(8,128)(2,1)} %fusion.1), channel_id=1, source_target_pairs={{0,8},{4,12},{8,0},{12,4},{16,24},{20,28},{24,16},{28,20},{1,9},{5... | collective-permute-start | bytes 3145736 | tf_op jit(solution)/shard_map/ppermute | solution.py:110
  243.2 25.3 %collective-permute-start.32 = (bf16[32,128,128]{2,1,0:T(8,128)(2,1)}, bf16[32,128,128]{2,1,0:T(8,128)(2,1)S(1)}, u32[]{:S(2)}, u32[]{:S(2)}) collective-permute-start(bf16[32,128,128]{2,1,0:T(8,128)(2,1)} %get-tuple-element.194), channel_id=1, source_target_pairs={{0,3},{1,2},{2,1},{3,0},{4,7},{5,6},{6,5},{7,4},{8,11},{9,10},{10,... | collective-permute-start | bytes 3145736 | tf_op jit(solution)/shard_map/ppermute | solution.py:110
  275.2 26.4 %collective-permute-start.36 = (bf16[32,128,128]{2,1,0:T(8,128)(2,1)}, bf16[32,128,128]{2,1,0:T(8,128)(2,1)S(1)}, u32[]{:S(2)}, u32[]{:S(2)}) collective-permute-start(bf16[32,128,128]{2,1,0:T(8,128)(2,1)} %get-tuple-element.214), channel_id=1, source_target_pairs={{0,2},{1,3},{2,0},{3,1},{4,6},{5,7},{6,4},{7,5},{8,10},{9,11},{10,... | collective-permute-start | bytes 3145736 | tf_op jit(solution)/shard_map/ppermute | solution.py:110
  275.9 26.6 %collective-permute-start.35 = (bf16[32,128,128]{2,1,0:T(8,128)(2,1)}, bf16[32,128,128]{2,1,0:T(8,128)(2,1)}, u32[]{:S(2)}, u32[]{:S(2)}) collective-permute-start(bf16[32,128,128]{2,1,0:T(8,128)(2,1)} %get-tuple-element.213), channel_id=1, source_target_pairs={{0,1},{1,0},{2,3},{3,2},{4,5},{5,4},{6,7},{7,6},{8,9},{9,8},{10,11... | collective-permute-start | bytes 3145736 | tf_op jit(solution)/shard_map/ppermute | solution.py:110
  (49 other events, 624.4 us)

commit v6 on v5

--- a/solution.py
+++ b/solution.py
@@ -12,7 +12,7 @@
 BF16 = jnp.bfloat16
 F32 = jnp.float32
 LANES = 128
-PAD = 8
+PAD = 1
 VMEM_BYTES = 60 * 1024 * 1024
 BYTES_PER_US = 1_200_000
 
@@ -286,7 +286,7 @@
         turned[pl.ds(o, size, stride=pitch), :] = g_ref[o].astype(F32)
 
     def load(b):
-        out_ref[b] = turned[pl.ds(pl.multiple_of(b * pitch, 8), home), :].astype(BF16)
+        out_ref[b] = turned[pl.ds(b * pitch, home), :].astype(BF16)
 
     each(home, store)
     each(size, load)
@@ -323,7 +323,7 @@
                 turned[pl.ds(b, size, stride=pitch), :] = dot_tn(w_ref[b], x_ref[b, :, lanes])
 
             def load(o):
-                out_ref[o] = turned[pl.ds(pl.multiple_of(o * pitch, 8), home), :].astype(BF16)
+                out_ref[o] = turned[pl.ds(o * pitch, home), :].astype(BF16)
 
             each(home, store)
             each(size, load)
@@ -364,7 +364,7 @@
         each(blocks, store)
 
     def load(b):
-        rows = pl.ds(pl.multiple_of(b * pitch, 8), blocks)
+        rows = pl.ds(b * pitch, blocks)
         e_b = jnp.concatenate([turned[s, rows, :].astype(BF16) for s in range(share)], axis=1)
         out_ref[b] = (g_ref[b].astype(F32) + dot_nn(w_ref[b], e_b)).astype(BF16)
         grad_ref[b] = dot_nt(x_ref[b], e_b).astype(BF16)
@@ -464,7 +464,7 @@
     @pl.when(phase == 1)
     def _():
         def body(k):
-            out_ref[k] = turned[pl.ds(pl.multiple_of((j * per + k) * pitch, 8), size), :].astype(BF16)
+            out_ref[k] = turned[pl.ds((j * per + k) * pitch, size), :].astype(BF16)
 
         each(per, body)
 
@@ -522,7 +522,7 @@
     phase, j = pl.program_id(0), pl.program_id(1)
 
     def rows(k):
-        return pl.ds(pl.multiple_of((j * per + k) * pitch, 8), size)
+        return pl.ds((j * per + k) * pitch, size)
 
     def column(k):
         return pl.ds(j * per + k, size, stride=pitch)
@@ -632,7 +632,7 @@
     phase, j = pl.program_id(0), pl.program_id(1)
 
     def rows(k):
-        return pl.ds(pl.multiple_of((j * per + k) * pitch, 8), size)
+        return pl.ds((j * per + k) * pitch, size)
 
     def column(k):
         return pl.ds(j * per + k, size, stride=pitch)
@@ -678,7 +678,7 @@
             base = place.onward(pos_ref, n) * per
 
             def body(k):
-                out_refs[n][k] = fourth[pl.ds(pl.multiple_of((base + k) * pitch, 8), size), :].astype(BF16)
+                out_refs[n][k] = fourth[pl.ds((base + k) * pitch, size), :].astype(BF16)
 
             each(per, body)
 
@@ -725,17 +725,19 @@
     place = Place(share, lax.axis_size("dp"))
     pos = place.position()
 
-    def gather(start, skip, *before):
-        ring = place.dp[skip]
-        got = [start] + ring.sends(after(start, *before))
-        return got if skip == 0 else jnp.stack(got)
-
-    def gathers(start):
-        for n in reversed(range(1, len(place.dp))):
+    def gather(start, n):
+        if n >= len(place.dp):
+            return start
+        got = [start] + place.dp[n].sends(start)
+        return got if n == 0 else jnp.stack(got)
+
+    def gather_far(start):
+        for n in reversed(range(2, len(place.dp))):
             start = gather(start, n)
         return start
 
-    last_dp = (lambda start: gather(start, 0)) if place.dp else (lambda start: [start])
+    def last_dp(start):
+        return gather(start, 0) if place.dp else [start]
 
     def cores(piece):
         return [piece] + place.core.sends(piece)
@@ -746,43 +748,46 @@
     def cross(pieces, n):
         return place.exchange(pieces, n) if n < share else None
 
+    def from_y(start):
+        return jnp.stack([start] + place.y.sends(start))
+
     n_one, n_two, n_three = (place.steps.index(step) if step in place.steps else share for step in [(0, 1), (1, 0), (1, 1)])
-    mine = jnp.stack([factors[3], factors[1], factors[2]])
-    from_y = [mine] + place.y.sends(mine)
-    one = first_left
-    g = {n: deal(place, pos, g_home, cut, n) for n in range(share) if n >= 2}
-    from_y, g = slot(place, (from_y, g))
-
-    wholes = [jnp.stack([part[n] for part in from_y]) for n in range(3)]
+    one = gather_far(first_left)
+    w_two = from_y(factors[3])
+    rest = from_y(jnp.stack([factors[1], factors[2]]))
+    g = {n: deal(place, pos, g_home, cut, n) for n in reversed(range(share))}
     got_three = cross(g, n_three)
-    one = last_dp(gathers(one))
-    wholes[0] = gathers(wholes[0])
-    g |= {n: deal(place, pos, g_home, cut, n) for n in range(share) if n < 2}
-    got_one = cross(g, n_one)
-    got_three, got_one, one, wholes, g = slot(place, (got_three, got_one, one, wholes, g))
+    w_two = gather_far(after(w_two, g[share - 1]))
+    one = last_dp(gather(after(one, rest), 1))
+    w_two = gather(w_two, 1)
+    got_three, one, w_two, rest, g = slot(place, (got_three, one, w_two, rest, g))
 
     got_two = cross(g, n_two)
-    right_two = last_dp(wholes[0])
-    wholes[1] = gathers(wholes[1])
+    right_two = last_dp(w_two)
+    w_one = gather(gather_far(rest[:, 0]), 1)
+    w_left = gather_far(rest[:, 1])
     one = join(place, pos, [p[..., None, :, :, :] for p in one])
     s = first_stage(place, pos, x_home, one, cut)
-    got_two, right_two, wholes, one, s = slot(place, (got_two, right_two, wholes, one, list(s)))
+    got_two, right_two, w_one, w_left, one, s, pos = slot(place, (got_two, right_two, w_one, w_left, one, list(s), pos))
+
+    s_three = cross(s, n_three)
+    right_one = last_dp(w_one)
+    w_left = gather(w_left, 1)
+    right_two = by_core([cores(p) for p in right_two])
+    s_one = cross(s, n_one)
+    got_one = cross(g, n_one)
+    s_three, s_one, right_one, w_left, right_two, g, got_one = slot(
+        place, (s_three, s_one, right_one, w_left, right_two, g, got_one)
+    )
     g_mid = [g[0], got_one, got_two, got_three][:share]
 
-    got_three = cross(s, n_three)
-    got_one = cross(s, n_one)
-    right_one = last_dp(wholes[1])
-    wholes[2] = gathers(wholes[2])
-    right_two = by_core([cores(p) for p in right_two])
-    got_three, got_one, right_one, wholes, right_two = slot(place, (got_three, got_one, right_one, wholes, right_two))
-
-    got_two = cross(s, n_two)
-    left_two = last_dp(wholes[2])
+    s_two = cross(s, n_two)
+    left_two = last_dp(w_left)
     left_core = cores(left_two[0])
     right_one = by_core([cores(p) for p in right_one])
     e_mid = back_two(place, pos, g_mid, right_two)
-    got_two, left_two, left_core, right_one, e_mid = slot(place, (got_two, left_two, left_core, right_one, e_mid))
-    s_mid = [s[0], got_one, got_two, got_three][:share]
+    s_two, left_two, left_core, right_one, e_mid = slot(place, (s_two, left_two, left_core, right_one, e_mid))
+    s_mid = [s[0], s_one, s_two, s_three][:share]
     left_two = by_core([left_core] + [cores(p) for p in left_two[1:]])
 
     act, grad_two, grad_one, e = middle(place, pos, s_mid, e_mid, right_one, left_two)
@@ -801,14 +806,15 @@
     x_step, near_step, far_step = (place.dp + [None] * 3)[:3]
 
     e_three = cross(e, n_three)
-    two = start_sum(*grad_two)
+    two, one_part = start_sum(*grad_two), start_sum(*grad_one)
     grad_three, s = forward_two(place, pos, act, g_mid, left_two, right_two)
-    e_three, kept, grad_three, s, e, grad_one = slot(place, (e_three, arrays_of(two), grad_three, s, e, grad_one))
-    hold([two], kept)
+    e_three, kept, grad_three, s, e = slot(place, (e_three, arrays_of(two, one_part), grad_three, s, e))
+    hold([two, one_part], kept)
 
     e_two = cross(e, n_two)
     two.step(x_step)
-    one_part, three = start_sum(*grad_one), start_sum(*grad_three)
+    one_part.step(near_step)
+    three = start_sum(*grad_three)
     e_one = cross(e, n_one)
     e_two, e_one, kept, s = slot(place, (e_two, e_one, arrays_of(two, one_part, three), s))
     hold([two, one_part, three], kept)
@@ -816,7 +822,7 @@
 
     s_three = cross(s, n_three)
     three.step(x_step)
-    one_part.step(near_step)
+    two.step(near_step)
     input_grad, lone = last_stage(place, pos, e_got, x_home, g_home, one)
     s_three, kept, lone, input_grad, s = slot(place, (s_three, arrays_of(two, one_part, three), lone, input_grad, s))
     hold([two, one_part, three], kept)
@@ -824,18 +830,17 @@
 
     s_two, s_one = cross(s, n_two), cross(s, n_one)
     one_part.step(x_step)
-    two.step(near_step)
     three.step(near_step)
+    two.step(far_step)
     lone.step(x_step)
     one_part.step(far_step)
-    two.step(far_step)
-    s_got = [s[0], s_one, s_two, s_three][:share]
+    three.step(far_step)
+    lone.step(near_step)
+    s_got = [after(s[0], lone.arrays[-1]), s_one, s_two, s_three][:share]
+    grad_ltwo = two.finish()
     grad_rone = one_part.finish()
-    lone.step(near_step)
-    grad_ltwo = two.finish()
-    three.step(far_step)
+    grad_rtwo = three.finish()
     grad_lone = lone.finish()
-    grad_rtwo = three.finish()
     mixed = add_home(place, pos, s_got, x_home)
     return mixed, input_grad, grad_lone, grad_rone, grad_ltwo, grad_rtwo
 

time: 342 us -> 323 us (0.944)
  waiting for transfers between devices: 147 us -> 132 us
  other arithmetic: 38 us -> 33.5 us
  starting transfers between devices: 47 us -> 51.5 us
  Pallas kernels: 103 us -> 99.4 us
    ppermute x49 -> x50, waiting for transfers between devices: 147 us -> 132 us  [send(): self.last = lax.ppermute(value, self.axis, pairs)]
    ppermute x49 -> x50, starting transfers between devices: 47 us -> 51.5 us  [send(): self.last = lax.ppermute(value, self.axis, pairs)]
    convert_element_type x14, other arithmetic: 23.9 us -> 19.7 us  [step(): self.cut(ring, lax.rem(ring.here() + step, ring.size)).astype(BF16)]
  transfers between devices with their start and end apart: 49 -> 50, of which waited for: 26 -> 26; matrix products, arithmetic and copies ran while one was open for 10% -> 9% of each run, Pallas kernels for 22% -> 22%
where the time goes in v6:
time: 323 us; the launch traced here: 322 us
  waiting for transfers between devices  132 us (41%)
  Pallas kernels  99.4 us (31%)
  starting transfers between devices  51.5 us (16%)
  other arithmetic  33.5 us (10%)
  local copies, waits for them, and re-layouts  4.7 us (1%)
    ppermute x50, waiting for transfers between devices, send(): self.last = lax.ppermute(value, self.axis, pairs)  132 us
    pallas_call x11, Pallas kernels, call(): pl.pallas_call(body, out_shape=out, grid_spec=spec, compiler_params=pltpu...  99.4 us
    ppermute x50, starting transfers between devices, send(): self.last = lax.ppermute(value, self.axis, pairs)  51.5 us
    convert_element_type x14, other arithmetic, step(): self.cut(ring, lax.rem(ring.here() + step, ring.size)).astype(BF16)  19.7 us
    add x4, other arithmetic, total(): return functools.reduce(jnp.add, [t.astype(F32) for t in terms])  7.34 us
  transfers between devices with their start and end apart: 50, of which 26 were waited for; matrix products, arithmetic and copies ran while one was open for 9% of the time, Pallas kernels for 22%

profile of v6, /device:TPU:0, one launch (start us, length us, event | category | flops | bytes accessed | tf_op | source)
XLA Modules:
  0.0 322.4 jit_solution(12384204240584897011)
XLA Ops:
  12.4 3.3 %shard_map.109 = bf16[128,32,128]{2,1,0:T(8,128)(2,1)} custom-call(s32[5]{0:T(128)} %stack.116.pos_ref, bf16[32,128,512]{2,1,0:T(8,128)(2,1)} %bitcast.200), custom_call_target="tpu_custom_call" | custom-call | bytes 4200000 | tf_op jit(solution)/shard_map/pallas_call | solution.py:61
  18.0 3.4 %collective-permute-start.4 = (bf16[2,32,16,128]{3,2,1,0:T(8,128)(2,1)S(1)}, bf16[2,32,16,128]{3,2,1,0:T(8,128)(2,1)S(1)}, u32[]{:S(2)}, u32[]{:S(2)}) collective-permute-start(bf16[2,32,16,128]{3,2,1,0:T(8,128)(2,1)S(1)} %pad_maximum_fusion.8), channel_id=1, source_target_pairs={{0,8},{4,12},{8,0},{12,4},{16,24},{20,28},{24,16},{28,20},{1,9},{5... | collective-permute-start | bytes 786440 | tf_op jit(solution)/shard_map/ppermute | solution.py:110
  21.3 9.8 %collective-permute-done.6 = bf16[2,32,16,128]{3,2,1,0:T(8,128)(2,1)S(1)} collective-permute-done((bf16[2,32,16,128]{3,2,1,0:T(8,128)(2,1)S(1)}, bf16[2,32,16,128]{3,2,1,0:T(8,128)(2,1)S(1)}, u32[]{:S(2)}, u32[]{:S(2)}) %collective-permute-start.6) | collective-permute-done | bytes 262176 | tf_op jit(solution)/shard_map/ppermute | solution.py:110
  32.9 3.2 shard_map.110.refs_0_
  52.4 7.4 %collective-permute-done.10 = bf16[2,32,16,128]{3,2,1,0:T(8,128)(2,1)S(1)} collective-permute-done((bf16[2,32,16,128]{3,2,1,0:T(8,128)(2,1)S(1)}, bf16[2,32,16,128]{3,2,1,0:T(8,128)(2,1)S(1)}, u32[]{:S(2)}, u32[]{:S(2)}) %collective-permute-start.10) | collective-permute-done | bytes 262176 | tf_op jit(solution)/shard_map/ppermute | solution.py:110
  66.4 8.5 %shard_map.114 = (bf16[128,32,128]{2,1,0:T(8,128)(2,1)}, bf16[128,32,128]{2,1,0:T(8,128)(2,1)}, bf16[128,32,128]{2,1,0:T(8,128)(2,1)}, bf16[128,32,128]{2,1,0:T(8,128)(2,1)}) custom-call(s32[5]{0:T(128)} %stack.116.pos_ref, bf16[32,128,512]{2,1,0:T(8,128)(2,1)} %bitcast.205, bf16[32,128,128]{2,1,0:T(8,128)(2,1)} %shard_map.113.w_ref.refs_6_), custom_call_target="tpu_custom_call" | custom-call | bytes 9600000 | tf_op jit(solution)/shard_map/pallas_call | solution.py:61
  74.9 3.4 %collective-permute-done.12 = bf16[2,32,16,128]{3,2,1,0:T(8,128)(2,1)} collective-permute-done((bf16[2,32,16,128]{3,2,1,0:T(8,128)(2,1)}, bf16[2,32,16,128]{3,2,1,0:T(8,128)(2,1)}, u32[]{:S(2)}, u32[]{:S(2)}) %collective-permute-start.12) | collective-permute-done | bytes 262176 | tf_op jit(solution)/shard_map/ppermute | solution.py:110
  89.9 5.8 %collective-permute-done.16 = bf16[2,2,32,16,128]{4,3,2,1,0:T(8,128)(2,1)S(1)} collective-permute-done((bf16[2,2,32,16,128]{4,3,2,1,0:T(8,128)(2,1)S(1)}, bf16[2,2,32,16,128]{4,3,2,1,0:T(8,128)(2,1)S(1)}, u32[]{:S(2)}, u32[]{:S(2)}) %collective-permute-start.16) | collective-permute-done | bytes 524320 | tf_op jit(solution)/shard_map/ppermute | solution.py:110
  95.7 14.2 %collective-permute-done.13.refs_3_ = bf16[128,32,128]{2,1,0:T(8,128)(2,1)S(1)} collective-permute-done((bf16[128,32,128]{2,1,0:T(8,128)(2,1)S(1)}, bf16[128,32,128]{2,1,0:T(8,128)(2,1)S(1)}, u32[]{:S(2)}, u32[]{:S(2)}) %collective-permute-start.13) | collective-permute-done | bytes 1048608 | tf_op jit(solution)/shard_map/ppermute | solution.py:110
  116.9 9.7 %shard_map.115.refs_12_ = bf16[128,128,128]{2,1,0:T(8,128)(2,1)} custom-call(s32[5]{0:T(128)} %stack.116.pos_ref, bf16[128,32,128]{2,1,0:T(8,128)(2,1)} %shard_map.110.refs_0_, bf16[128,32,128]{2,1,0:T(8,128)(2,1)} %collective-permute-done.19.refs_1_, bf16[128,32,128]{2,1,0:T(8,128)(2,1)} %copy-done.3, bf16[128,32,128]{2,1,0:T(8,128)(2,1)} %copy-done.2, ...), custom_call_target="tpu_custom_call" | custom-call | bytes 12000000 | tf_op jit(solution)/shard_map/pallas_call | solution.py:61
  126.6 9.8 %collective-permute-done.20.refs_2_ = bf16[128,32,128]{2,1,0:T(8,128)(2,1)} collective-permute-done((bf16[128,32,128]{2,1,0:T(8,128)(2,1)}, bf16[128,32,128]{2,1,0:T(8,128)(2,1)}, u32[]{:S(2)}, u32[]{:S(2)}) %collective-permute-start.20) | collective-permute-done | bytes 1048608 | tf_op jit(solution)/shard_map/ppermute | solution.py:110
  142.7 28.4 %shard_map.116 = (bf16[128,128,128]{2,1,0:T(8,128)(2,1)}, bf16[2,32,128,128]{3,2,1,0:T(8,128)(2,1)}, bf16[2,32,128,128]{3,2,1,0:T(8,128)(2,1)}, bf16[2,32,128,12...) custom-call(s32[5]{0:T(128)} %stack.116.pos_ref, ...), custom_call_target="tpu_custom_call" | custom-call | bytes 31200000 | tf_op jit(solution)/shard_map/pallas_call | solution.py:61
  172.4 20.8 %shard_map.117 = (bf16[2,32,128,128]{3,2,1,0:T(8,128)(2,1)}, bf16[2,32,128,128]{3,2,1,0:T(8,128)(2,1)}, bf16[32,128,128]{2,1,0:T(8,128)(2,1)}, bf16[32,128,128]{...) custom-call(s32[5]{0:T(128)} %stack.116.pos_ref, ...), custom_call_target="tpu_custom_call" | custom-call | bytes 24000000 | tf_op jit(solution)/shard_map/pallas_call | solution.py:61
  193.2 3.9 %collective-permute-done.26.refs_3_ = bf16[128,32,128]{2,1,0:T(8,128)(2,1)S(1)} collective-permute-done((bf16[128,32,128]{2,1,0:T(8,128)(2,1)}, bf16[128,32,128]{2,1,0:T(8,128)(2,1)S(1)}, u32[]{:S(2)}, u32[]{:S(2)}) %collective-permute-start.26) | collective-permute-done | bytes 1048608 | tf_op jit(solution)/shard_map/ppermute | solution.py:110
  203.7 20.8 %collective-permute-done.32 = bf16[2,32,2,2,16,128]{5,4,1,3,2,0:T(8,128)(2,1)S(1)} collective-permute-done((bf16[2,32,2,2,16,128]{5,4,1,3,2,0:T(8,128)(2,1)S(1)}, bf16[2,32,2,2,16,128]{5,4,1,3,2,0:T(8,128)(2,1)S(1)}, u32[]{:S(2)}, u32[]{:S(2)}) %collective-permute-start.32) | collective-permute-done | bytes 1048608 | tf_op jit(solution)/shard_map/ppermute | solution.py:110
  234.6 9.4 %shard_map.118 = (bf16[32,128,512]{2,1,0:T(8,128)(2,1)}, bf16[32,128,128]{2,1,0:T(8,128)(2,1)}) custom-call(s32[5]{0:T(128)} %stack.116.pos_ref, bf16[128,32,128]{2,1,0:T(8,128)(2,1)} %get-tuple-element.209.refs_0_, bf16[128,32,128]{2,1,0:T(8,128)(2,1)} %collective-permute-done.30.refs_1_, bf16[128,32,128]{2,1,0:T(8,128)(2,1)} %collective-permute-done.29.refs_2_, ...), custom_call_target="tpu_custom_call" | custom-call | bytes 12000000 | tf_op jit(solution)/shard_map/pallas_call | solution.py:61
  244.0 4.1 %collective-permute-done.35 = bf16[2,32,2,16,128]{4,3,1,2,0:T(8,128)(2,1)} collective-permute-done((bf16[2,32,2,16,128]{4,3,1,2,0:T(8,128)(2,1)}, bf16[2,32,2,16,128]{4,3,1,2,0:T(8,128)(2,1)}, u32[]{:S(2)}, u32[]{:S(2)}) %collective-permute-start.35) | collective-permute-done | bytes 524320 | tf_op jit(solution)/shard_map/ppermute | solution.py:110
  248.1 6.6 %collective-permute-done.36 = bf16[2,32,2,2,16,128]{5,4,1,3,2,0:T(8,128)(2,1)} collective-permute-done((bf16[2,32,2,2,16,128]{5,4,1,3,2,0:T(8,128)(2,1)}, bf16[2,32,2,2,16,128]{5,4,1,3,2,0:T(8,128)(2,1)}, u32[]{:S(2)}, u32[]{:S(2)}) %collective-permute-start.36) | collective-permute-done | bytes 1048608 | tf_op jit(solution)/shard_map/ppermute | solution.py:110
  265.9 5.8 %collective-permute-done.37 = bf16[2,32,2,16,128]{4,3,1,2,0:T(8,128)(2,1)S(1)} collective-permute-done((bf16[2,32,2,16,128]{4,3,1,2,0:T(8,128)(2,1)S(1)}, bf16[2,32,2,16,128]{4,3,1,2,0:T(8,128)(2,1)S(1)}, u32[]{:S(2)}, u32[]{:S(2)}) %collective-permute-start.37) | collective-permute-done | bytes 524320 | tf_op jit(solution)/shard_map/ppermute | solution.py:110
  277.2 8.0 %collective-permute-done.39 = bf16[2,32,2,16,128]{4,3,1,2,0:T(8,128)(2,1)S(1)} collective-permute-done((bf16[2,32,2,16,128]{4,3,1,2,0:T(8,128)(2,1)S(1)}, bf16[2,32,2,16,128]{4,3,1,2,0:T(8,128)(2,1)S(1)}, u32[]{:S(2)}, u32[]{:S(2)}) %collective-permute-start.39) | collective-permute-done | bytes 524320 | tf_op jit(solution)/shard_map/ppermute | solution.py:110
  286.4 3.9 %collective-permute-done.44 = bf16[2,32,16,128]{3,2,1,0:T(8,128)(2,1)S(1)} collective-permute-done((bf16[2,32,16,128]{3,2,1,0:T(8,128)(2,1)S(1)}, bf16[2,32,16,128]{3,2,1,0:T(8,128)(2,1)S(1)}, u32[]{:S(2)}, u32[]{:S(2)}) %collective-permute-start.44) | collective-permute-done | bytes 262176 | tf_op jit(solution)/shard_map/ppermute | solution.py:110
  292.5 4.8 %collective-permute-start.40 = (bf16[32,2,16,128]{3,2,0,1:T(8,128)(2,1)S(1)}, bf16[32,2,16,128]{3,2,0,1:T(8,128)(2,1)S(1)}, u32[]{:S(2)}, u32[]{:S(2)}) collective-permute-start(bf16[32,2,16,128]{3,2,0,1:T(8,128)(2,1)S(1)} %fusion.9), channel_id=1, source_target_pairs={{0,8},{4,12},{8,0},{12,4},{16,24},{20,28},{24,16},{28,20},{1,9},{5... | collective-permute-start | bytes 786440 | tf_op jit(solution)/shard_map/ppermute | solution.py:110
  297.4 5.7 %collective-permute-done.45 = bf16[2,32,16,128]{3,2,1,0:T(8,128)(2,1)S(1)} collective-permute-done((bf16[2,32,16,128]{3,2,1,0:T(8,128)(2,1)S(1)}, bf16[2,32,16,128]{3,2,1,0:T(8,128)(2,1)S(1)}, u32[]{:S(2)}, u32[]{:S(2)}) %collective-permute-start.45) | collective-permute-done | bytes 262176 | tf_op jit(solution)/shard_map/ppermute | solution.py:110
  311.8 7.0 %shard_map.119 = bf16[32,128,512]{2,1,0:T(8,128)(2,1)} custom-call(s32[5]{0:T(128)} %stack.116.pos_ref, bf16[32,128,128]{2,1,0:T(8,128)(2,1)} %get-tuple-element.229.refs_0_, bf16[32,128,128]{2,1,0:T(8,128)(2,1)} %collective-permute-done.41.refs_1_, bf16[32,128,128]{2,1,0:T(8,128)(2,1)} %copy-done.13, bf16[32,128,128]{2,1,0:T(8,128)(2,1)} %copy-done.12, ...), custom_call_target="tpu_custom_call" | custom-call | bytes 7200000 | tf_op jit(solution)/shard_map/pallas_call | solution.py:61
  (183 shorter events, 114.0 us)
Async XLA Ops:
  15.7 30.3 %collective-permute-start = (bf16[128,32,128]{2,1,0:T(8,128)(2,1)}, bf16[128,32,128]{2,1,0:T(8,128)(2,1)S(1)}, u32[]{:S(2)}, u32[]{:S(2)}) collective-permute-start(bf16[128,32,128]{2,1,0:T(8,128)(2,1)} %shard_map.109), channel_id=1, source_target_pairs={{0,3},{1,2},{2,1},{3,0},{4,7},{5,6},{6,5},{7,4},{8,11},{9,10},{10,... | collective-permute-start | bytes 3145736 | tf_op jit(solution)/shard_map/ppermute | solution.py:110
  48.7 33.9 %collective-permute-start.8 = (bf16[128,32,128]{2,1,0:T(8,128)(2,1)}, bf16[128,32,128]{2,1,0:T(8,128)(2,1)S(1)}, u32[]{:S(2)}, u32[]{:S(2)}) collective-permute-start(bf16[128,32,128]{2,1,0:T(8,128)(2,1)} %shard_map.112), channel_id=1, source_target_pairs={{0,2},{1,3},{2,0},{3,1},{4,6},{5,7},{6,4},{7,5},{8,10},{9,11},{10,... | collective-permute-start | bytes 3145736 | tf_op jit(solution)/shard_map/ppermute | solution.py:110
  50.9 31.6 %collective-permute-start.9 = (bf16[2,2,2,32,16,128]{5,4,3,2,1,0:T(8,128)(2,1)S(1)}, bf16[2,2,2,32,16,128]{5,4,3,2,1,0:T(8,128)(2,1)}, u32[]{:S(2)}, u32[]{:S(2)}) collective-permute-start(bf16[2,2,2,32,16,128]{5,4,3,2,1,0:T(8,128)(2,1)S(1)} %pad_maximum_fusion.refs_4_.refs_8_), channel_id=1, source_target_pairs={{0,4},{4,0},{8,12},{12,8},{16,20},{20,16},{24,28},{28,24},{1,5},{5... | collective-permute-start | bytes 3145736 | tf_op jit(solution)/shard_map/ppermute | solution.py:110
  63.4 26.5 %collective-permute-start.19 = (bf16[128,32,128]{2,1,0:T(8,128)(2,1)}, bf16[128,32,128]{2,1,0:T(8,128)(2,1)}, u32[]{:S(2)}, u32[]{:S(2)}) collective-permute-start(bf16[128,32,128]{2,1,0:T(8,128)(2,1)} %shard_map.111), channel_id=1, source_target_pairs={{0,1},{1,0},{2,3},{3,2},{4,5},{5,4},{6,7},{7,6},{8,9},{9,8},{10,11... | collective-permute-start | bytes 3145736 | tf_op jit(solution)/shard_map/ppermute | solution.py:110
  84.2 25.7 %collective-permute-start.13 = (bf16[128,32,128]{2,1,0:T(8,128)(2,1)S(1)}, bf16[128,32,128]{2,1,0:T(8,128)(2,1)S(1)}, u32[]{:S(2)}, u32[]{:S(2)}) collective-permute-start(bf16[128,32,128]{2,1,0:T(8,128)(2,1)S(1)} %copy-done.31), channel_id=1, source_target_pairs={{0,3},{1,2},{2,1},{3,0},{4,7},{5,6},{6,5},{7,4},{8,11},{9,10},{10,... | collective-permute-start | bytes 3145736 | tf_op jit(solution)/shard_map/ppermute | solution.py:110
  87.0 26.0 %collective-permute-start.14 = (bf16[128,32,128]{2,1,0:T(8,128)(2,1)S(1)}, bf16[128,32,128]{2,1,0:T(8,128)(2,1)S(1)}, u32[]{:S(2)}, u32[]{:S(2)}) collective-permute-start(bf16[128,32,128]{2,1,0:T(8,128)(2,1)S(1)} %copy-done.30), channel_id=1, source_target_pairs={{0,1},{1,0},{2,3},{3,2},{4,5},{5,4},{6,7},{7,6},{8,9},{9,8},{10,11... | collective-permute-start | bytes 3145736 | tf_op jit(solution)/shard_map/ppermute | solution.py:110
  88.4 25.4 %collective-permute-start.15 = (bf16[2,2,2,32,16,128]{5,4,3,2,1,0:T(8,128)(2,1)}, bf16[2,2,2,32,16,128]{5,4,3,2,1,0:T(8,128)(2,1)}, u32[]{:S(2)}, u32[]{:S(2)}) collective-permute-start(bf16[2,2,2,32,16,128]{5,4,3,2,1,0:T(8,128)(2,1)} %pad_maximum_fusion.1.refs_4_), channel_id=1, source_target_pairs={{0,4},{4,0},{8,12},{12,8},{16,20},{20,16},{24,28},{28,24},{1,5},{5... | collective-permute-start | bytes 3145736 | tf_op jit(solution)/shard_map/ppermute | solution.py:110
  89.9 23.9 %collective-permute-start.17 = (bf16[2,2,2,32,16,128]{5,4,3,2,1,0:T(8,128)(2,1)S(1)}, bf16[2,2,2,32,16,128]{5,4,3,2,1,0:T(8,128)(2,1)S(1)}, u32[]{:S(2)}, u32[]{:S(2)}) collective-permute-start(bf16[2,2,2,32,16,128]{5,4,3,2,1,0:T(8,128)(2,1)S(1)} %pad_maximum_fusion.refs_4_.refs_8_), channel_id=1, source_target_pairs={{0,1},{1,0},{2,3},{3,2},{4,5},{5,4},{6,7},{7,6},{8,9},{9,8},{10,11... | collective-permute-start | bytes 3145736 | tf_op jit(solution)/shard_map/ppermute | solution.py:110
  109.9 26.4 %collective-permute-start.20 = (bf16[128,32,128]{2,1,0:T(8,128)(2,1)}, bf16[128,32,128]{2,1,0:T(8,128)(2,1)}, u32[]{:S(2)}, u32[]{:S(2)}) collective-permute-start(bf16[128,32,128]{2,1,0:T(8,128)(2,1)} %get-tuple-element.151), channel_id=1, source_target_pairs={{0,2},{1,3},{2,0},{3,1},{4,6},{5,7},{6,4},{7,5},{8,10},{9,11},{10,... | collective-permute-start | bytes 3145736 | tf_op jit(solution)/shard_map/ppermute | solution.py:110
  114.8 24.2 %collective-permute-start.21 = (bf16[2,2,2,32,16,128]{5,4,3,2,1,0:T(8,128)(2,1)S(1)}, bf16[2,2,2,32,16,128]{5,4,3,2,1,0:T(8,128)(2,1)S(1)}, u32[]{:S(2)}, u32[]{:S(2)}) collective-permute-start(bf16[2,2,2,32,16,128]{5,4,3,2,1,0:T(8,128)(2,1)S(1)} %pad_maximum_fusion.2.refs_8_.refs_4_), channel_id=1, source_target_pairs={{0,4},{4,0},{8,12},{12,8},{16,20},{20,16},{24,28},{28,24},{1,5},{5... | collective-permute-start | bytes 3145736 | tf_op jit(solution)/shard_map/ppermute | solution.py:110
  116.3 22.7 %collective-permute-start.22 = (bf16[2,2,2,32,16,128]{5,4,3,2,1,0:T(8,128)(2,1)S(1)}, bf16[2,2,2,32,16,128]{5,4,3,2,1,0:T(8,128)(2,1)}, u32[]{:S(2)}, u32[]{:S(2)}) collective-permute-start(bf16[2,2,2,32,16,128]{5,4,3,2,1,0:T(8,128)(2,1)S(1)} %pad_maximum_fusion.2.refs_8_.refs_4_), channel_id=1, source_target_pairs={{0,1},{1,0},{2,3},{3,2},{4,5},{5,4},{6,7},{7,6},{8,9},{9,8},{10,11... | collective-permute-start | bytes 3145736 | tf_op jit(solution)/shard_map/ppermute | solution.py:110
  116.3 22.7 %collective-permute-start.23 = (bf16[2,2,2,32,16,128]{5,4,3,2,1,0:T(8,128)(2,1)}, bf16[2,2,2,32,16,128]{5,4,3,2,1,0:T(8,128)(2,1)}, u32[]{:S(2)}, u32[]{:S(2)}) collective-permute-start(bf16[2,2,2,32,16,128]{5,4,3,2,1,0:T(8,128)(2,1)} %pad_maximum_fusion.1.refs_4_), channel_id=1, source_target_pairs={{0,1},{1,0},{2,3},{3,2},{4,5},{5,4},{6,7},{7,6},{8,9},{9,8},{10,11... | collective-permute-start | bytes 3145736 | tf_op jit(solution)/shard_map/ppermute | solution.py:110
  171.1 26.0 %collective-permute-start.27 = (bf16[2,32,128,128]{3,2,1,0:T(8,128)(2,1)}, bf16[2,32,128,128]{3,2,1,0:T(8,128)(2,1)}, u32[]{:S(2)}, u32[]{:S(2)}) collective-permute-start(bf16[2,32,128,128]{3,2,1,0:T(8,128)(2,1)} %get-tuple-element.175), channel_id=1, source_target_pairs={{0,1},{1,0},{2,3},{3,2},{4,5},{5,4},{6,7},{7,6},{8,9},{9,8},{10,11... | collective-permute-start | bytes 6291464 | tf_op jit(solution)/shard_map/ppermute | solution.py:110
  171.3 25.8 %collective-permute-start.28 = (bf16[2,32,128,128]{3,2,1,0:T(8,128)(2,1)}, bf16[2,32,128,128]{3,2,1,0:T(8,128)(2,1)}, u32[]{:S(2)}, u32[]{:S(2)}) collective-permute-start(bf16[2,32,128,128]{3,2,1,0:T(8,128)(2,1)} %get-tuple-element.177), channel_id=1, source_target_pairs={{0,1},{1,0},{2,3},{3,2},{4,5},{5,4},{6,7},{7,6},{8,9},{9,8},{10,11... | collective-permute-start | bytes 6291464 | tf_op jit(solution)/shard_map/ppermute | solution.py:110
  171.7 25.4 %collective-permute-start.26 = (bf16[128,32,128]{2,1,0:T(8,128)(2,1)}, bf16[128,32,128]{2,1,0:T(8,128)(2,1)S(1)}, u32[]{:S(2)}, u32[]{:S(2)}) collective-permute-start(bf16[128,32,128]{2,1,0:T(8,128)(2,1)} %get-tuple-element.173), channel_id=1, source_target_pairs={{0,3},{1,2},{2,1},{3,0},{4,7},{5,6},{6,5},{7,4},{8,11},{9,10},{10,... | collective-permute-start | bytes 3145736 | tf_op jit(solution)/shard_map/ppermute | solution.py:110
  197.1 30.6 %collective-permute-start.33 = (bf16[2,32,128,128]{3,2,1,0:T(8,128)(2,1)}, bf16[2,32,128,128]{3,2,1,0:T(8,128)(2,1)}, u32[]{:S(2)}, u32[]{:S(2)}) collective-permute-start(bf16[2,32,128,128]{3,2,1,0:T(8,128)(2,1)} %get-tuple-element.195), channel_id=1, source_target_pairs={{0,1},{1,0},{2,3},{3,2},{4,5},{5,4},{6,7},{7,6},{8,9},{9,8},{10,11... | collective-permute-start | bytes 6291464 | tf_op jit(solution)/shard_map/ppermute | solution.py:110
  199.1 25.5 %collective-permute-start.32 = (bf16[2,32,2,2,16,128]{5,4,1,3,2,0:T(8,128)(2,1)S(1)}, bf16[2,32,2,2,16,128]{5,4,1,3,2,0:T(8,128)(2,1)S(1)}, u32[]{:S(2)}, u32[]{:S(2)}) collective-permute-start(bf16[2,32,2,2,16,128]{5,4,1,3,2,0:T(8,128)(2,1)S(1)} %fusion.1), channel_id=1, source_target_pairs={{0,8},{4,12},{8,0},{12,4},{16,24},{20,28},{24,16},{28,20},{1,9},{5... | collective-permute-start | bytes 3145736 | tf_op jit(solution)/shard_map/ppermute | solution.py:110
  201.1 25.4 %collective-permute-start.31 = (bf16[2,32,2,2,16,128]{5,4,1,3,2,0:T(8,128)(2,1)S(1)}, bf16[2,32,2,2,16,128]{5,4,1,3,2,0:T(8,128)(2,1)}, u32[]{:S(2)}, u32[]{:S(2)}) collective-permute-start(bf16[2,32,2,2,16,128]{5,4,1,3,2,0:T(8,128)(2,1)S(1)} %fusion), channel_id=1, source_target_pairs={{0,4},{4,0},{8,12},{12,8},{16,20},{20,16},{24,28},{28,24},{1,5},{5... | collective-permute-start | bytes 3145736 | tf_op jit(solution)/shard_map/ppermute | solution.py:110
  202.6 25.1 %collective-permute-start.29 = (bf16[128,32,128]{2,1,0:T(8,128)(2,1)S(1)}, bf16[128,32,128]{2,1,0:T(8,128)(2,1)}, u32[]{:S(2)}, u32[]{:S(2)}) collective-permute-start(bf16[128,32,128]{2,1,0:T(8,128)(2,1)S(1)} %copy-done.29), channel_id=1, source_target_pairs={{0,2},{1,3},{2,0},{3,1},{4,6},{5,7},{6,4},{7,5},{8,10},{9,11},{10,... | collective-permute-start | bytes 3145736 | tf_op jit(solution)/shard_map/ppermute | solution.py:110
  203.7 24.0 %collective-permute-start.30 = (bf16[128,32,128]{2,1,0:T(8,128)(2,1)S(1)}, bf16[128,32,128]{2,1,0:T(8,128)(2,1)}, u32[]{:S(2)}, u32[]{:S(2)}) collective-permute-start(bf16[128,32,128]{2,1,0:T(8,128)(2,1)S(1)} %copy-done.28), channel_id=1, source_target_pairs={{0,1},{1,0},{2,3},{3,2},{4,5},{5,4},{6,7},{7,6},{8,9},{9,8},{10,11... | collective-permute-start | bytes 3145736 | tf_op jit(solution)/shard_map/ppermute | solution.py:110
  230.3 24.4 %collective-permute-start.36 = (bf16[2,32,2,2,16,128]{5,4,1,3,2,0:T(8,128)(2,1)}, bf16[2,32,2,2,16,128]{5,4,1,3,2,0:T(8,128)(2,1)}, u32[]{:S(2)}, u32[]{:S(2)}) collective-permute-start(bf16[2,32,2,2,16,128]{5,4,1,3,2,0:T(8,128)(2,1)} %fusion.2), channel_id=1, source_target_pairs={{0,4},{4,0},{8,12},{12,8},{16,20},{20,16},{24,28},{28,24},{1,5},{5... | collective-permute-start | bytes 3145736 | tf_op jit(solution)/shard_map/ppermute | solution.py:110
  230.8 25.2 %collective-permute-start.34 = (bf16[32,128,128]{2,1,0:T(8,128)(2,1)}, bf16[32,128,128]{2,1,0:T(8,128)(2,1)S(1)}, u32[]{:S(2)}, u32[]{:S(2)}) collective-permute-start(bf16[32,128,128]{2,1,0:T(8,128)(2,1)} %get-tuple-element.200), channel_id=1, source_target_pairs={{0,3},{1,2},{2,1},{3,0},{4,7},{5,6},{6,5},{7,4},{8,11},{9,10},{10,... | collective-permute-start | bytes 3145736 | tf_op jit(solution)/shard_map/ppermute | solution.py:110
  264.8 26.6 %collective-permute-start.42 = (bf16[32,128,128]{2,1,0:T(8,128)(2,1)S(1)}, bf16[32,128,128]{2,1,0:T(8,128)(2,1)S(1)}, u32[]{:S(2)}, u32[]{:S(2)}) collective-permute-start(bf16[32,128,128]{2,1,0:T(8,128)(2,1)S(1)} %copy-done.27), channel_id=1, source_target_pairs={{0,2},{1,3},{2,0},{3,1},{4,6},{5,7},{6,4},{7,5},{8,10},{9,11},{10,... | collective-permute-start | bytes 3145736 | tf_op jit(solution)/shard_map/ppermute | solution.py:110
  265.8 46.0 %collective-permute-start.41 = (bf16[32,128,128]{2,1,0:T(8,128)(2,1)S(1)}, bf16[32,128,128]{2,1,0:T(8,128)(2,1)}, u32[]{:S(2)}, u32[]{:S(2)}) collective-permute-start(bf16[32,128,128]{2,1,0:T(8,128)(2,1)S(1)} %copy-done.26), channel_id=1, source_target_pairs={{0,1},{1,0},{2,3},{3,2},{4,5},{5,4},{6,7},{7,6},{8,9},{9,8},{10,11... | collective-permute-start | bytes 3145736 | tf_op jit(solution)/shard_map/ppermute | solution.py:110
  (58 other events, 688.0 us)

commit v7 on v6

--- a/solution.py
+++ b/solution.py
@@ -150,6 +150,7 @@
         dims = [ring.size if isinstance(ring, Ring) else ring for ring in rings]
         self.arrays = [a.reshape(dims + list(tail)) for a in arrays]
         self.rings = [rings] * len(arrays)
+        self.ready = []
 
     def cut(self, ring=None, index=None):
         out = []
@@ -163,11 +164,18 @@
             out.append(array)
         return total(out)
 
+    def parts(self, ring):
+        return [self.cut(ring, lax.rem(ring.here() + step, ring.size)).astype(BF16) for step in range(1, ring.size)]
+
+    def prepare(self, ring):
+        self.ready = self.parts(ring) if ring in self.left else []
+
     def step(self, ring):
         if ring not in self.left:
             return
         rest = [r for r in self.left if r is not ring]
-        parts = [self.cut(ring, lax.rem(ring.here() + step, ring.size)).astype(BF16) for step in range(1, ring.size)]
+        parts = self.ready or self.parts(ring)
+        self.ready = []
         got = [ring.send(part, step + 1) for step, part in enumerate(parts)]
         self.arrays, self.rings, self.left = self.arrays + got, self.rings + [rest] * len(got), rest
 
@@ -227,24 +235,26 @@
         return self.crossed
 
 
-def piece_copies(place, pos_ref, pieces, whole, sems):
-    copies = []
-    order = range(len(place.dp))
-    home, rows, _ = pieces[0][0].shape[-3:]
-    inner = [range(place.rows[n]) for n in order[1:]]
-    for c, row in enumerate(pieces):
-        for d, ref in enumerate(row):
-            lead = ref.shape[:-3]
-            for back in itertools.product(*inner, range(lead[-1])):
-                at = 0
-                for n, step in zip(order, (d,) + back[:-1]):
-                    at += turned_back(pos_ref[2 + n], step, place.rows[n]) * place.dp[n].stride
-                group = 0
-                if len(pieces) > 1 or lead[-1] > 1:
-                    group = turned_back(pos_ref[0], back[-1], place.far) * place.near + turned_back(pos_ref[1], c, place.near)
-                dst = whole.at[pl.ds(group * home, home), pl.ds(pl.multiple_of(at * rows, rows), rows), :]
-                copies.append(pltpu.make_async_copy(ref.at[back], dst, sems.at[len(copies)]))
-    return copies
+def piece_copies(pieces, whole, sems):
+    flat_whole = [whole.at[c, d] for c in range(len(pieces)) for d in range(len(pieces[0]))]
+    return [pltpu.make_async_copy(ref, dst, sems.at[n]) for n, (ref, dst) in enumerate(zip(flat(pieces), flat_whole))]
+
+
+def block_reader(place, pos_ref, whole, group):
+    lead = ()
+    if group is not None:
+        lead = (turned_back(pos_ref[0], group // place.near, place.far),)
+    core = 0 if group is None else turned_back(pos_ref[1], lax.rem(group, place.near), place.near)
+    places = []
+    for d in range(math.prod(place.rows)):
+        steps = [turned_back(pos_ref[2 + n], d // ring.stride % ring.size, ring.size) for n, ring in enumerate(place.dp)]
+        places.append((core, *(steps or [0]), *lead))
+    return lambda k: jnp.concatenate([whole[(*at, k)] for at in places], axis=0)
+
+
+def whole_scratch(pieces):
+    dims = (len(pieces), len(pieces[0])) + pieces[0][0].shape
+    return [pltpu.VMEM(dims, BF16), pltpu.SemaphoreType.DMA((dims[0] * dims[1],))]
 
 
 def share_copies(place, pos_ref, parts, whole, sems):
@@ -259,10 +269,6 @@
 def finish(copies):
     for copy in copies:
         copy.wait()
-
-
-def n_copies(place):
-    return place.far * place.near * math.prod(place.rows)
 
 
 def anywhere(count):
@@ -307,11 +313,20 @@
     )
 
 
-def first_kernel(place, pos_ref, x_ref, w_ref, *refs):
-    *out_refs, turned = refs
+def first_kernel(place, pos_ref, x_ref, *refs):
+    share = place.far * place.near
+    pieces, out_refs = refs[: -share - 3], refs[-share - 3 : -3]
+    turned, whole, sems = refs[-3:]
     home, size, _ = x_ref.shape
     cut = out_refs[0].shape[2]
     pitch = home + PAD
+    copies = piece_copies([pieces], whole, sems)
+    block = block_reader(place, pos_ref, whole, None)
+
+    @pl.when(pl.program_id(0) == 0)
+    def _():
+        run(copies)
+        finish(copies)
 
     for n, out_ref in enumerate(out_refs):
 
@@ -320,7 +335,7 @@
             lanes = pl.ds(pl.multiple_of(place.onward(pos_ref, n) * cut, cut), cut)
 
             def store(b):
-                turned[pl.ds(b, size, stride=pitch), :] = dot_tn(w_ref[b], x_ref[b, :, lanes])
+                turned[pl.ds(b, size, stride=pitch), :] = dot_tn(block(b), x_ref[b, :, lanes])
 
             def load(o):
                 out_ref[o] = turned[pl.ds(o * pitch, home), :].astype(BF16)
@@ -336,13 +351,10 @@
         functools.partial(first_kernel, place),
         (shape((size, home, cut)),) * share,
         (share,),
-        [
-            pl.BlockSpec((home, size, tokens), lambda s, pos: (0, 0, 0)),
-            pl.BlockSpec((home, size, size), lambda s, pos: (0, 0, 0)),
-        ],
+        [pl.BlockSpec((home, size, tokens), lambda s, pos: (0, 0, 0))] + anywhere(len(left_one)),
         (pl.BlockSpec((size, home, cut), lambda s, pos: (0, 0, 0)),) * share,
-        [pltpu.VMEM((size * (home + PAD), cut), F32)],
-        (x_home, left_one),
+        [pltpu.VMEM((size * (home + PAD), cut), F32)] + whole_scratch([left_one]),
+        (x_home, *left_one),
         us=8,
         scalars=pos,
     )
@@ -350,10 +362,17 @@
 
 def last_kernel(place, pos_ref, *refs):
     share = place.far * place.near
-    e_refs = refs[:share]
-    x_ref, g_ref, w_ref, out_ref, grad_ref, turned = refs[share:]
+    e_refs, x_ref, g_ref = refs[:share], refs[share], refs[share + 1]
+    pieces, (out_ref, grad_ref, turned, whole, sems) = refs[share + 2 : -5], refs[-5:]
     blocks, per, cut = e_refs[0].shape
     pitch = blocks + PAD
+    copies = piece_copies([pieces], whole, sems)
+    block = block_reader(place, pos_ref, whole, None)
+    first = pl.program_id(0) * per
+
+    @pl.when(pl.program_id(0) == 0)
+    def _():
+        run(copies)
 
     for n in range(share):
         s = place.source(pos_ref, n)
@@ -362,11 +381,15 @@
             turned[s, pl.ds(o, per, stride=pitch), :] = e_refs[n][o].astype(F32)
 
         each(blocks, store)
+
+    @pl.when(pl.program_id(0) == 0)
+    def _():
+        finish(copies)
 
     def load(b):
         rows = pl.ds(b * pitch, blocks)
         e_b = jnp.concatenate([turned[s, rows, :].astype(BF16) for s in range(share)], axis=1)
-        out_ref[b] = (g_ref[b].astype(F32) + dot_nn(w_ref[b], e_b)).astype(BF16)
+        out_ref[b] = (g_ref[b].astype(F32) + dot_nn(block(first + b), e_b)).astype(BF16)
         grad_ref[b] = dot_nt(x_ref[b], e_b).astype(BF16)
 
     each(per, load, 4)
@@ -383,10 +406,10 @@
         functools.partial(last_kernel, place),
         (shape(g_home.shape), shape((home, size, size))),
         (home // per,),
-        [pl.BlockSpec((blocks, per, cut), lambda h, pos: (0, h, 0))] * share + [wide, wide, factor],
+        [pl.BlockSpec((blocks, per, cut), lambda h, pos: (0, h, 0))] * share + [wide, wide] + anywhere(len(left_one)),
         (wide, factor),
-        [pltpu.VMEM((share, per * (blocks + PAD), cut), F32)],
-        (*e_got, x_home, g_home, left_one),
+        [pltpu.VMEM((share, per * (blocks + PAD), cut), F32)] + whole_scratch([left_one]),
+        (*e_got, x_home, g_home, *left_one),
         us=10,
         scalars=pos,
     )
@@ -417,47 +440,27 @@
     )
 
 
-def join_kernel(place, pos_ref, *refs):
-    *pieces, out_ref, sems = refs
-    copies = piece_copies(place, pos_ref, [pieces], out_ref, sems)
-    run(copies)
-    finish(copies)
-
-
-def join(place, pos, pieces):
-    home, rows, size = pieces[0].shape[-3:]
-    return call(
-        functools.partial(join_kernel, place),
-        shape((home, rows * math.prod(place.rows), size)),
-        (1,),
-        anywhere(len(pieces)),
-        pl.BlockSpec((home, rows * math.prod(place.rows), size), lambda i, pos: (0, 0, 0)),
-        [pltpu.SemaphoreType.DMA((math.prod(place.rows),))],
-        tuple(pieces),
-        us=3,
-        scalars=pos,
-    )
-
-
 def back_two_kernel(place, pos_ref, *refs):
     share = place.far * place.near
     g_parts, factor = refs[:share], unflat(place, refs[share:-6])
-    out_ref, turned, g_all, w_all, g_sems, w_sems = refs[-6:]
+    out_ref, turned, g_all, g_sems, w_all, w_sems = refs[-6:]
     per, size, _ = out_ref.shape
     pitch = size + PAD
     phase, j = pl.program_id(0), pl.program_id(1)
 
     @pl.when((phase == 0) & (j == 0))
     def _():
-        copies = share_copies(place, pos_ref, g_parts, g_all, g_sems) + piece_copies(place, pos_ref, factor, w_all, w_sems)
+        copies = share_copies(place, pos_ref, g_parts, g_all, g_sems) + piece_copies(factor, w_all, w_sems)
         run(copies)
         finish(copies)
 
     @pl.when(phase == 0)
     def _():
+        block = block_reader(place, pos_ref, w_all, j)
+
         def body(k):
             b = j * per + k
-            turned[pl.ds(b, size, stride=pitch), :] = dot_nn(w_all[b], stacked(g_all, b))
+            turned[pl.ds(b, size, stride=pitch), :] = dot_nn(block(k), stacked(g_all, b))
 
         each(per, body)
 
@@ -471,11 +474,11 @@
 
 def middle_sizes(place, parts):
     blocks, home, cut = parts[0].shape
-    return blocks, home, cut, len(parts), (blocks, blocks, blocks)
+    return blocks, home, cut, len(parts)
 
 
 def back_two(place, pos, g_mid, right_two):
-    blocks, home, cut, share, whole = middle_sizes(place, g_mid)
+    blocks, home, cut, share = middle_sizes(place, g_mid)
     at = during(1, share)
     return call(
         functools.partial(back_two_kernel, place),
@@ -486,10 +489,9 @@
         [
             pltpu.VMEM((blocks * (blocks + PAD), cut), F32),
             pltpu.VMEM((share, blocks, home, cut), BF16),
-            pltpu.VMEM(whole, BF16),
             pltpu.SemaphoreType.DMA((share,)),
-            pltpu.SemaphoreType.DMA((n_copies(place),)),
-        ],
+        ]
+        + whole_scratch(right_two),
         (*g_mid, *flat(right_two)),
         us=10,
         scalars=pos,
@@ -515,7 +517,7 @@
     one, two, rest = unflat(place, rest[:wide]), unflat(place, rest[wide : 2 * wide]), rest[2 * wide :]
     e_ref, act_ref, keep_two, send_two, keep_one, send_one, *rest = rest
     out_refs, rest = rest[:share], rest[share:]
-    turned, hidden, e_one, s_all, one_all, two_all, s_sems, one_sems, two_sems = rest
+    turned, hidden, e_one, s_all, s_sems, one_all, one_sems, two_all, two_sems = rest
     per, size, cut = act_ref.shape
     home = s_all.shape[2]
     pitch = size + PAD
@@ -528,20 +530,21 @@
         return pl.ds(j * per + k, size, stride=pitch)
 
     def second():
-        return piece_copies(place, pos_ref, two, two_all, two_sems)
+        return piece_copies(two, two_all, two_sems)
 
     @pl.when((phase == 0) & (j == 0))
     def _():
-        copies = share_copies(place, pos_ref, s_parts, s_all, s_sems) + piece_copies(place, pos_ref, one, one_all, one_sems)
+        copies = share_copies(place, pos_ref, s_parts, s_all, s_sems) + piece_copies(one, one_all, one_sems)
         run(copies)
         run(second())
         finish(copies)
 
     @pl.when(phase == 0)
     def _():
+        block = block_reader(place, pos_ref, one_all, j)
+
         def body(k):
-            b = j * per + k
-            turned[column(k), :] = dot_tn(one_all[b], stacked(s_all, b))
+            turned[column(k), :] = dot_tn(block(k), stacked(s_all, j * per + k))
 
         each(per, body)
 
@@ -551,6 +554,8 @@
 
     @pl.when(phase == 1)
     def _():
+        block = block_reader(place, pos_ref, two_all, j)
+
         def with_out(grad_ref):
             def body(k):
                 v = turned[rows(k), :].astype(BF16).astype(F32)
@@ -558,7 +563,7 @@
                 act = value.astype(BF16)
                 act_ref[k] = act
                 e = e_ref[k]
-                hidden[column(k), :] = slope * dot_nn(two_all[j * per + k], e)
+                hidden[column(k), :] = slope * dot_nn(block(k), e)
                 grad_ref[0, k] = dot_nt(act, e).astype(BF16)
 
             each(per, body, 8)
@@ -567,11 +572,13 @@
 
     @pl.when(phase == 2)
     def _():
+        block = block_reader(place, pos_ref, one_all, j)
+
         def with_out(grad_ref):
             def body(k):
                 b = j * per + k
                 h = hidden[rows(k), :].astype(BF16)
-                e_one[k] = dot_nn(one_all[b], h).astype(BF16)
+                e_one[k] = dot_nn(block(k), h).astype(BF16)
                 grad_ref[0, k] = dot_nt(stacked(s_all, b), h).astype(BF16)
 
             each(per, body)
@@ -590,7 +597,7 @@
 
 
 def middle(place, pos, s_mid, e_mid, right_one, left_two):
-    blocks, home, cut, share, whole = middle_sizes(place, s_mid)
+    blocks, home, cut, share = middle_sizes(place, s_mid)
     at = [during(phase, share) for phase in range(3)]
     block = pl.BlockSpec((home, blocks, cut), lambda p, j, pos: (at[1](p, j), 0, 0))
     two, two_specs = grad_specs(place, 1, home, blocks, share)
@@ -606,12 +613,10 @@
         + [
             pltpu.VMEM((home, blocks, cut), BF16),
             pltpu.VMEM((share, blocks, home, cut), BF16),
-            pltpu.VMEM(whole, BF16),
-            pltpu.VMEM(whole, BF16),
             pltpu.SemaphoreType.DMA((share,)),
-            pltpu.SemaphoreType.DMA((n_copies(place),)),
-            pltpu.SemaphoreType.DMA((n_copies(place),)),
-        ],
+        ]
+        + whole_scratch(right_one)
+        + whole_scratch(left_two),
         (*s_mid, *flat(right_one), *flat(left_two), e_mid),
         us=26,
         scalars=pos,
@@ -626,7 +631,7 @@
     left, right, rest = unflat(place, rest[:wide]), unflat(place, rest[wide : 2 * wide]), rest[2 * wide :]
     act_ref, keep_ref, send_ref, *rest = rest
     out_refs, rest = rest[:share], rest[share:]
-    turned, fourth, g_all, left_all, right_all, g_sems, left_sems, right_sems = rest
+    turned, fourth, g_all, g_sems, left_all, left_sems, right_all, right_sems = rest
     per, size, _ = act_ref.shape
     pitch = size + PAD
     phase, j = pl.program_id(0), pl.program_id(1)
@@ -638,19 +643,21 @@
         return pl.ds(j * per + k, size, stride=pitch)
 
     def second():
-        return piece_copies(place, pos_ref, right, right_all, right_sems) + share_copies(place, pos_ref, g_parts, g_all, g_sems)
+        return piece_copies(right, right_all, right_sems) + share_copies(place, pos_ref, g_parts, g_all, g_sems)
 
     @pl.when((phase == 0) & (j == 0))
     def _():
-        copies = piece_copies(place, pos_ref, left, left_all, left_sems)
+        copies = piece_copies(left, left_all, left_sems)
         run(copies)
         run(second())
         finish(copies)
 
     @pl.when(phase == 0)
     def _():
+        block = block_reader(place, pos_ref, left_all, j)
+
         def body(k):
-            turned[column(k), :] = dot_tn(left_all[j * per + k], act_ref[k])
+            turned[column(k), :] = dot_tn(block(k), act_ref[k])
 
         each(per, body)
 
@@ -660,11 +667,13 @@
 
     @pl.when(phase == 1)
     def _():
+        block = block_reader(place, pos_ref, right_all, j)
+
         def with_out(grad_ref):
             def body(k):
                 b = j * per + k
                 third = turned[rows(k), :].astype(BF16)
-                fourth[column(k), :] = dot_tn(right_all[b], third)
+                fourth[column(k), :] = dot_tn(block(k), third)
                 grad_ref[0, k] = dot_nt(third, stacked(g_all, b)).astype(BF16)
 
             each(per, body)
@@ -684,7 +693,7 @@
 
 
 def forward_two(place, pos, act, g_mid, left_two, right_two):
-    blocks, home, cut, share, whole = middle_sizes(place, g_mid)
+    blocks, home, cut, share = middle_sizes(place, g_mid)
     at = during(0, share)
     grad, grad_spec = grad_specs(place, 1, home, blocks, share)
     out = call(
@@ -696,12 +705,10 @@
         [pltpu.VMEM((blocks * (blocks + PAD), cut), F32)] * 2
         + [
             pltpu.VMEM((share, blocks, home, cut), BF16),
-            pltpu.VMEM(whole, BF16),
-            pltpu.VMEM(whole, BF16),
             pltpu.SemaphoreType.DMA((share,)),
-            pltpu.SemaphoreType.DMA((n_copies(place),)),
-            pltpu.SemaphoreType.DMA((n_copies(place),)),
-        ],
+        ]
+        + whole_scratch(left_two)
+        + whole_scratch(right_two),
         (*g_mid, *flat(left_two), *flat(right_two), act),
         us=20,
         scalars=pos,
@@ -754,11 +761,11 @@
     n_one, n_two, n_three = (place.steps.index(step) if step in place.steps else share for step in [(0, 1), (1, 0), (1, 1)])
     one = gather_far(first_left)
     w_two = from_y(factors[3])
-    rest = from_y(jnp.stack([factors[1], factors[2]]))
+    rest = from_y(after(jnp.stack([factors[1], factors[2]]), one))
     g = {n: deal(place, pos, g_home, cut, n) for n in reversed(range(share))}
     got_three = cross(g, n_three)
     w_two = gather_far(after(w_two, g[share - 1]))
-    one = last_dp(gather(after(one, rest), 1))
+    one = last_dp(gather(one, 1))
     w_two = gather(w_two, 1)
     got_three, one, w_two, rest, g = slot(place, (got_three, one, w_two, rest, g))
 
@@ -766,7 +773,6 @@
     right_two = last_dp(w_two)
     w_one = gather(gather_far(rest[:, 0]), 1)
     w_left = gather_far(rest[:, 1])
-    one = join(place, pos, [p[..., None, :, :, :] for p in one])
     s = first_stage(place, pos, x_home, one, cut)
     got_two, right_two, w_one, w_left, one, s, pos = slot(place, (got_two, right_two, w_one, w_left, one, list(s), pos))
 
@@ -798,16 +804,18 @@
 
     def hold(parts, arrays):
         for part, kept in zip(parts, arrays):
-            part.arrays = kept
+            part.arrays, part.ready = kept
 
     def arrays_of(*parts):
-        return [part.arrays for part in parts]
+        return [(part.arrays, part.ready) for part in parts]
 
     x_step, near_step, far_step = (place.dp + [None] * 3)[:3]
 
     e_three = cross(e, n_three)
     two, one_part = start_sum(*grad_two), start_sum(*grad_one)
     grad_three, s = forward_two(place, pos, act, g_mid, left_two, right_two)
+    two.prepare(x_step)
+    one_part.prepare(near_step)
     e_three, kept, grad_three, s, e = slot(place, (e_three, arrays_of(two, one_part), grad_three, s, e))
     hold([two, one_part], kept)
 
@@ -816,6 +824,7 @@
     one_part.step(near_step)
     three = start_sum(*grad_three)
     e_one = cross(e, n_one)
+    three.prepare(x_step)
     e_two, e_one, kept, s = slot(place, (e_two, e_one, arrays_of(two, one_part, three), s))
     hold([two, one_part, three], kept)
     e_got = [e[0], e_one, e_two, e_three][:share]
@@ -824,19 +833,29 @@
     three.step(x_step)
     two.step(near_step)
     input_grad, lone = last_stage(place, pos, e_got, x_home, g_home, one)
-    s_three, kept, lone, input_grad, s = slot(place, (s_three, arrays_of(two, one_part, three), lone, input_grad, s))
-    hold([two, one_part, three], kept)
     lone = Sum([lone], [home] + place.dp[::-1], (rows, size))
-
-    s_two, s_one = cross(s, n_two), cross(s, n_one)
-    one_part.step(x_step)
+    one_part.prepare(x_step)
+    lone.prepare(x_step)
+    s_three, kept, input_grad, s = slot(place, (s_three, arrays_of(two, one_part, three, lone), input_grad, s))
+    hold([two, one_part, three, lone], kept)
+
+    s_two = cross(s, n_two)
+    lone.step(x_step)
     three.step(near_step)
     two.step(far_step)
-    lone.step(x_step)
+    kept = slot(place, arrays_of(two, one_part, three, lone))
+    hold([two, one_part, three, lone], kept)
+
+    one_part.step(x_step)
+    lone.step(near_step)
+    three.step(far_step)
+    s_one = cross(s, n_one)
+    s_two, s_one, kept = slot(place, (s_two, s_one, arrays_of(two, one_part, three, lone)))
+    hold([two, one_part, three, lone], kept)
+
     one_part.step(far_step)
-    three.step(far_step)
-    lone.step(near_step)
-    s_got = [after(s[0], lone.arrays[-1]), s_one, s_two, s_three][:share]
+    lone.step(far_step)
+    s_got = [s[0], s_one, s_two, s_three][:share]
     grad_ltwo = two.finish()
     grad_rone = one_part.finish()
     grad_rtwo = three.finish()

time: 323 us -> 326 us (level)
  starting transfers between devices: 51.5 us -> 47.7 us
    ppermute x50, starting transfers between devices: 51.5 us -> 47.7 us  [send(): self.last = lax.ppermute(value, self.axis, pairs)]
    pallas_call x11 -> x10, Pallas kernels: 99.4 us -> 97.7 us  [call(): pl.pallas_call(body, out_shape=out, grid_spec=spec, compiler_params=pltpu...]
  transfers between devices with their start and end apart: 50 -> 50, of which waited for: 26 -> 27; matrix products, arithmetic and copies ran while one was open for 9% -> 10% of each run, Pallas kernels for 22% -> 21%
where the time goes in v7:
time: 326 us; the launch traced here: 325 us
  waiting for transfers between devices  135 us (41%)
  Pallas kernels  97.7 us (30%)
  starting transfers between devices  47.7 us (15%)
  other arithmetic  36 us (11%)
  local copies, waits for them, and re-layouts  7.79 us (2%)
    ppermute x50, waiting for transfers between devices, send(): self.last = lax.ppermute(value, self.axis, pairs)  135 us
    pallas_call x10, Pallas kernels, call(): pl.pallas_call(body, out_shape=out, grid_spec=spec, compiler_params=pltpu...  97.7 us
    ppermute x50, starting transfers between devices, send(): self.last = lax.ppermute(value, self.axis, pairs)  47.7 us
    convert_element_type x14, other arithmetic, parts(): self.cut(ring, lax.rem(ring.here() + step, ring.size)).astype(BF16)  22.9 us
    add x4, other arithmetic, total(): return functools.reduce(jnp.add, [t.astype(F32) for t in terms])  7.54 us
  transfers between devices with their start and end apart: 50, of which 27 were waited for; matrix products, arithmetic and copies ran while one was open for 10% of the time, Pallas kernels for 21%

profile of v7, /device:TPU:0, one launch (start us, length us, event | category | flops | bytes accessed | tf_op | source)
XLA Modules:
  0.0 325.3 jit_solution(1274088127695647793)
XLA Ops:
  6.9 3.3 %shard_map.109 = bf16[128,32,128]{2,1,0:T(8,128)(2,1)} custom-call(s32[5]{0:T(128)} %stack.116.pos_ref, bf16[32,128,512]{2,1,0:T(8,128)(2,1)} %bitcast.186), custom_call_target="tpu_custom_call" | custom-call | bytes 4200000 | tf_op jit(solution)/shard_map/pallas_call | solution.py:61
  12.6 4.1 %collective-permute-start.2 = (bf16[2,32,16,128]{3,2,1,0:T(8,128)(2,1)S(1)}, bf16[2,32,16,128]{3,2,1,0:T(8,128)(2,1)S(1)}, u32[]{:S(2)}, u32[]{:S(2)}) collective-permute-start(bf16[2,32,16,128]{3,2,1,0:T(8,128)(2,1)S(1)} %get-tuple-element.321), channel_id=1, source_target_pairs={{0,8},{4,12},{8,0},{12,4},{16,24},{20,28},{24,16},{28,20},{1,9},{5... | collective-permute-start | bytes 786440 | tf_op jit(solution)/shard_map/ppermute | solution.py:110
  16.7 9.6 %collective-permute-done.5 = bf16[2,32,16,128]{3,2,1,0:T(8,128)(2,1)S(1)} collective-permute-done((bf16[2,32,16,128]{3,2,1,0:T(8,128)(2,1)S(1)}, bf16[2,32,16,128]{3,2,1,0:T(8,128)(2,1)S(1)}, u32[]{:S(2)}, u32[]{:S(2)}) %collective-permute-start.5) | collective-permute-done | bytes 262176 | tf_op jit(solution)/shard_map/ppermute | solution.py:110
  30.5 3.1 shard_map.110.refs_0_
  33.6 3.1 shard_map.111
  36.7 3.1 shard_map.112
  51.0 8.9 %collective-permute-done.10 = bf16[2,32,16,128]{3,2,1,0:T(8,128)(2,1)S(1)} collective-permute-done((bf16[2,32,16,128]{3,2,1,0:T(8,128)(2,1)S(1)}, bf16[2,32,16,128]{3,2,1,0:T(8,128)(2,1)S(1)}, u32[]{:S(2)}, u32[]{:S(2)}) %collective-permute-start.10) | collective-permute-done | bytes 262176 | tf_op jit(solution)/shard_map/ppermute | solution.py:110
  61.7 3.4 %collective-permute-start.12 = (bf16[2,32,16,128]{3,2,1,0:T(8,128)(2,1)}, bf16[2,32,16,128]{3,2,1,0:T(8,128)(2,1)}, u32[]{:S(2)}, u32[]{:S(2)}) collective-permute-start(bf16[2,32,16,128]{3,2,1,0:T(8,128)(2,1)} %get-tuple-element.167), channel_id=1, source_target_pairs={{0,16},{4,20},{8,24},{12,28},{16,0},{20,4},{24,8},{28,12},{1,17},{... | collective-permute-start | bytes 786440 | tf_op jit(solution)/shard_map/ppermute | solution.py:110
  65.1 9.5 %shard_map.113 = (bf16[128,32,128]{2,1,0:T(8,128)(2,1)}, bf16[128,32,128]{2,1,0:T(8,128)(2,1)}, bf16[128,32,128]{2,1,0:T(8,128)(2,1)}, bf16[128,32,128]{2,1,0:T(8,128)(2,1)}) custom-call(s32[5]{0:T(128)} %stack.116.pos_ref, bf16[32,128,512]{2,1,0:T(8,128)(2,1)} %bitcast.191, bf16[2,2,32,16,128]{4,3,2,1,0:T(8,128)(2,1)} %copy-done.2, ...), custom_call_target="tpu_custom_call" | custom-call | bytes 9600000 | tf_op jit(solution)/shard_map/pallas_call | solution.py:61
  74.7 4.4 %collective-permute-done.12 = bf16[2,32,16,128]{3,2,1,0:T(8,128)(2,1)} collective-permute-done((bf16[2,32,16,128]{3,2,1,0:T(8,128)(2,1)}, bf16[2,32,16,128]{3,2,1,0:T(8,128)(2,1)}, u32[]{:S(2)}, u32[]{:S(2)}) %collective-permute-start.12) | collective-permute-done | bytes 262176 | tf_op jit(solution)/shard_map/ppermute | solution.py:110
  82.8 3.5 %collective-permute-start.16 = (bf16[2,2,32,16,128]{4,3,2,1,0:T(8,128)(2,1)S(1)}, bf16[2,2,32,16,128]{4,3,2,1,0:T(8,128)(2,1)S(1)}, u32[]{:S(2)}, u32[]{:S(2)}) collective-permute-start(bf16[2,2,32,16,128]{4,3,2,1,0:T(8,128)(2,1)S(1)} %pad_maximum_fusion.7), channel_id=1, source_target_pairs={{0,8},{4,12},{8,0},{12,4},{16,24},{20,28},{24,16},{28,20},{1,9},{5... | collective-permute-start | bytes 1572872 | tf_op jit(solution)/shard_map/ppermute | solution.py:110
  89.4 8.5 %collective-permute-done.16 = bf16[2,2,32,16,128]{4,3,2,1,0:T(8,128)(2,1)S(1)} collective-permute-done((bf16[2,2,32,16,128]{4,3,2,1,0:T(8,128)(2,1)S(1)}, bf16[2,2,32,16,128]{4,3,2,1,0:T(8,128)(2,1)S(1)}, u32[]{:S(2)}, u32[]{:S(2)}) %collective-permute-start.16) | collective-permute-done | bytes 524320 | tf_op jit(solution)/shard_map/ppermute | solution.py:110
  98.1 13.7 %collective-permute-done.13.refs_3_ = bf16[128,32,128]{2,1,0:T(8,128)(2,1)S(1)} collective-permute-done((bf16[128,32,128]{2,1,0:T(8,128)(2,1)S(1)}, bf16[128,32,128]{2,1,0:T(8,128)(2,1)S(1)}, u32[]{:S(2)}, u32[]{:S(2)}) %collective-permute-start.13) | collective-permute-done | bytes 1048608 | tf_op jit(solution)/shard_map/ppermute | solution.py:110
  116.4 9.4 %shard_map.114.refs_12_ = bf16[128,128,128]{2,1,0:T(8,128)(2,1)} custom-call(s32[5]{0:T(128)} %stack.116.pos_ref, bf16[128,32,128]{2,1,0:T(8,128)(2,1)} %shard_map.110.refs_0_, bf16[128,32,128]{2,1,0:T(8,128)(2,1)} %collective-permute-done.19.refs_1_, bf16[128,32,128]{2,1,0:T(8,128)(2,1)} %copy-done.4, bf16[128,32,128]{2,1,0:T(8,128)(2,1)} %copy-done.3, ...), custom_call_target="tpu_custom_call" | custom-call | bytes 12000000 | tf_op jit(solution)/shard_map/pallas_call | solution.py:61
  125.8 11.7 %collective-permute-done.20.refs_2_ = bf16[128,32,128]{2,1,0:T(8,128)(2,1)} collective-permute-done((bf16[128,32,128]{2,1,0:T(8,128)(2,1)}, bf16[128,32,128]{2,1,0:T(8,128)(2,1)}, u32[]{:S(2)}, u32[]{:S(2)}) %collective-permute-start.20) | collective-permute-done | bytes 1048608 | tf_op jit(solution)/shard_map/ppermute | solution.py:110
  142.5 28.0 %shard_map.115 = (bf16[128,128,128]{2,1,0:T(8,128)(2,1)}, bf16[2,32,128,128]{3,2,1,0:T(8,128)(2,1)}, bf16[2,32,128,128]{3,2,1,0:T(8,128)(2,1)}, bf16[2,32,128,12...) custom-call(s32[5]{0:T(128)} %stack.116.pos_ref, ...), custom_call_target="tpu_custom_call" | custom-call | bytes 31200000 | tf_op jit(solution)/shard_map/pallas_call | solution.py:61
  171.9 20.0 %shard_map.116 = (bf16[2,32,128,128]{3,2,1,0:T(8,128)(2,1)}, bf16[2,32,128,128]{3,2,1,0:T(8,128)(2,1)}, bf16[32,128,128]{2,1,0:T(8,128)(2,1)}, bf16[32,128,128]{...) custom-call(s32[5]{0:T(128)} %stack.116.pos_ref, ...), custom_call_target="tpu_custom_call" | custom-call | bytes 24000000 | tf_op jit(solution)/shard_map/pallas_call | solution.py:61
  202.3 19.9 %collective-permute-done.29.refs_2_ = bf16[128,32,128]{2,1,0:T(8,128)(2,1)S(1)} collective-permute-done((bf16[128,32,128]{2,1,0:T(8,128)(2,1)}, bf16[128,32,128]{2,1,0:T(8,128)(2,1)S(1)}, u32[]{:S(2)}, u32[]{:S(2)}) %collective-permute-start.29) | collective-permute-done | bytes 1048608 | tf_op jit(solution)/shard_map/ppermute | solution.py:110
  229.0 11.2 %shard_map.117 = (bf16[32,128,512]{2,1,0:T(8,128)(2,1)}, bf16[32,128,128]{2,1,0:T(8,128)(2,1)}) custom-call(s32[5]{0:T(128)} %stack.116.pos_ref, bf16[128,32,128]{2,1,0:T(8,128)(2,1)} %get-tuple-element.246.refs_0_, bf16[128,32,128]{2,1,0:T(8,128)(2,1)} %copy-done.22, bf16[128,32,128]{2,1,0:T(8,128)(2,1)} %copy-done.21, bf16[128,32,128]{2,1,0:T(8,128)(2,1)} %copy-done.20, ...), custom_call_target="tpu_custom_call" | custom-call | bytes 12000000 | tf_op jit(solution)/shard_map/pallas_call | solution.py:61
  244.3 6.4 %collective-permute-done.34.refs_3_ = bf16[32,128,128]{2,1,0:T(8,128)(2,1)S(1)} collective-permute-done((bf16[32,128,128]{2,1,0:T(8,128)(2,1)}, bf16[32,128,128]{2,1,0:T(8,128)(2,1)S(1)}, u32[]{:S(2)}, u32[]{:S(2)}) %collective-permute-start.34) | collective-permute-done | bytes 1048608 | tf_op jit(solution)/shard_map/ppermute | solution.py:110
  258.7 13.2 %collective-permute-done.39 = bf16[2,32,16,128]{3,2,1,0:T(8,128)(2,1)S(1)} collective-permute-done((bf16[2,32,16,128]{3,2,1,0:T(8,128)(2,1)S(1)}, bf16[2,32,16,128]{3,2,1,0:T(8,128)(2,1)S(1)}, u32[]{:S(2)}, u32[]{:S(2)}) %collective-permute-start.39) | collective-permute-done | bytes 262176 | tf_op jit(solution)/shard_map/ppermute | solution.py:110
  280.0 7.9 %collective-permute-done.44 = bf16[32,2,16,128]{3,2,0,1:T(8,128)(2,1)} collective-permute-done((bf16[32,2,16,128]{3,2,0,1:T(8,128)(2,1)}, bf16[32,2,16,128]{3,2,0,1:T(8,128)(2,1)}, u32[]{:S(2)}, u32[]{:S(2)}) %collective-permute-start.44) | collective-permute-done | bytes 262176 | tf_op jit(solution)/shard_map/ppermute | solution.py:110
  287.9 5.2 %collective-permute-done.43 = bf16[2,32,16,128]{3,2,1,0:T(8,128)(2,1)} collective-permute-done((bf16[2,32,16,128]{3,2,1,0:T(8,128)(2,1)S(1)}, bf16[2,32,16,128]{3,2,1,0:T(8,128)(2,1)}, u32[]{:S(2)}, u32[]{:S(2)}) %collective-permute-start.43) | collective-permute-done | bytes 262176 | tf_op jit(solution)/shard_map/ppermute | solution.py:110
  298.3 7.0 %shard_map.118 = bf16[32,128,512]{2,1,0:T(8,128)(2,1)} custom-call(s32[5]{0:T(128)} %stack.116.pos_ref, bf16[32,128,128]{2,1,0:T(8,128)(2,1)} %get-tuple-element.257.refs_0_, bf16[32,128,128]{2,1,0:T(8,128)(2,1)} %collective-permute-done.38.refs_1_, bf16[32,128,128]{2,1,0:T(8,128)(2,1)} %collective-permute-done.37.refs_2_, bf16[32,128,128]{2,1,0:T(8,128)(2,1)} %copy-done.14, ...), custom_call_target="tpu_custom_call" | custom-call | bytes 7200000 | tf_op jit(solution)/shard_map/pallas_call | solution.py:61
  (182 shorter events, 106.1 us)
Async XLA Ops:
  12.5 30.8 %collective-permute-start = (bf16[128,32,128]{2,1,0:T(8,128)(2,1)}, bf16[128,32,128]{2,1,0:T(8,128)(2,1)S(1)}, u32[]{:S(2)}, u32[]{:S(2)}) collective-permute-start(bf16[128,32,128]{2,1,0:T(8,128)(2,1)} %shard_map.109), channel_id=1, source_target_pairs={{0,3},{1,2},{2,1},{3,0},{4,7},{5,6},{6,5},{7,4},{8,11},{9,10},{10,... | collective-permute-start | bytes 3145736 | tf_op jit(solution)/shard_map/ppermute | solution.py:110
  47.1 35.8 %collective-permute-start.8 = (bf16[128,32,128]{2,1,0:T(8,128)(2,1)}, bf16[128,32,128]{2,1,0:T(8,128)(2,1)S(1)}, u32[]{:S(2)}, u32[]{:S(2)}) collective-permute-start(bf16[128,32,128]{2,1,0:T(8,128)(2,1)} %shard_map.112), channel_id=1, source_target_pairs={{0,2},{1,3},{2,0},{3,1},{4,6},{5,7},{6,4},{7,5},{8,10},{9,11},{10,... | collective-permute-start | bytes 3145736 | tf_op jit(solution)/shard_map/ppermute | solution.py:110
  49.5 33.3 %collective-permute-start.9 = (bf16[2,2,2,32,16,128]{5,4,3,2,1,0:T(8,128)(2,1)S(1)}, bf16[2,2,2,32,16,128]{5,4,3,2,1,0:T(8,128)(2,1)}, u32[]{:S(2)}, u32[]{:S(2)}) collective-permute-start(bf16[2,2,2,32,16,128]{5,4,3,2,1,0:T(8,128)(2,1)S(1)} %pad_maximum_fusion.refs_4_.refs_8_), channel_id=1, source_target_pairs={{0,4},{4,0},{8,12},{12,8},{16,20},{20,16},{24,28},{28,24},{1,5},{5... | collective-permute-start | bytes 3145736 | tf_op jit(solution)/shard_map/ppermute | solution.py:110
  65.1 24.3 %collective-permute-start.19 = (bf16[128,32,128]{2,1,0:T(8,128)(2,1)}, bf16[128,32,128]{2,1,0:T(8,128)(2,1)}, u32[]{:S(2)}, u32[]{:S(2)}) collective-permute-start(bf16[128,32,128]{2,1,0:T(8,128)(2,1)} %shard_map.111), channel_id=1, source_target_pairs={{0,1},{1,0},{2,3},{3,2},{4,5},{5,4},{6,7},{7,6},{8,9},{9,8},{10,11... | collective-permute-start | bytes 3145736 | tf_op jit(solution)/shard_map/ppermute | solution.py:110
  86.4 25.4 %collective-permute-start.13 = (bf16[128,32,128]{2,1,0:T(8,128)(2,1)S(1)}, bf16[128,32,128]{2,1,0:T(8,128)(2,1)S(1)}, u32[]{:S(2)}, u32[]{:S(2)}) collective-permute-start(bf16[128,32,128]{2,1,0:T(8,128)(2,1)S(1)} %copy-done.31), channel_id=1, source_target_pairs={{0,3},{1,2},{2,1},{3,0},{4,7},{5,6},{6,5},{7,4},{8,11},{9,10},{10,... | collective-permute-start | bytes 3145736 | tf_op jit(solution)/shard_map/ppermute | solution.py:110
  86.7 26.0 %collective-permute-start.14 = (bf16[128,32,128]{2,1,0:T(8,128)(2,1)S(1)}, bf16[128,32,128]{2,1,0:T(8,128)(2,1)S(1)}, u32[]{:S(2)}, u32[]{:S(2)}) collective-permute-start(bf16[128,32,128]{2,1,0:T(8,128)(2,1)S(1)} %copy-done.30), channel_id=1, source_target_pairs={{0,1},{1,0},{2,3},{3,2},{4,5},{5,4},{6,7},{7,6},{8,9},{9,8},{10,11... | collective-permute-start | bytes 3145736 | tf_op jit(solution)/shard_map/ppermute | solution.py:110
  88.0 25.4 %collective-permute-start.15 = (bf16[2,2,2,32,16,128]{5,4,3,2,1,0:T(8,128)(2,1)}, bf16[2,2,2,32,16,128]{5,4,3,2,1,0:T(8,128)(2,1)}, u32[]{:S(2)}, u32[]{:S(2)}) collective-permute-start(bf16[2,2,2,32,16,128]{5,4,3,2,1,0:T(8,128)(2,1)} %pad_maximum_fusion.1.refs_4_), channel_id=1, source_target_pairs={{0,4},{4,0},{8,12},{12,8},{16,20},{20,16},{24,28},{28,24},{1,5},{5... | collective-permute-start | bytes 3145736 | tf_op jit(solution)/shard_map/ppermute | solution.py:110
  89.4 23.9 %collective-permute-start.17 = (bf16[2,2,2,32,16,128]{5,4,3,2,1,0:T(8,128)(2,1)S(1)}, bf16[2,2,2,32,16,128]{5,4,3,2,1,0:T(8,128)(2,1)S(1)}, u32[]{:S(2)}, u32[]{:S(2)}) collective-permute-start(bf16[2,2,2,32,16,128]{5,4,3,2,1,0:T(8,128)(2,1)S(1)} %pad_maximum_fusion.refs_4_.refs_8_), channel_id=1, source_target_pairs={{0,1},{1,0},{2,3},{3,2},{4,5},{5,4},{6,7},{7,6},{8,9},{9,8},{10,11... | collective-permute-start | bytes 3145736 | tf_op jit(solution)/shard_map/ppermute | solution.py:110
  111.8 25.6 %collective-permute-start.20 = (bf16[128,32,128]{2,1,0:T(8,128)(2,1)}, bf16[128,32,128]{2,1,0:T(8,128)(2,1)}, u32[]{:S(2)}, u32[]{:S(2)}) collective-permute-start(bf16[128,32,128]{2,1,0:T(8,128)(2,1)} %get-tuple-element.185), channel_id=1, source_target_pairs={{0,2},{1,3},{2,0},{3,1},{4,6},{5,7},{6,4},{7,5},{8,10},{9,11},{10,... | collective-permute-start | bytes 3145736 | tf_op jit(solution)/shard_map/ppermute | solution.py:110
  114.3 24.4 %collective-permute-start.21 = (bf16[2,2,2,32,16,128]{5,4,3,2,1,0:T(8,128)(2,1)S(1)}, bf16[2,2,2,32,16,128]{5,4,3,2,1,0:T(8,128)(2,1)S(1)}, u32[]{:S(2)}, u32[]{:S(2)}) collective-permute-start(bf16[2,2,2,32,16,128]{5,4,3,2,1,0:T(8,128)(2,1)S(1)} %pad_maximum_fusion.2.refs_8_.refs_4_), channel_id=1, source_target_pairs={{0,4},{4,0},{8,12},{12,8},{16,20},{20,16},{24,28},{28,24},{1,5},{5... | collective-permute-start | bytes 3145736 | tf_op jit(solution)/shard_map/ppermute | solution.py:110
  115.8 23.0 %collective-permute-start.22 = (bf16[2,2,2,32,16,128]{5,4,3,2,1,0:T(8,128)(2,1)S(1)}, bf16[2,2,2,32,16,128]{5,4,3,2,1,0:T(8,128)(2,1)}, u32[]{:S(2)}, u32[]{:S(2)}) collective-permute-start(bf16[2,2,2,32,16,128]{5,4,3,2,1,0:T(8,128)(2,1)S(1)} %pad_maximum_fusion.2.refs_8_.refs_4_), channel_id=1, source_target_pairs={{0,1},{1,0},{2,3},{3,2},{4,5},{5,4},{6,7},{7,6},{8,9},{9,8},{10,11... | collective-permute-start | bytes 3145736 | tf_op jit(solution)/shard_map/ppermute | solution.py:110
  115.8 23.0 %collective-permute-start.23 = (bf16[2,2,2,32,16,128]{5,4,3,2,1,0:T(8,128)(2,1)}, bf16[2,2,2,32,16,128]{5,4,3,2,1,0:T(8,128)(2,1)}, u32[]{:S(2)}, u32[]{:S(2)}) collective-permute-start(bf16[2,2,2,32,16,128]{5,4,3,2,1,0:T(8,128)(2,1)} %pad_maximum_fusion.1.refs_4_), channel_id=1, source_target_pairs={{0,1},{1,0},{2,3},{3,2},{4,5},{5,4},{6,7},{7,6},{8,9},{9,8},{10,11... | collective-permute-start | bytes 3145736 | tf_op jit(solution)/shard_map/ppermute | solution.py:110
  116.3 22.5 %collective-permute-start.24 = (bf16[2,2,2,32,16,128]{5,4,3,2,1,0:T(8,128)(2,1)}, bf16[2,2,2,32,16,128]{5,4,3,2,1,0:T(8,128)(2,1)}, u32[]{:S(2)}, u32[]{:S(2)}) collective-permute-start(bf16[2,2,2,32,16,128]{5,4,3,2,1,0:T(8,128)(2,1)} %collective-permute-done.15.refs_5_), channel_id=1, source_target_pairs={{0,1},{1,0},{2,3},{3,2},{4,5},{5,4},{6,7},{7,6},{8,9},{9,8},{10,11... | collective-permute-start | bytes 3145736 | tf_op jit(solution)/shard_map/ppermute | solution.py:110
  170.5 21.4 %collective-permute-start.28 = (bf16[2,32,128,128]{3,2,1,0:T(8,128)(2,1)}, bf16[2,32,128,128]{3,2,1,0:T(8,128)(2,1)}, u32[]{:S(2)}, u32[]{:S(2)}) collective-permute-start(bf16[2,32,128,128]{3,2,1,0:T(8,128)(2,1)} %get-tuple-element.211), channel_id=1, source_target_pairs={{0,1},{1,0},{2,3},{3,2},{4,5},{5,4},{6,7},{7,6},{8,9},{9,8},{10,11... | collective-permute-start | bytes 6291464 | tf_op jit(solution)/shard_map/ppermute | solution.py:110
  170.7 23.0 %collective-permute-start.27 = (bf16[2,32,128,128]{3,2,1,0:T(8,128)(2,1)}, bf16[2,32,128,128]{3,2,1,0:T(8,128)(2,1)}, u32[]{:S(2)}, u32[]{:S(2)}) collective-permute-start(bf16[2,32,128,128]{3,2,1,0:T(8,128)(2,1)} %get-tuple-element.209), channel_id=1, source_target_pairs={{0,1},{1,0},{2,3},{3,2},{4,5},{5,4},{6,7},{7,6},{8,9},{9,8},{10,11... | collective-permute-start | bytes 6291464 | tf_op jit(solution)/shard_map/ppermute | solution.py:110
  171.1 25.4 %collective-permute-start.26 = (bf16[128,32,128]{2,1,0:T(8,128)(2,1)}, bf16[128,32,128]{2,1,0:T(8,128)(2,1)S(1)}, u32[]{:S(2)}, u32[]{:S(2)}) collective-permute-start(bf16[128,32,128]{2,1,0:T(8,128)(2,1)} %get-tuple-element.207), channel_id=1, source_target_pairs={{0,3},{1,2},{2,1},{3,0},{4,7},{5,6},{6,5},{7,4},{8,11},{9,10},{10,... | collective-permute-start | bytes 3145736 | tf_op jit(solution)/shard_map/ppermute | solution.py:110
  196.6 25.7 %collective-permute-start.29 = (bf16[128,32,128]{2,1,0:T(8,128)(2,1)}, bf16[128,32,128]{2,1,0:T(8,128)(2,1)S(1)}, u32[]{:S(2)}, u32[]{:S(2)}) collective-permute-start(bf16[128,32,128]{2,1,0:T(8,128)(2,1)} %get-tuple-element.222), channel_id=1, source_target_pairs={{0,2},{1,3},{2,0},{3,1},{4,6},{5,7},{6,4},{7,5},{8,10},{9,11},{10,... | collective-permute-start | bytes 3145736 | tf_op jit(solution)/shard_map/ppermute | solution.py:110
  197.8 24.5 %collective-permute-start.30 = (bf16[128,32,128]{2,1,0:T(8,128)(2,1)}, bf16[128,32,128]{2,1,0:T(8,128)(2,1)S(1)}, u32[]{:S(2)}, u32[]{:S(2)}) collective-permute-start(bf16[128,32,128]{2,1,0:T(8,128)(2,1)} %get-tuple-element.223), channel_id=1, source_target_pairs={{0,1},{1,0},{2,3},{3,2},{4,5},{5,4},{6,7},{7,6},{8,9},{9,8},{10,11... | collective-permute-start | bytes 3145736 | tf_op jit(solution)/shard_map/ppermute | solution.py:110
  197.9 25.5 %collective-permute-start.31 = (bf16[2,32,2,2,16,128]{5,4,1,3,2,0:T(8,128)(2,1)S(1)}, bf16[2,32,2,2,16,128]{5,4,1,3,2,0:T(8,128)(2,1)S(1)}, u32[]{:S(2)}, u32[]{:S(2)}) collective-permute-start(bf16[2,32,2,2,16,128]{5,4,1,3,2,0:T(8,128)(2,1)S(1)} %fusion), channel_id=1, source_target_pairs={{0,4},{4,0},{8,12},{12,8},{16,20},{20,16},{24,28},{28,24},{1,5},{5... | collective-permute-start | bytes 3145736 | tf_op jit(solution)/shard_map/ppermute | solution.py:110
  199.2 25.2 %collective-permute-start.32 = (bf16[2,32,2,2,16,128]{5,4,1,3,2,0:T(8,128)(2,1)S(1)}, bf16[2,32,2,2,16,128]{5,4,1,3,2,0:T(8,128)(2,1)S(1)}, u32[]{:S(2)}, u32[]{:S(2)}) collective-permute-start(bf16[2,32,2,2,16,128]{5,4,1,3,2,0:T(8,128)(2,1)S(1)} %fusion.1), channel_id=1, source_target_pairs={{0,8},{4,12},{8,0},{12,4},{16,24},{20,28},{24,16},{28,20},{1,9},{5... | collective-permute-start | bytes 3145736 | tf_op jit(solution)/shard_map/ppermute | solution.py:110
  225.5 25.2 %collective-permute-start.34 = (bf16[32,128,128]{2,1,0:T(8,128)(2,1)}, bf16[32,128,128]{2,1,0:T(8,128)(2,1)S(1)}, u32[]{:S(2)}, u32[]{:S(2)}) collective-permute-start(bf16[32,128,128]{2,1,0:T(8,128)(2,1)} %get-tuple-element.236), channel_id=1, source_target_pairs={{0,3},{1,2},{2,1},{3,0},{4,7},{5,6},{6,5},{7,4},{8,11},{9,10},{10,... | collective-permute-start | bytes 3145736 | tf_op jit(solution)/shard_map/ppermute | solution.py:110
  225.5 26.4 %collective-permute-start.36 = (bf16[2,32,2,2,16,128]{5,4,1,3,2,0:T(8,128)(2,1)}, bf16[2,32,2,2,16,128]{5,4,1,3,2,0:T(8,128)(2,1)}, u32[]{:S(2)}, u32[]{:S(2)}) collective-permute-start(bf16[2,32,2,2,16,128]{5,4,1,3,2,0:T(8,128)(2,1)} %fusion.2), channel_id=1, source_target_pairs={{0,4},{4,0},{8,12},{12,8},{16,20},{20,16},{24,28},{28,24},{1,5},{5... | collective-permute-start | bytes 3145736 | tf_op jit(solution)/shard_map/ppermute | solution.py:110
  255.3 37.8 %collective-permute-start.37 = (bf16[32,128,128]{2,1,0:T(8,128)(2,1)}, bf16[32,128,128]{2,1,0:T(8,128)(2,1)}, u32[]{:S(2)}, u32[]{:S(2)}) collective-permute-start(bf16[32,128,128]{2,1,0:T(8,128)(2,1)} %get-tuple-element.258), channel_id=1, source_target_pairs={{0,2},{1,3},{2,0},{3,1},{4,6},{5,7},{6,4},{7,5},{8,10},{9,11},{10,... | collective-permute-start | bytes 3145736 | tf_op jit(solution)/shard_map/ppermute | solution.py:110
  256.5 36.7 %collective-permute-start.38 = (bf16[32,128,128]{2,1,0:T(8,128)(2,1)}, bf16[32,128,128]{2,1,0:T(8,128)(2,1)}, u32[]{:S(2)}, u32[]{:S(2)}) collective-permute-start(bf16[32,128,128]{2,1,0:T(8,128)(2,1)} %get-tuple-element.259), channel_id=1, source_target_pairs={{0,1},{1,0},{2,3},{3,2},{4,5},{5,4},{6,7},{7,6},{8,9},{9,8},{10,11... | collective-permute-start | bytes 3145736 | tf_op jit(solution)/shard_map/ppermute | solution.py:110
  (58 other events, 712.8 us)

commit v8 on v7

--- a/solution.py
+++ b/solution.py
@@ -38,16 +38,39 @@
     return jnp.einsum(form, left, right, preferred_element_type=F32)
 
 
+def dot(left, right, left_dim, right_dim):
+    return lax.dot_general(left, right, (((left_dim,), (right_dim,)), ((), ())), preferred_element_type=F32)
+
+
+def dots(lefts, rights, left_dim, right_dim):
+    if len(lefts) == 1:
+        return [dot(lefts[0], rights[0], left_dim, right_dim)]
+    zero = jnp.zeros_like(rights[0])
+    upper = jnp.concatenate([rights[0], zero], axis=1)
+    lower = jnp.concatenate([zero, rights[1]], axis=1)
+    out = dot(jnp.concatenate(lefts, axis=left_dim), jnp.concatenate([upper, lower], axis=0), left_dim, right_dim)
+    half = out.shape[1] // 2
+    return [out[:, :half], out[:, half:]]
+
+
+def dots_nn(lefts, rights):
+    return dots(lefts, rights, 1, 0)
+
+
+def dots_tn(lefts, rights):
+    return dots(lefts, rights, 0, 0)
+
+
+def dots_nt(lefts, rights):
+    return dots(lefts, rights, 1, 1)
+
+
 def dot_nn(left, right):
-    return lax.dot_general(left, right, (((1,), (0,)), ((), ())), preferred_element_type=F32)
-
-
-def dot_tn(left, right):
-    return lax.dot_general(left, right, (((0,), (0,)), ((), ())), preferred_element_type=F32)
+    return dot(left, right, 1, 0)
 
 
 def dot_nt(left, right):
-    return lax.dot_general(left, right, (((1,), (1,)), ((), ())), preferred_element_type=F32)
+    return dot(left, right, 1, 1)
 
 
 def call(body, out, grid, in_specs, out_specs, scratch, args, us, scalars=None):
@@ -67,6 +90,11 @@
         ),
         cost_estimate=pl.CostEstimate(flops=0, bytes_accessed=int(us * BYTES_PER_US), transcendentals=0),
     )(*(() if scalars is None else (scalars,)), *args)
+
+
+def pairs(count, body, unroll=8):
+    group = 2 if count % 2 == 0 else 1
+    each(count // group, lambda n: body([n * group + i for i in range(group)]), unroll)
 
 
 def shape(dims, dtype=BF16):
@@ -183,6 +211,18 @@
         for ring in [r for r in self.left[::-1] if isinstance(r, Ring)]:
             self.step(ring)
         return self.cut()
+
+
+def finish_together(sums, rings, last):
+    for part in sums:
+        for ring in rings:
+            part.step(ring)
+    sends = list(zip(*[part.parts(last) for part in sums]))
+    got = [last.send(jnp.stack(send), step + 1) for step, send in enumerate(sends)]
+    for n, part in enumerate(sums):
+        part.left = [r for r in part.left if r is not last]
+        part.arrays, part.rings = part.arrays + [g[n] for g in got], part.rings + [part.left] * len(got)
+    return [part.cut() for part in sums]
 
 
 def total(terms):
@@ -334,13 +374,15 @@
         def _():
             lanes = pl.ds(pl.multiple_of(place.onward(pos_ref, n) * cut, cut), cut)
 
-            def store(b):
-                turned[pl.ds(b, size, stride=pitch), :] = dot_tn(block(b), x_ref[b, :, lanes])
+            def store(bs):
+                out = dots_tn([block(b) for b in bs], [x_ref[b, :, lanes] for b in bs])
+                for b, y in zip(bs, out):
+                    turned[pl.ds(b, size, stride=pitch), :] = y
 
             def load(o):
                 out_ref[o] = turned[pl.ds(o * pitch, home), :].astype(BF16)
 
-            each(home, store)
+            pairs(home, store)
             each(size, load)
 
 
@@ -458,11 +500,12 @@
     def _():
         block = block_reader(place, pos_ref, w_all, j)
 
-        def body(k):
-            b = j * per + k
-            turned[pl.ds(b, size, stride=pitch), :] = dot_nn(block(k), stacked(g_all, b))
-
-        each(per, body)
+        def body(ks):
+            out = dots_nn([block(k) for k in ks], [stacked(g_all, j * per + k) for k in ks])
+            for k, y in zip(ks, out):
+                turned[pl.ds(j * per + k, size, stride=pitch), :] = y
+
+        pairs(per, body)
 
     @pl.when(phase == 1)
     def _():
@@ -543,10 +586,12 @@
     def _():
         block = block_reader(place, pos_ref, one_all, j)
 
-        def body(k):
-            turned[column(k), :] = dot_tn(block(k), stacked(s_all, j * per + k))
-
-        each(per, body)
+        def body(ks):
+            out = dots_tn([block(k) for k in ks], [stacked(s_all, j * per + k) for k in ks])
+            for k, y in zip(ks, out):
+                turned[column(k), :] = y
+
+        pairs(per, body)
 
     @pl.when((phase == 1) & (j == 0))
     def _():
@@ -557,16 +602,19 @@
         block = block_reader(place, pos_ref, two_all, j)
 
         def with_out(grad_ref):
-            def body(k):
-                v = turned[rows(k), :].astype(BF16).astype(F32)
-                value, slope = gelu_both(v)
-                act = value.astype(BF16)
-                act_ref[k] = act
-                e = e_ref[k]
-                hidden[column(k), :] = slope * dot_nn(block(k), e)
-                grad_ref[0, k] = dot_nt(act, e).astype(BF16)
-
-            each(per, body, 8)
+            def body(ks):
+                acts, slopes, es = [], [], [e_ref[k] for k in ks]
+                for k in ks:
+                    value, slope = gelu_both(turned[rows(k), :].astype(BF16).astype(F32))
+                    acts.append(value.astype(BF16))
+                    slopes.append(slope)
+                    act_ref[k] = acts[-1]
+                for k, slope, y in zip(ks, slopes, dots_nn([block(k) for k in ks], es)):
+                    hidden[column(k), :] = slope * y
+                for k, y in zip(ks, dots_nt(acts, es)):
+                    grad_ref[0, k] = y.astype(BF16)
+
+            pairs(per, body, 4)
 
         either(place, pos_ref, j, keep_two, send_two, with_out)
 
@@ -575,13 +623,14 @@
         block = block_reader(place, pos_ref, one_all, j)
 
         def with_out(grad_ref):
-            def body(k):
-                b = j * per + k
-                h = hidden[rows(k), :].astype(BF16)
-                e_one[k] = dot_nn(block(k), h).astype(BF16)
-                grad_ref[0, k] = dot_nt(stacked(s_all, b), h).astype(BF16)
-
-            each(per, body)
+            def body(ks):
+                hs = [hidden[rows(k), :].astype(BF16) for k in ks]
+                for k, y in zip(ks, dots_nn([block(k) for k in ks], hs)):
+                    e_one[k] = y.astype(BF16)
+                for k, y in zip(ks, dots_nt([stacked(s_all, j * per + k) for k in ks], hs)):
+                    grad_ref[0, k] = y.astype(BF16)
+
+            pairs(per, body)
 
         either(place, pos_ref, j, keep_one, send_one, with_out)
         for n in range(share):
@@ -656,10 +705,11 @@
     def _():
         block = block_reader(place, pos_ref, left_all, j)
 
-        def body(k):
-            turned[column(k), :] = dot_tn(block(k), act_ref[k])
-
-        each(per, body)
+        def body(ks):
+            for k, y in zip(ks, dots_tn([block(k) for k in ks], [act_ref[k] for k in ks])):
+                turned[column(k), :] = y
+
+        pairs(per, body)
 
     @pl.when((phase == 1) & (j == 0))
     def _():
@@ -670,13 +720,14 @@
         block = block_reader(place, pos_ref, right_all, j)
 
         def with_out(grad_ref):
-            def body(k):
-                b = j * per + k
-                third = turned[rows(k), :].astype(BF16)
-                fourth[column(k), :] = dot_tn(block(k), third)
-                grad_ref[0, k] = dot_nt(third, stacked(g_all, b)).astype(BF16)
-
-            each(per, body)
+            def body(ks):
+                thirds = [turned[rows(k), :].astype(BF16) for k in ks]
+                for k, y in zip(ks, dots_tn([block(k) for k in ks], thirds)):
+                    fourth[column(k), :] = y
+                for k, y in zip(ks, dots_nt(thirds, [stacked(g_all, j * per + k) for k in ks])):
+                    grad_ref[0, k] = y.astype(BF16)
+
+            pairs(per, body)
 
         either(place, pos_ref, j, keep_ref, send_ref, with_out)
 
@@ -831,34 +882,24 @@
 
     s_three = cross(s, n_three)
     three.step(x_step)
+    one_part.step(far_step)
     two.step(near_step)
     input_grad, lone = last_stage(place, pos, e_got, x_home, g_home, one)
     lone = Sum([lone], [home] + place.dp[::-1], (rows, size))
-    one_part.prepare(x_step)
     lone.prepare(x_step)
     s_three, kept, input_grad, s = slot(place, (s_three, arrays_of(two, one_part, three, lone), input_grad, s))
     hold([two, one_part, three, lone], kept)
 
     s_two = cross(s, n_two)
     lone.step(x_step)
+    two.step(far_step)
     three.step(near_step)
-    two.step(far_step)
-    kept = slot(place, arrays_of(two, one_part, three, lone))
-    hold([two, one_part, three, lone], kept)
-
     one_part.step(x_step)
     lone.step(near_step)
     three.step(far_step)
     s_one = cross(s, n_one)
-    s_two, s_one, kept = slot(place, (s_two, s_one, arrays_of(two, one_part, three, lone)))
-    hold([two, one_part, three, lone], kept)
-
-    one_part.step(far_step)
-    lone.step(far_step)
     s_got = [s[0], s_one, s_two, s_three][:share]
-    grad_ltwo = two.finish()
-    grad_rone = one_part.finish()
-    grad_rtwo = three.finish()
+    grad_ltwo, grad_rone, grad_rtwo = finish_together([two, one_part, three], place.dp, place.y)
     grad_lone = lone.finish()
     mixed = add_home(place, pos, s_got, x_home)
     return mixed, input_grad, grad_lone, grad_rone, grad_ltwo, grad_rtwo

time: 326 us -> 320 us (0.982)
  waiting for transfers between devices: 135 us -> 129 us
    ppermute x50 -> x48, waiting for transfers between devices: 135 us -> 129 us  [send(): self.last = lax.ppermute(value, self.axis, pairs)]
    add x4 -> x3, other arithmetic: 7.54 us -> 5.9 us  [total(): return functools.reduce(jnp.add, [t.astype(F32) for t in terms])]
    ppermute x50 -> x48, starting transfers between devices: 47.7 us -> 49.1 us  [send(): self.last = lax.ppermute(value, self.axis, pairs)]
  transfers between devices with their start and end apart: 50 -> 48, of which waited for: 27 -> 25; matrix products, arithmetic and copies ran while one was open for 10% -> 10% of each run, Pallas kernels for 21% -> 22%
where the time goes in v8:
time: 320 us; the launch traced here: 319 us
  waiting for transfers between devices  129 us (40%)
  Pallas kernels  97.9 us (31%)
  starting transfers between devices  49.1 us (15%)
  other arithmetic  34.9 us (11%)
  local copies, waits for them, and re-layouts  6.53 us (2%)
    ppermute x48, waiting for transfers between devices, send(): self.last = lax.ppermute(value, self.axis, pairs)  129 us
    pallas_call x10, Pallas kernels, call(): pl.pallas_call(body, out_shape=out, grid_spec=spec, compiler_params=pltpu...  97.9 us
    ppermute x48, starting transfers between devices, send(): self.last = lax.ppermute(value, self.axis, pairs)  49.1 us
    convert_element_type x14, other arithmetic, parts(): self.cut(ring, lax.rem(ring.here() + step, ring.size)).astype(BF16)  23.4 us
  transfers between devices with their start and end apart: 48, of which 25 were waited for; matrix products, arithmetic and copies ran while one was open for 10% of the time, Pallas kernels for 22%

profile of v8, /device:TPU:0, one launch (start us, length us, event | category | flops | bytes accessed | tf_op | source)
XLA Modules:
  0.0 318.5 jit_solution(11656936224193217894)
XLA Ops:
  6.9 3.3 %shard_map.109 = bf16[128,32,128]{2,1,0:T(8,128)(2,1)} custom-call(s32[5]{0:T(128)} %stack.122.pos_ref, bf16[32,128,512]{2,1,0:T(8,128)(2,1)} %bitcast.194), custom_call_target="tpu_custom_call" | custom-call | bytes 4200000 | tf_op jit(solution)/shard_map/pallas_call | solution.py:84
  12.6 4.1 %collective-permute-start.2 = (bf16[2,32,16,128]{3,2,1,0:T(8,128)(2,1)S(1)}, bf16[2,32,16,128]{3,2,1,0:T(8,128)(2,1)S(1)}, u32[]{:S(2)}, u32[]{:S(2)}) collective-permute-start(bf16[2,32,16,128]{3,2,1,0:T(8,128)(2,1)S(1)} %get-tuple-element.259), channel_id=1, source_target_pairs={{0,8},{4,12},{8,0},{12,4},{16,24},{20,28},{24,16},{28,20},{1,9},{5... | collective-permute-start | bytes 786440 | tf_op jit(solution)/shard_map/ppermute | solution.py:138
  16.7 9.6 %collective-permute-done.5 = bf16[2,32,16,128]{3,2,1,0:T(8,128)(2,1)S(1)} collective-permute-done((bf16[2,32,16,128]{3,2,1,0:T(8,128)(2,1)S(1)}, bf16[2,32,16,128]{3,2,1,0:T(8,128)(2,1)S(1)}, u32[]{:S(2)}, u32[]{:S(2)}) %collective-permute-start.5) | collective-permute-done | bytes 262176 | tf_op jit(solution)/shard_map/ppermute | solution.py:138
  30.5 3.1 shard_map.110.refs_0_
  33.6 3.1 shard_map.111
  51.1 8.9 %collective-permute-done.10 = bf16[2,32,16,128]{3,2,1,0:T(8,128)(2,1)S(1)} collective-permute-done((bf16[2,32,16,128]{3,2,1,0:T(8,128)(2,1)S(1)}, bf16[2,32,16,128]{3,2,1,0:T(8,128)(2,1)S(1)}, u32[]{:S(2)}, u32[]{:S(2)}) %collective-permute-start.10) | collective-permute-done | bytes 262176 | tf_op jit(solution)/shard_map/ppermute | solution.py:138
  61.8 3.4 %collective-permute-start.12 = (bf16[2,32,16,128]{3,2,1,0:T(8,128)(2,1)}, bf16[2,32,16,128]{3,2,1,0:T(8,128)(2,1)}, u32[]{:S(2)}, u32[]{:S(2)}) collective-permute-start(bf16[2,32,16,128]{3,2,1,0:T(8,128)(2,1)} %get-tuple-element.135), channel_id=1, source_target_pairs={{0,16},{4,20},{8,24},{12,28},{16,0},{20,4},{24,8},{28,12},{1,17},{... | collective-permute-start | bytes 786440 | tf_op jit(solution)/shard_map/ppermute | solution.py:138
  65.1 9.6 %shard_map.113 = (bf16[128,32,128]{2,1,0:T(8,128)(2,1)}, bf16[128,32,128]{2,1,0:T(8,128)(2,1)}, bf16[128,32,128]{2,1,0:T(8,128)(2,1)}, bf16[128,32,128]{2,1,0:T(8,128)(2,1)}) custom-call(s32[5]{0:T(128)} %stack.122.pos_ref, bf16[32,128,512]{2,1,0:T(8,128)(2,1)} %bitcast.199, bf16[2,2,32,16,128]{4,3,2,1,0:T(8,128)(2,1)} %copy-done.2, ...), custom_call_target="tpu_custom_call" | custom-call | bytes 9600000 | tf_op jit(solution)/shard_map/pallas_call | solution.py:84
  74.8 4.3 %collective-permute-done.12 = bf16[2,32,16,128]{3,2,1,0:T(8,128)(2,1)} collective-permute-done((bf16[2,32,16,128]{3,2,1,0:T(8,128)(2,1)}, bf16[2,32,16,128]{3,2,1,0:T(8,128)(2,1)}, u32[]{:S(2)}, u32[]{:S(2)}) %collective-permute-start.12) | collective-permute-done | bytes 262176 | tf_op jit(solution)/shard_map/ppermute | solution.py:138
  82.9 3.5 %collective-permute-start.16 = (bf16[2,2,32,16,128]{4,3,2,1,0:T(8,128)(2,1)S(1)}, bf16[2,2,32,16,128]{4,3,2,1,0:T(8,128)(2,1)S(1)}, u32[]{:S(2)}, u32[]{:S(2)}) collective-permute-start(bf16[2,2,32,16,128]{4,3,2,1,0:T(8,128)(2,1)S(1)} %pad_maximum_fusion.7), channel_id=1, source_target_pairs={{0,8},{4,12},{8,0},{12,4},{16,24},{20,28},{24,16},{28,20},{1,9},{5... | collective-permute-start | bytes 1572872 | tf_op jit(solution)/shard_map/ppermute | solution.py:138
  89.5 8.5 %collective-permute-done.16 = bf16[2,2,32,16,128]{4,3,2,1,0:T(8,128)(2,1)S(1)} collective-permute-done((bf16[2,2,32,16,128]{4,3,2,1,0:T(8,128)(2,1)S(1)}, bf16[2,2,32,16,128]{4,3,2,1,0:T(8,128)(2,1)S(1)}, u32[]{:S(2)}, u32[]{:S(2)}) %collective-permute-start.16) | collective-permute-done | bytes 524320 | tf_op jit(solution)/shard_map/ppermute | solution.py:138
  98.2 13.7 %collective-permute-done.13.refs_3_ = bf16[128,32,128]{2,1,0:T(8,128)(2,1)S(1)} collective-permute-done((bf16[128,32,128]{2,1,0:T(8,128)(2,1)S(1)}, bf16[128,32,128]{2,1,0:T(8,128)(2,1)S(1)}, u32[]{:S(2)}, u32[]{:S(2)}) %collective-permute-start.13) | collective-permute-done | bytes 1048608 | tf_op jit(solution)/shard_map/ppermute | solution.py:138
  116.5 9.5 %shard_map.114.refs_12_ = bf16[128,128,128]{2,1,0:T(8,128)(2,1)} custom-call(s32[5]{0:T(128)} %stack.122.pos_ref, bf16[128,32,128]{2,1,0:T(8,128)(2,1)} %shard_map.110.refs_0_, bf16[128,32,128]{2,1,0:T(8,128)(2,1)} %collective-permute-done.19.refs_1_, bf16[128,32,128]{2,1,0:T(8,128)(2,1)} %copy-done.4, bf16[128,32,128]{2,1,0:T(8,128)(2,1)} %copy-done.3, ...), custom_call_target="tpu_custom_call" | custom-call | bytes 12000000 | tf_op jit(solution)/shard_map/pallas_call | solution.py:84
  126.0 11.5 %collective-permute-done.20.refs_2_ = bf16[128,32,128]{2,1,0:T(8,128)(2,1)} collective-permute-done((bf16[128,32,128]{2,1,0:T(8,128)(2,1)}, bf16[128,32,128]{2,1,0:T(8,128)(2,1)}, u32[]{:S(2)}, u32[]{:S(2)}) %collective-permute-start.20) | collective-permute-done | bytes 1048608 | tf_op jit(solution)/shard_map/ppermute | solution.py:138
  142.6 28.0 %shard_map.115 = (bf16[128,128,128]{2,1,0:T(8,128)(2,1)}, bf16[2,32,128,128]{3,2,1,0:T(8,128)(2,1)}, bf16[2,32,128,128]{3,2,1,0:T(8,128)(2,1)}, bf16[2,32,128,12...) custom-call(s32[5]{0:T(128)} %stack.122.pos_ref, ...), custom_call_target="tpu_custom_call" | custom-call | bytes 31200000 | tf_op jit(solution)/shard_map/pallas_call | solution.py:84
  172.0 19.8 %shard_map.116 = (bf16[2,32,128,128]{3,2,1,0:T(8,128)(2,1)}, bf16[2,32,128,128]{3,2,1,0:T(8,128)(2,1)}, bf16[32,128,128]{2,1,0:T(8,128)(2,1)}, bf16[32,128,128]{...) custom-call(s32[5]{0:T(128)} %stack.122.pos_ref, ...), custom_call_target="tpu_custom_call" | custom-call | bytes 24000000 | tf_op jit(solution)/shard_map/pallas_call | solution.py:84
  203.9 18.6 %collective-permute-done.29.refs_2_ = bf16[128,32,128]{2,1,0:T(8,128)(2,1)} collective-permute-done((bf16[128,32,128]{2,1,0:T(8,128)(2,1)}, bf16[128,32,128]{2,1,0:T(8,128)(2,1)}, u32[]{:S(2)}, u32[]{:S(2)}) %collective-permute-start.29) | collective-permute-done | bytes 1048608 | tf_op jit(solution)/shard_map/ppermute | solution.py:138
  230.5 11.4 %shard_map.117 = (bf16[32,128,512]{2,1,0:T(8,128)(2,1)}, bf16[32,128,128]{2,1,0:T(8,128)(2,1)}) custom-call(s32[5]{0:T(128)} %stack.122.pos_ref, bf16[128,32,128]{2,1,0:T(8,128)(2,1)} %get-tuple-element.214.refs_0_, bf16[128,32,128]{2,1,0:T(8,128)(2,1)} %collective-permute-done.30.refs_1_, bf16[128,32,128]{2,1,0:T(8,128)(2,1)} %collective-permute-done.29.refs_2_, ...), custom_call_target="tpu_custom_call" | custom-call | bytes 12000000 | tf_op jit(solution)/shard_map/pallas_call | solution.py:84
  243.8 9.7 %collective-permute-done.36 = bf16[2,32,2,16,128]{4,3,1,2,0:T(8,128)(2,1)} collective-permute-done((bf16[2,32,2,16,128]{4,3,1,2,0:T(8,128)(2,1)S(1)}, bf16[2,32,2,16,128]{4,3,1,2,0:T(8,128)(2,1)}, u32[]{:S(2)}, u32[]{:S(2)}) %collective-permute-start.36) | collective-permute-done | bytes 524320 | tf_op jit(solution)/shard_map/ppermute | solution.py:138
  264.9 11.5 %collective-permute-done.43 = bf16[2,32,16,128]{3,2,1,0:T(8,128)(2,1)} collective-permute-done((bf16[2,32,16,128]{3,2,1,0:T(8,128)(2,1)S(1)}, bf16[2,32,16,128]{3,2,1,0:T(8,128)(2,1)}, u32[]{:S(2)}, u32[]{:S(2)}) %collective-permute-start.43) | collective-permute-done | bytes 262176 | tf_op jit(solution)/shard_map/ppermute | solution.py:138
  280.0 3.3 %collective-permute-start.44 = (bf16[2,32,16,128]{3,2,1,0:T(8,128)(2,1)S(1)}, bf16[2,32,16,128]{3,2,1,0:T(8,128)(2,1)S(1)}, u32[]{:S(2)}, u32[]{:S(2)}) collective-permute-start(bf16[2,32,16,128]{3,2,1,0:T(8,128)(2,1)S(1)} %fusion.8), channel_id=1, source_target_pairs={{0,16},{4,20},{8,24},{12,28},{16,0},{20,4},{24,8},{28,12},{1,17},{... | collective-permute-start | bytes 786440 | tf_op jit(solution)/shard_map/ppermute | solution.py:138
  285.8 8.2 %collective-permute-done.44 = bf16[2,32,16,128]{3,2,1,0:T(8,128)(2,1)S(1)} collective-permute-done((bf16[2,32,16,128]{3,2,1,0:T(8,128)(2,1)S(1)}, bf16[2,32,16,128]{3,2,1,0:T(8,128)(2,1)S(1)}, u32[]{:S(2)}, u32[]{:S(2)}) %collective-permute-start.44) | collective-permute-done | bytes 262176 | tf_op jit(solution)/shard_map/ppermute | solution.py:138
  299.0 6.7 %collective-permute-done.45 = bf16[32,16,128]{2,1,0:T(8,128)(2,1)S(1)} collective-permute-done((bf16[32,16,128]{2,1,0:T(8,128)(2,1)}, bf16[32,16,128]{2,1,0:T(8,128)(2,1)S(1)}, u32[]{:S(2)}, u32[]{:S(2)}) %collective-permute-start.45) | collective-permute-done | bytes 131104 | tf_op jit(solution)/shard_map/ppermute | solution.py:138
  307.4 6.9 %shard_map.118 = bf16[32,128,512]{2,1,0:T(8,128)(2,1)} custom-call(s32[5]{0:T(128)} %stack.122.pos_ref, bf16[32,128,128]{2,1,0:T(8,128)(2,1)} %get-tuple-element.225.refs_0_, bf16[32,128,128]{2,1,0:T(8,128)(2,1)} %collective-permute-done.38.refs_1_, bf16[32,128,128]{2,1,0:T(8,128)(2,1)} %collective-permute-done.39.refs_2_, bf16[32,128,128]{2,1,0:T(8,128)(2,1)} %copy-done.12, ...), custom_call_target="tpu_custom_call" | custom-call | bytes 7200000 | tf_op jit(solution)/shard_map/pallas_call | solution.py:84
  (160 shorter events, 97.2 us)
Async XLA Ops:
  12.5 30.8 %collective-permute-start = (bf16[128,32,128]{2,1,0:T(8,128)(2,1)}, bf16[128,32,128]{2,1,0:T(8,128)(2,1)S(1)}, u32[]{:S(2)}, u32[]{:S(2)}) collective-permute-start(bf16[128,32,128]{2,1,0:T(8,128)(2,1)} %shard_map.109), channel_id=1, source_target_pairs={{0,3},{1,2},{2,1},{3,0},{4,7},{5,6},{6,5},{7,4},{8,11},{9,10},{10,... | collective-permute-start | bytes 3145736 | tf_op jit(solution)/shard_map/ppermute | solution.py:138
  47.1 35.8 %collective-permute-start.8 = (bf16[128,32,128]{2,1,0:T(8,128)(2,1)}, bf16[128,32,128]{2,1,0:T(8,128)(2,1)S(1)}, u32[]{:S(2)}, u32[]{:S(2)}) collective-permute-start(bf16[128,32,128]{2,1,0:T(8,128)(2,1)} %shard_map.112), channel_id=1, source_target_pairs={{0,2},{1,3},{2,0},{3,1},{4,6},{5,7},{6,4},{7,5},{8,10},{9,11},{10,... | collective-permute-start | bytes 3145736 | tf_op jit(solution)/shard_map/ppermute | solution.py:138
  49.5 33.4 %collective-permute-start.9 = (bf16[2,2,2,32,16,128]{5,4,3,2,1,0:T(8,128)(2,1)S(1)}, bf16[2,2,2,32,16,128]{5,4,3,2,1,0:T(8,128)(2,1)}, u32[]{:S(2)}, u32[]{:S(2)}) collective-permute-start(bf16[2,2,2,32,16,128]{5,4,3,2,1,0:T(8,128)(2,1)S(1)} %pad_maximum_fusion.refs_4_.refs_8_), channel_id=1, source_target_pairs={{0,4},{4,0},{8,12},{12,8},{16,20},{20,16},{24,28},{28,24},{1,5},{5... | collective-permute-start | bytes 3145736 | tf_op jit(solution)/shard_map/ppermute | solution.py:138
  65.1 24.4 %collective-permute-start.19 = (bf16[128,32,128]{2,1,0:T(8,128)(2,1)}, bf16[128,32,128]{2,1,0:T(8,128)(2,1)}, u32[]{:S(2)}, u32[]{:S(2)}) collective-permute-start(bf16[128,32,128]{2,1,0:T(8,128)(2,1)} %shard_map.111), channel_id=1, source_target_pairs={{0,1},{1,0},{2,3},{3,2},{4,5},{5,4},{6,7},{7,6},{8,9},{9,8},{10,11... | collective-permute-start | bytes 3145736 | tf_op jit(solution)/shard_map/ppermute | solution.py:138
  86.5 25.4 %collective-permute-start.13 = (bf16[128,32,128]{2,1,0:T(8,128)(2,1)S(1)}, bf16[128,32,128]{2,1,0:T(8,128)(2,1)S(1)}, u32[]{:S(2)}, u32[]{:S(2)}) collective-permute-start(bf16[128,32,128]{2,1,0:T(8,128)(2,1)S(1)} %copy-done.22), channel_id=1, source_target_pairs={{0,3},{1,2},{2,1},{3,0},{4,7},{5,6},{6,5},{7,4},{8,11},{9,10},{10,... | collective-permute-start | bytes 3145736 | tf_op jit(solution)/shard_map/ppermute | solution.py:138
  86.8 26.0 %collective-permute-start.14 = (bf16[128,32,128]{2,1,0:T(8,128)(2,1)S(1)}, bf16[128,32,128]{2,1,0:T(8,128)(2,1)S(1)}, u32[]{:S(2)}, u32[]{:S(2)}) collective-permute-start(bf16[128,32,128]{2,1,0:T(8,128)(2,1)S(1)} %copy-done.21), channel_id=1, source_target_pairs={{0,1},{1,0},{2,3},{3,2},{4,5},{5,4},{6,7},{7,6},{8,9},{9,8},{10,11... | collective-permute-start | bytes 3145736 | tf_op jit(solution)/shard_map/ppermute | solution.py:138
  88.1 25.4 %collective-permute-start.15 = (bf16[2,2,2,32,16,128]{5,4,3,2,1,0:T(8,128)(2,1)}, bf16[2,2,2,32,16,128]{5,4,3,2,1,0:T(8,128)(2,1)}, u32[]{:S(2)}, u32[]{:S(2)}) collective-permute-start(bf16[2,2,2,32,16,128]{5,4,3,2,1,0:T(8,128)(2,1)} %pad_maximum_fusion.1.refs_4_), channel_id=1, source_target_pairs={{0,4},{4,0},{8,12},{12,8},{16,20},{20,16},{24,28},{28,24},{1,5},{5... | collective-permute-start | bytes 3145736 | tf_op jit(solution)/shard_map/ppermute | solution.py:138
  89.5 23.9 %collective-permute-start.17 = (bf16[2,2,2,32,16,128]{5,4,3,2,1,0:T(8,128)(2,1)S(1)}, bf16[2,2,2,32,16,128]{5,4,3,2,1,0:T(8,128)(2,1)S(1)}, u32[]{:S(2)}, u32[]{:S(2)}) collective-permute-start(bf16[2,2,2,32,16,128]{5,4,3,2,1,0:T(8,128)(2,1)S(1)} %pad_maximum_fusion.refs_4_.refs_8_), channel_id=1, source_target_pairs={{0,1},{1,0},{2,3},{3,2},{4,5},{5,4},{6,7},{7,6},{8,9},{9,8},{10,11... | collective-permute-start | bytes 3145736 | tf_op jit(solution)/shard_map/ppermute | solution.py:138
  111.9 25.6 %collective-permute-start.20 = (bf16[128,32,128]{2,1,0:T(8,128)(2,1)}, bf16[128,32,128]{2,1,0:T(8,128)(2,1)}, u32[]{:S(2)}, u32[]{:S(2)}) collective-permute-start(bf16[128,32,128]{2,1,0:T(8,128)(2,1)} %get-tuple-element.153), channel_id=1, source_target_pairs={{0,2},{1,3},{2,0},{3,1},{4,6},{5,7},{6,4},{7,5},{8,10},{9,11},{10,... | collective-permute-start | bytes 3145736 | tf_op jit(solution)/shard_map/ppermute | solution.py:138
  114.4 24.5 %collective-permute-start.21 = (bf16[2,2,2,32,16,128]{5,4,3,2,1,0:T(8,128)(2,1)S(1)}, bf16[2,2,2,32,16,128]{5,4,3,2,1,0:T(8,128)(2,1)S(1)}, u32[]{:S(2)}, u32[]{:S(2)}) collective-permute-start(bf16[2,2,2,32,16,128]{5,4,3,2,1,0:T(8,128)(2,1)S(1)} %pad_maximum_fusion.2.refs_8_.refs_4_), channel_id=1, source_target_pairs={{0,4},{4,0},{8,12},{12,8},{16,20},{20,16},{24,28},{28,24},{1,5},{5... | collective-permute-start | bytes 3145736 | tf_op jit(solution)/shard_map/ppermute | solution.py:138
  115.9 23.0 %collective-permute-start.22 = (bf16[2,2,2,32,16,128]{5,4,3,2,1,0:T(8,128)(2,1)S(1)}, bf16[2,2,2,32,16,128]{5,4,3,2,1,0:T(8,128)(2,1)}, u32[]{:S(2)}, u32[]{:S(2)}) collective-permute-start(bf16[2,2,2,32,16,128]{5,4,3,2,1,0:T(8,128)(2,1)S(1)} %pad_maximum_fusion.2.refs_8_.refs_4_), channel_id=1, source_target_pairs={{0,1},{1,0},{2,3},{3,2},{4,5},{5,4},{6,7},{7,6},{8,9},{9,8},{10,11... | collective-permute-start | bytes 3145736 | tf_op jit(solution)/shard_map/ppermute | solution.py:138
  115.9 23.0 %collective-permute-start.23 = (bf16[2,2,2,32,16,128]{5,4,3,2,1,0:T(8,128)(2,1)}, bf16[2,2,2,32,16,128]{5,4,3,2,1,0:T(8,128)(2,1)}, u32[]{:S(2)}, u32[]{:S(2)}) collective-permute-start(bf16[2,2,2,32,16,128]{5,4,3,2,1,0:T(8,128)(2,1)} %pad_maximum_fusion.1.refs_4_), channel_id=1, source_target_pairs={{0,1},{1,0},{2,3},{3,2},{4,5},{5,4},{6,7},{7,6},{8,9},{9,8},{10,11... | collective-permute-start | bytes 3145736 | tf_op jit(solution)/shard_map/ppermute | solution.py:138
  170.8 22.7 %collective-permute-start.27 = (bf16[2,32,128,128]{3,2,1,0:T(8,128)(2,1)}, bf16[2,32,128,128]{3,2,1,0:T(8,128)(2,1)}, u32[]{:S(2)}, u32[]{:S(2)}) collective-permute-start(bf16[2,32,128,128]{3,2,1,0:T(8,128)(2,1)} %get-tuple-element.177), channel_id=1, source_target_pairs={{0,1},{1,0},{2,3},{3,2},{4,5},{5,4},{6,7},{7,6},{8,9},{9,8},{10,11... | collective-permute-start | bytes 6291464 | tf_op jit(solution)/shard_map/ppermute | solution.py:138
  171.2 25.5 %collective-permute-start.26 = (bf16[128,32,128]{2,1,0:T(8,128)(2,1)}, bf16[128,32,128]{2,1,0:T(8,128)(2,1)}, u32[]{:S(2)}, u32[]{:S(2)}) collective-permute-start(bf16[128,32,128]{2,1,0:T(8,128)(2,1)} %get-tuple-element.175), channel_id=1, source_target_pairs={{0,3},{1,2},{2,1},{3,0},{4,7},{5,6},{6,5},{7,4},{8,11},{9,10},{10,... | collective-permute-start | bytes 3145736 | tf_op jit(solution)/shard_map/ppermute | solution.py:138
  196.8 25.8 %collective-permute-start.29 = (bf16[128,32,128]{2,1,0:T(8,128)(2,1)}, bf16[128,32,128]{2,1,0:T(8,128)(2,1)}, u32[]{:S(2)}, u32[]{:S(2)}) collective-permute-start(bf16[128,32,128]{2,1,0:T(8,128)(2,1)} %get-tuple-element.190), channel_id=1, source_target_pairs={{0,2},{1,3},{2,0},{3,1},{4,6},{5,7},{6,4},{7,5},{8,10},{9,11},{10,... | collective-permute-start | bytes 3145736 | tf_op jit(solution)/shard_map/ppermute | solution.py:138
  197.9 24.6 %collective-permute-start.30 = (bf16[128,32,128]{2,1,0:T(8,128)(2,1)}, bf16[128,32,128]{2,1,0:T(8,128)(2,1)}, u32[]{:S(2)}, u32[]{:S(2)}) collective-permute-start(bf16[128,32,128]{2,1,0:T(8,128)(2,1)} %get-tuple-element.191), channel_id=1, source_target_pairs={{0,1},{1,0},{2,3},{3,2},{4,5},{5,4},{6,7},{7,6},{8,9},{9,8},{10,11... | collective-permute-start | bytes 3145736 | tf_op jit(solution)/shard_map/ppermute | solution.py:138
  198.0 25.8 %collective-permute-start.31 = (bf16[2,32,2,2,16,128]{5,4,1,3,2,0:T(8,128)(2,1)}, bf16[2,32,2,2,16,128]{5,4,1,3,2,0:T(8,128)(2,1)}, u32[]{:S(2)}, u32[]{:S(2)}) collective-permute-start(bf16[2,32,2,2,16,128]{5,4,1,3,2,0:T(8,128)(2,1)} %fusion), channel_id=1, source_target_pairs={{0,4},{4,0},{8,12},{12,8},{16,20},{20,16},{24,28},{28,24},{1,5},{5... | collective-permute-start | bytes 3145736 | tf_op jit(solution)/shard_map/ppermute | solution.py:138
  199.3 25.3 %collective-permute-start.32 = (bf16[2,32,2,2,16,128]{5,4,1,3,2,0:T(8,128)(2,1)S(1)}, bf16[2,32,2,2,16,128]{5,4,1,3,2,0:T(8,128)(2,1)}, u32[]{:S(2)}, u32[]{:S(2)}) collective-permute-start(bf16[2,32,2,2,16,128]{5,4,1,3,2,0:T(8,128)(2,1)S(1)} %fusion.1), channel_id=1, source_target_pairs={{0,8},{4,12},{8,0},{12,4},{16,24},{20,28},{24,16},{28,20},{1,9},{5... | collective-permute-start | bytes 3145736 | tf_op jit(solution)/shard_map/ppermute | solution.py:138
  224.7 31.0 %collective-permute-start.34 = (bf16[32,128,128]{2,1,0:T(8,128)(2,1)}, bf16[32,128,128]{2,1,0:T(8,128)(2,1)S(1)}, u32[]{:S(2)}, u32[]{:S(2)}) collective-permute-start(bf16[32,128,128]{2,1,0:T(8,128)(2,1)} %get-tuple-element.204), channel_id=1, source_target_pairs={{0,3},{1,2},{2,1},{3,0},{4,7},{5,6},{6,5},{7,4},{8,11},{9,10},{10,... | collective-permute-start | bytes 3145736 | tf_op jit(solution)/shard_map/ppermute | solution.py:138
  224.7 31.0 %collective-permute-start.37 = (bf16[2,32,2,2,16,128]{5,4,1,3,2,0:T(8,128)(2,1)}, bf16[2,32,2,2,16,128]{5,4,1,3,2,0:T(8,128)(2,1)}, u32[]{:S(2)}, u32[]{:S(2)}) collective-permute-start(bf16[2,32,2,2,16,128]{5,4,1,3,2,0:T(8,128)(2,1)} %fusion.2), channel_id=1, source_target_pairs={{0,4},{4,0},{8,12},{12,8},{16,20},{20,16},{24,28},{28,24},{1,5},{5... | collective-permute-start | bytes 3145736 | tf_op jit(solution)/shard_map/ppermute | solution.py:138
  226.8 26.7 %collective-permute-start.36 = (bf16[2,32,2,16,128]{4,3,1,2,0:T(8,128)(2,1)S(1)}, bf16[2,32,2,16,128]{4,3,1,2,0:T(8,128)(2,1)}, u32[]{:S(2)}, u32[]{:S(2)}) collective-permute-start(bf16[2,32,2,16,128]{4,3,1,2,0:T(8,128)(2,1)S(1)} %fusion.4), channel_id=1, source_target_pairs={{0,16},{4,20},{8,24},{12,28},{16,0},{20,4},{24,8},{28,12},{1,17},{... | collective-permute-start | bytes 1572872 | tf_op jit(solution)/shard_map/ppermute | solution.py:138
  229.9 25.8 %collective-permute-start.35 = (bf16[2,32,2,16,128]{4,3,1,2,0:T(8,128)(2,1)}, bf16[2,32,2,16,128]{4,3,1,2,0:T(8,128)(2,1)}, u32[]{:S(2)}, u32[]{:S(2)}) collective-permute-start(bf16[2,32,2,16,128]{4,3,1,2,0:T(8,128)(2,1)} %fusion.5), channel_id=1, source_target_pairs={{0,8},{4,12},{8,0},{12,4},{16,24},{20,28},{24,16},{28,20},{1,9},{5... | collective-permute-start | bytes 1572872 | tf_op jit(solution)/shard_map/ppermute | solution.py:138
  262.5 33.4 %collective-permute-start.39 = (bf16[32,128,128]{2,1,0:T(8,128)(2,1)}, bf16[32,128,128]{2,1,0:T(8,128)(2,1)}, u32[]{:S(2)}, u32[]{:S(2)}) collective-permute-start(bf16[32,128,128]{2,1,0:T(8,128)(2,1)} %get-tuple-element.227), channel_id=1, source_target_pairs={{0,2},{1,3},{2,0},{3,1},{4,6},{5,7},{6,4},{7,5},{8,10},{9,11},{10,... | collective-permute-start | bytes 3145736 | tf_op jit(solution)/shard_map/ppermute | solution.py:138
  263.6 43.8 %collective-permute-start.38 = (bf16[32,128,128]{2,1,0:T(8,128)(2,1)}, bf16[32,128,128]{2,1,0:T(8,128)(2,1)}, u32[]{:S(2)}, u32[]{:S(2)}) collective-permute-start(bf16[32,128,128]{2,1,0:T(8,128)(2,1)} %get-tuple-element.226), channel_id=1, source_target_pairs={{0,1},{1,0},{2,3},{3,2},{4,5},{5,4},{6,7},{7,6},{8,9},{9,8},{10,11... | collective-permute-start | bytes 3145736 | tf_op jit(solution)/shard_map/ppermute | solution.py:138
  (47 other events, 620.7 us)

commit v9 on v8

--- a/solution.py
+++ b/solution.py
@@ -12,7 +12,7 @@
 BF16 = jnp.bfloat16
 F32 = jnp.float32
 LANES = 128
-PAD = 1
+TILE = 16
 VMEM_BYTES = 60 * 1024 * 1024
 BYTES_PER_US = 1_200_000
 
@@ -95,6 +95,12 @@
 def pairs(count, body, unroll=8):
     group = 2 if count % 2 == 0 else 1
     each(count // group, lambda n: body([n * group + i for i in range(group)]), unroll)
+
+
+def turn(source, out_ref, at):
+    n, size, _ = source.shape
+    for i in range(0, size, TILE):
+        out_ref[i : i + TILE, pl.ds(pl.multiple_of(at, TILE), n), :] = jnp.swapaxes(source[:, i : i + TILE, :], 0, 1)
 
 
 def shape(dims, dtype=BF16):
@@ -324,18 +330,9 @@
     return [refs[c * wide : (c + 1) * wide] for c in range(place.near)]
 
 
-def deal_kernel(pos_ref, g_ref, out_ref, turned):
-    home, size, _ = g_ref.shape
-    pitch = home + PAD
-
-    def store(o):
-        turned[pl.ds(o, size, stride=pitch), :] = g_ref[o].astype(F32)
-
-    def load(b):
-        out_ref[b] = turned[pl.ds(b * pitch, home), :].astype(BF16)
-
-    each(home, store)
-    each(size, load)
+def deal_kernel(pos_ref, g_ref, out_ref):
+    for o in range(0, g_ref.shape[0], TILE):
+        turn(g_ref.at[o : o + TILE], out_ref, o)
 
 
 def deal(place, pos, g_home, cut, n):
@@ -346,7 +343,7 @@
         (1,),
         [pl.BlockSpec((home, size, cut), lambda i, pos: (0, 0, place.onward(pos, n)))],
         pl.BlockSpec((size, home, cut), lambda i, pos: (0, 0, 0)),
-        [pltpu.VMEM((size * (home + PAD), cut), F32)],
+        [],
         (g_home,),
         us=3.5,
         scalars=pos,
@@ -356,10 +353,9 @@
 def first_kernel(place, pos_ref, x_ref, *refs):
     share = place.far * place.near
     pieces, out_refs = refs[: -share - 3], refs[-share - 3 : -3]
-    turned, whole, sems = refs[-3:]
-    home, size, _ = x_ref.shape
+    stage, whole, sems = refs[-3:]
+    home = x_ref.shape[0]
     cut = out_refs[0].shape[2]
-    pitch = home + PAD
     copies = piece_copies([pieces], whole, sems)
     block = block_reader(place, pos_ref, whole, None)
 
@@ -374,16 +370,15 @@
         def _():
             lanes = pl.ds(pl.multiple_of(place.onward(pos_ref, n) * cut, cut), cut)
 
-            def store(bs):
-                out = dots_tn([block(b) for b in bs], [x_ref[b, :, lanes] for b in bs])
-                for b, y in zip(bs, out):
-                    turned[pl.ds(b, size, stride=pitch), :] = y
-
-            def load(o):
-                out_ref[o] = turned[pl.ds(o * pitch, home), :].astype(BF16)
-
-            pairs(home, store)
-            each(size, load)
+            for b in range(0, home, TILE):
+
+                def store(ks):
+                    out = dots_tn([block(b + k) for k in ks], [x_ref[b + k, :, lanes] for k in ks])
+                    for k, y in zip(ks, out):
+                        stage[b + k] = y.astype(BF16)
+
+                pairs(TILE, store)
+                turn(stage.at[b : b + TILE], out_ref, b)
 
 
 def first_stage(place, pos, x_home, left_one, cut):
@@ -395,7 +390,7 @@
         (share,),
         [pl.BlockSpec((home, size, tokens), lambda s, pos: (0, 0, 0))] + anywhere(len(left_one)),
         (pl.BlockSpec((size, home, cut), lambda s, pos: (0, 0, 0)),) * share,
-        [pltpu.VMEM((size * (home + PAD), cut), F32)] + whole_scratch([left_one]),
+        [pltpu.VMEM((home, size, cut), BF16)] + whole_scratch([left_one]),
         (x_home, *left_one),
         us=8,
         scalars=pos,
@@ -406,8 +401,7 @@
     share = place.far * place.near
     e_refs, x_ref, g_ref = refs[:share], refs[share], refs[share + 1]
     pieces, (out_ref, grad_ref, turned, whole, sems) = refs[share + 2 : -5], refs[-5:]
-    blocks, per, cut = e_refs[0].shape
-    pitch = blocks + PAD
+    blocks, per, _ = e_refs[0].shape
     copies = piece_copies([pieces], whole, sems)
     block = block_reader(place, pos_ref, whole, None)
     first = pl.program_id(0) * per
@@ -417,20 +411,16 @@
         run(copies)
 
     for n in range(share):
-        s = place.source(pos_ref, n)
-
-        def store(o):
-            turned[s, pl.ds(o, per, stride=pitch), :] = e_refs[n][o].astype(F32)
-
-        each(blocks, store)
+        into = turned.at[place.source(pos_ref, n)]
+        for o in range(0, blocks, TILE):
+            turn(e_refs[n].at[o : o + TILE], into, o)
 
     @pl.when(pl.program_id(0) == 0)
     def _():
         finish(copies)
 
     def load(b):
-        rows = pl.ds(b * pitch, blocks)
-        e_b = jnp.concatenate([turned[s, rows, :].astype(BF16) for s in range(share)], axis=1)
+        e_b = jnp.concatenate([turned[s, b] for s in range(share)], axis=1)
         out_ref[b] = (g_ref[b].astype(F32) + dot_nn(block(first + b), e_b)).astype(BF16)
         grad_ref[b] = dot_nt(x_ref[b], e_b).astype(BF16)
 
@@ -450,7 +440,7 @@
         (home // per,),
         [pl.BlockSpec((blocks, per, cut), lambda h, pos: (0, h, 0))] * share + [wide, wide] + anywhere(len(left_one)),
         (wide, factor),
-        [pltpu.VMEM((share, per * (blocks + PAD), cut), F32)] + whole_scratch([left_one]),
+        [pltpu.VMEM((share, per, blocks, cut), BF16)] + whole_scratch([left_one]),
         (*e_got, x_home, g_home, *left_one),
         us=10,
         scalars=pos,
@@ -484,10 +474,9 @@
 
 def back_two_kernel(place, pos_ref, *refs):
     share = place.far * place.near
-    g_parts, factor = refs[:share], unflat(place, refs[share:-6])
-    out_ref, turned, g_all, g_sems, w_all, w_sems = refs[-6:]
-    per, size, _ = out_ref.shape
-    pitch = size + PAD
+    g_parts, factor = refs[:share], unflat(place, refs[share:-7])
+    out_ref, turned, stage, g_all, g_sems, w_all, w_sems = refs[-7:]
+    per = out_ref.shape[0]
     phase, j = pl.program_id(0), pl.program_id(1)
 
     @pl.when((phase == 0) & (j == 0))
@@ -503,16 +492,22 @@
         def body(ks):
             out = dots_nn([block(k) for k in ks], [stacked(g_all, j * per + k) for k in ks])
             for k, y in zip(ks, out):
-                turned[pl.ds(j * per + k, size, stride=pitch), :] = y
-
-        pairs(per, body)
+                stage[k] = y.astype(BF16)
+
+        staged(per, body, stage, turned, j)
 
     @pl.when(phase == 1)
     def _():
         def body(k):
-            out_ref[k] = turned[pl.ds((j * per + k) * pitch, size), :].astype(BF16)
+            out_ref[k] = turned[j * per + k]
 
         each(per, body)
+
+
+def staged(per, body, stage, turned, j):
+    for k in range(0, per, TILE):
+        pairs(TILE, lambda ks: body([k + i for i in ks]))
+        turn(stage.at[k : k + TILE], turned, j * per + k)
 
 
 def middle_sizes(place, parts):
@@ -530,7 +525,8 @@
         anywhere(share + len(flat(right_two))),
         pl.BlockSpec((home, blocks, cut), lambda p, j, pos: (at(p, j), 0, 0)),
         [
-            pltpu.VMEM((blocks * (blocks + PAD), cut), F32),
+            pltpu.VMEM((blocks, blocks, cut), BF16),
+            pltpu.VMEM((home, blocks, cut), BF16),
             pltpu.VMEM((share, blocks, home, cut), BF16),
             pltpu.SemaphoreType.DMA((share,)),
         ]
@@ -561,16 +557,8 @@
     e_ref, act_ref, keep_two, send_two, keep_one, send_one, *rest = rest
     out_refs, rest = rest[:share], rest[share:]
     turned, hidden, e_one, s_all, s_sems, one_all, one_sems, two_all, two_sems = rest
-    per, size, cut = act_ref.shape
-    home = s_all.shape[2]
-    pitch = size + PAD
+    per, home = act_ref.shape[0], s_all.shape[2]
     phase, j = pl.program_id(0), pl.program_id(1)
-
-    def rows(k):
-        return pl.ds((j * per + k) * pitch, size)
-
-    def column(k):
-        return pl.ds(j * per + k, size, stride=pitch)
 
     def second():
         return piece_copies(two, two_all, two_sems)
@@ -589,9 +577,9 @@
         def body(ks):
             out = dots_tn([block(k) for k in ks], [stacked(s_all, j * per + k) for k in ks])
             for k, y in zip(ks, out):
-                turned[column(k), :] = y
-
-        pairs(per, body)
+                e_one[k] = y.astype(BF16)
+
+        staged(per, body, e_one, turned, j)
 
     @pl.when((phase == 1) & (j == 0))
     def _():
@@ -605,16 +593,16 @@
             def body(ks):
                 acts, slopes, es = [], [], [e_ref[k] for k in ks]
                 for k in ks:
-                    value, slope = gelu_both(turned[rows(k), :].astype(BF16).astype(F32))
+                    value, slope = gelu_both(turned[j * per + k].astype(F32))
                     acts.append(value.astype(BF16))
                     slopes.append(slope)
                     act_ref[k] = acts[-1]
                 for k, slope, y in zip(ks, slopes, dots_nn([block(k) for k in ks], es)):
-                    hidden[column(k), :] = slope * y
+                    e_one[k] = (slope * y).astype(BF16)
                 for k, y in zip(ks, dots_nt(acts, es)):
                     grad_ref[0, k] = y.astype(BF16)
 
-            pairs(per, body, 4)
+            staged(per, body, e_one, hidden, j)
 
         either(place, pos_ref, j, keep_two, send_two, with_out)
 
@@ -624,7 +612,7 @@
 
         def with_out(grad_ref):
             def body(ks):
-                hs = [hidden[rows(k), :].astype(BF16) for k in ks]
+                hs = [hidden[j * per + k] for k in ks]
                 for k, y in zip(ks, dots_nn([block(k) for k in ks], hs)):
                     e_one[k] = y.astype(BF16)
                 for k, y in zip(ks, dots_nt([stacked(s_all, j * per + k) for k in ks], hs)):
@@ -658,7 +646,7 @@
         (3, share),
         anywhere(share + 2 * len(flat(right_one))) + [block],
         (block, *two_specs, *one_specs) + (piece,) * share,
-        [pltpu.VMEM((blocks * (blocks + PAD), cut), F32)] * 2
+        [pltpu.VMEM((blocks, blocks, cut), BF16)] * 2
         + [
             pltpu.VMEM((home, blocks, cut), BF16),
             pltpu.VMEM((share, blocks, home, cut), BF16),
@@ -675,21 +663,14 @@
 
 def forward_two_kernel(place, pos_ref, *refs):
     share = place.far * place.near
-    wide = (len(refs) - (2 * share + 11)) // 2
+    wide = (len(refs) - (2 * share + 12)) // 2
     g_parts, rest = refs[:share], refs[share:]
     left, right, rest = unflat(place, rest[:wide]), unflat(place, rest[wide : 2 * wide]), rest[2 * wide :]
     act_ref, keep_ref, send_ref, *rest = rest
     out_refs, rest = rest[:share], rest[share:]
-    turned, fourth, g_all, g_sems, left_all, left_sems, right_all, right_sems = rest
-    per, size, _ = act_ref.shape
-    pitch = size + PAD
+    turned, fourth, stage, g_all, g_sems, left_all, left_sems, right_all, right_sems = rest
+    per = act_ref.shape[0]
     phase, j = pl.program_id(0), pl.program_id(1)
-
-    def rows(k):
-        return pl.ds((j * per + k) * pitch, size)
-
-    def column(k):
-        return pl.ds(j * per + k, size, stride=pitch)
 
     def second():
         return piece_copies(right, right_all, right_sems) + share_copies(place, pos_ref, g_parts, g_all, g_sems)
@@ -707,9 +688,9 @@
 
         def body(ks):
             for k, y in zip(ks, dots_tn([block(k) for k in ks], [act_ref[k] for k in ks])):
-                turned[column(k), :] = y
-
-        pairs(per, body)
+                stage[k] = y.astype(BF16)
+
+        staged(per, body, stage, turned, j)
 
     @pl.when((phase == 1) & (j == 0))
     def _():
@@ -721,13 +702,13 @@
 
         def with_out(grad_ref):
             def body(ks):
-                thirds = [turned[rows(k), :].astype(BF16) for k in ks]
+                thirds = [turned[j * per + k] for k in ks]
                 for k, y in zip(ks, dots_tn([block(k) for k in ks], thirds)):
-                    fourth[column(k), :] = y
+                    stage[k] = y.astype(BF16)
                 for k, y in zip(ks, dots_nt(thirds, [stacked(g_all, j * per + k) for k in ks])):
                     grad_ref[0, k] = y.astype(BF16)
 
-            pairs(per, body)
+            staged(per, body, stage, fourth, j)
 
         either(place, pos_ref, j, keep_ref, send_ref, with_out)
 
@@ -738,7 +719,7 @@
             base = place.onward(pos_ref, n) * per
 
             def body(k):
-                out_refs[n][k] = fourth[pl.ds((base + k) * pitch, size), :].astype(BF16)
+                out_refs[n][k] = fourth[base + k]
 
             each(per, body)
 
@@ -753,8 +734,9 @@
         (3, share),
         anywhere(share + 2 * len(flat(left_two))) + [pl.BlockSpec((home, blocks, cut), lambda p, j, pos: (at(p, j), 0, 0))],
         (*grad_spec,) + (pl.BlockSpec((home, blocks, cut), lambda p, j, pos: (0, 0, 0)),) * share,
-        [pltpu.VMEM((blocks * (blocks + PAD), cut), F32)] * 2
+        [pltpu.VMEM((blocks, blocks, cut), BF16)] * 2
         + [
+            pltpu.VMEM((home, blocks, cut), BF16),
             pltpu.VMEM((share, blocks, home, cut), BF16),
             pltpu.SemaphoreType.DMA((share,)),
         ]

time: 320 us -> 321 us (level)
  no operation moved by 1% of the time
where the time goes in v9:
time: 321 us; the launch traced here: 320 us
  waiting for transfers between devices  129 us (40%)
  Pallas kernels  99.3 us (31%)
  starting transfers between devices  49 us (15%)
  other arithmetic  34.9 us (11%)
  local copies, waits for them, and re-layouts  6.53 us (2%)
    ppermute x48, waiting for transfers between devices, send(): self.last = lax.ppermute(value, self.axis, pairs)  129 us
    pallas_call x10, Pallas kernels, call(): pl.pallas_call(body, out_shape=out, grid_spec=spec, compiler_params=pltpu...  99.3 us
    ppermute x48, starting transfers between devices, send(): self.last = lax.ppermute(value, self.axis, pairs)  49 us
    convert_element_type x14, other arithmetic, parts(): self.cut(ring, lax.rem(ring.here() + step, ring.size)).astype(BF16)  23.4 us
  transfers between devices with their start and end apart: 48, of which 25 were waited for; matrix products, arithmetic and copies ran while one was open for 10% of the time, Pallas kernels for 22%

profile of v9, /device:TPU:0, one launch (start us, length us, event | category | flops | bytes accessed | tf_op | source)
XLA Modules:
  0.0 319.6 jit_solution(16231868130187321536)
XLA Ops:
  6.9 3.3 %shard_map.109 = bf16[128,32,128]{2,1,0:T(8,128)(2,1)} custom-call(s32[5]{0:T(128)} %stack.122.pos_ref, bf16[32,128,512]{2,1,0:T(8,128)(2,1)} %bitcast.194), custom_call_target="tpu_custom_call" | custom-call | bytes 4200000 | tf_op jit(solution)/shard_map/pallas_call | solution.py:84
  12.6 4.1 %collective-permute-start.2 = (bf16[2,32,16,128]{3,2,1,0:T(8,128)(2,1)S(1)}, bf16[2,32,16,128]{3,2,1,0:T(8,128)(2,1)S(1)}, u32[]{:S(2)}, u32[]{:S(2)}) collective-permute-start(bf16[2,32,16,128]{3,2,1,0:T(8,128)(2,1)S(1)} %get-tuple-element.259), channel_id=1, source_target_pairs={{0,8},{4,12},{8,0},{12,4},{16,24},{20,28},{24,16},{28,20},{1,9},{5... | collective-permute-start | bytes 786440 | tf_op jit(solution)/shard_map/ppermute | solution.py:144
  16.7 9.6 %collective-permute-done.5 = bf16[2,32,16,128]{3,2,1,0:T(8,128)(2,1)S(1)} collective-permute-done((bf16[2,32,16,128]{3,2,1,0:T(8,128)(2,1)S(1)}, bf16[2,32,16,128]{3,2,1,0:T(8,128)(2,1)S(1)}, u32[]{:S(2)}, u32[]{:S(2)}) %collective-permute-start.5) | collective-permute-done | bytes 262176 | tf_op jit(solution)/shard_map/ppermute | solution.py:144
  30.5 3.2 shard_map.110.refs_0_
  33.7 3.2 shard_map.111
  51.1 8.9 %collective-permute-done.10 = bf16[2,32,16,128]{3,2,1,0:T(8,128)(2,1)S(1)} collective-permute-done((bf16[2,32,16,128]{3,2,1,0:T(8,128)(2,1)S(1)}, bf16[2,32,16,128]{3,2,1,0:T(8,128)(2,1)S(1)}, u32[]{:S(2)}, u32[]{:S(2)}) %collective-permute-start.10) | collective-permute-done | bytes 262176 | tf_op jit(solution)/shard_map/ppermute | solution.py:144
  61.8 3.4 %collective-permute-start.12 = (bf16[2,32,16,128]{3,2,1,0:T(8,128)(2,1)}, bf16[2,32,16,128]{3,2,1,0:T(8,128)(2,1)}, u32[]{:S(2)}, u32[]{:S(2)}) collective-permute-start(bf16[2,32,16,128]{3,2,1,0:T(8,128)(2,1)} %get-tuple-element.135), channel_id=1, source_target_pairs={{0,16},{4,20},{8,24},{12,28},{16,0},{20,4},{24,8},{28,12},{1,17},{... | collective-permute-start | bytes 786440 | tf_op jit(solution)/shard_map/ppermute | solution.py:144
  65.1 9.4 %shard_map.113 = (bf16[128,32,128]{2,1,0:T(8,128)(2,1)}, bf16[128,32,128]{2,1,0:T(8,128)(2,1)}, bf16[128,32,128]{2,1,0:T(8,128)(2,1)}, bf16[128,32,128]{2,1,0:T(8,128)(2,1)}) custom-call(s32[5]{0:T(128)} %stack.122.pos_ref, bf16[32,128,512]{2,1,0:T(8,128)(2,1)} %bitcast.199, bf16[2,2,32,16,128]{4,3,2,1,0:T(8,128)(2,1)} %copy-done.2, ...), custom_call_target="tpu_custom_call" | custom-call | bytes 9600000 | tf_op jit(solution)/shard_map/pallas_call | solution.py:84
  74.6 4.5 %collective-permute-done.12 = bf16[2,32,16,128]{3,2,1,0:T(8,128)(2,1)} collective-permute-done((bf16[2,32,16,128]{3,2,1,0:T(8,128)(2,1)}, bf16[2,32,16,128]{3,2,1,0:T(8,128)(2,1)}, u32[]{:S(2)}, u32[]{:S(2)}) %collective-permute-start.12) | collective-permute-done | bytes 262176 | tf_op jit(solution)/shard_map/ppermute | solution.py:144
  82.9 3.5 %collective-permute-start.16 = (bf16[2,2,32,16,128]{4,3,2,1,0:T(8,128)(2,1)S(1)}, bf16[2,2,32,16,128]{4,3,2,1,0:T(8,128)(2,1)S(1)}, u32[]{:S(2)}, u32[]{:S(2)}) collective-permute-start(bf16[2,2,32,16,128]{4,3,2,1,0:T(8,128)(2,1)S(1)} %pad_maximum_fusion.7), channel_id=1, source_target_pairs={{0,8},{4,12},{8,0},{12,4},{16,24},{20,28},{24,16},{28,20},{1,9},{5... | collective-permute-start | bytes 1572872 | tf_op jit(solution)/shard_map/ppermute | solution.py:144
  89.5 8.5 %collective-permute-done.16 = bf16[2,2,32,16,128]{4,3,2,1,0:T(8,128)(2,1)S(1)} collective-permute-done((bf16[2,2,32,16,128]{4,3,2,1,0:T(8,128)(2,1)S(1)}, bf16[2,2,32,16,128]{4,3,2,1,0:T(8,128)(2,1)S(1)}, u32[]{:S(2)}, u32[]{:S(2)}) %collective-permute-start.16) | collective-permute-done | bytes 524320 | tf_op jit(solution)/shard_map/ppermute | solution.py:144
  98.2 13.7 %collective-permute-done.13.refs_3_ = bf16[128,32,128]{2,1,0:T(8,128)(2,1)S(1)} collective-permute-done((bf16[128,32,128]{2,1,0:T(8,128)(2,1)S(1)}, bf16[128,32,128]{2,1,0:T(8,128)(2,1)S(1)}, u32[]{:S(2)}, u32[]{:S(2)}) %collective-permute-start.13) | collective-permute-done | bytes 1048608 | tf_op jit(solution)/shard_map/ppermute | solution.py:144
  116.5 9.8 %shard_map.114.refs_12_ = bf16[128,128,128]{2,1,0:T(8,128)(2,1)} custom-call(s32[5]{0:T(128)} %stack.122.pos_ref, bf16[128,32,128]{2,1,0:T(8,128)(2,1)} %shard_map.110.refs_0_, bf16[128,32,128]{2,1,0:T(8,128)(2,1)} %collective-permute-done.19.refs_1_, bf16[128,32,128]{2,1,0:T(8,128)(2,1)} %copy-done.4, bf16[128,32,128]{2,1,0:T(8,128)(2,1)} %copy-done.3, ...), custom_call_target="tpu_custom_call" | custom-call | bytes 12000000 | tf_op jit(solution)/shard_map/pallas_call | solution.py:84
  126.3 11.2 %collective-permute-done.20.refs_2_ = bf16[128,32,128]{2,1,0:T(8,128)(2,1)} collective-permute-done((bf16[128,32,128]{2,1,0:T(8,128)(2,1)}, bf16[128,32,128]{2,1,0:T(8,128)(2,1)}, u32[]{:S(2)}, u32[]{:S(2)}) %collective-permute-start.20) | collective-permute-done | bytes 1048608 | tf_op jit(solution)/shard_map/ppermute | solution.py:144
  142.6 29.1 %shard_map.115 = (bf16[128,128,128]{2,1,0:T(8,128)(2,1)}, bf16[2,32,128,128]{3,2,1,0:T(8,128)(2,1)}, bf16[2,32,128,128]{3,2,1,0:T(8,128)(2,1)}, bf16[2,32,128,12...) custom-call(s32[5]{0:T(128)} %stack.122.pos_ref, ...), custom_call_target="tpu_custom_call" | custom-call | bytes 31200000 | tf_op jit(solution)/shard_map/pallas_call | solution.py:84
  173.1 19.8 %shard_map.116 = (bf16[2,32,128,128]{3,2,1,0:T(8,128)(2,1)}, bf16[2,32,128,128]{3,2,1,0:T(8,128)(2,1)}, bf16[32,128,128]{2,1,0:T(8,128)(2,1)}, bf16[32,128,128]{...) custom-call(s32[5]{0:T(128)} %stack.122.pos_ref, ...), custom_call_target="tpu_custom_call" | custom-call | bytes 24000000 | tf_op jit(solution)/shard_map/pallas_call | solution.py:84
  205.0 18.6 %collective-permute-done.29.refs_2_ = bf16[128,32,128]{2,1,0:T(8,128)(2,1)} collective-permute-done((bf16[128,32,128]{2,1,0:T(8,128)(2,1)}, bf16[128,32,128]{2,1,0:T(8,128)(2,1)}, u32[]{:S(2)}, u32[]{:S(2)}) %collective-permute-start.29) | collective-permute-done | bytes 1048608 | tf_op jit(solution)/shard_map/ppermute | solution.py:144
  231.6 11.3 %shard_map.117 = (bf16[32,128,512]{2,1,0:T(8,128)(2,1)}, bf16[32,128,128]{2,1,0:T(8,128)(2,1)}) custom-call(s32[5]{0:T(128)} %stack.122.pos_ref, bf16[128,32,128]{2,1,0:T(8,128)(2,1)} %get-tuple-element.214.refs_0_, bf16[128,32,128]{2,1,0:T(8,128)(2,1)} %collective-permute-done.30.refs_1_, bf16[128,32,128]{2,1,0:T(8,128)(2,1)} %collective-permute-done.29.refs_2_, ...), custom_call_target="tpu_custom_call" | custom-call | bytes 12000000 | tf_op jit(solution)/shard_map/pallas_call | solution.py:84
  244.8 9.8 %collective-permute-done.36 = bf16[2,32,2,16,128]{4,3,1,2,0:T(8,128)(2,1)} collective-permute-done((bf16[2,32,2,16,128]{4,3,1,2,0:T(8,128)(2,1)S(1)}, bf16[2,32,2,16,128]{4,3,1,2,0:T(8,128)(2,1)}, u32[]{:S(2)}, u32[]{:S(2)}) %collective-permute-start.36) | collective-permute-done | bytes 524320 | tf_op jit(solution)/shard_map/ppermute | solution.py:144
  266.0 11.5 %collective-permute-done.43 = bf16[2,32,16,128]{3,2,1,0:T(8,128)(2,1)} collective-permute-done((bf16[2,32,16,128]{3,2,1,0:T(8,128)(2,1)S(1)}, bf16[2,32,16,128]{3,2,1,0:T(8,128)(2,1)}, u32[]{:S(2)}, u32[]{:S(2)}) %collective-permute-start.43) | collective-permute-done | bytes 262176 | tf_op jit(solution)/shard_map/ppermute | solution.py:144
  281.2 3.2 %collective-permute-start.44 = (bf16[2,32,16,128]{3,2,1,0:T(8,128)(2,1)S(1)}, bf16[2,32,16,128]{3,2,1,0:T(8,128)(2,1)S(1)}, u32[]{:S(2)}, u32[]{:S(2)}) collective-permute-start(bf16[2,32,16,128]{3,2,1,0:T(8,128)(2,1)S(1)} %fusion.8), channel_id=1, source_target_pairs={{0,16},{4,20},{8,24},{12,28},{16,0},{20,4},{24,8},{28,12},{1,17},{... | collective-permute-start | bytes 786440 | tf_op jit(solution)/shard_map/ppermute | solution.py:144
  287.0 8.0 %collective-permute-done.44 = bf16[2,32,16,128]{3,2,1,0:T(8,128)(2,1)S(1)} collective-permute-done((bf16[2,32,16,128]{3,2,1,0:T(8,128)(2,1)S(1)}, bf16[2,32,16,128]{3,2,1,0:T(8,128)(2,1)S(1)}, u32[]{:S(2)}, u32[]{:S(2)}) %collective-permute-start.44) | collective-permute-done | bytes 262176 | tf_op jit(solution)/shard_map/ppermute | solution.py:144
  300.1 6.7 %collective-permute-done.45 = bf16[32,16,128]{2,1,0:T(8,128)(2,1)S(1)} collective-permute-done((bf16[32,16,128]{2,1,0:T(8,128)(2,1)}, bf16[32,16,128]{2,1,0:T(8,128)(2,1)S(1)}, u32[]{:S(2)}, u32[]{:S(2)}) %collective-permute-start.45) | collective-permute-done | bytes 131104 | tf_op jit(solution)/shard_map/ppermute | solution.py:144
  308.5 6.9 %shard_map.118 = bf16[32,128,512]{2,1,0:T(8,128)(2,1)} custom-call(s32[5]{0:T(128)} %stack.122.pos_ref, bf16[32,128,128]{2,1,0:T(8,128)(2,1)} %get-tuple-element.225.refs_0_, bf16[32,128,128]{2,1,0:T(8,128)(2,1)} %collective-permute-done.38.refs_1_, bf16[32,128,128]{2,1,0:T(8,128)(2,1)} %collective-permute-done.39.refs_2_, bf16[32,128,128]{2,1,0:T(8,128)(2,1)} %copy-done.12, ...), custom_call_target="tpu_custom_call" | custom-call | bytes 7200000 | tf_op jit(solution)/shard_map/pallas_call | solution.py:84
  (160 shorter events, 97.1 us)
Async XLA Ops:
  12.5 30.8 %collective-permute-start = (bf16[128,32,128]{2,1,0:T(8,128)(2,1)}, bf16[128,32,128]{2,1,0:T(8,128)(2,1)S(1)}, u32[]{:S(2)}, u32[]{:S(2)}) collective-permute-start(bf16[128,32,128]{2,1,0:T(8,128)(2,1)} %shard_map.109), channel_id=1, source_target_pairs={{0,3},{1,2},{2,1},{3,0},{4,7},{5,6},{6,5},{7,4},{8,11},{9,10},{10,... | collective-permute-start | bytes 3145736 | tf_op jit(solution)/shard_map/ppermute | solution.py:144
  47.1 35.8 %collective-permute-start.8 = (bf16[128,32,128]{2,1,0:T(8,128)(2,1)}, bf16[128,32,128]{2,1,0:T(8,128)(2,1)S(1)}, u32[]{:S(2)}, u32[]{:S(2)}) collective-permute-start(bf16[128,32,128]{2,1,0:T(8,128)(2,1)} %shard_map.112), channel_id=1, source_target_pairs={{0,2},{1,3},{2,0},{3,1},{4,6},{5,7},{6,4},{7,5},{8,10},{9,11},{10,... | collective-permute-start | bytes 3145736 | tf_op jit(solution)/shard_map/ppermute | solution.py:144
  49.5 33.4 %collective-permute-start.9 = (bf16[2,2,2,32,16,128]{5,4,3,2,1,0:T(8,128)(2,1)S(1)}, bf16[2,2,2,32,16,128]{5,4,3,2,1,0:T(8,128)(2,1)}, u32[]{:S(2)}, u32[]{:S(2)}) collective-permute-start(bf16[2,2,2,32,16,128]{5,4,3,2,1,0:T(8,128)(2,1)S(1)} %pad_maximum_fusion.refs_4_.refs_8_), channel_id=1, source_target_pairs={{0,4},{4,0},{8,12},{12,8},{16,20},{20,16},{24,28},{28,24},{1,5},{5... | collective-permute-start | bytes 3145736 | tf_op jit(solution)/shard_map/ppermute | solution.py:144
  65.1 24.4 %collective-permute-start.19 = (bf16[128,32,128]{2,1,0:T(8,128)(2,1)}, bf16[128,32,128]{2,1,0:T(8,128)(2,1)}, u32[]{:S(2)}, u32[]{:S(2)}) collective-permute-start(bf16[128,32,128]{2,1,0:T(8,128)(2,1)} %shard_map.111), channel_id=1, source_target_pairs={{0,1},{1,0},{2,3},{3,2},{4,5},{5,4},{6,7},{7,6},{8,9},{9,8},{10,11... | collective-permute-start | bytes 3145736 | tf_op jit(solution)/shard_map/ppermute | solution.py:144
  86.5 25.4 %collective-permute-start.13 = (bf16[128,32,128]{2,1,0:T(8,128)(2,1)S(1)}, bf16[128,32,128]{2,1,0:T(8,128)(2,1)S(1)}, u32[]{:S(2)}, u32[]{:S(2)}) collective-permute-start(bf16[128,32,128]{2,1,0:T(8,128)(2,1)S(1)} %copy-done.22), channel_id=1, source_target_pairs={{0,3},{1,2},{2,1},{3,0},{4,7},{5,6},{6,5},{7,4},{8,11},{9,10},{10,... | collective-permute-start | bytes 3145736 | tf_op jit(solution)/shard_map/ppermute | solution.py:144
  86.8 26.0 %collective-permute-start.14 = (bf16[128,32,128]{2,1,0:T(8,128)(2,1)S(1)}, bf16[128,32,128]{2,1,0:T(8,128)(2,1)S(1)}, u32[]{:S(2)}, u32[]{:S(2)}) collective-permute-start(bf16[128,32,128]{2,1,0:T(8,128)(2,1)S(1)} %copy-done.21), channel_id=1, source_target_pairs={{0,1},{1,0},{2,3},{3,2},{4,5},{5,4},{6,7},{7,6},{8,9},{9,8},{10,11... | collective-permute-start | bytes 3145736 | tf_op jit(solution)/shard_map/ppermute | solution.py:144
  88.1 25.4 %collective-permute-start.15 = (bf16[2,2,2,32,16,128]{5,4,3,2,1,0:T(8,128)(2,1)}, bf16[2,2,2,32,16,128]{5,4,3,2,1,0:T(8,128)(2,1)}, u32[]{:S(2)}, u32[]{:S(2)}) collective-permute-start(bf16[2,2,2,32,16,128]{5,4,3,2,1,0:T(8,128)(2,1)} %pad_maximum_fusion.1.refs_4_), channel_id=1, source_target_pairs={{0,4},{4,0},{8,12},{12,8},{16,20},{20,16},{24,28},{28,24},{1,5},{5... | collective-permute-start | bytes 3145736 | tf_op jit(solution)/shard_map/ppermute | solution.py:144
  89.5 23.9 %collective-permute-start.17 = (bf16[2,2,2,32,16,128]{5,4,3,2,1,0:T(8,128)(2,1)S(1)}, bf16[2,2,2,32,16,128]{5,4,3,2,1,0:T(8,128)(2,1)S(1)}, u32[]{:S(2)}, u32[]{:S(2)}) collective-permute-start(bf16[2,2,2,32,16,128]{5,4,3,2,1,0:T(8,128)(2,1)S(1)} %pad_maximum_fusion.refs_4_.refs_8_), channel_id=1, source_target_pairs={{0,1},{1,0},{2,3},{3,2},{4,5},{5,4},{6,7},{7,6},{8,9},{9,8},{10,11... | collective-permute-start | bytes 3145736 | tf_op jit(solution)/shard_map/ppermute | solution.py:144
  111.9 25.6 %collective-permute-start.20 = (bf16[128,32,128]{2,1,0:T(8,128)(2,1)}, bf16[128,32,128]{2,1,0:T(8,128)(2,1)}, u32[]{:S(2)}, u32[]{:S(2)}) collective-permute-start(bf16[128,32,128]{2,1,0:T(8,128)(2,1)} %get-tuple-element.153), channel_id=1, source_target_pairs={{0,2},{1,3},{2,0},{3,1},{4,6},{5,7},{6,4},{7,5},{8,10},{9,11},{10,... | collective-permute-start | bytes 3145736 | tf_op jit(solution)/shard_map/ppermute | solution.py:144
  114.4 24.5 %collective-permute-start.21 = (bf16[2,2,2,32,16,128]{5,4,3,2,1,0:T(8,128)(2,1)S(1)}, bf16[2,2,2,32,16,128]{5,4,3,2,1,0:T(8,128)(2,1)S(1)}, u32[]{:S(2)}, u32[]{:S(2)}) collective-permute-start(bf16[2,2,2,32,16,128]{5,4,3,2,1,0:T(8,128)(2,1)S(1)} %pad_maximum_fusion.2.refs_8_.refs_4_), channel_id=1, source_target_pairs={{0,4},{4,0},{8,12},{12,8},{16,20},{20,16},{24,28},{28,24},{1,5},{5... | collective-permute-start | bytes 3145736 | tf_op jit(solution)/shard_map/ppermute | solution.py:144
  115.9 23.0 %collective-permute-start.22 = (bf16[2,2,2,32,16,128]{5,4,3,2,1,0:T(8,128)(2,1)S(1)}, bf16[2,2,2,32,16,128]{5,4,3,2,1,0:T(8,128)(2,1)}, u32[]{:S(2)}, u32[]{:S(2)}) collective-permute-start(bf16[2,2,2,32,16,128]{5,4,3,2,1,0:T(8,128)(2,1)S(1)} %pad_maximum_fusion.2.refs_8_.refs_4_), channel_id=1, source_target_pairs={{0,1},{1,0},{2,3},{3,2},{4,5},{5,4},{6,7},{7,6},{8,9},{9,8},{10,11... | collective-permute-start | bytes 3145736 | tf_op jit(solution)/shard_map/ppermute | solution.py:144
  115.9 23.0 %collective-permute-start.23 = (bf16[2,2,2,32,16,128]{5,4,3,2,1,0:T(8,128)(2,1)}, bf16[2,2,2,32,16,128]{5,4,3,2,1,0:T(8,128)(2,1)}, u32[]{:S(2)}, u32[]{:S(2)}) collective-permute-start(bf16[2,2,2,32,16,128]{5,4,3,2,1,0:T(8,128)(2,1)} %pad_maximum_fusion.1.refs_4_), channel_id=1, source_target_pairs={{0,1},{1,0},{2,3},{3,2},{4,5},{5,4},{6,7},{7,6},{8,9},{9,8},{10,11... | collective-permute-start | bytes 3145736 | tf_op jit(solution)/shard_map/ppermute | solution.py:144
  171.9 22.8 %collective-permute-start.27 = (bf16[2,32,128,128]{3,2,1,0:T(8,128)(2,1)}, bf16[2,32,128,128]{3,2,1,0:T(8,128)(2,1)}, u32[]{:S(2)}, u32[]{:S(2)}) collective-permute-start(bf16[2,32,128,128]{3,2,1,0:T(8,128)(2,1)} %get-tuple-element.177), channel_id=1, source_target_pairs={{0,1},{1,0},{2,3},{3,2},{4,5},{5,4},{6,7},{7,6},{8,9},{9,8},{10,11... | collective-permute-start | bytes 6291464 | tf_op jit(solution)/shard_map/ppermute | solution.py:144
  172.3 25.5 %collective-permute-start.26 = (bf16[128,32,128]{2,1,0:T(8,128)(2,1)}, bf16[128,32,128]{2,1,0:T(8,128)(2,1)}, u32[]{:S(2)}, u32[]{:S(2)}) collective-permute-start(bf16[128,32,128]{2,1,0:T(8,128)(2,1)} %get-tuple-element.175), channel_id=1, source_target_pairs={{0,3},{1,2},{2,1},{3,0},{4,7},{5,6},{6,5},{7,4},{8,11},{9,10},{10,... | collective-permute-start | bytes 3145736 | tf_op jit(solution)/shard_map/ppermute | solution.py:144
  197.9 25.8 %collective-permute-start.29 = (bf16[128,32,128]{2,1,0:T(8,128)(2,1)}, bf16[128,32,128]{2,1,0:T(8,128)(2,1)}, u32[]{:S(2)}, u32[]{:S(2)}) collective-permute-start(bf16[128,32,128]{2,1,0:T(8,128)(2,1)} %get-tuple-element.190), channel_id=1, source_target_pairs={{0,2},{1,3},{2,0},{3,1},{4,6},{5,7},{6,4},{7,5},{8,10},{9,11},{10,... | collective-permute-start | bytes 3145736 | tf_op jit(solution)/shard_map/ppermute | solution.py:144
  199.0 24.6 %collective-permute-start.30 = (bf16[128,32,128]{2,1,0:T(8,128)(2,1)}, bf16[128,32,128]{2,1,0:T(8,128)(2,1)}, u32[]{:S(2)}, u32[]{:S(2)}) collective-permute-start(bf16[128,32,128]{2,1,0:T(8,128)(2,1)} %get-tuple-element.191), channel_id=1, source_target_pairs={{0,1},{1,0},{2,3},{3,2},{4,5},{5,4},{6,7},{7,6},{8,9},{9,8},{10,11... | collective-permute-start | bytes 3145736 | tf_op jit(solution)/shard_map/ppermute | solution.py:144
  199.1 25.8 %collective-permute-start.31 = (bf16[2,32,2,2,16,128]{5,4,1,3,2,0:T(8,128)(2,1)}, bf16[2,32,2,2,16,128]{5,4,1,3,2,0:T(8,128)(2,1)}, u32[]{:S(2)}, u32[]{:S(2)}) collective-permute-start(bf16[2,32,2,2,16,128]{5,4,1,3,2,0:T(8,128)(2,1)} %fusion), channel_id=1, source_target_pairs={{0,4},{4,0},{8,12},{12,8},{16,20},{20,16},{24,28},{28,24},{1,5},{5... | collective-permute-start | bytes 3145736 | tf_op jit(solution)/shard_map/ppermute | solution.py:144
  200.4 25.3 %collective-permute-start.32 = (bf16[2,32,2,2,16,128]{5,4,1,3,2,0:T(8,128)(2,1)S(1)}, bf16[2,32,2,2,16,128]{5,4,1,3,2,0:T(8,128)(2,1)}, u32[]{:S(2)}, u32[]{:S(2)}) collective-permute-start(bf16[2,32,2,2,16,128]{5,4,1,3,2,0:T(8,128)(2,1)S(1)} %fusion.1), channel_id=1, source_target_pairs={{0,8},{4,12},{8,0},{12,4},{16,24},{20,28},{24,16},{28,20},{1,9},{5... | collective-permute-start | bytes 3145736 | tf_op jit(solution)/shard_map/ppermute | solution.py:144
  225.7 31.1 %collective-permute-start.34 = (bf16[32,128,128]{2,1,0:T(8,128)(2,1)}, bf16[32,128,128]{2,1,0:T(8,128)(2,1)S(1)}, u32[]{:S(2)}, u32[]{:S(2)}) collective-permute-start(bf16[32,128,128]{2,1,0:T(8,128)(2,1)} %get-tuple-element.204), channel_id=1, source_target_pairs={{0,3},{1,2},{2,1},{3,0},{4,7},{5,6},{6,5},{7,4},{8,11},{9,10},{10,... | collective-permute-start | bytes 3145736 | tf_op jit(solution)/shard_map/ppermute | solution.py:144
  225.7 31.1 %collective-permute-start.37 = (bf16[2,32,2,2,16,128]{5,4,1,3,2,0:T(8,128)(2,1)}, bf16[2,32,2,2,16,128]{5,4,1,3,2,0:T(8,128)(2,1)}, u32[]{:S(2)}, u32[]{:S(2)}) collective-permute-start(bf16[2,32,2,2,16,128]{5,4,1,3,2,0:T(8,128)(2,1)} %fusion.2), channel_id=1, source_target_pairs={{0,4},{4,0},{8,12},{12,8},{16,20},{20,16},{24,28},{28,24},{1,5},{5... | collective-permute-start | bytes 3145736 | tf_op jit(solution)/shard_map/ppermute | solution.py:144
  227.8 26.8 %collective-permute-start.36 = (bf16[2,32,2,16,128]{4,3,1,2,0:T(8,128)(2,1)S(1)}, bf16[2,32,2,16,128]{4,3,1,2,0:T(8,128)(2,1)}, u32[]{:S(2)}, u32[]{:S(2)}) collective-permute-start(bf16[2,32,2,16,128]{4,3,1,2,0:T(8,128)(2,1)S(1)} %fusion.4), channel_id=1, source_target_pairs={{0,16},{4,20},{8,24},{12,28},{16,0},{20,4},{24,8},{28,12},{1,17},{... | collective-permute-start | bytes 1572872 | tf_op jit(solution)/shard_map/ppermute | solution.py:144
  231.0 25.7 %collective-permute-start.35 = (bf16[2,32,2,16,128]{4,3,1,2,0:T(8,128)(2,1)}, bf16[2,32,2,16,128]{4,3,1,2,0:T(8,128)(2,1)}, u32[]{:S(2)}, u32[]{:S(2)}) collective-permute-start(bf16[2,32,2,16,128]{4,3,1,2,0:T(8,128)(2,1)} %fusion.5), channel_id=1, source_target_pairs={{0,8},{4,12},{8,0},{12,4},{16,24},{20,28},{24,16},{28,20},{1,9},{5... | collective-permute-start | bytes 1572872 | tf_op jit(solution)/shard_map/ppermute | solution.py:144
  263.6 33.4 %collective-permute-start.39 = (bf16[32,128,128]{2,1,0:T(8,128)(2,1)}, bf16[32,128,128]{2,1,0:T(8,128)(2,1)}, u32[]{:S(2)}, u32[]{:S(2)}) collective-permute-start(bf16[32,128,128]{2,1,0:T(8,128)(2,1)} %get-tuple-element.227), channel_id=1, source_target_pairs={{0,2},{1,3},{2,0},{3,1},{4,6},{5,7},{6,4},{7,5},{8,10},{9,11},{10,... | collective-permute-start | bytes 3145736 | tf_op jit(solution)/shard_map/ppermute | solution.py:144
  264.7 43.8 %collective-permute-start.38 = (bf16[32,128,128]{2,1,0:T(8,128)(2,1)}, bf16[32,128,128]{2,1,0:T(8,128)(2,1)}, u32[]{:S(2)}, u32[]{:S(2)}) collective-permute-start(bf16[32,128,128]{2,1,0:T(8,128)(2,1)} %get-tuple-element.226), channel_id=1, source_target_pairs={{0,1},{1,0},{2,3},{3,2},{4,5},{5,4},{6,7},{7,6},{8,9},{9,8},{10,11... | collective-permute-start | bytes 3145736 | tf_op jit(solution)/shard_map/ppermute | solution.py:144
  (47 other events, 621.3 us)

commit v10 on v9

--- a/solution.py
+++ b/solution.py
@@ -204,13 +204,13 @@
     def prepare(self, ring):
         self.ready = self.parts(ring) if ring in self.left else []
 
-    def step(self, ring):
+    def step(self, ring, *before):
         if ring not in self.left:
             return
         rest = [r for r in self.left if r is not ring]
         parts = self.ready or self.parts(ring)
         self.ready = []
-        got = [ring.send(part, step + 1) for step, part in enumerate(parts)]
+        got = [ring.send(after(part, *before), step + 1) for step, part in enumerate(parts)]
         self.arrays, self.rings, self.left = self.arrays + got, self.rings + [rest] * len(got), rest
 
     def finish(self):
@@ -219,12 +219,12 @@
         return self.cut()
 
 
-def finish_together(sums, rings, last):
+def finish_together(sums, rings, last, *before):
     for part in sums:
         for ring in rings:
             part.step(ring)
     sends = list(zip(*[part.parts(last) for part in sums]))
-    got = [last.send(jnp.stack(send), step + 1) for step, send in enumerate(sends)]
+    got = [last.send(after(jnp.stack(send), *before), step + 1) for step, send in enumerate(sends)]
     for n, part in enumerate(sums):
         part.left = [r for r in part.left if r is not last]
         part.arrays, part.rings = part.arrays + [g[n] for g in got], part.rings + [part.left] * len(got)
@@ -793,19 +793,19 @@
 
     n_one, n_two, n_three = (place.steps.index(step) if step in place.steps else share for step in [(0, 1), (1, 0), (1, 1)])
     one = gather_far(first_left)
-    w_two = from_y(factors[3])
-    rest = from_y(after(jnp.stack([factors[1], factors[2]]), one))
+    rest = from_y(jnp.stack([factors[3], factors[1], factors[2]]))
     g = {n: deal(place, pos, g_home, cut, n) for n in reversed(range(share))}
     got_three = cross(g, n_three)
-    w_two = gather_far(after(w_two, g[share - 1]))
+    w_two = gather_far(after(rest[:, 0], g[share - 1]))
     one = last_dp(gather(one, 1))
+    w_one = gather_far(rest[:, 1])
     w_two = gather(w_two, 1)
-    got_three, one, w_two, rest, g = slot(place, (got_three, one, w_two, rest, g))
+    got_three, one, w_two, w_one, rest, g = slot(place, (got_three, one, w_two, w_one, rest, g))
 
     got_two = cross(g, n_two)
     right_two = last_dp(w_two)
-    w_one = gather(gather_far(rest[:, 0]), 1)
-    w_left = gather_far(rest[:, 1])
+    w_one = gather(w_one, 1)
+    w_left = gather_far(rest[:, 2])
     s = first_stage(place, pos, x_home, one, cut)
     got_two, right_two, w_one, w_left, one, s, pos = slot(place, (got_two, right_two, w_one, w_left, one, list(s), pos))
 
@@ -878,12 +878,12 @@
     three.step(near_step)
     one_part.step(x_step)
     lone.step(near_step)
-    three.step(far_step)
+    three.step(far_step, lone.arrays[-1], *([s_two] if n_two < share else []))
     s_one = cross(s, n_one)
     s_got = [s[0], s_one, s_two, s_three][:share]
-    grad_ltwo, grad_rone, grad_rtwo = finish_together([two, one_part, three], place.dp, place.y)
+    mixed = add_home(place, pos, s_got, x_home)
+    grad_ltwo, grad_rone, grad_rtwo = finish_together([two, one_part, three], place.dp, place.y, mixed)
     grad_lone = lone.finish()
-    mixed = add_home(place, pos, s_got, x_home)
     return mixed, input_grad, grad_lone, grad_rone, grad_ltwo, grad_rtwo
 
 

time: 321 us -> 313 us (0.975)
  waiting for transfers between devices: 129 us -> 122 us
  starting transfers between devices: 49 us -> 44.5 us
  other arithmetic: 34.9 us -> 38.4 us
    ppermute x48 -> x47, waiting for transfers between devices: 129 us -> 122 us  [send(): self.last = lax.ppermute(value, self.axis, pairs)]
    ppermute x48 -> x47, starting transfers between devices: 49 us -> 44.5 us  [send(): self.last = lax.ppermute(value, self.axis, pairs)]
    another operation x8 -> x9, other arithmetic: 5.46 us -> 7.17 us  [gather(): return got if n == 0 else jnp.stack(got)]
  transfers between devices with their start and end apart: 48 -> 47, of which waited for: 25 -> 26; matrix products, arithmetic and copies ran while one was open for 10% -> 11% of each run, Pallas kernels for 22% -> 23%
where the time goes in v10:
time: 313 us; the launch traced here: 311 us
  waiting for transfers between devices  122 us (39%)
  Pallas kernels  99.2 us (32%)
  starting transfers between devices  44.5 us (14%)
  other arithmetic  38.4 us (12%)
  local copies, waits for them, and re-layouts  6.26 us (2%)
    ppermute x47, waiting for transfers between devices, send(): self.last = lax.ppermute(value, self.axis, pairs)  122 us
    pallas_call x10, Pallas kernels, call(): pl.pallas_call(body, out_shape=out, grid_spec=spec, compiler_params=pltpu...  99.2 us
    ppermute x47, starting transfers between devices, send(): self.last = lax.ppermute(value, self.axis, pairs)  44.5 us
    convert_element_type x14, other arithmetic, parts(): self.cut(ring, lax.rem(ring.here() + step, ring.size)).astype(BF16)  24.1 us
    another operation x9, other arithmetic, gather(): return got if n == 0 else jnp.stack(got)  7.17 us
  transfers between devices with their start and end apart: 47, of which 26 were waited for; matrix products, arithmetic and copies ran while one was open for 11% of the time, Pallas kernels for 23%

profile of v10, /device:TPU:0, one launch (start us, length us, event | category | flops | bytes accessed | tf_op | source)
XLA Modules:
  0.0 311.4 jit_solution(4328397872046639987)
XLA Ops:
  8.0 3.3 %shard_map.109 = bf16[128,32,128]{2,1,0:T(8,128)(2,1)} custom-call(s32[5]{0:T(128)} %stack.116.pos_ref, bf16[32,128,512]{2,1,0:T(8,128)(2,1)} %bitcast.195), custom_call_target="tpu_custom_call" | custom-call | bytes 4200000 | tf_op jit(solution)/shard_map/pallas_call | solution.py:84
  18.5 9.6 %collective-permute-done.5 = bf16[2,32,16,128]{3,2,1,0:T(8,128)(2,1)S(1)} collective-permute-done((bf16[2,32,16,128]{3,2,1,0:T(8,128)(2,1)S(1)}, bf16[2,32,16,128]{3,2,1,0:T(8,128)(2,1)S(1)}, u32[]{:S(2)}, u32[]{:S(2)}) %collective-permute-start.5) | collective-permute-done | bytes 262176 | tf_op jit(solution)/shard_map/ppermute | solution.py:144
  29.8 3.1 %collective-permute-start.7 = (bf16[2,32,16,128]{3,2,1,0:T(8,128)(2,1)S(1)}, bf16[2,32,16,128]{3,2,1,0:T(8,128)(2,1)}, u32[]{:S(2)}, u32[]{:S(2)}) collective-permute-start(bf16[2,32,16,128]{3,2,1,0:T(8,128)(2,1)S(1)} %get-tuple-element.131), channel_id=1, source_target_pairs={{0,16},{4,20},{8,24},{12,28},{16,0},{20,4},{24,8},{28,12},{1,17},{... | collective-permute-start | bytes 786440 | tf_op jit(solution)/shard_map/ppermute | solution.py:144
  34.6 3.2 %shard_map.110.refs_0_ = bf16[128,32,128]{2,1,0:T(8,128)(2,1)} custom-call(s32[5]{0:T(128)} %stack.116.pos_ref, bf16[32,128,512]{2,1,0:T(8,128)(2,1)} %bitcast.196), custom_call_target="tpu_custom_call" | custom-call | bytes 4200000 | tf_op jit(solution)/shard_map/pallas_call | solution.py:84
  37.8 3.2 %shard_map.111 = bf16[128,32,128]{2,1,0:T(8,128)(2,1)} custom-call(s32[5]{0:T(128)} %stack.116.pos_ref, bf16[32,128,512]{2,1,0:T(8,128)(2,1)} %bitcast.197), custom_call_target="tpu_custom_call" | custom-call | bytes 4200000 | tf_op jit(solution)/shard_map/pallas_call | solution.py:84
  40.9 3.2 %shard_map.112 = bf16[128,32,128]{2,1,0:T(8,128)(2,1)} custom-call(s32[5]{0:T(128)} %stack.116.pos_ref, bf16[32,128,512]{2,1,0:T(8,128)(2,1)} %bitcast.198), custom_call_target="tpu_custom_call" | custom-call | bytes 4200000 | tf_op jit(solution)/shard_map/pallas_call | solution.py:84
  44.2 3.7 %collective-permute-done.7 = bf16[2,32,16,128]{3,2,1,0:T(8,128)(2,1)} collective-permute-done((bf16[2,32,16,128]{3,2,1,0:T(8,128)(2,1)S(1)}, bf16[2,32,16,128]{3,2,1,0:T(8,128)(2,1)}, u32[]{:S(2)}, u32[]{:S(2)}) %collective-permute-start.7) | collective-permute-done | bytes 262176 | tf_op jit(solution)/shard_map/ppermute | solution.py:144
  57.9 9.5 %shard_map.113 = (bf16[128,32,128]{2,1,0:T(8,128)(2,1)}, bf16[128,32,128]{2,1,0:T(8,128)(2,1)}, bf16[128,32,128]{2,1,0:T(8,128)(2,1)}, bf16[128,32,128]{2,1,0:T(8,128)(2,1)}) custom-call(s32[5]{0:T(128)} %stack.116.pos_ref, bf16[32,128,512]{2,1,0:T(8,128)(2,1)} %bitcast.200, bf16[2,2,32,16,128]{4,3,2,1,0:T(8,128)(2,1)} %copy-done.2, ...), custom_call_target="tpu_custom_call" | custom-call | bytes 9600000 | tf_op jit(solution)/shard_map/pallas_call | solution.py:84
  67.5 5.9 %collective-permute-done.11 = bf16[2,32,16,128]{3,2,1,0:T(8,128)(2,1)} collective-permute-done((bf16[2,32,16,128]{3,2,1,0:T(8,128)(2,1)}, bf16[2,32,16,128]{3,2,1,0:T(8,128)(2,1)}, u32[]{:S(2)}, u32[]{:S(2)}) %collective-permute-start.11) | collective-permute-done | bytes 262176 | tf_op jit(solution)/shard_map/ppermute | solution.py:144
  76.8 3.3 %collective-permute-start.15 = (bf16[2,2,32,16,128]{4,3,2,1,0:T(8,128)(2,1)S(1)}, bf16[2,2,32,16,128]{4,3,2,1,0:T(8,128)(2,1)S(1)}, u32[]{:S(2)}, u32[]{:S(2)}) collective-permute-start(bf16[2,2,32,16,128]{4,3,2,1,0:T(8,128)(2,1)S(1)} %pad_maximum_fusion.7), channel_id=1, source_target_pairs={{0,8},{4,12},{8,0},{12,4},{16,24},{20,28},{24,16},{28,20},{1,9},{5... | collective-permute-start | bytes 1572872 | tf_op jit(solution)/shard_map/ppermute | solution.py:144
  83.4 8.2 %collective-permute-done.15 = bf16[2,2,32,16,128]{4,3,2,1,0:T(8,128)(2,1)S(1)} collective-permute-done((bf16[2,2,32,16,128]{4,3,2,1,0:T(8,128)(2,1)S(1)}, bf16[2,2,32,16,128]{4,3,2,1,0:T(8,128)(2,1)S(1)}, u32[]{:S(2)}, u32[]{:S(2)}) %collective-permute-start.15) | collective-permute-done | bytes 524320 | tf_op jit(solution)/shard_map/ppermute | solution.py:144
  91.7 13.7 %collective-permute-done.12.refs_3_ = bf16[128,32,128]{2,1,0:T(8,128)(2,1)S(1)} collective-permute-done((bf16[128,32,128]{2,1,0:T(8,128)(2,1)S(1)}, bf16[128,32,128]{2,1,0:T(8,128)(2,1)S(1)}, u32[]{:S(2)}, u32[]{:S(2)}) %collective-permute-start.12) | collective-permute-done | bytes 1048608 | tf_op jit(solution)/shard_map/ppermute | solution.py:144
  110.3 9.8 %shard_map.114.refs_12_ = bf16[128,128,128]{2,1,0:T(8,128)(2,1)} custom-call(s32[5]{0:T(128)} %stack.116.pos_ref, bf16[128,32,128]{2,1,0:T(8,128)(2,1)} %shard_map.110.refs_0_, bf16[128,32,128]{2,1,0:T(8,128)(2,1)} %collective-permute-done.18.refs_1_, bf16[128,32,128]{2,1,0:T(8,128)(2,1)} %copy-done.4, bf16[128,32,128]{2,1,0:T(8,128)(2,1)} %copy-done.3, ...), custom_call_target="tpu_custom_call" | custom-call | bytes 12000000 | tf_op jit(solution)/shard_map/pallas_call | solution.py:84
  120.2 11.0 %collective-permute-done.19.refs_2_ = bf16[128,32,128]{2,1,0:T(8,128)(2,1)} collective-permute-done((bf16[128,32,128]{2,1,0:T(8,128)(2,1)}, bf16[128,32,128]{2,1,0:T(8,128)(2,1)}, u32[]{:S(2)}, u32[]{:S(2)}) %collective-permute-start.19) | collective-permute-done | bytes 1048608 | tf_op jit(solution)/shard_map/ppermute | solution.py:144
  136.3 29.1 %shard_map.115 = (bf16[128,128,128]{2,1,0:T(8,128)(2,1)}, bf16[2,32,128,128]{3,2,1,0:T(8,128)(2,1)}, bf16[2,32,128,128]{3,2,1,0:T(8,128)(2,1)}, bf16[2,32,128,12...) custom-call(s32[5]{0:T(128)} %stack.116.pos_ref, ...), custom_call_target="tpu_custom_call" | custom-call | bytes 31200000 | tf_op jit(solution)/shard_map/pallas_call | solution.py:84
  166.9 19.8 %shard_map.116 = (bf16[2,32,128,128]{3,2,1,0:T(8,128)(2,1)}, bf16[2,32,128,128]{3,2,1,0:T(8,128)(2,1)}, bf16[32,128,128]{2,1,0:T(8,128)(2,1)}, bf16[32,128,128]{...) custom-call(s32[5]{0:T(128)} %stack.116.pos_ref, ...), custom_call_target="tpu_custom_call" | custom-call | bytes 24000000 | tf_op jit(solution)/shard_map/pallas_call | solution.py:84
  198.8 18.6 %collective-permute-done.28.refs_2_ = bf16[128,32,128]{2,1,0:T(8,128)(2,1)} collective-permute-done((bf16[128,32,128]{2,1,0:T(8,128)(2,1)}, bf16[128,32,128]{2,1,0:T(8,128)(2,1)}, u32[]{:S(2)}, u32[]{:S(2)}) %collective-permute-start.28) | collective-permute-done | bytes 1048608 | tf_op jit(solution)/shard_map/ppermute | solution.py:144
  226.7 11.3 %shard_map.117 = (bf16[32,128,512]{2,1,0:T(8,128)(2,1)}, bf16[32,128,128]{2,1,0:T(8,128)(2,1)}) custom-call(s32[5]{0:T(128)} %stack.116.pos_ref, bf16[128,32,128]{2,1,0:T(8,128)(2,1)} %get-tuple-element.214.refs_0_, bf16[128,32,128]{2,1,0:T(8,128)(2,1)} %collective-permute-done.29.refs_1_, bf16[128,32,128]{2,1,0:T(8,128)(2,1)} %collective-permute-done.28.refs_2_, ...), custom_call_target="tpu_custom_call" | custom-call | bytes 12000000 | tf_op jit(solution)/shard_map/pallas_call | solution.py:84
  239.9 9.3 %collective-permute-done.35 = bf16[2,32,2,16,128]{4,3,1,2,0:T(8,128)(2,1)S(1)} collective-permute-done((bf16[2,32,2,16,128]{4,3,1,2,0:T(8,128)(2,1)}, bf16[2,32,2,16,128]{4,3,1,2,0:T(8,128)(2,1)S(1)}, u32[]{:S(2)}, u32[]{:S(2)}) %collective-permute-start.35) | collective-permute-done | bytes 524320 | tf_op jit(solution)/shard_map/ppermute | solution.py:144
  260.3 4.5 %collective-permute-done.39 = bf16[32,2,2,16,128]{4,3,0,2,1:T(8,128)(2,1)} collective-permute-done((bf16[32,2,2,16,128]{4,3,0,2,1:T(8,128)(2,1)}, bf16[32,2,2,16,128]{4,3,0,2,1:T(8,128)(2,1)}, u32[]{:S(2)}, u32[]{:S(2)}) %collective-permute-start.39) | collective-permute-done | bytes 524320 | tf_op jit(solution)/shard_map/ppermute | solution.py:144
  265.9 9.0 %collective-permute-done.40 = bf16[2,32,2,16,128]{4,3,1,2,0:T(8,128)(2,1)} collective-permute-done((bf16[2,32,2,16,128]{4,3,1,2,0:T(8,128)(2,1)}, bf16[2,32,2,16,128]{4,3,1,2,0:T(8,128)(2,1)}, u32[]{:S(2)}, u32[]{:S(2)}) %collective-permute-start.40) | collective-permute-done | bytes 524320 | tf_op jit(solution)/shard_map/ppermute | solution.py:144
  278.1 3.5 %collective-permute-done.41 = bf16[32,2,16,128]{3,2,0,1:T(8,128)(2,1)S(1)} collective-permute-done((bf16[32,2,16,128]{3,2,0,1:T(8,128)(2,1)S(1)}, bf16[32,2,16,128]{3,2,0,1:T(8,128)(2,1)S(1)}, u32[]{:S(2)}, u32[]{:S(2)}) %collective-permute-start.41) | collective-permute-done | bytes 262176 | tf_op jit(solution)/shard_map/ppermute | solution.py:144
  284.5 6.8 %shard_map.118 = bf16[32,128,512]{2,1,0:T(8,128)(2,1)} custom-call(s32[5]{0:T(128)} %stack.116.pos_ref, bf16[32,128,128]{2,1,0:T(8,128)(2,1)} %get-tuple-element.225.refs_0_, bf16[32,128,128]{2,1,0:T(8,128)(2,1)} %collective-permute-done.37.refs_1_, bf16[32,128,128]{2,1,0:T(8,128)(2,1)} %collective-permute-done.38.refs_2_, bf16[32,128,128]{2,1,0:T(8,128)(2,1)} %copy-done.11, ...), custom_call_target="tpu_custom_call" | custom-call | bytes 7200000 | tf_op jit(solution)/shard_map/pallas_call | solution.py:84
  298.3 7.2 %collective-permute-done.44 = bf16[32,16,128]{2,1,0:T(8,128)(2,1)S(1)} collective-permute-done((bf16[32,16,128]{2,1,0:T(8,128)(2,1)}, bf16[32,16,128]{2,1,0:T(8,128)(2,1)S(1)}, u32[]{:S(2)}, u32[]{:S(2)}) %collective-permute-start.44) | collective-permute-done | bytes 131104 | tf_op jit(solution)/shard_map/ppermute | solution.py:144
  (154 shorter events, 100.6 us)
Async XLA Ops:
  16.8 34.6 %collective-permute-start = (bf16[128,32,128]{2,1,0:T(8,128)(2,1)}, bf16[128,32,128]{2,1,0:T(8,128)(2,1)S(1)}, u32[]{:S(2)}, u32[]{:S(2)}) collective-permute-start(bf16[128,32,128]{2,1,0:T(8,128)(2,1)} %shard_map.109), channel_id=1, source_target_pairs={{0,3},{1,2},{2,1},{3,0},{4,7},{5,6},{6,5},{7,4},{8,11},{9,10},{10,... | collective-permute-start | bytes 3145736 | tf_op jit(solution)/shard_map/ppermute | solution.py:144
  51.5 25.2 %collective-permute-start.8 = (bf16[128,32,128]{2,1,0:T(8,128)(2,1)}, bf16[128,32,128]{2,1,0:T(8,128)(2,1)S(1)}, u32[]{:S(2)}, u32[]{:S(2)}) collective-permute-start(bf16[128,32,128]{2,1,0:T(8,128)(2,1)} %shard_map.112), channel_id=1, source_target_pairs={{0,2},{1,3},{2,0},{3,1},{4,6},{5,7},{6,4},{7,5},{8,10},{9,11},{10,... | collective-permute-start | bytes 3145736 | tf_op jit(solution)/shard_map/ppermute | solution.py:144
  52.6 24.2 %collective-permute-start.9 = (bf16[2,2,2,32,16,128]{5,4,3,2,1,0:T(8,128)(2,1)S(1)}, bf16[2,2,2,32,16,128]{5,4,3,2,1,0:T(8,128)(2,1)}, u32[]{:S(2)}, u32[]{:S(2)}) collective-permute-start(bf16[2,2,2,32,16,128]{5,4,3,2,1,0:T(8,128)(2,1)S(1)} %pad_maximum_fusion.refs_4_.refs_8_), channel_id=1, source_target_pairs={{0,4},{4,0},{8,12},{12,8},{16,20},{20,16},{24,28},{28,24},{1,5},{5... | collective-permute-start | bytes 3145736 | tf_op jit(solution)/shard_map/ppermute | solution.py:144
  57.9 25.4 %collective-permute-start.18 = (bf16[128,32,128]{2,1,0:T(8,128)(2,1)}, bf16[128,32,128]{2,1,0:T(8,128)(2,1)}, u32[]{:S(2)}, u32[]{:S(2)}) collective-permute-start(bf16[128,32,128]{2,1,0:T(8,128)(2,1)} %shard_map.111), channel_id=1, source_target_pairs={{0,1},{1,0},{2,3},{3,2},{4,5},{5,4},{6,7},{7,6},{8,9},{9,8},{10,11... | collective-permute-start | bytes 3145736 | tf_op jit(solution)/shard_map/ppermute | solution.py:144
  80.1 25.3 %collective-permute-start.12 = (bf16[128,32,128]{2,1,0:T(8,128)(2,1)S(1)}, bf16[128,32,128]{2,1,0:T(8,128)(2,1)S(1)}, u32[]{:S(2)}, u32[]{:S(2)}) collective-permute-start(bf16[128,32,128]{2,1,0:T(8,128)(2,1)S(1)} %copy-done.20), channel_id=1, source_target_pairs={{0,3},{1,2},{2,1},{3,0},{4,7},{5,6},{6,5},{7,4},{8,11},{9,10},{10,... | collective-permute-start | bytes 3145736 | tf_op jit(solution)/shard_map/ppermute | solution.py:144
  80.1 26.0 %collective-permute-start.13 = (bf16[128,32,128]{2,1,0:T(8,128)(2,1)S(1)}, bf16[128,32,128]{2,1,0:T(8,128)(2,1)S(1)}, u32[]{:S(2)}, u32[]{:S(2)}) collective-permute-start(bf16[128,32,128]{2,1,0:T(8,128)(2,1)S(1)} %copy-done.19), channel_id=1, source_target_pairs={{0,1},{1,0},{2,3},{3,2},{4,5},{5,4},{6,7},{7,6},{8,9},{9,8},{10,11... | collective-permute-start | bytes 3145736 | tf_op jit(solution)/shard_map/ppermute | solution.py:144
  81.9 25.4 %collective-permute-start.14 = (bf16[2,2,2,32,16,128]{5,4,3,2,1,0:T(8,128)(2,1)}, bf16[2,2,2,32,16,128]{5,4,3,2,1,0:T(8,128)(2,1)}, u32[]{:S(2)}, u32[]{:S(2)}) collective-permute-start(bf16[2,2,2,32,16,128]{5,4,3,2,1,0:T(8,128)(2,1)} %pad_maximum_fusion.1.refs_4_), channel_id=1, source_target_pairs={{0,4},{4,0},{8,12},{12,8},{16,20},{20,16},{24,28},{28,24},{1,5},{5... | collective-permute-start | bytes 3145736 | tf_op jit(solution)/shard_map/ppermute | solution.py:144
  83.4 23.9 %collective-permute-start.16 = (bf16[2,2,2,32,16,128]{5,4,3,2,1,0:T(8,128)(2,1)S(1)}, bf16[2,2,2,32,16,128]{5,4,3,2,1,0:T(8,128)(2,1)S(1)}, u32[]{:S(2)}, u32[]{:S(2)}) collective-permute-start(bf16[2,2,2,32,16,128]{5,4,3,2,1,0:T(8,128)(2,1)S(1)} %pad_maximum_fusion.refs_4_.refs_8_), channel_id=1, source_target_pairs={{0,1},{1,0},{2,3},{3,2},{4,5},{5,4},{6,7},{7,6},{8,9},{9,8},{10,11... | collective-permute-start | bytes 3145736 | tf_op jit(solution)/shard_map/ppermute | solution.py:144
  105.4 25.8 %collective-permute-start.19 = (bf16[128,32,128]{2,1,0:T(8,128)(2,1)}, bf16[128,32,128]{2,1,0:T(8,128)(2,1)}, u32[]{:S(2)}, u32[]{:S(2)}) collective-permute-start(bf16[128,32,128]{2,1,0:T(8,128)(2,1)} %get-tuple-element.153), channel_id=1, source_target_pairs={{0,2},{1,3},{2,0},{3,1},{4,6},{5,7},{6,4},{7,5},{8,10},{9,11},{10,... | collective-permute-start | bytes 3145736 | tf_op jit(solution)/shard_map/ppermute | solution.py:144
  108.2 24.3 %collective-permute-start.20 = (bf16[2,2,2,32,16,128]{5,4,3,2,1,0:T(8,128)(2,1)S(1)}, bf16[2,2,2,32,16,128]{5,4,3,2,1,0:T(8,128)(2,1)S(1)}, u32[]{:S(2)}, u32[]{:S(2)}) collective-permute-start(bf16[2,2,2,32,16,128]{5,4,3,2,1,0:T(8,128)(2,1)S(1)} %pad_maximum_fusion.2.refs_8_.refs_4_), channel_id=1, source_target_pairs={{0,4},{4,0},{8,12},{12,8},{16,20},{20,16},{24,28},{28,24},{1,5},{5... | collective-permute-start | bytes 3145736 | tf_op jit(solution)/shard_map/ppermute | solution.py:144
  109.7 22.8 %collective-permute-start.21 = (bf16[2,2,2,32,16,128]{5,4,3,2,1,0:T(8,128)(2,1)S(1)}, bf16[2,2,2,32,16,128]{5,4,3,2,1,0:T(8,128)(2,1)}, u32[]{:S(2)}, u32[]{:S(2)}) collective-permute-start(bf16[2,2,2,32,16,128]{5,4,3,2,1,0:T(8,128)(2,1)S(1)} %pad_maximum_fusion.2.refs_8_.refs_4_), channel_id=1, source_target_pairs={{0,1},{1,0},{2,3},{3,2},{4,5},{5,4},{6,7},{7,6},{8,9},{9,8},{10,11... | collective-permute-start | bytes 3145736 | tf_op jit(solution)/shard_map/ppermute | solution.py:144
  109.8 22.8 %collective-permute-start.22 = (bf16[2,2,2,32,16,128]{5,4,3,2,1,0:T(8,128)(2,1)}, bf16[2,2,2,32,16,128]{5,4,3,2,1,0:T(8,128)(2,1)}, u32[]{:S(2)}, u32[]{:S(2)}) collective-permute-start(bf16[2,2,2,32,16,128]{5,4,3,2,1,0:T(8,128)(2,1)} %pad_maximum_fusion.1.refs_4_), channel_id=1, source_target_pairs={{0,1},{1,0},{2,3},{3,2},{4,5},{5,4},{6,7},{7,6},{8,9},{9,8},{10,11... | collective-permute-start | bytes 3145736 | tf_op jit(solution)/shard_map/ppermute | solution.py:144
  166.0 25.5 %collective-permute-start.25 = (bf16[128,32,128]{2,1,0:T(8,128)(2,1)}, bf16[128,32,128]{2,1,0:T(8,128)(2,1)}, u32[]{:S(2)}, u32[]{:S(2)}) collective-permute-start(bf16[128,32,128]{2,1,0:T(8,128)(2,1)} %get-tuple-element.175), channel_id=1, source_target_pairs={{0,3},{1,2},{2,1},{3,0},{4,7},{5,6},{6,5},{7,4},{8,11},{9,10},{10,... | collective-permute-start | bytes 3145736 | tf_op jit(solution)/shard_map/ppermute | solution.py:144
  191.6 25.8 %collective-permute-start.28 = (bf16[128,32,128]{2,1,0:T(8,128)(2,1)}, bf16[128,32,128]{2,1,0:T(8,128)(2,1)}, u32[]{:S(2)}, u32[]{:S(2)}) collective-permute-start(bf16[128,32,128]{2,1,0:T(8,128)(2,1)} %get-tuple-element.190), channel_id=1, source_target_pairs={{0,2},{1,3},{2,0},{3,1},{4,6},{5,7},{6,4},{7,5},{8,10},{9,11},{10,... | collective-permute-start | bytes 3145736 | tf_op jit(solution)/shard_map/ppermute | solution.py:144
  192.8 24.6 %collective-permute-start.29 = (bf16[128,32,128]{2,1,0:T(8,128)(2,1)}, bf16[128,32,128]{2,1,0:T(8,128)(2,1)}, u32[]{:S(2)}, u32[]{:S(2)}) collective-permute-start(bf16[128,32,128]{2,1,0:T(8,128)(2,1)} %get-tuple-element.191), channel_id=1, source_target_pairs={{0,1},{1,0},{2,3},{3,2},{4,5},{5,4},{6,7},{7,6},{8,9},{9,8},{10,11... | collective-permute-start | bytes 3145736 | tf_op jit(solution)/shard_map/ppermute | solution.py:144
  192.8 25.8 %collective-permute-start.30 = (bf16[2,32,2,2,16,128]{5,4,1,3,2,0:T(8,128)(2,1)}, bf16[2,32,2,2,16,128]{5,4,1,3,2,0:T(8,128)(2,1)}, u32[]{:S(2)}, u32[]{:S(2)}) collective-permute-start(bf16[2,32,2,2,16,128]{5,4,1,3,2,0:T(8,128)(2,1)} %fusion), channel_id=1, source_target_pairs={{0,4},{4,0},{8,12},{12,8},{16,20},{20,16},{24,28},{28,24},{1,5},{5... | collective-permute-start | bytes 3145736 | tf_op jit(solution)/shard_map/ppermute | solution.py:144
  194.3 25.3 %collective-permute-start.31 = (bf16[2,32,2,2,16,128]{5,4,1,3,2,0:T(8,128)(2,1)S(1)}, bf16[2,32,2,2,16,128]{5,4,1,3,2,0:T(8,128)(2,1)}, u32[]{:S(2)}, u32[]{:S(2)}) collective-permute-start(bf16[2,32,2,2,16,128]{5,4,1,3,2,0:T(8,128)(2,1)S(1)} %fusion.1), channel_id=1, source_target_pairs={{0,8},{4,12},{8,0},{12,4},{16,24},{20,28},{24,16},{28,20},{1,9},{5... | collective-permute-start | bytes 3145736 | tf_op jit(solution)/shard_map/ppermute | solution.py:144
  219.6 31.2 %collective-permute-start.33 = (bf16[32,128,128]{2,1,0:T(8,128)(2,1)}, bf16[32,128,128]{2,1,0:T(8,128)(2,1)S(1)}, u32[]{:S(2)}, u32[]{:S(2)}) collective-permute-start(bf16[32,128,128]{2,1,0:T(8,128)(2,1)} %get-tuple-element.204), channel_id=1, source_target_pairs={{0,3},{1,2},{2,1},{3,0},{4,7},{5,6},{6,5},{7,4},{8,11},{9,10},{10,... | collective-permute-start | bytes 3145736 | tf_op jit(solution)/shard_map/ppermute | solution.py:144
  219.6 31.2 %collective-permute-start.36 = (bf16[2,32,2,2,16,128]{5,4,1,3,2,0:T(8,128)(2,1)}, bf16[2,32,2,2,16,128]{5,4,1,3,2,0:T(8,128)(2,1)}, u32[]{:S(2)}, u32[]{:S(2)}) collective-permute-start(bf16[2,32,2,2,16,128]{5,4,1,3,2,0:T(8,128)(2,1)} %fusion.2), channel_id=1, source_target_pairs={{0,4},{4,0},{8,12},{12,8},{16,20},{20,16},{24,28},{28,24},{1,5},{5... | collective-permute-start | bytes 3145736 | tf_op jit(solution)/shard_map/ppermute | solution.py:144
  222.6 26.6 %collective-permute-start.35 = (bf16[2,32,2,16,128]{4,3,1,2,0:T(8,128)(2,1)}, bf16[2,32,2,16,128]{4,3,1,2,0:T(8,128)(2,1)S(1)}, u32[]{:S(2)}, u32[]{:S(2)}) collective-permute-start(bf16[2,32,2,16,128]{4,3,1,2,0:T(8,128)(2,1)} %fusion.4), channel_id=1, source_target_pairs={{0,16},{4,20},{8,24},{12,28},{16,0},{20,4},{24,8},{28,12},{1,17},{... | collective-permute-start | bytes 1572872 | tf_op jit(solution)/shard_map/ppermute | solution.py:144
  225.1 25.8 %collective-permute-start.34 = (bf16[2,32,2,16,128]{4,3,1,2,0:T(8,128)(2,1)}, bf16[2,32,2,16,128]{4,3,1,2,0:T(8,128)(2,1)}, u32[]{:S(2)}, u32[]{:S(2)}) collective-permute-start(bf16[2,32,2,16,128]{4,3,1,2,0:T(8,128)(2,1)} %fusion.5), channel_id=1, source_target_pairs={{0,8},{4,12},{8,0},{12,4},{16,24},{20,28},{24,16},{28,20},{1,9},{5... | collective-permute-start | bytes 1572872 | tf_op jit(solution)/shard_map/ppermute | solution.py:144
  252.4 29.1 %collective-permute-start.38 = (bf16[32,128,128]{2,1,0:T(8,128)(2,1)}, bf16[32,128,128]{2,1,0:T(8,128)(2,1)}, u32[]{:S(2)}, u32[]{:S(2)}) collective-permute-start(bf16[32,128,128]{2,1,0:T(8,128)(2,1)} %get-tuple-element.227), channel_id=1, source_target_pairs={{0,2},{1,3},{2,0},{3,1},{4,6},{5,7},{6,4},{7,5},{8,10},{9,11},{10,... | collective-permute-start | bytes 3145736 | tf_op jit(solution)/shard_map/ppermute | solution.py:144
  257.3 24.2 %collective-permute-start.42 = (bf16[2,32,16,128]{3,2,1,0:T(8,128)(2,1)S(1)}, bf16[2,32,16,128]{3,2,1,0:T(8,128)(2,1)S(1)}, u32[]{:S(2)}, u32[]{:S(2)}) collective-permute-start(bf16[2,32,16,128]{3,2,1,0:T(8,128)(2,1)S(1)} %fusion.7), channel_id=1, source_target_pairs={{0,16},{4,20},{8,24},{12,28},{16,0},{20,4},{24,8},{28,12},{1,17},{... | collective-permute-start | bytes 786440 | tf_op jit(solution)/shard_map/ppermute | solution.py:144
  260.3 24.2 %collective-permute-start.37 = (bf16[32,128,128]{2,1,0:T(8,128)(2,1)}, bf16[32,128,128]{2,1,0:T(8,128)(2,1)}, u32[]{:S(2)}, u32[]{:S(2)}) collective-permute-start(bf16[32,128,128]{2,1,0:T(8,128)(2,1)} %get-tuple-element.226), channel_id=1, source_target_pairs={{0,1},{1,0},{2,3},{3,2},{4,5},{5,4},{6,7},{7,6},{8,9},{9,8},{10,11... | collective-permute-start | bytes 3145736 | tf_op jit(solution)/shard_map/ppermute | solution.py:144
  (44 other events, 547.6 us)

commit v11 on v10

--- a/solution.py
+++ b/solution.py
@@ -215,8 +215,13 @@
 
     def finish(self):
         for ring in [r for r in self.left[::-1] if isinstance(r, Ring)]:
+            count = len(self.arrays)
             self.step(ring)
-        return self.cut()
+        if not any(isinstance(r, Ring) for r in self.rings[0]):
+            return self.cut()
+        got, self.arrays = self.arrays[count:], self.arrays[:count]
+        own, got = lax.optimization_barrier((self.cut(), got))
+        return total([own] + got)
 
 
 def finish_together(sums, rings, last, *before):
@@ -225,10 +230,10 @@
             part.step(ring)
     sends = list(zip(*[part.parts(last) for part in sums]))
     got = [last.send(after(jnp.stack(send), *before), step + 1) for step, send in enumerate(sends)]
-    for n, part in enumerate(sums):
+    for part in sums:
         part.left = [r for r in part.left if r is not last]
-        part.arrays, part.rings = part.arrays + [g[n] for g in got], part.rings + [part.left] * len(got)
-    return [part.cut() for part in sums]
+    own, got = lax.optimization_barrier(([part.cut() for part in sums], got))
+    return [total([mine] + [g[n] for g in got]) for n, mine in enumerate(own)]
 
 
 def total(terms):
@@ -567,8 +572,8 @@
     def _():
         copies = share_copies(place, pos_ref, s_parts, s_all, s_sems) + piece_copies(one, one_all, one_sems)
         run(copies)
+        finish(copies)
         run(second())
-        finish(copies)
 
     @pl.when(phase == 0)
     def _():
@@ -679,8 +684,8 @@
     def _():
         copies = piece_copies(left, left_all, left_sems)
         run(copies)
+        finish(copies)
         run(second())
-        finish(copies)
 
     @pl.when(phase == 0)
     def _():
@@ -878,7 +883,7 @@
     three.step(near_step)
     one_part.step(x_step)
     lone.step(near_step)
-    three.step(far_step, lone.arrays[-1], *([s_two] if n_two < share else []))
+    three.step(far_step, lone.arrays[-1])
     s_one = cross(s, n_one)
     s_got = [s[0], s_one, s_two, s_three][:share]
     mixed = add_home(place, pos, s_got, x_home)

time: 313 us -> 307 us (0.981)
  other arithmetic: 38.4 us -> 34.7 us
  transfers between devices with their start and end apart: 47 -> 47, of which waited for: 26 -> 27; matrix products, arithmetic and copies ran while one was open for 11% -> 11% of each run, Pallas kernels for 23% -> 23%
where the time goes in v11:
time: 307 us; the launch traced here: 306 us
  waiting for transfers between devices  122 us (40%)
  Pallas kernels  98.2 us (32%)
  starting transfers between devices  45.5 us (15%)
  other arithmetic  34.7 us (11%)
  local copies, waits for them, and re-layouts  4.88 us (2%)
    ppermute x47, waiting for transfers between devices, send(): self.last = lax.ppermute(value, self.axis, pairs)  122 us
    pallas_call x10, Pallas kernels, call(): pl.pallas_call(body, out_shape=out, grid_spec=spec, compiler_params=pltpu...  98.2 us
    ppermute x47, starting transfers between devices, send(): self.last = lax.ppermute(value, self.axis, pairs)  45.5 us
    convert_element_type x14, other arithmetic, parts(): self.cut(ring, lax.rem(ring.here() + step, ring.size)).astype(BF16)  21.2 us
    another operation x9, other arithmetic, gather(): return got if n == 0 else jnp.stack(got)  7.22 us
  transfers between devices with their start and end apart: 47, of which 27 were waited for; matrix products, arithmetic and copies ran while one was open for 11% of the time, Pallas kernels for 23%

profile of v11, /device:TPU:0, one launch (start us, length us, event | category | flops | bytes accessed | tf_op | source)
XLA Modules:
  0.0 306.3 jit_solution(506016559039918871)
XLA Ops:
  8.0 3.3 %shard_map.109 = bf16[128,32,128]{2,1,0:T(8,128)(2,1)} custom-call(s32[5]{0:T(128)} %stack.116.pos_ref, bf16[32,128,512]{2,1,0:T(8,128)(2,1)} %bitcast.189), custom_call_target="tpu_custom_call" | custom-call | bytes 4200000 | tf_op jit(solution)/shard_map/pallas_call | solution.py:84
  18.5 9.6 %collective-permute-done.5 = bf16[2,32,16,128]{3,2,1,0:T(8,128)(2,1)S(1)} collective-permute-done((bf16[2,32,16,128]{3,2,1,0:T(8,128)(2,1)S(1)}, bf16[2,32,16,128]{3,2,1,0:T(8,128)(2,1)S(1)}, u32[]{:S(2)}, u32[]{:S(2)}) %collective-permute-start.5) | collective-permute-done | bytes 262176 | tf_op jit(solution)/shard_map/ppermute | solution.py:144
  29.8 3.2 %collective-permute-start.7 = (bf16[2,32,16,128]{3,2,1,0:T(8,128)(2,1)S(1)}, bf16[2,32,16,128]{3,2,1,0:T(8,128)(2,1)}, u32[]{:S(2)}, u32[]{:S(2)}) collective-permute-start(bf16[2,32,16,128]{3,2,1,0:T(8,128)(2,1)S(1)} %get-tuple-element.137), channel_id=1, source_target_pairs={{0,16},{4,20},{8,24},{12,28},{16,0},{20,4},{24,8},{28,12},{1,17},{... | collective-permute-start | bytes 786440 | tf_op jit(solution)/shard_map/ppermute | solution.py:144
  34.6 3.2 %shard_map.110.refs_0_ = bf16[128,32,128]{2,1,0:T(8,128)(2,1)} custom-call(s32[5]{0:T(128)} %stack.116.pos_ref, bf16[32,128,512]{2,1,0:T(8,128)(2,1)} %bitcast.190), custom_call_target="tpu_custom_call" | custom-call | bytes 4200000 | tf_op jit(solution)/shard_map/pallas_call | solution.py:84
  37.8 3.2 %shard_map.111 = bf16[128,32,128]{2,1,0:T(8,128)(2,1)} custom-call(s32[5]{0:T(128)} %stack.116.pos_ref, bf16[32,128,512]{2,1,0:T(8,128)(2,1)} %bitcast.191), custom_call_target="tpu_custom_call" | custom-call | bytes 4200000 | tf_op jit(solution)/shard_map/pallas_call | solution.py:84
  41.0 3.2 %shard_map.112 = bf16[128,32,128]{2,1,0:T(8,128)(2,1)} custom-call(s32[5]{0:T(128)} %stack.116.pos_ref, bf16[32,128,512]{2,1,0:T(8,128)(2,1)} %bitcast.192), custom_call_target="tpu_custom_call" | custom-call | bytes 4200000 | tf_op jit(solution)/shard_map/pallas_call | solution.py:84
  44.2 3.7 %collective-permute-done.7 = bf16[2,32,16,128]{3,2,1,0:T(8,128)(2,1)} collective-permute-done((bf16[2,32,16,128]{3,2,1,0:T(8,128)(2,1)S(1)}, bf16[2,32,16,128]{3,2,1,0:T(8,128)(2,1)}, u32[]{:S(2)}, u32[]{:S(2)}) %collective-permute-start.7) | collective-permute-done | bytes 262176 | tf_op jit(solution)/shard_map/ppermute | solution.py:144
  57.9 9.4 %shard_map.113 = (bf16[128,32,128]{2,1,0:T(8,128)(2,1)}, bf16[128,32,128]{2,1,0:T(8,128)(2,1)}, bf16[128,32,128]{2,1,0:T(8,128)(2,1)}, bf16[128,32,128]{2,1,0:T(8,128)(2,1)}) custom-call(s32[5]{0:T(128)} %stack.116.pos_ref, bf16[32,128,512]{2,1,0:T(8,128)(2,1)} %bitcast.194, bf16[2,2,32,16,128]{4,3,2,1,0:T(8,128)(2,1)} %copy-done.2, ...), custom_call_target="tpu_custom_call" | custom-call | bytes 9600000 | tf_op jit(solution)/shard_map/pallas_call | solution.py:84
  67.4 6.0 %collective-permute-done.11 = bf16[2,32,16,128]{3,2,1,0:T(8,128)(2,1)} collective-permute-done((bf16[2,32,16,128]{3,2,1,0:T(8,128)(2,1)}, bf16[2,32,16,128]{3,2,1,0:T(8,128)(2,1)}, u32[]{:S(2)}, u32[]{:S(2)}) %collective-permute-start.11) | collective-permute-done | bytes 262176 | tf_op jit(solution)/shard_map/ppermute | solution.py:144
  76.8 3.3 %collective-permute-start.15 = (bf16[2,2,32,16,128]{4,3,2,1,0:T(8,128)(2,1)S(1)}, bf16[2,2,32,16,128]{4,3,2,1,0:T(8,128)(2,1)S(1)}, u32[]{:S(2)}, u32[]{:S(2)}) collective-permute-start(bf16[2,2,32,16,128]{4,3,2,1,0:T(8,128)(2,1)S(1)} %pad_maximum_fusion.7), channel_id=1, source_target_pairs={{0,8},{4,12},{8,0},{12,4},{16,24},{20,28},{24,16},{28,20},{1,9},{5... | collective-permute-start | bytes 1572872 | tf_op jit(solution)/shard_map/ppermute | solution.py:144
  83.4 8.2 %collective-permute-done.15 = bf16[2,2,32,16,128]{4,3,2,1,0:T(8,128)(2,1)S(1)} collective-permute-done((bf16[2,2,32,16,128]{4,3,2,1,0:T(8,128)(2,1)S(1)}, bf16[2,2,32,16,128]{4,3,2,1,0:T(8,128)(2,1)S(1)}, u32[]{:S(2)}, u32[]{:S(2)}) %collective-permute-start.15) | collective-permute-done | bytes 524320 | tf_op jit(solution)/shard_map/ppermute | solution.py:144
  91.7 13.7 %collective-permute-done.12.refs_3_ = bf16[128,32,128]{2,1,0:T(8,128)(2,1)S(1)} collective-permute-done((bf16[128,32,128]{2,1,0:T(8,128)(2,1)S(1)}, bf16[128,32,128]{2,1,0:T(8,128)(2,1)S(1)}, u32[]{:S(2)}, u32[]{:S(2)}) %collective-permute-start.12) | collective-permute-done | bytes 1048608 | tf_op jit(solution)/shard_map/ppermute | solution.py:144
  110.3 9.8 %shard_map.114.refs_12_ = bf16[128,128,128]{2,1,0:T(8,128)(2,1)} custom-call(s32[5]{0:T(128)} %stack.116.pos_ref, bf16[128,32,128]{2,1,0:T(8,128)(2,1)} %shard_map.110.refs_0_, bf16[128,32,128]{2,1,0:T(8,128)(2,1)} %collective-permute-done.18.refs_1_, bf16[128,32,128]{2,1,0:T(8,128)(2,1)} %copy-done.4, bf16[128,32,128]{2,1,0:T(8,128)(2,1)} %copy-done.3, ...), custom_call_target="tpu_custom_call" | custom-call | bytes 12000000 | tf_op jit(solution)/shard_map/pallas_call | solution.py:84
  120.2 11.0 %collective-permute-done.19.refs_2_ = bf16[128,32,128]{2,1,0:T(8,128)(2,1)} collective-permute-done((bf16[128,32,128]{2,1,0:T(8,128)(2,1)}, bf16[128,32,128]{2,1,0:T(8,128)(2,1)}, u32[]{:S(2)}, u32[]{:S(2)}) %collective-permute-start.19) | collective-permute-done | bytes 1048608 | tf_op jit(solution)/shard_map/ppermute | solution.py:144
  136.4 27.9 %shard_map.115 = (bf16[128,128,128]{2,1,0:T(8,128)(2,1)}, bf16[2,32,128,128]{3,2,1,0:T(8,128)(2,1)}, bf16[2,32,128,128]{3,2,1,0:T(8,128)(2,1)}, bf16[2,32,128,12...) custom-call(s32[5]{0:T(128)} %stack.116.pos_ref, ...), custom_call_target="tpu_custom_call" | custom-call | bytes 31200000 | tf_op jit(solution)/shard_map/pallas_call | solution.py:84
  165.5 19.9 %shard_map.116 = (bf16[2,32,128,128]{3,2,1,0:T(8,128)(2,1)}, bf16[2,32,128,128]{3,2,1,0:T(8,128)(2,1)}, bf16[32,128,128]{2,1,0:T(8,128)(2,1)}, bf16[32,128,128]{...) custom-call(s32[5]{0:T(128)} %stack.116.pos_ref, ...), custom_call_target="tpu_custom_call" | custom-call | bytes 24000000 | tf_op jit(solution)/shard_map/pallas_call | solution.py:84
  197.6 18.6 %collective-permute-done.28.refs_2_ = bf16[128,32,128]{2,1,0:T(8,128)(2,1)} collective-permute-done((bf16[128,32,128]{2,1,0:T(8,128)(2,1)}, bf16[128,32,128]{2,1,0:T(8,128)(2,1)}, u32[]{:S(2)}, u32[]{:S(2)}) %collective-permute-start.28) | collective-permute-done | bytes 1048608 | tf_op jit(solution)/shard_map/ppermute | solution.py:144
  225.4 11.3 %shard_map.117 = (bf16[32,128,512]{2,1,0:T(8,128)(2,1)}, bf16[32,128,128]{2,1,0:T(8,128)(2,1)}) custom-call(s32[5]{0:T(128)} %stack.116.pos_ref, bf16[128,32,128]{2,1,0:T(8,128)(2,1)} %get-tuple-element.220.refs_0_, bf16[128,32,128]{2,1,0:T(8,128)(2,1)} %collective-permute-done.29.refs_1_, bf16[128,32,128]{2,1,0:T(8,128)(2,1)} %collective-permute-done.28.refs_2_, ...), custom_call_target="tpu_custom_call" | custom-call | bytes 12000000 | tf_op jit(solution)/shard_map/pallas_call | solution.py:84
  238.0 10.1 %collective-permute-done.35 = bf16[2,32,2,16,128]{4,3,1,2,0:T(8,128)(2,1)} collective-permute-done((bf16[2,32,2,16,128]{4,3,1,2,0:T(8,128)(2,1)}, bf16[2,32,2,16,128]{4,3,1,2,0:T(8,128)(2,1)}, u32[]{:S(2)}, u32[]{:S(2)}) %collective-permute-start.35) | collective-permute-done | bytes 524320 | tf_op jit(solution)/shard_map/ppermute | solution.py:144
  259.9 5.7 %collective-permute-done.42 = bf16[2,32,16,128]{3,2,1,0:T(8,128)(2,1)S(1)} collective-permute-done((bf16[2,32,16,128]{3,2,1,0:T(8,128)(2,1)S(1)}, bf16[2,32,16,128]{3,2,1,0:T(8,128)(2,1)S(1)}, u32[]{:S(2)}, u32[]{:S(2)}) %collective-permute-start.42) | collective-permute-done | bytes 262176 | tf_op jit(solution)/shard_map/ppermute | solution.py:144
  268.4 5.7 %collective-permute-done.40 = bf16[2,32,2,16,128]{4,3,1,2,0:T(8,128)(2,1)S(1)} collective-permute-done((bf16[2,32,2,16,128]{4,3,1,2,0:T(8,128)(2,1)S(1)}, bf16[2,32,2,16,128]{4,3,1,2,0:T(8,128)(2,1)S(1)}, u32[]{:S(2)}, u32[]{:S(2)}) %collective-permute-start.40) | collective-permute-done | bytes 524320 | tf_op jit(solution)/shard_map/ppermute | solution.py:144
  276.8 4.0 %collective-permute-done.41 = bf16[32,2,16,128]{3,2,0,1:T(8,128)(2,1)S(1)} collective-permute-done((bf16[32,2,16,128]{3,2,0,1:T(8,128)(2,1)S(1)}, bf16[32,2,16,128]{3,2,0,1:T(8,128)(2,1)S(1)}, u32[]{:S(2)}, u32[]{:S(2)}) %collective-permute-start.41) | collective-permute-done | bytes 262176 | tf_op jit(solution)/shard_map/ppermute | solution.py:144
  284.0 7.0 %shard_map.118 = bf16[32,128,512]{2,1,0:T(8,128)(2,1)} custom-call(s32[5]{0:T(128)} %stack.116.pos_ref, bf16[32,128,128]{2,1,0:T(8,128)(2,1)} %get-tuple-element.231.refs_0_, bf16[32,128,128]{2,1,0:T(8,128)(2,1)} %collective-permute-done.37.refs_1_, bf16[32,128,128]{2,1,0:T(8,128)(2,1)} %collective-permute-done.38.refs_2_, bf16[32,128,128]{2,1,0:T(8,128)(2,1)} %copy-done.11, ...), custom_call_target="tpu_custom_call" | custom-call | bytes 7200000 | tf_op jit(solution)/shard_map/pallas_call | solution.py:84
  296.6 7.1 %collective-permute-done.44 = bf16[32,16,128]{2,1,0:T(8,128)(2,1)S(1)} collective-permute-done((bf16[32,16,128]{2,1,0:T(8,128)(2,1)S(1)}, bf16[32,16,128]{2,1,0:T(8,128)(2,1)S(1)}, u32[]{:S(2)}, u32[]{:S(2)}) %collective-permute-start.44) | collective-permute-done | bytes 131104 | tf_op jit(solution)/shard_map/ppermute | solution.py:144
  (158 shorter events, 97.2 us)
Async XLA Ops:
  16.8 34.6 %collective-permute-start = (bf16[128,32,128]{2,1,0:T(8,128)(2,1)}, bf16[128,32,128]{2,1,0:T(8,128)(2,1)S(1)}, u32[]{:S(2)}, u32[]{:S(2)}) collective-permute-start(bf16[128,32,128]{2,1,0:T(8,128)(2,1)} %shard_map.109), channel_id=1, source_target_pairs={{0,3},{1,2},{2,1},{3,0},{4,7},{5,6},{6,5},{7,4},{8,11},{9,10},{10,... | collective-permute-start | bytes 3145736 | tf_op jit(solution)/shard_map/ppermute | solution.py:144
  51.5 25.2 %collective-permute-start.8 = (bf16[128,32,128]{2,1,0:T(8,128)(2,1)}, bf16[128,32,128]{2,1,0:T(8,128)(2,1)S(1)}, u32[]{:S(2)}, u32[]{:S(2)}) collective-permute-start(bf16[128,32,128]{2,1,0:T(8,128)(2,1)} %shard_map.112), channel_id=1, source_target_pairs={{0,2},{1,3},{2,0},{3,1},{4,6},{5,7},{6,4},{7,5},{8,10},{9,11},{10,... | collective-permute-start | bytes 3145736 | tf_op jit(solution)/shard_map/ppermute | solution.py:144
  52.6 24.2 %collective-permute-start.9 = (bf16[2,2,2,32,16,128]{5,4,3,2,1,0:T(8,128)(2,1)S(1)}, bf16[2,2,2,32,16,128]{5,4,3,2,1,0:T(8,128)(2,1)}, u32[]{:S(2)}, u32[]{:S(2)}) collective-permute-start(bf16[2,2,2,32,16,128]{5,4,3,2,1,0:T(8,128)(2,1)S(1)} %pad_maximum_fusion.refs_4_.refs_8_), channel_id=1, source_target_pairs={{0,4},{4,0},{8,12},{12,8},{16,20},{20,16},{24,28},{28,24},{1,5},{5... | collective-permute-start | bytes 3145736 | tf_op jit(solution)/shard_map/ppermute | solution.py:144
  57.9 25.5 %collective-permute-start.18 = (bf16[128,32,128]{2,1,0:T(8,128)(2,1)}, bf16[128,32,128]{2,1,0:T(8,128)(2,1)}, u32[]{:S(2)}, u32[]{:S(2)}) collective-permute-start(bf16[128,32,128]{2,1,0:T(8,128)(2,1)} %shard_map.111), channel_id=1, source_target_pairs={{0,1},{1,0},{2,3},{3,2},{4,5},{5,4},{6,7},{7,6},{8,9},{9,8},{10,11... | collective-permute-start | bytes 3145736 | tf_op jit(solution)/shard_map/ppermute | solution.py:144
  80.1 25.3 %collective-permute-start.12 = (bf16[128,32,128]{2,1,0:T(8,128)(2,1)S(1)}, bf16[128,32,128]{2,1,0:T(8,128)(2,1)S(1)}, u32[]{:S(2)}, u32[]{:S(2)}) collective-permute-start(bf16[128,32,128]{2,1,0:T(8,128)(2,1)S(1)} %copy-done.21), channel_id=1, source_target_pairs={{0,3},{1,2},{2,1},{3,0},{4,7},{5,6},{6,5},{7,4},{8,11},{9,10},{10,... | collective-permute-start | bytes 3145736 | tf_op jit(solution)/shard_map/ppermute | solution.py:144
  80.1 26.0 %collective-permute-start.13 = (bf16[128,32,128]{2,1,0:T(8,128)(2,1)S(1)}, bf16[128,32,128]{2,1,0:T(8,128)(2,1)S(1)}, u32[]{:S(2)}, u32[]{:S(2)}) collective-permute-start(bf16[128,32,128]{2,1,0:T(8,128)(2,1)S(1)} %copy-done.20), channel_id=1, source_target_pairs={{0,1},{1,0},{2,3},{3,2},{4,5},{5,4},{6,7},{7,6},{8,9},{9,8},{10,11... | collective-permute-start | bytes 3145736 | tf_op jit(solution)/shard_map/ppermute | solution.py:144
  81.9 25.4 %collective-permute-start.14 = (bf16[2,2,2,32,16,128]{5,4,3,2,1,0:T(8,128)(2,1)}, bf16[2,2,2,32,16,128]{5,4,3,2,1,0:T(8,128)(2,1)}, u32[]{:S(2)}, u32[]{:S(2)}) collective-permute-start(bf16[2,2,2,32,16,128]{5,4,3,2,1,0:T(8,128)(2,1)} %pad_maximum_fusion.1.refs_4_), channel_id=1, source_target_pairs={{0,4},{4,0},{8,12},{12,8},{16,20},{20,16},{24,28},{28,24},{1,5},{5... | collective-permute-start | bytes 3145736 | tf_op jit(solution)/shard_map/ppermute | solution.py:144
  83.4 23.9 %collective-permute-start.16 = (bf16[2,2,2,32,16,128]{5,4,3,2,1,0:T(8,128)(2,1)S(1)}, bf16[2,2,2,32,16,128]{5,4,3,2,1,0:T(8,128)(2,1)S(1)}, u32[]{:S(2)}, u32[]{:S(2)}) collective-permute-start(bf16[2,2,2,32,16,128]{5,4,3,2,1,0:T(8,128)(2,1)S(1)} %pad_maximum_fusion.refs_4_.refs_8_), channel_id=1, source_target_pairs={{0,1},{1,0},{2,3},{3,2},{4,5},{5,4},{6,7},{7,6},{8,9},{9,8},{10,11... | collective-permute-start | bytes 3145736 | tf_op jit(solution)/shard_map/ppermute | solution.py:144
  105.4 25.8 %collective-permute-start.19 = (bf16[128,32,128]{2,1,0:T(8,128)(2,1)}, bf16[128,32,128]{2,1,0:T(8,128)(2,1)}, u32[]{:S(2)}, u32[]{:S(2)}) collective-permute-start(bf16[128,32,128]{2,1,0:T(8,128)(2,1)} %get-tuple-element.159), channel_id=1, source_target_pairs={{0,2},{1,3},{2,0},{3,1},{4,6},{5,7},{6,4},{7,5},{8,10},{9,11},{10,... | collective-permute-start | bytes 3145736 | tf_op jit(solution)/shard_map/ppermute | solution.py:144
  108.2 24.4 %collective-permute-start.20 = (bf16[2,2,2,32,16,128]{5,4,3,2,1,0:T(8,128)(2,1)S(1)}, bf16[2,2,2,32,16,128]{5,4,3,2,1,0:T(8,128)(2,1)S(1)}, u32[]{:S(2)}, u32[]{:S(2)}) collective-permute-start(bf16[2,2,2,32,16,128]{5,4,3,2,1,0:T(8,128)(2,1)S(1)} %pad_maximum_fusion.2.refs_8_.refs_4_), channel_id=1, source_target_pairs={{0,4},{4,0},{8,12},{12,8},{16,20},{20,16},{24,28},{28,24},{1,5},{5... | collective-permute-start | bytes 3145736 | tf_op jit(solution)/shard_map/ppermute | solution.py:144
  109.7 22.9 %collective-permute-start.21 = (bf16[2,2,2,32,16,128]{5,4,3,2,1,0:T(8,128)(2,1)S(1)}, bf16[2,2,2,32,16,128]{5,4,3,2,1,0:T(8,128)(2,1)}, u32[]{:S(2)}, u32[]{:S(2)}) collective-permute-start(bf16[2,2,2,32,16,128]{5,4,3,2,1,0:T(8,128)(2,1)S(1)} %pad_maximum_fusion.2.refs_8_.refs_4_), channel_id=1, source_target_pairs={{0,1},{1,0},{2,3},{3,2},{4,5},{5,4},{6,7},{7,6},{8,9},{9,8},{10,11... | collective-permute-start | bytes 3145736 | tf_op jit(solution)/shard_map/ppermute | solution.py:144
  109.7 22.9 %collective-permute-start.22 = (bf16[2,2,2,32,16,128]{5,4,3,2,1,0:T(8,128)(2,1)}, bf16[2,2,2,32,16,128]{5,4,3,2,1,0:T(8,128)(2,1)}, u32[]{:S(2)}, u32[]{:S(2)}) collective-permute-start(bf16[2,2,2,32,16,128]{5,4,3,2,1,0:T(8,128)(2,1)} %pad_maximum_fusion.1.refs_4_), channel_id=1, source_target_pairs={{0,1},{1,0},{2,3},{3,2},{4,5},{5,4},{6,7},{7,6},{8,9},{9,8},{10,11... | collective-permute-start | bytes 3145736 | tf_op jit(solution)/shard_map/ppermute | solution.py:144
  164.4 22.8 %collective-permute-start.26 = (bf16[2,32,128,128]{3,2,1,0:T(8,128)(2,1)}, bf16[2,32,128,128]{3,2,1,0:T(8,128)(2,1)}, u32[]{:S(2)}, u32[]{:S(2)}) collective-permute-start(bf16[2,32,128,128]{3,2,1,0:T(8,128)(2,1)} %get-tuple-element.183), channel_id=1, source_target_pairs={{0,1},{1,0},{2,3},{3,2},{4,5},{5,4},{6,7},{7,6},{8,9},{9,8},{10,11... | collective-permute-start | bytes 6291464 | tf_op jit(solution)/shard_map/ppermute | solution.py:144
  164.8 25.5 %collective-permute-start.25 = (bf16[128,32,128]{2,1,0:T(8,128)(2,1)}, bf16[128,32,128]{2,1,0:T(8,128)(2,1)}, u32[]{:S(2)}, u32[]{:S(2)}) collective-permute-start(bf16[128,32,128]{2,1,0:T(8,128)(2,1)} %get-tuple-element.181), channel_id=1, source_target_pairs={{0,3},{1,2},{2,1},{3,0},{4,7},{5,6},{6,5},{7,4},{8,11},{9,10},{10,... | collective-permute-start | bytes 3145736 | tf_op jit(solution)/shard_map/ppermute | solution.py:144
  190.4 25.8 %collective-permute-start.28 = (bf16[128,32,128]{2,1,0:T(8,128)(2,1)}, bf16[128,32,128]{2,1,0:T(8,128)(2,1)}, u32[]{:S(2)}, u32[]{:S(2)}) collective-permute-start(bf16[128,32,128]{2,1,0:T(8,128)(2,1)} %get-tuple-element.196), channel_id=1, source_target_pairs={{0,2},{1,3},{2,0},{3,1},{4,6},{5,7},{6,4},{7,5},{8,10},{9,11},{10,... | collective-permute-start | bytes 3145736 | tf_op jit(solution)/shard_map/ppermute | solution.py:144
  191.4 24.7 %collective-permute-start.29 = (bf16[128,32,128]{2,1,0:T(8,128)(2,1)}, bf16[128,32,128]{2,1,0:T(8,128)(2,1)}, u32[]{:S(2)}, u32[]{:S(2)}) collective-permute-start(bf16[128,32,128]{2,1,0:T(8,128)(2,1)} %get-tuple-element.197), channel_id=1, source_target_pairs={{0,1},{1,0},{2,3},{3,2},{4,5},{5,4},{6,7},{7,6},{8,9},{9,8},{10,11... | collective-permute-start | bytes 3145736 | tf_op jit(solution)/shard_map/ppermute | solution.py:144
  191.5 25.8 %collective-permute-start.30 = (bf16[2,32,2,2,16,128]{5,4,1,3,2,0:T(8,128)(2,1)}, bf16[2,32,2,2,16,128]{5,4,1,3,2,0:T(8,128)(2,1)}, u32[]{:S(2)}, u32[]{:S(2)}) collective-permute-start(bf16[2,32,2,2,16,128]{5,4,1,3,2,0:T(8,128)(2,1)} %fusion), channel_id=1, source_target_pairs={{0,4},{4,0},{8,12},{12,8},{16,20},{20,16},{24,28},{28,24},{1,5},{5... | collective-permute-start | bytes 3145736 | tf_op jit(solution)/shard_map/ppermute | solution.py:144
  193.0 25.3 %collective-permute-start.31 = (bf16[2,32,2,2,16,128]{5,4,1,3,2,0:T(8,128)(2,1)S(1)}, bf16[2,32,2,2,16,128]{5,4,1,3,2,0:T(8,128)(2,1)}, u32[]{:S(2)}, u32[]{:S(2)}) collective-permute-start(bf16[2,32,2,2,16,128]{5,4,1,3,2,0:T(8,128)(2,1)S(1)} %fusion.1), channel_id=1, source_target_pairs={{0,8},{4,12},{8,0},{12,4},{16,24},{20,28},{24,16},{28,20},{1,9},{5... | collective-permute-start | bytes 3145736 | tf_op jit(solution)/shard_map/ppermute | solution.py:144
  218.3 31.3 %collective-permute-start.33 = (bf16[32,128,128]{2,1,0:T(8,128)(2,1)}, bf16[32,128,128]{2,1,0:T(8,128)(2,1)S(1)}, u32[]{:S(2)}, u32[]{:S(2)}) collective-permute-start(bf16[32,128,128]{2,1,0:T(8,128)(2,1)} %get-tuple-element.210), channel_id=1, source_target_pairs={{0,3},{1,2},{2,1},{3,0},{4,7},{5,6},{6,5},{7,4},{8,11},{9,10},{10,... | collective-permute-start | bytes 3145736 | tf_op jit(solution)/shard_map/ppermute | solution.py:144
  218.3 31.3 %collective-permute-start.36 = (bf16[2,32,2,2,16,128]{5,4,1,3,2,0:T(8,128)(2,1)}, bf16[2,32,2,2,16,128]{5,4,1,3,2,0:T(8,128)(2,1)}, u32[]{:S(2)}, u32[]{:S(2)}) collective-permute-start(bf16[2,32,2,2,16,128]{5,4,1,3,2,0:T(8,128)(2,1)} %fusion.2), channel_id=1, source_target_pairs={{0,4},{4,0},{8,12},{12,8},{16,20},{20,16},{24,28},{28,24},{1,5},{5... | collective-permute-start | bytes 3145736 | tf_op jit(solution)/shard_map/ppermute | solution.py:144
  221.3 26.8 %collective-permute-start.35 = (bf16[2,32,2,16,128]{4,3,1,2,0:T(8,128)(2,1)}, bf16[2,32,2,16,128]{4,3,1,2,0:T(8,128)(2,1)}, u32[]{:S(2)}, u32[]{:S(2)}) collective-permute-start(bf16[2,32,2,16,128]{4,3,1,2,0:T(8,128)(2,1)} %fusion.4), channel_id=1, source_target_pairs={{0,16},{4,20},{8,24},{12,28},{16,0},{20,4},{24,8},{28,12},{1,17},{... | collective-permute-start | bytes 1572872 | tf_op jit(solution)/shard_map/ppermute | solution.py:144
  223.8 25.8 %collective-permute-start.34 = (bf16[2,32,2,16,128]{4,3,1,2,0:T(8,128)(2,1)}, bf16[2,32,2,16,128]{4,3,1,2,0:T(8,128)(2,1)}, u32[]{:S(2)}, u32[]{:S(2)}) collective-permute-start(bf16[2,32,2,16,128]{4,3,1,2,0:T(8,128)(2,1)} %fusion.5), channel_id=1, source_target_pairs={{0,8},{4,12},{8,0},{12,4},{16,24},{20,28},{24,16},{28,20},{1,9},{5... | collective-permute-start | bytes 1572872 | tf_op jit(solution)/shard_map/ppermute | solution.py:144
  257.5 26.4 %collective-permute-start.37 = (bf16[32,128,128]{2,1,0:T(8,128)(2,1)S(1)}, bf16[32,128,128]{2,1,0:T(8,128)(2,1)}, u32[]{:S(2)}, u32[]{:S(2)}) collective-permute-start(bf16[32,128,128]{2,1,0:T(8,128)(2,1)S(1)} %copy-done.19), channel_id=1, source_target_pairs={{0,1},{1,0},{2,3},{3,2},{4,5},{5,4},{6,7},{7,6},{8,9},{9,8},{10,11... | collective-permute-start | bytes 3145736 | tf_op jit(solution)/shard_map/ppermute | solution.py:144
  257.5 26.4 %collective-permute-start.38 = (bf16[32,128,128]{2,1,0:T(8,128)(2,1)S(1)}, bf16[32,128,128]{2,1,0:T(8,128)(2,1)}, u32[]{:S(2)}, u32[]{:S(2)}) collective-permute-start(bf16[32,128,128]{2,1,0:T(8,128)(2,1)S(1)} %copy-done.18), channel_id=1, source_target_pairs={{0,2},{1,3},{2,0},{3,1},{4,6},{5,7},{6,4},{7,5},{8,10},{9,11},{10,... | collective-permute-start | bytes 3145736 | tf_op jit(solution)/shard_map/ppermute | solution.py:144
  (45 other events, 597.2 us)

commit v12 on v11

--- a/solution.py
+++ b/solution.py
@@ -303,9 +303,42 @@
     return lambda k: jnp.concatenate([whole[(*at, k)] for at in places], axis=0)
 
 
-def whole_scratch(pieces):
+def whole_scratch(pieces, grouped=False):
     dims = (len(pieces), len(pieces[0])) + pieces[0][0].shape
-    return [pltpu.VMEM(dims, BF16), pltpu.SemaphoreType.DMA((dims[0] * dims[1],))]
+    sems = (dims[0], dims[1], dims[-4]) if grouped else (dims[0] * dims[1],)
+    return [pltpu.VMEM(dims, BF16), pltpu.SemaphoreType.DMA(sems)]
+
+
+def group_of(ref, y):
+    return ref.at[(slice(None),) * (len(ref.shape) - 4) + (y,)]
+
+
+def group_copies(pieces, whole, sems):
+    copies = []
+    for c, row in enumerate(pieces):
+        for d, ref in enumerate(row):
+            for y in range(ref.shape[-4]):
+                dst = group_of(whole.at[c, d], y)
+                copies.append(pltpu.make_async_copy(group_of(ref, y), dst, sems.at[c, d, y]))
+    return copies
+
+
+def copies_of_group(place, pos_ref, pieces, whole, sems, group):
+    y = turned_back(pos_ref[0], group // place.near, place.far)
+    c = turned_back(pos_ref[1], lax.rem(group, place.near), place.near)
+    copies = []
+    for d, ref in enumerate(pieces[0]):
+        dst = group_of(whole.at[c, d], y)
+        copies.append(pltpu.make_async_copy(group_of(ref, y), dst, sems.at[c, d, y]))
+    return copies
+
+
+def share_group(place, pos_ref, parts, whole, sems, group, per):
+    at = pl.ds(group * per, per)
+    return [
+        pltpu.make_async_copy(ref.at[at], whole.at[place.source(pos_ref, n), at], sems.at[n, group])
+        for n, ref in enumerate(parts)
+    ]
 
 
 def share_copies(place, pos_ref, parts, whole, sems):
@@ -570,10 +603,18 @@
 
     @pl.when((phase == 0) & (j == 0))
     def _():
-        copies = share_copies(place, pos_ref, s_parts, s_all, s_sems) + piece_copies(one, one_all, one_sems)
-        run(copies)
-        finish(copies)
+        run(group_copies(one, one_all, one_sems))
+        for group in range(share):
+            run(share_group(place, pos_ref, s_parts, s_all, s_sems, group, per))
+
+    @pl.when((phase == 0) & (j == min(1, share - 1)))
+    def _():
         run(second())
+
+    @pl.when(phase == 0)
+    def _():
+        finish(copies_of_group(place, pos_ref, one, one_all, one_sems, j))
+        finish(share_group(place, pos_ref, s_parts, s_all, s_sems, j, per))
 
     @pl.when(phase == 0)
     def _():
@@ -655,9 +696,9 @@
         + [
             pltpu.VMEM((home, blocks, cut), BF16),
             pltpu.VMEM((share, blocks, home, cut), BF16),
-            pltpu.SemaphoreType.DMA((share,)),
+            pltpu.SemaphoreType.DMA((share, share)),
         ]
-        + whole_scratch(right_one)
+        + whole_scratch(right_one, True)
         + whole_scratch(left_two),
         (*s_mid, *flat(right_one), *flat(left_two), e_mid),
         us=26,
@@ -682,10 +723,15 @@
 
     @pl.when((phase == 0) & (j == 0))
     def _():
-        copies = piece_copies(left, left_all, left_sems)
-        run(copies)
-        finish(copies)
+        run(group_copies(left, left_all, left_sems))
+
+    @pl.when((phase == 0) & (j == min(1, share - 1)))
+    def _():
         run(second())
+
+    @pl.when(phase == 0)
+    def _():
+        finish(copies_of_group(place, pos_ref, left, left_all, left_sems, j))
 
     @pl.when(phase == 0)
     def _():
@@ -745,7 +791,7 @@
             pltpu.VMEM((share, blocks, home, cut), BF16),
             pltpu.SemaphoreType.DMA((share,)),
         ]
-        + whole_scratch(left_two)
+        + whole_scratch(left_two, True)
         + whole_scratch(right_two),
         (*g_mid, *flat(left_two), *flat(right_two), act),
         us=20,

time: 307 us -> 307 us (level)
  no operation moved by 1% of the time
where the time goes in v12:
time: 307 us; the launch traced here: 306 us
  waiting for transfers between devices  121 us (39%)
  Pallas kernels  96.5 us (31%)
  starting transfers between devices  47.2 us (15%)
  other arithmetic  34.7 us (11%)
  local copies, waits for them, and re-layouts  4.88 us (2%)
    ppermute x47, waiting for transfers between devices, send(): self.last = lax.ppermute(value, self.axis, pairs)  121 us
    pallas_call x10, Pallas kernels, call(): pl.pallas_call(body, out_shape=out, grid_spec=spec, compiler_params=pltpu...  96.5 us
    ppermute x47, starting transfers between devices, send(): self.last = lax.ppermute(value, self.axis, pairs)  47.2 us
    convert_element_type x14, other arithmetic, parts(): self.cut(ring, lax.rem(ring.here() + step, ring.size)).astype(BF16)  21.2 us
    another operation x9, other arithmetic, gather(): return got if n == 0 else jnp.stack(got)  7.22 us
  transfers between devices with their start and end apart: 47, of which 27 were waited for; matrix products, arithmetic and copies ran while one was open for 11% of the time, Pallas kernels for 23%

profile of v12, /device:TPU:0, one launch (start us, length us, event | category | flops | bytes accessed | tf_op | source)
XLA Modules:
  0.0 305.7 jit_solution(15988539533087685655)
XLA Ops:
  8.0 3.3 %shard_map.109 = bf16[128,32,128]{2,1,0:T(8,128)(2,1)} custom-call(s32[5]{0:T(128)} %stack.116.pos_ref, bf16[32,128,512]{2,1,0:T(8,128)(2,1)} %bitcast.189), custom_call_target="tpu_custom_call" | custom-call | bytes 4200000 | tf_op jit(solution)/shard_map/pallas_call | solution.py:84
  18.5 9.6 %collective-permute-done.5 = bf16[2,32,16,128]{3,2,1,0:T(8,128)(2,1)S(1)} collective-permute-done((bf16[2,32,16,128]{3,2,1,0:T(8,128)(2,1)S(1)}, bf16[2,32,16,128]{3,2,1,0:T(8,128)(2,1)S(1)}, u32[]{:S(2)}, u32[]{:S(2)}) %collective-permute-start.5) | collective-permute-done | bytes 262176 | tf_op jit(solution)/shard_map/ppermute | solution.py:144
  29.8 3.2 %collective-permute-start.7 = (bf16[2,32,16,128]{3,2,1,0:T(8,128)(2,1)S(1)}, bf16[2,32,16,128]{3,2,1,0:T(8,128)(2,1)}, u32[]{:S(2)}, u32[]{:S(2)}) collective-permute-start(bf16[2,32,16,128]{3,2,1,0:T(8,128)(2,1)S(1)} %get-tuple-element.137), channel_id=1, source_target_pairs={{0,16},{4,20},{8,24},{12,28},{16,0},{20,4},{24,8},{28,12},{1,17},{... | collective-permute-start | bytes 786440 | tf_op jit(solution)/shard_map/ppermute | solution.py:144
  34.6 3.2 %shard_map.110.refs_0_ = bf16[128,32,128]{2,1,0:T(8,128)(2,1)} custom-call(s32[5]{0:T(128)} %stack.116.pos_ref, bf16[32,128,512]{2,1,0:T(8,128)(2,1)} %bitcast.190), custom_call_target="tpu_custom_call" | custom-call | bytes 4200000 | tf_op jit(solution)/shard_map/pallas_call | solution.py:84
  37.8 3.2 %shard_map.111 = bf16[128,32,128]{2,1,0:T(8,128)(2,1)} custom-call(s32[5]{0:T(128)} %stack.116.pos_ref, bf16[32,128,512]{2,1,0:T(8,128)(2,1)} %bitcast.191), custom_call_target="tpu_custom_call" | custom-call | bytes 4200000 | tf_op jit(solution)/shard_map/pallas_call | solution.py:84
  41.0 3.2 %shard_map.112 = bf16[128,32,128]{2,1,0:T(8,128)(2,1)} custom-call(s32[5]{0:T(128)} %stack.116.pos_ref, bf16[32,128,512]{2,1,0:T(8,128)(2,1)} %bitcast.192), custom_call_target="tpu_custom_call" | custom-call | bytes 4200000 | tf_op jit(solution)/shard_map/pallas_call | solution.py:84
  44.2 3.7 %collective-permute-done.7 = bf16[2,32,16,128]{3,2,1,0:T(8,128)(2,1)} collective-permute-done((bf16[2,32,16,128]{3,2,1,0:T(8,128)(2,1)S(1)}, bf16[2,32,16,128]{3,2,1,0:T(8,128)(2,1)}, u32[]{:S(2)}, u32[]{:S(2)}) %collective-permute-start.7) | collective-permute-done | bytes 262176 | tf_op jit(solution)/shard_map/ppermute | solution.py:144
  57.9 9.4 %shard_map.113 = (bf16[128,32,128]{2,1,0:T(8,128)(2,1)}, bf16[128,32,128]{2,1,0:T(8,128)(2,1)}, bf16[128,32,128]{2,1,0:T(8,128)(2,1)}, bf16[128,32,128]{2,1,0:T(8,128)(2,1)}) custom-call(s32[5]{0:T(128)} %stack.116.pos_ref, bf16[32,128,512]{2,1,0:T(8,128)(2,1)} %bitcast.194, bf16[2,2,32,16,128]{4,3,2,1,0:T(8,128)(2,1)} %copy-done.2, ...), custom_call_target="tpu_custom_call" | custom-call | bytes 9600000 | tf_op jit(solution)/shard_map/pallas_call | solution.py:84
  67.4 6.0 %collective-permute-done.11 = bf16[2,32,16,128]{3,2,1,0:T(8,128)(2,1)} collective-permute-done((bf16[2,32,16,128]{3,2,1,0:T(8,128)(2,1)}, bf16[2,32,16,128]{3,2,1,0:T(8,128)(2,1)}, u32[]{:S(2)}, u32[]{:S(2)}) %collective-permute-start.11) | collective-permute-done | bytes 262176 | tf_op jit(solution)/shard_map/ppermute | solution.py:144
  76.8 3.3 %collective-permute-start.15 = (bf16[2,2,32,16,128]{4,3,2,1,0:T(8,128)(2,1)S(1)}, bf16[2,2,32,16,128]{4,3,2,1,0:T(8,128)(2,1)S(1)}, u32[]{:S(2)}, u32[]{:S(2)}) collective-permute-start(bf16[2,2,32,16,128]{4,3,2,1,0:T(8,128)(2,1)S(1)} %pad_maximum_fusion.7), channel_id=1, source_target_pairs={{0,8},{4,12},{8,0},{12,4},{16,24},{20,28},{24,16},{28,20},{1,9},{5... | collective-permute-start | bytes 1572872 | tf_op jit(solution)/shard_map/ppermute | solution.py:144
  83.4 8.2 %collective-permute-done.15 = bf16[2,2,32,16,128]{4,3,2,1,0:T(8,128)(2,1)S(1)} collective-permute-done((bf16[2,2,32,16,128]{4,3,2,1,0:T(8,128)(2,1)S(1)}, bf16[2,2,32,16,128]{4,3,2,1,0:T(8,128)(2,1)S(1)}, u32[]{:S(2)}, u32[]{:S(2)}) %collective-permute-start.15) | collective-permute-done | bytes 524320 | tf_op jit(solution)/shard_map/ppermute | solution.py:144
  91.7 13.7 %collective-permute-done.12.refs_3_ = bf16[128,32,128]{2,1,0:T(8,128)(2,1)S(1)} collective-permute-done((bf16[128,32,128]{2,1,0:T(8,128)(2,1)S(1)}, bf16[128,32,128]{2,1,0:T(8,128)(2,1)S(1)}, u32[]{:S(2)}, u32[]{:S(2)}) %collective-permute-start.12) | collective-permute-done | bytes 1048608 | tf_op jit(solution)/shard_map/ppermute | solution.py:144
  110.3 9.8 %shard_map.114.refs_12_ = bf16[128,128,128]{2,1,0:T(8,128)(2,1)} custom-call(s32[5]{0:T(128)} %stack.116.pos_ref, bf16[128,32,128]{2,1,0:T(8,128)(2,1)} %shard_map.110.refs_0_, bf16[128,32,128]{2,1,0:T(8,128)(2,1)} %collective-permute-done.18.refs_1_, bf16[128,32,128]{2,1,0:T(8,128)(2,1)} %copy-done.4, bf16[128,32,128]{2,1,0:T(8,128)(2,1)} %copy-done.3, ...), custom_call_target="tpu_custom_call" | custom-call | bytes 12000000 | tf_op jit(solution)/shard_map/pallas_call | solution.py:84
  120.2 11.0 %collective-permute-done.19.refs_2_ = bf16[128,32,128]{2,1,0:T(8,128)(2,1)} collective-permute-done((bf16[128,32,128]{2,1,0:T(8,128)(2,1)}, bf16[128,32,128]{2,1,0:T(8,128)(2,1)}, u32[]{:S(2)}, u32[]{:S(2)}) %collective-permute-start.19) | collective-permute-done | bytes 1048608 | tf_op jit(solution)/shard_map/ppermute | solution.py:144
  136.4 26.6 %shard_map.115 = (bf16[128,128,128]{2,1,0:T(8,128)(2,1)}, bf16[2,32,128,128]{3,2,1,0:T(8,128)(2,1)}, bf16[2,32,128,128]{3,2,1,0:T(8,128)(2,1)}, bf16[2,32,128,12...) custom-call(s32[5]{0:T(128)} %stack.116.pos_ref, ...), custom_call_target="tpu_custom_call" | custom-call | bytes 31200000 | tf_op jit(solution)/shard_map/pallas_call | solution.py:84
  165.4 19.4 %shard_map.116 = (bf16[2,32,128,128]{3,2,1,0:T(8,128)(2,1)}, bf16[2,32,128,128]{3,2,1,0:T(8,128)(2,1)}, bf16[32,128,128]{2,1,0:T(8,128)(2,1)}, bf16[32,128,128]{...) custom-call(s32[5]{0:T(128)} %stack.116.pos_ref, ...), custom_call_target="tpu_custom_call" | custom-call | bytes 24000000 | tf_op jit(solution)/shard_map/pallas_call | solution.py:84
  196.9 18.5 %collective-permute-done.28.refs_2_ = bf16[128,32,128]{2,1,0:T(8,128)(2,1)} collective-permute-done((bf16[128,32,128]{2,1,0:T(8,128)(2,1)}, bf16[128,32,128]{2,1,0:T(8,128)(2,1)}, u32[]{:S(2)}, u32[]{:S(2)}) %collective-permute-start.28) | collective-permute-done | bytes 1048608 | tf_op jit(solution)/shard_map/ppermute | solution.py:144
  225.1 11.3 %shard_map.117 = (bf16[32,128,512]{2,1,0:T(8,128)(2,1)}, bf16[32,128,128]{2,1,0:T(8,128)(2,1)}) custom-call(s32[5]{0:T(128)} %stack.116.pos_ref, bf16[128,32,128]{2,1,0:T(8,128)(2,1)} %get-tuple-element.220.refs_0_, bf16[128,32,128]{2,1,0:T(8,128)(2,1)} %collective-permute-done.29.refs_1_, bf16[128,32,128]{2,1,0:T(8,128)(2,1)} %collective-permute-done.28.refs_2_, ...), custom_call_target="tpu_custom_call" | custom-call | bytes 12000000 | tf_op jit(solution)/shard_map/pallas_call | solution.py:84
  237.7 9.9 %collective-permute-done.35 = bf16[2,32,2,16,128]{4,3,1,2,0:T(8,128)(2,1)} collective-permute-done((bf16[2,32,2,16,128]{4,3,1,2,0:T(8,128)(2,1)}, bf16[2,32,2,16,128]{4,3,1,2,0:T(8,128)(2,1)}, u32[]{:S(2)}, u32[]{:S(2)}) %collective-permute-start.35) | collective-permute-done | bytes 524320 | tf_op jit(solution)/shard_map/ppermute | solution.py:144
  259.4 5.5 %collective-permute-done.42 = bf16[2,32,16,128]{3,2,1,0:T(8,128)(2,1)S(1)} collective-permute-done((bf16[2,32,16,128]{3,2,1,0:T(8,128)(2,1)S(1)}, bf16[2,32,16,128]{3,2,1,0:T(8,128)(2,1)S(1)}, u32[]{:S(2)}, u32[]{:S(2)}) %collective-permute-start.42) | collective-permute-done | bytes 262176 | tf_op jit(solution)/shard_map/ppermute | solution.py:144
  267.9 5.7 %collective-permute-done.40 = bf16[2,32,2,16,128]{4,3,1,2,0:T(8,128)(2,1)S(1)} collective-permute-done((bf16[2,32,2,16,128]{4,3,1,2,0:T(8,128)(2,1)S(1)}, bf16[2,32,2,16,128]{4,3,1,2,0:T(8,128)(2,1)S(1)}, u32[]{:S(2)}, u32[]{:S(2)}) %collective-permute-start.40) | collective-permute-done | bytes 524320 | tf_op jit(solution)/shard_map/ppermute | solution.py:144
  276.3 4.0 %collective-permute-done.41 = bf16[32,2,16,128]{3,2,0,1:T(8,128)(2,1)S(1)} collective-permute-done((bf16[32,2,16,128]{3,2,0,1:T(8,128)(2,1)S(1)}, bf16[32,2,16,128]{3,2,0,1:T(8,128)(2,1)S(1)}, u32[]{:S(2)}, u32[]{:S(2)}) %collective-permute-start.41) | collective-permute-done | bytes 262176 | tf_op jit(solution)/shard_map/ppermute | solution.py:144
  283.3 7.0 %shard_map.118 = bf16[32,128,512]{2,1,0:T(8,128)(2,1)} custom-call(s32[5]{0:T(128)} %stack.116.pos_ref, bf16[32,128,128]{2,1,0:T(8,128)(2,1)} %get-tuple-element.231.refs_0_, bf16[32,128,128]{2,1,0:T(8,128)(2,1)} %collective-permute-done.37.refs_1_, bf16[32,128,128]{2,1,0:T(8,128)(2,1)} %collective-permute-done.38.refs_2_, bf16[32,128,128]{2,1,0:T(8,128)(2,1)} %copy-done.11, ...), custom_call_target="tpu_custom_call" | custom-call | bytes 7200000 | tf_op jit(solution)/shard_map/pallas_call | solution.py:84
  296.2 6.7 %collective-permute-done.44 = bf16[32,16,128]{2,1,0:T(8,128)(2,1)S(1)} collective-permute-done((bf16[32,16,128]{2,1,0:T(8,128)(2,1)S(1)}, bf16[32,16,128]{2,1,0:T(8,128)(2,1)S(1)}, u32[]{:S(2)}, u32[]{:S(2)}) %collective-permute-start.44) | collective-permute-done | bytes 131104 | tf_op jit(solution)/shard_map/ppermute | solution.py:144
  (158 shorter events, 99.2 us)
Async XLA Ops:
  16.8 34.6 %collective-permute-start = (bf16[128,32,128]{2,1,0:T(8,128)(2,1)}, bf16[128,32,128]{2,1,0:T(8,128)(2,1)S(1)}, u32[]{:S(2)}, u32[]{:S(2)}) collective-permute-start(bf16[128,32,128]{2,1,0:T(8,128)(2,1)} %shard_map.109), channel_id=1, source_target_pairs={{0,3},{1,2},{2,1},{3,0},{4,7},{5,6},{6,5},{7,4},{8,11},{9,10},{10,... | collective-permute-start | bytes 3145736 | tf_op jit(solution)/shard_map/ppermute | solution.py:144
  51.5 25.2 %collective-permute-start.8 = (bf16[128,32,128]{2,1,0:T(8,128)(2,1)}, bf16[128,32,128]{2,1,0:T(8,128)(2,1)S(1)}, u32[]{:S(2)}, u32[]{:S(2)}) collective-permute-start(bf16[128,32,128]{2,1,0:T(8,128)(2,1)} %shard_map.112), channel_id=1, source_target_pairs={{0,2},{1,3},{2,0},{3,1},{4,6},{5,7},{6,4},{7,5},{8,10},{9,11},{10,... | collective-permute-start | bytes 3145736 | tf_op jit(solution)/shard_map/ppermute | solution.py:144
  52.6 24.2 %collective-permute-start.9 = (bf16[2,2,2,32,16,128]{5,4,3,2,1,0:T(8,128)(2,1)S(1)}, bf16[2,2,2,32,16,128]{5,4,3,2,1,0:T(8,128)(2,1)}, u32[]{:S(2)}, u32[]{:S(2)}) collective-permute-start(bf16[2,2,2,32,16,128]{5,4,3,2,1,0:T(8,128)(2,1)S(1)} %pad_maximum_fusion.refs_4_.refs_8_), channel_id=1, source_target_pairs={{0,4},{4,0},{8,12},{12,8},{16,20},{20,16},{24,28},{28,24},{1,5},{5... | collective-permute-start | bytes 3145736 | tf_op jit(solution)/shard_map/ppermute | solution.py:144
  57.9 25.5 %collective-permute-start.18 = (bf16[128,32,128]{2,1,0:T(8,128)(2,1)}, bf16[128,32,128]{2,1,0:T(8,128)(2,1)}, u32[]{:S(2)}, u32[]{:S(2)}) collective-permute-start(bf16[128,32,128]{2,1,0:T(8,128)(2,1)} %shard_map.111), channel_id=1, source_target_pairs={{0,1},{1,0},{2,3},{3,2},{4,5},{5,4},{6,7},{7,6},{8,9},{9,8},{10,11... | collective-permute-start | bytes 3145736 | tf_op jit(solution)/shard_map/ppermute | solution.py:144
  80.1 25.3 %collective-permute-start.12 = (bf16[128,32,128]{2,1,0:T(8,128)(2,1)S(1)}, bf16[128,32,128]{2,1,0:T(8,128)(2,1)S(1)}, u32[]{:S(2)}, u32[]{:S(2)}) collective-permute-start(bf16[128,32,128]{2,1,0:T(8,128)(2,1)S(1)} %copy-done.21), channel_id=1, source_target_pairs={{0,3},{1,2},{2,1},{3,0},{4,7},{5,6},{6,5},{7,4},{8,11},{9,10},{10,... | collective-permute-start | bytes 3145736 | tf_op jit(solution)/shard_map/ppermute | solution.py:144
  80.1 26.0 %collective-permute-start.13 = (bf16[128,32,128]{2,1,0:T(8,128)(2,1)S(1)}, bf16[128,32,128]{2,1,0:T(8,128)(2,1)S(1)}, u32[]{:S(2)}, u32[]{:S(2)}) collective-permute-start(bf16[128,32,128]{2,1,0:T(8,128)(2,1)S(1)} %copy-done.20), channel_id=1, source_target_pairs={{0,1},{1,0},{2,3},{3,2},{4,5},{5,4},{6,7},{7,6},{8,9},{9,8},{10,11... | collective-permute-start | bytes 3145736 | tf_op jit(solution)/shard_map/ppermute | solution.py:144
  81.9 25.4 %collective-permute-start.14 = (bf16[2,2,2,32,16,128]{5,4,3,2,1,0:T(8,128)(2,1)}, bf16[2,2,2,32,16,128]{5,4,3,2,1,0:T(8,128)(2,1)}, u32[]{:S(2)}, u32[]{:S(2)}) collective-permute-start(bf16[2,2,2,32,16,128]{5,4,3,2,1,0:T(8,128)(2,1)} %pad_maximum_fusion.1.refs_4_), channel_id=1, source_target_pairs={{0,4},{4,0},{8,12},{12,8},{16,20},{20,16},{24,28},{28,24},{1,5},{5... | collective-permute-start | bytes 3145736 | tf_op jit(solution)/shard_map/ppermute | solution.py:144
  83.4 23.9 %collective-permute-start.16 = (bf16[2,2,2,32,16,128]{5,4,3,2,1,0:T(8,128)(2,1)S(1)}, bf16[2,2,2,32,16,128]{5,4,3,2,1,0:T(8,128)(2,1)S(1)}, u32[]{:S(2)}, u32[]{:S(2)}) collective-permute-start(bf16[2,2,2,32,16,128]{5,4,3,2,1,0:T(8,128)(2,1)S(1)} %pad_maximum_fusion.refs_4_.refs_8_), channel_id=1, source_target_pairs={{0,1},{1,0},{2,3},{3,2},{4,5},{5,4},{6,7},{7,6},{8,9},{9,8},{10,11... | collective-permute-start | bytes 3145736 | tf_op jit(solution)/shard_map/ppermute | solution.py:144
  105.4 25.8 %collective-permute-start.19 = (bf16[128,32,128]{2,1,0:T(8,128)(2,1)}, bf16[128,32,128]{2,1,0:T(8,128)(2,1)}, u32[]{:S(2)}, u32[]{:S(2)}) collective-permute-start(bf16[128,32,128]{2,1,0:T(8,128)(2,1)} %get-tuple-element.159), channel_id=1, source_target_pairs={{0,2},{1,3},{2,0},{3,1},{4,6},{5,7},{6,4},{7,5},{8,10},{9,11},{10,... | collective-permute-start | bytes 3145736 | tf_op jit(solution)/shard_map/ppermute | solution.py:144
  108.2 24.4 %collective-permute-start.20 = (bf16[2,2,2,32,16,128]{5,4,3,2,1,0:T(8,128)(2,1)S(1)}, bf16[2,2,2,32,16,128]{5,4,3,2,1,0:T(8,128)(2,1)S(1)}, u32[]{:S(2)}, u32[]{:S(2)}) collective-permute-start(bf16[2,2,2,32,16,128]{5,4,3,2,1,0:T(8,128)(2,1)S(1)} %pad_maximum_fusion.2.refs_8_.refs_4_), channel_id=1, source_target_pairs={{0,4},{4,0},{8,12},{12,8},{16,20},{20,16},{24,28},{28,24},{1,5},{5... | collective-permute-start | bytes 3145736 | tf_op jit(solution)/shard_map/ppermute | solution.py:144
  109.7 22.9 %collective-permute-start.21 = (bf16[2,2,2,32,16,128]{5,4,3,2,1,0:T(8,128)(2,1)S(1)}, bf16[2,2,2,32,16,128]{5,4,3,2,1,0:T(8,128)(2,1)}, u32[]{:S(2)}, u32[]{:S(2)}) collective-permute-start(bf16[2,2,2,32,16,128]{5,4,3,2,1,0:T(8,128)(2,1)S(1)} %pad_maximum_fusion.2.refs_8_.refs_4_), channel_id=1, source_target_pairs={{0,1},{1,0},{2,3},{3,2},{4,5},{5,4},{6,7},{7,6},{8,9},{9,8},{10,11... | collective-permute-start | bytes 3145736 | tf_op jit(solution)/shard_map/ppermute | solution.py:144
  109.7 22.9 %collective-permute-start.22 = (bf16[2,2,2,32,16,128]{5,4,3,2,1,0:T(8,128)(2,1)}, bf16[2,2,2,32,16,128]{5,4,3,2,1,0:T(8,128)(2,1)}, u32[]{:S(2)}, u32[]{:S(2)}) collective-permute-start(bf16[2,2,2,32,16,128]{5,4,3,2,1,0:T(8,128)(2,1)} %pad_maximum_fusion.1.refs_4_), channel_id=1, source_target_pairs={{0,1},{1,0},{2,3},{3,2},{4,5},{5,4},{6,7},{7,6},{8,9},{9,8},{10,11... | collective-permute-start | bytes 3145736 | tf_op jit(solution)/shard_map/ppermute | solution.py:144
  164.1 22.5 %collective-permute-start.26 = (bf16[2,32,128,128]{3,2,1,0:T(8,128)(2,1)}, bf16[2,32,128,128]{3,2,1,0:T(8,128)(2,1)}, u32[]{:S(2)}, u32[]{:S(2)}) collective-permute-start(bf16[2,32,128,128]{3,2,1,0:T(8,128)(2,1)} %get-tuple-element.183), channel_id=1, source_target_pairs={{0,1},{1,0},{2,3},{3,2},{4,5},{5,4},{6,7},{7,6},{8,9},{9,8},{10,11... | collective-permute-start | bytes 6291464 | tf_op jit(solution)/shard_map/ppermute | solution.py:144
  164.2 25.2 %collective-permute-start.25 = (bf16[128,32,128]{2,1,0:T(8,128)(2,1)}, bf16[128,32,128]{2,1,0:T(8,128)(2,1)}, u32[]{:S(2)}, u32[]{:S(2)}) collective-permute-start(bf16[128,32,128]{2,1,0:T(8,128)(2,1)} %get-tuple-element.181), channel_id=1, source_target_pairs={{0,3},{1,2},{2,1},{3,0},{4,7},{5,6},{6,5},{7,4},{8,11},{9,10},{10,... | collective-permute-start | bytes 3145736 | tf_op jit(solution)/shard_map/ppermute | solution.py:144
  189.9 25.4 %collective-permute-start.28 = (bf16[128,32,128]{2,1,0:T(8,128)(2,1)}, bf16[128,32,128]{2,1,0:T(8,128)(2,1)}, u32[]{:S(2)}, u32[]{:S(2)}) collective-permute-start(bf16[128,32,128]{2,1,0:T(8,128)(2,1)} %get-tuple-element.196), channel_id=1, source_target_pairs={{0,2},{1,3},{2,0},{3,1},{4,6},{5,7},{6,4},{7,5},{8,10},{9,11},{10,... | collective-permute-start | bytes 3145736 | tf_op jit(solution)/shard_map/ppermute | solution.py:144
  191.0 24.4 %collective-permute-start.29 = (bf16[128,32,128]{2,1,0:T(8,128)(2,1)}, bf16[128,32,128]{2,1,0:T(8,128)(2,1)}, u32[]{:S(2)}, u32[]{:S(2)}) collective-permute-start(bf16[128,32,128]{2,1,0:T(8,128)(2,1)} %get-tuple-element.197), channel_id=1, source_target_pairs={{0,1},{1,0},{2,3},{3,2},{4,5},{5,4},{6,7},{7,6},{8,9},{9,8},{10,11... | collective-permute-start | bytes 3145736 | tf_op jit(solution)/shard_map/ppermute | solution.py:144
  191.0 25.9 %collective-permute-start.30 = (bf16[2,32,2,2,16,128]{5,4,1,3,2,0:T(8,128)(2,1)}, bf16[2,32,2,2,16,128]{5,4,1,3,2,0:T(8,128)(2,1)}, u32[]{:S(2)}, u32[]{:S(2)}) collective-permute-start(bf16[2,32,2,2,16,128]{5,4,1,3,2,0:T(8,128)(2,1)} %fusion), channel_id=1, source_target_pairs={{0,4},{4,0},{8,12},{12,8},{16,20},{20,16},{24,28},{28,24},{1,5},{5... | collective-permute-start | bytes 3145736 | tf_op jit(solution)/shard_map/ppermute | solution.py:144
  192.5 25.4 %collective-permute-start.31 = (bf16[2,32,2,2,16,128]{5,4,1,3,2,0:T(8,128)(2,1)S(1)}, bf16[2,32,2,2,16,128]{5,4,1,3,2,0:T(8,128)(2,1)}, u32[]{:S(2)}, u32[]{:S(2)}) collective-permute-start(bf16[2,32,2,2,16,128]{5,4,1,3,2,0:T(8,128)(2,1)S(1)} %fusion.1), channel_id=1, source_target_pairs={{0,8},{4,12},{8,0},{12,4},{16,24},{20,28},{24,16},{28,20},{1,9},{5... | collective-permute-start | bytes 3145736 | tf_op jit(solution)/shard_map/ppermute | solution.py:144
  217.9 31.3 %collective-permute-start.33 = (bf16[32,128,128]{2,1,0:T(8,128)(2,1)}, bf16[32,128,128]{2,1,0:T(8,128)(2,1)S(1)}, u32[]{:S(2)}, u32[]{:S(2)}) collective-permute-start(bf16[32,128,128]{2,1,0:T(8,128)(2,1)} %get-tuple-element.210), channel_id=1, source_target_pairs={{0,3},{1,2},{2,1},{3,0},{4,7},{5,6},{6,5},{7,4},{8,11},{9,10},{10,... | collective-permute-start | bytes 3145736 | tf_op jit(solution)/shard_map/ppermute | solution.py:144
  217.9 31.2 %collective-permute-start.36 = (bf16[2,32,2,2,16,128]{5,4,1,3,2,0:T(8,128)(2,1)}, bf16[2,32,2,2,16,128]{5,4,1,3,2,0:T(8,128)(2,1)}, u32[]{:S(2)}, u32[]{:S(2)}) collective-permute-start(bf16[2,32,2,2,16,128]{5,4,1,3,2,0:T(8,128)(2,1)} %fusion.2), channel_id=1, source_target_pairs={{0,4},{4,0},{8,12},{12,8},{16,20},{20,16},{24,28},{28,24},{1,5},{5... | collective-permute-start | bytes 3145736 | tf_op jit(solution)/shard_map/ppermute | solution.py:144
  220.9 26.6 %collective-permute-start.35 = (bf16[2,32,2,16,128]{4,3,1,2,0:T(8,128)(2,1)}, bf16[2,32,2,16,128]{4,3,1,2,0:T(8,128)(2,1)}, u32[]{:S(2)}, u32[]{:S(2)}) collective-permute-start(bf16[2,32,2,16,128]{4,3,1,2,0:T(8,128)(2,1)} %fusion.4), channel_id=1, source_target_pairs={{0,16},{4,20},{8,24},{12,28},{16,0},{20,4},{24,8},{28,12},{1,17},{... | collective-permute-start | bytes 1572872 | tf_op jit(solution)/shard_map/ppermute | solution.py:144
  223.4 25.7 %collective-permute-start.34 = (bf16[2,32,2,16,128]{4,3,1,2,0:T(8,128)(2,1)}, bf16[2,32,2,16,128]{4,3,1,2,0:T(8,128)(2,1)}, u32[]{:S(2)}, u32[]{:S(2)}) collective-permute-start(bf16[2,32,2,16,128]{4,3,1,2,0:T(8,128)(2,1)} %fusion.5), channel_id=1, source_target_pairs={{0,8},{4,12},{8,0},{12,4},{16,24},{20,28},{24,16},{28,20},{1,9},{5... | collective-permute-start | bytes 1572872 | tf_op jit(solution)/shard_map/ppermute | solution.py:144
  257.1 26.2 %collective-permute-start.37 = (bf16[32,128,128]{2,1,0:T(8,128)(2,1)S(1)}, bf16[32,128,128]{2,1,0:T(8,128)(2,1)}, u32[]{:S(2)}, u32[]{:S(2)}) collective-permute-start(bf16[32,128,128]{2,1,0:T(8,128)(2,1)S(1)} %copy-done.19), channel_id=1, source_target_pairs={{0,1},{1,0},{2,3},{3,2},{4,5},{5,4},{6,7},{7,6},{8,9},{9,8},{10,11... | collective-permute-start | bytes 3145736 | tf_op jit(solution)/shard_map/ppermute | solution.py:144
  257.1 26.2 %collective-permute-start.38 = (bf16[32,128,128]{2,1,0:T(8,128)(2,1)S(1)}, bf16[32,128,128]{2,1,0:T(8,128)(2,1)}, u32[]{:S(2)}, u32[]{:S(2)}) collective-permute-start(bf16[32,128,128]{2,1,0:T(8,128)(2,1)S(1)} %copy-done.18), channel_id=1, source_target_pairs={{0,2},{1,3},{2,0},{3,1},{4,6},{5,7},{6,4},{7,5},{8,10},{9,11},{10,... | collective-permute-start | bytes 3145736 | tf_op jit(solution)/shard_map/ppermute | solution.py:144
  (45 other events, 596.6 us)

commit v13 on v12

--- a/solution.py
+++ b/solution.py
@@ -709,12 +709,12 @@
 
 def forward_two_kernel(place, pos_ref, *refs):
     share = place.far * place.near
-    wide = (len(refs) - (2 * share + 12)) // 2
+    wide = (len(refs) - (2 * share + 13)) // 2
     g_parts, rest = refs[:share], refs[share:]
     left, right, rest = unflat(place, rest[:wide]), unflat(place, rest[wide : 2 * wide]), rest[2 * wide :]
     act_ref, keep_ref, send_ref, *rest = rest
     out_refs, rest = rest[:share], rest[share:]
-    turned, fourth, stage, g_all, g_sems, left_all, left_sems, right_all, right_sems = rest
+    turned, fourth, stage, g_all, g_sems, out_sems, left_all, left_sems, right_all, right_sems = rest
     per = act_ref.shape[0]
     phase, j = pl.program_id(0), pl.program_id(1)
 
@@ -763,16 +763,14 @@
 
         either(place, pos_ref, j, keep_ref, send_ref, with_out)
 
-    for n in range(share):
-
-        @pl.when((phase == 2) & (j == n))
-        def _():
-            base = place.onward(pos_ref, n) * per
-
-            def body(k):
-                out_refs[n][k] = fourth[base + k]
-
-            each(per, body)
+    @pl.when((phase == 1) & (j == share - 1))
+    def _():
+        copies = []
+        for n in range(share):
+            mine = fourth.at[pl.ds(place.onward(pos_ref, n) * per, per)]
+            copies.append(pltpu.make_async_copy(mine, out_refs[n], out_sems.at[n]))
+        run(copies)
+        finish(copies)
 
 
 def forward_two(place, pos, act, g_mid, left_two, right_two):
@@ -782,13 +780,14 @@
     out = call(
         functools.partial(forward_two_kernel, place),
         (*grad,) + (shape((home, blocks, cut)),) * share,
-        (3, share),
+        (2, share),
         anywhere(share + 2 * len(flat(left_two))) + [pl.BlockSpec((home, blocks, cut), lambda p, j, pos: (at(p, j), 0, 0))],
-        (*grad_spec,) + (pl.BlockSpec((home, blocks, cut), lambda p, j, pos: (0, 0, 0)),) * share,
+        (*grad_spec, *anywhere(share)),
         [pltpu.VMEM((blocks, blocks, cut), BF16)] * 2
         + [
             pltpu.VMEM((home, blocks, cut), BF16),
             pltpu.VMEM((share, blocks, home, cut), BF16),
+            pltpu.SemaphoreType.DMA((share,)),
             pltpu.SemaphoreType.DMA((share,)),
         ]
         + whole_scratch(left_two, True)

time: 307 us -> 307 us (level)
  no operation moved by 1% of the time
where the time goes in v13:
time: 307 us; the launch traced here: 306 us
  waiting for transfers between devices  122 us (40%)
  Pallas kernels  96.1 us (31%)
  starting transfers between devices  47 us (15%)
  other arithmetic  34.7 us (11%)
  local copies, waits for them, and re-layouts  4.88 us (2%)
    ppermute x47, waiting for transfers between devices, send(): self.last = lax.ppermute(value, self.axis, pairs)  122 us
    pallas_call x10, Pallas kernels, call(): pl.pallas_call(body, out_shape=out, grid_spec=spec, compiler_params=pltpu...  96.1 us
    ppermute x47, starting transfers between devices, send(): self.last = lax.ppermute(value, self.axis, pairs)  47 us
    convert_element_type x14, other arithmetic, parts(): self.cut(ring, lax.rem(ring.here() + step, ring.size)).astype(BF16)  21.2 us
    another operation x9, other arithmetic, gather(): return got if n == 0 else jnp.stack(got)  7.22 us
  transfers between devices with their start and end apart: 47, of which 27 were waited for; matrix products, arithmetic and copies ran while one was open for 11% of the time, Pallas kernels for 23%

profile of v13, /device:TPU:0, one launch (start us, length us, event | category | flops | bytes accessed | tf_op | source)
XLA Modules:
  0.0 305.7 jit_solution(3197019465095223158)
XLA Ops:
  8.0 3.3 %shard_map.109 = bf16[128,32,128]{2,1,0:T(8,128)(2,1)} custom-call(s32[5]{0:T(128)} %stack.116.pos_ref, bf16[32,128,512]{2,1,0:T(8,128)(2,1)} %bitcast.189), custom_call_target="tpu_custom_call" | custom-call | bytes 4200000 | tf_op jit(solution)/shard_map/pallas_call | solution.py:84
  18.5 9.6 %collective-permute-done.5 = bf16[2,32,16,128]{3,2,1,0:T(8,128)(2,1)S(1)} collective-permute-done((bf16[2,32,16,128]{3,2,1,0:T(8,128)(2,1)S(1)}, bf16[2,32,16,128]{3,2,1,0:T(8,128)(2,1)S(1)}, u32[]{:S(2)}, u32[]{:S(2)}) %collective-permute-start.5) | collective-permute-done | bytes 262176 | tf_op jit(solution)/shard_map/ppermute | solution.py:144
  29.8 3.2 %collective-permute-start.7 = (bf16[2,32,16,128]{3,2,1,0:T(8,128)(2,1)S(1)}, bf16[2,32,16,128]{3,2,1,0:T(8,128)(2,1)}, u32[]{:S(2)}, u32[]{:S(2)}) collective-permute-start(bf16[2,32,16,128]{3,2,1,0:T(8,128)(2,1)S(1)} %get-tuple-element.137), channel_id=1, source_target_pairs={{0,16},{4,20},{8,24},{12,28},{16,0},{20,4},{24,8},{28,12},{1,17},{... | collective-permute-start | bytes 786440 | tf_op jit(solution)/shard_map/ppermute | solution.py:144
  34.6 3.2 %shard_map.110.refs_0_ = bf16[128,32,128]{2,1,0:T(8,128)(2,1)} custom-call(s32[5]{0:T(128)} %stack.116.pos_ref, bf16[32,128,512]{2,1,0:T(8,128)(2,1)} %bitcast.190), custom_call_target="tpu_custom_call" | custom-call | bytes 4200000 | tf_op jit(solution)/shard_map/pallas_call | solution.py:84
  37.8 3.2 %shard_map.111 = bf16[128,32,128]{2,1,0:T(8,128)(2,1)} custom-call(s32[5]{0:T(128)} %stack.116.pos_ref, bf16[32,128,512]{2,1,0:T(8,128)(2,1)} %bitcast.191), custom_call_target="tpu_custom_call" | custom-call | bytes 4200000 | tf_op jit(solution)/shard_map/pallas_call | solution.py:84
  41.0 3.2 %shard_map.112 = bf16[128,32,128]{2,1,0:T(8,128)(2,1)} custom-call(s32[5]{0:T(128)} %stack.116.pos_ref, bf16[32,128,512]{2,1,0:T(8,128)(2,1)} %bitcast.192), custom_call_target="tpu_custom_call" | custom-call | bytes 4200000 | tf_op jit(solution)/shard_map/pallas_call | solution.py:84
  44.2 3.7 %collective-permute-done.7 = bf16[2,32,16,128]{3,2,1,0:T(8,128)(2,1)} collective-permute-done((bf16[2,32,16,128]{3,2,1,0:T(8,128)(2,1)S(1)}, bf16[2,32,16,128]{3,2,1,0:T(8,128)(2,1)}, u32[]{:S(2)}, u32[]{:S(2)}) %collective-permute-start.7) | collective-permute-done | bytes 262176 | tf_op jit(solution)/shard_map/ppermute | solution.py:144
  57.9 9.4 %shard_map.113 = (bf16[128,32,128]{2,1,0:T(8,128)(2,1)}, bf16[128,32,128]{2,1,0:T(8,128)(2,1)}, bf16[128,32,128]{2,1,0:T(8,128)(2,1)}, bf16[128,32,128]{2,1,0:T(8,128)(2,1)}) custom-call(s32[5]{0:T(128)} %stack.116.pos_ref, bf16[32,128,512]{2,1,0:T(8,128)(2,1)} %bitcast.194, bf16[2,2,32,16,128]{4,3,2,1,0:T(8,128)(2,1)} %copy-done.2, ...), custom_call_target="tpu_custom_call" | custom-call | bytes 9600000 | tf_op jit(solution)/shard_map/pallas_call | solution.py:84
  67.4 6.0 %collective-permute-done.11 = bf16[2,32,16,128]{3,2,1,0:T(8,128)(2,1)} collective-permute-done((bf16[2,32,16,128]{3,2,1,0:T(8,128)(2,1)}, bf16[2,32,16,128]{3,2,1,0:T(8,128)(2,1)}, u32[]{:S(2)}, u32[]{:S(2)}) %collective-permute-start.11) | collective-permute-done | bytes 262176 | tf_op jit(solution)/shard_map/ppermute | solution.py:144
  76.8 3.3 %collective-permute-start.15 = (bf16[2,2,32,16,128]{4,3,2,1,0:T(8,128)(2,1)S(1)}, bf16[2,2,32,16,128]{4,3,2,1,0:T(8,128)(2,1)S(1)}, u32[]{:S(2)}, u32[]{:S(2)}) collective-permute-start(bf16[2,2,32,16,128]{4,3,2,1,0:T(8,128)(2,1)S(1)} %pad_maximum_fusion.7), channel_id=1, source_target_pairs={{0,8},{4,12},{8,0},{12,4},{16,24},{20,28},{24,16},{28,20},{1,9},{5... | collective-permute-start | bytes 1572872 | tf_op jit(solution)/shard_map/ppermute | solution.py:144
  83.4 8.2 %collective-permute-done.15 = bf16[2,2,32,16,128]{4,3,2,1,0:T(8,128)(2,1)S(1)} collective-permute-done((bf16[2,2,32,16,128]{4,3,2,1,0:T(8,128)(2,1)S(1)}, bf16[2,2,32,16,128]{4,3,2,1,0:T(8,128)(2,1)S(1)}, u32[]{:S(2)}, u32[]{:S(2)}) %collective-permute-start.15) | collective-permute-done | bytes 524320 | tf_op jit(solution)/shard_map/ppermute | solution.py:144
  91.7 13.7 %collective-permute-done.12.refs_3_ = bf16[128,32,128]{2,1,0:T(8,128)(2,1)S(1)} collective-permute-done((bf16[128,32,128]{2,1,0:T(8,128)(2,1)S(1)}, bf16[128,32,128]{2,1,0:T(8,128)(2,1)S(1)}, u32[]{:S(2)}, u32[]{:S(2)}) %collective-permute-start.12) | collective-permute-done | bytes 1048608 | tf_op jit(solution)/shard_map/ppermute | solution.py:144
  110.3 9.8 %shard_map.114.refs_12_ = bf16[128,128,128]{2,1,0:T(8,128)(2,1)} custom-call(s32[5]{0:T(128)} %stack.116.pos_ref, bf16[128,32,128]{2,1,0:T(8,128)(2,1)} %shard_map.110.refs_0_, bf16[128,32,128]{2,1,0:T(8,128)(2,1)} %collective-permute-done.18.refs_1_, bf16[128,32,128]{2,1,0:T(8,128)(2,1)} %copy-done.4, bf16[128,32,128]{2,1,0:T(8,128)(2,1)} %copy-done.3, ...), custom_call_target="tpu_custom_call" | custom-call | bytes 12000000 | tf_op jit(solution)/shard_map/pallas_call | solution.py:84
  120.2 11.0 %collective-permute-done.19.refs_2_ = bf16[128,32,128]{2,1,0:T(8,128)(2,1)} collective-permute-done((bf16[128,32,128]{2,1,0:T(8,128)(2,1)}, bf16[128,32,128]{2,1,0:T(8,128)(2,1)}, u32[]{:S(2)}, u32[]{:S(2)}) %collective-permute-start.19) | collective-permute-done | bytes 1048608 | tf_op jit(solution)/shard_map/ppermute | solution.py:144
  136.4 26.6 %shard_map.115 = (bf16[128,128,128]{2,1,0:T(8,128)(2,1)}, bf16[2,32,128,128]{3,2,1,0:T(8,128)(2,1)}, bf16[2,32,128,128]{3,2,1,0:T(8,128)(2,1)}, bf16[2,32,128,12...) custom-call(s32[5]{0:T(128)} %stack.116.pos_ref, ...), custom_call_target="tpu_custom_call" | custom-call | bytes 31200000 | tf_op jit(solution)/shard_map/pallas_call | solution.py:84
  165.4 19.1 %shard_map.116 = (bf16[2,32,128,128]{3,2,1,0:T(8,128)(2,1)}, bf16[2,32,128,128]{3,2,1,0:T(8,128)(2,1)}, bf16[32,128,128]{2,1,0:T(8,128)(2,1)}, bf16[32,128,128]{...) custom-call(s32[5]{0:T(128)} %stack.116.pos_ref, ...), custom_call_target="tpu_custom_call" | custom-call | bytes 24000000 | tf_op jit(solution)/shard_map/pallas_call | solution.py:84
  196.7 18.6 %collective-permute-done.28.refs_2_ = bf16[128,32,128]{2,1,0:T(8,128)(2,1)} collective-permute-done((bf16[128,32,128]{2,1,0:T(8,128)(2,1)}, bf16[128,32,128]{2,1,0:T(8,128)(2,1)}, u32[]{:S(2)}, u32[]{:S(2)}) %collective-permute-start.28) | collective-permute-done | bytes 1048608 | tf_op jit(solution)/shard_map/ppermute | solution.py:144
  224.9 11.3 %shard_map.117 = (bf16[32,128,512]{2,1,0:T(8,128)(2,1)}, bf16[32,128,128]{2,1,0:T(8,128)(2,1)}) custom-call(s32[5]{0:T(128)} %stack.116.pos_ref, bf16[128,32,128]{2,1,0:T(8,128)(2,1)} %get-tuple-element.220.refs_0_, bf16[128,32,128]{2,1,0:T(8,128)(2,1)} %collective-permute-done.29.refs_1_, bf16[128,32,128]{2,1,0:T(8,128)(2,1)} %collective-permute-done.28.refs_2_, ...), custom_call_target="tpu_custom_call" | custom-call | bytes 12000000 | tf_op jit(solution)/shard_map/pallas_call | solution.py:84
  237.5 9.9 %collective-permute-done.35 = bf16[2,32,2,16,128]{4,3,1,2,0:T(8,128)(2,1)} collective-permute-done((bf16[2,32,2,16,128]{4,3,1,2,0:T(8,128)(2,1)}, bf16[2,32,2,16,128]{4,3,1,2,0:T(8,128)(2,1)}, u32[]{:S(2)}, u32[]{:S(2)}) %collective-permute-start.35) | collective-permute-done | bytes 524320 | tf_op jit(solution)/shard_map/ppermute | solution.py:144
  259.4 5.5 %collective-permute-done.42 = bf16[2,32,16,128]{3,2,1,0:T(8,128)(2,1)S(1)} collective-permute-done((bf16[2,32,16,128]{3,2,1,0:T(8,128)(2,1)S(1)}, bf16[2,32,16,128]{3,2,1,0:T(8,128)(2,1)S(1)}, u32[]{:S(2)}, u32[]{:S(2)}) %collective-permute-start.42) | collective-permute-done | bytes 262176 | tf_op jit(solution)/shard_map/ppermute | solution.py:144
  267.7 5.7 %collective-permute-done.40 = bf16[2,32,2,16,128]{4,3,1,2,0:T(8,128)(2,1)S(1)} collective-permute-done((bf16[2,32,2,16,128]{4,3,1,2,0:T(8,128)(2,1)S(1)}, bf16[2,32,2,16,128]{4,3,1,2,0:T(8,128)(2,1)S(1)}, u32[]{:S(2)}, u32[]{:S(2)}) %collective-permute-start.40) | collective-permute-done | bytes 524320 | tf_op jit(solution)/shard_map/ppermute | solution.py:144
  276.1 4.0 %collective-permute-done.41 = bf16[32,2,16,128]{3,2,0,1:T(8,128)(2,1)S(1)} collective-permute-done((bf16[32,2,16,128]{3,2,0,1:T(8,128)(2,1)S(1)}, bf16[32,2,16,128]{3,2,0,1:T(8,128)(2,1)S(1)}, u32[]{:S(2)}, u32[]{:S(2)}) %collective-permute-start.41) | collective-permute-done | bytes 262176 | tf_op jit(solution)/shard_map/ppermute | solution.py:144
  283.1 7.0 %shard_map.118 = bf16[32,128,512]{2,1,0:T(8,128)(2,1)} custom-call(s32[5]{0:T(128)} %stack.116.pos_ref, bf16[32,128,128]{2,1,0:T(8,128)(2,1)} %get-tuple-element.231.refs_0_, bf16[32,128,128]{2,1,0:T(8,128)(2,1)} %collective-permute-done.37.refs_1_, bf16[32,128,128]{2,1,0:T(8,128)(2,1)} %collective-permute-done.38.refs_2_, bf16[32,128,128]{2,1,0:T(8,128)(2,1)} %copy-done.11, ...), custom_call_target="tpu_custom_call" | custom-call | bytes 7200000 | tf_op jit(solution)/shard_map/pallas_call | solution.py:84
  296.0 6.9 %collective-permute-done.44 = bf16[32,16,128]{2,1,0:T(8,128)(2,1)S(1)} collective-permute-done((bf16[32,16,128]{2,1,0:T(8,128)(2,1)S(1)}, bf16[32,16,128]{2,1,0:T(8,128)(2,1)S(1)}, u32[]{:S(2)}, u32[]{:S(2)}) %collective-permute-start.44) | collective-permute-done | bytes 131104 | tf_op jit(solution)/shard_map/ppermute | solution.py:144
  (158 shorter events, 99.1 us)
Async XLA Ops:
  16.8 34.6 %collective-permute-start = (bf16[128,32,128]{2,1,0:T(8,128)(2,1)}, bf16[128,32,128]{2,1,0:T(8,128)(2,1)S(1)}, u32[]{:S(2)}, u32[]{:S(2)}) collective-permute-start(bf16[128,32,128]{2,1,0:T(8,128)(2,1)} %shard_map.109), channel_id=1, source_target_pairs={{0,3},{1,2},{2,1},{3,0},{4,7},{5,6},{6,5},{7,4},{8,11},{9,10},{10,... | collective-permute-start | bytes 3145736 | tf_op jit(solution)/shard_map/ppermute | solution.py:144
  51.5 25.2 %collective-permute-start.8 = (bf16[128,32,128]{2,1,0:T(8,128)(2,1)}, bf16[128,32,128]{2,1,0:T(8,128)(2,1)S(1)}, u32[]{:S(2)}, u32[]{:S(2)}) collective-permute-start(bf16[128,32,128]{2,1,0:T(8,128)(2,1)} %shard_map.112), channel_id=1, source_target_pairs={{0,2},{1,3},{2,0},{3,1},{4,6},{5,7},{6,4},{7,5},{8,10},{9,11},{10,... | collective-permute-start | bytes 3145736 | tf_op jit(solution)/shard_map/ppermute | solution.py:144
  52.6 24.2 %collective-permute-start.9 = (bf16[2,2,2,32,16,128]{5,4,3,2,1,0:T(8,128)(2,1)S(1)}, bf16[2,2,2,32,16,128]{5,4,3,2,1,0:T(8,128)(2,1)}, u32[]{:S(2)}, u32[]{:S(2)}) collective-permute-start(bf16[2,2,2,32,16,128]{5,4,3,2,1,0:T(8,128)(2,1)S(1)} %pad_maximum_fusion.refs_4_.refs_8_), channel_id=1, source_target_pairs={{0,4},{4,0},{8,12},{12,8},{16,20},{20,16},{24,28},{28,24},{1,5},{5... | collective-permute-start | bytes 3145736 | tf_op jit(solution)/shard_map/ppermute | solution.py:144
  57.9 25.5 %collective-permute-start.18 = (bf16[128,32,128]{2,1,0:T(8,128)(2,1)}, bf16[128,32,128]{2,1,0:T(8,128)(2,1)}, u32[]{:S(2)}, u32[]{:S(2)}) collective-permute-start(bf16[128,32,128]{2,1,0:T(8,128)(2,1)} %shard_map.111), channel_id=1, source_target_pairs={{0,1},{1,0},{2,3},{3,2},{4,5},{5,4},{6,7},{7,6},{8,9},{9,8},{10,11... | collective-permute-start | bytes 3145736 | tf_op jit(solution)/shard_map/ppermute | solution.py:144
  80.1 25.3 %collective-permute-start.12 = (bf16[128,32,128]{2,1,0:T(8,128)(2,1)S(1)}, bf16[128,32,128]{2,1,0:T(8,128)(2,1)S(1)}, u32[]{:S(2)}, u32[]{:S(2)}) collective-permute-start(bf16[128,32,128]{2,1,0:T(8,128)(2,1)S(1)} %copy-done.21), channel_id=1, source_target_pairs={{0,3},{1,2},{2,1},{3,0},{4,7},{5,6},{6,5},{7,4},{8,11},{9,10},{10,... | collective-permute-start | bytes 3145736 | tf_op jit(solution)/shard_map/ppermute | solution.py:144
  80.1 26.0 %collective-permute-start.13 = (bf16[128,32,128]{2,1,0:T(8,128)(2,1)S(1)}, bf16[128,32,128]{2,1,0:T(8,128)(2,1)S(1)}, u32[]{:S(2)}, u32[]{:S(2)}) collective-permute-start(bf16[128,32,128]{2,1,0:T(8,128)(2,1)S(1)} %copy-done.20), channel_id=1, source_target_pairs={{0,1},{1,0},{2,3},{3,2},{4,5},{5,4},{6,7},{7,6},{8,9},{9,8},{10,11... | collective-permute-start | bytes 3145736 | tf_op jit(solution)/shard_map/ppermute | solution.py:144
  81.9 25.4 %collective-permute-start.14 = (bf16[2,2,2,32,16,128]{5,4,3,2,1,0:T(8,128)(2,1)}, bf16[2,2,2,32,16,128]{5,4,3,2,1,0:T(8,128)(2,1)}, u32[]{:S(2)}, u32[]{:S(2)}) collective-permute-start(bf16[2,2,2,32,16,128]{5,4,3,2,1,0:T(8,128)(2,1)} %pad_maximum_fusion.1.refs_4_), channel_id=1, source_target_pairs={{0,4},{4,0},{8,12},{12,8},{16,20},{20,16},{24,28},{28,24},{1,5},{5... | collective-permute-start | bytes 3145736 | tf_op jit(solution)/shard_map/ppermute | solution.py:144
  83.4 23.9 %collective-permute-start.16 = (bf16[2,2,2,32,16,128]{5,4,3,2,1,0:T(8,128)(2,1)S(1)}, bf16[2,2,2,32,16,128]{5,4,3,2,1,0:T(8,128)(2,1)S(1)}, u32[]{:S(2)}, u32[]{:S(2)}) collective-permute-start(bf16[2,2,2,32,16,128]{5,4,3,2,1,0:T(8,128)(2,1)S(1)} %pad_maximum_fusion.refs_4_.refs_8_), channel_id=1, source_target_pairs={{0,1},{1,0},{2,3},{3,2},{4,5},{5,4},{6,7},{7,6},{8,9},{9,8},{10,11... | collective-permute-start | bytes 3145736 | tf_op jit(solution)/shard_map/ppermute | solution.py:144
  105.4 25.8 %collective-permute-start.19 = (bf16[128,32,128]{2,1,0:T(8,128)(2,1)}, bf16[128,32,128]{2,1,0:T(8,128)(2,1)}, u32[]{:S(2)}, u32[]{:S(2)}) collective-permute-start(bf16[128,32,128]{2,1,0:T(8,128)(2,1)} %get-tuple-element.159), channel_id=1, source_target_pairs={{0,2},{1,3},{2,0},{3,1},{4,6},{5,7},{6,4},{7,5},{8,10},{9,11},{10,... | collective-permute-start | bytes 3145736 | tf_op jit(solution)/shard_map/ppermute | solution.py:144
  108.2 24.4 %collective-permute-start.20 = (bf16[2,2,2,32,16,128]{5,4,3,2,1,0:T(8,128)(2,1)S(1)}, bf16[2,2,2,32,16,128]{5,4,3,2,1,0:T(8,128)(2,1)S(1)}, u32[]{:S(2)}, u32[]{:S(2)}) collective-permute-start(bf16[2,2,2,32,16,128]{5,4,3,2,1,0:T(8,128)(2,1)S(1)} %pad_maximum_fusion.2.refs_8_.refs_4_), channel_id=1, source_target_pairs={{0,4},{4,0},{8,12},{12,8},{16,20},{20,16},{24,28},{28,24},{1,5},{5... | collective-permute-start | bytes 3145736 | tf_op jit(solution)/shard_map/ppermute | solution.py:144
  109.7 22.9 %collective-permute-start.21 = (bf16[2,2,2,32,16,128]{5,4,3,2,1,0:T(8,128)(2,1)S(1)}, bf16[2,2,2,32,16,128]{5,4,3,2,1,0:T(8,128)(2,1)}, u32[]{:S(2)}, u32[]{:S(2)}) collective-permute-start(bf16[2,2,2,32,16,128]{5,4,3,2,1,0:T(8,128)(2,1)S(1)} %pad_maximum_fusion.2.refs_8_.refs_4_), channel_id=1, source_target_pairs={{0,1},{1,0},{2,3},{3,2},{4,5},{5,4},{6,7},{7,6},{8,9},{9,8},{10,11... | collective-permute-start | bytes 3145736 | tf_op jit(solution)/shard_map/ppermute | solution.py:144
  109.7 22.9 %collective-permute-start.22 = (bf16[2,2,2,32,16,128]{5,4,3,2,1,0:T(8,128)(2,1)}, bf16[2,2,2,32,16,128]{5,4,3,2,1,0:T(8,128)(2,1)}, u32[]{:S(2)}, u32[]{:S(2)}) collective-permute-start(bf16[2,2,2,32,16,128]{5,4,3,2,1,0:T(8,128)(2,1)} %pad_maximum_fusion.1.refs_4_), channel_id=1, source_target_pairs={{0,1},{1,0},{2,3},{3,2},{4,5},{5,4},{6,7},{7,6},{8,9},{9,8},{10,11... | collective-permute-start | bytes 3145736 | tf_op jit(solution)/shard_map/ppermute | solution.py:144
  110.2 22.4 %collective-permute-start.23 = (bf16[2,2,2,32,16,128]{5,4,3,2,1,0:T(8,128)(2,1)}, bf16[2,2,2,32,16,128]{5,4,3,2,1,0:T(8,128)(2,1)}, u32[]{:S(2)}, u32[]{:S(2)}) collective-permute-start(bf16[2,2,2,32,16,128]{5,4,3,2,1,0:T(8,128)(2,1)} %collective-permute-done.14.refs_5_), channel_id=1, source_target_pairs={{0,1},{1,0},{2,3},{3,2},{4,5},{5,4},{6,7},{7,6},{8,9},{9,8},{10,11... | collective-permute-start | bytes 3145736 | tf_op jit(solution)/shard_map/ppermute | solution.py:144
  164.2 25.2 %collective-permute-start.25 = (bf16[128,32,128]{2,1,0:T(8,128)(2,1)}, bf16[128,32,128]{2,1,0:T(8,128)(2,1)}, u32[]{:S(2)}, u32[]{:S(2)}) collective-permute-start(bf16[128,32,128]{2,1,0:T(8,128)(2,1)} %get-tuple-element.181), channel_id=1, source_target_pairs={{0,3},{1,2},{2,1},{3,0},{4,7},{5,6},{6,5},{7,4},{8,11},{9,10},{10,... | collective-permute-start | bytes 3145736 | tf_op jit(solution)/shard_map/ppermute | solution.py:144
  189.8 25.5 %collective-permute-start.28 = (bf16[128,32,128]{2,1,0:T(8,128)(2,1)}, bf16[128,32,128]{2,1,0:T(8,128)(2,1)}, u32[]{:S(2)}, u32[]{:S(2)}) collective-permute-start(bf16[128,32,128]{2,1,0:T(8,128)(2,1)} %get-tuple-element.196), channel_id=1, source_target_pairs={{0,2},{1,3},{2,0},{3,1},{4,6},{5,7},{6,4},{7,5},{8,10},{9,11},{10,... | collective-permute-start | bytes 3145736 | tf_op jit(solution)/shard_map/ppermute | solution.py:144
  191.0 24.3 %collective-permute-start.29 = (bf16[128,32,128]{2,1,0:T(8,128)(2,1)}, bf16[128,32,128]{2,1,0:T(8,128)(2,1)}, u32[]{:S(2)}, u32[]{:S(2)}) collective-permute-start(bf16[128,32,128]{2,1,0:T(8,128)(2,1)} %get-tuple-element.197), channel_id=1, source_target_pairs={{0,1},{1,0},{2,3},{3,2},{4,5},{5,4},{6,7},{7,6},{8,9},{9,8},{10,11... | collective-permute-start | bytes 3145736 | tf_op jit(solution)/shard_map/ppermute | solution.py:144
  191.0 25.9 %collective-permute-start.30 = (bf16[2,32,2,2,16,128]{5,4,1,3,2,0:T(8,128)(2,1)}, bf16[2,32,2,2,16,128]{5,4,1,3,2,0:T(8,128)(2,1)}, u32[]{:S(2)}, u32[]{:S(2)}) collective-permute-start(bf16[2,32,2,2,16,128]{5,4,1,3,2,0:T(8,128)(2,1)} %fusion), channel_id=1, source_target_pairs={{0,4},{4,0},{8,12},{12,8},{16,20},{20,16},{24,28},{28,24},{1,5},{5... | collective-permute-start | bytes 3145736 | tf_op jit(solution)/shard_map/ppermute | solution.py:144
  192.4 25.4 %collective-permute-start.31 = (bf16[2,32,2,2,16,128]{5,4,1,3,2,0:T(8,128)(2,1)S(1)}, bf16[2,32,2,2,16,128]{5,4,1,3,2,0:T(8,128)(2,1)}, u32[]{:S(2)}, u32[]{:S(2)}) collective-permute-start(bf16[2,32,2,2,16,128]{5,4,1,3,2,0:T(8,128)(2,1)S(1)} %fusion.1), channel_id=1, source_target_pairs={{0,8},{4,12},{8,0},{12,4},{16,24},{20,28},{24,16},{28,20},{1,9},{5... | collective-permute-start | bytes 3145736 | tf_op jit(solution)/shard_map/ppermute | solution.py:144
  217.8 31.1 %collective-permute-start.33 = (bf16[32,128,128]{2,1,0:T(8,128)(2,1)}, bf16[32,128,128]{2,1,0:T(8,128)(2,1)S(1)}, u32[]{:S(2)}, u32[]{:S(2)}) collective-permute-start(bf16[32,128,128]{2,1,0:T(8,128)(2,1)} %get-tuple-element.210), channel_id=1, source_target_pairs={{0,3},{1,2},{2,1},{3,0},{4,7},{5,6},{6,5},{7,4},{8,11},{9,10},{10,... | collective-permute-start | bytes 3145736 | tf_op jit(solution)/shard_map/ppermute | solution.py:144
  217.9 31.1 %collective-permute-start.36 = (bf16[2,32,2,2,16,128]{5,4,1,3,2,0:T(8,128)(2,1)}, bf16[2,32,2,2,16,128]{5,4,1,3,2,0:T(8,128)(2,1)}, u32[]{:S(2)}, u32[]{:S(2)}) collective-permute-start(bf16[2,32,2,2,16,128]{5,4,1,3,2,0:T(8,128)(2,1)} %fusion.2), channel_id=1, source_target_pairs={{0,4},{4,0},{8,12},{12,8},{16,20},{20,16},{24,28},{28,24},{1,5},{5... | collective-permute-start | bytes 3145736 | tf_op jit(solution)/shard_map/ppermute | solution.py:144
  220.8 26.7 %collective-permute-start.35 = (bf16[2,32,2,16,128]{4,3,1,2,0:T(8,128)(2,1)}, bf16[2,32,2,16,128]{4,3,1,2,0:T(8,128)(2,1)}, u32[]{:S(2)}, u32[]{:S(2)}) collective-permute-start(bf16[2,32,2,16,128]{4,3,1,2,0:T(8,128)(2,1)} %fusion.4), channel_id=1, source_target_pairs={{0,16},{4,20},{8,24},{12,28},{16,0},{20,4},{24,8},{28,12},{1,17},{... | collective-permute-start | bytes 1572872 | tf_op jit(solution)/shard_map/ppermute | solution.py:144
  223.3 25.7 %collective-permute-start.34 = (bf16[2,32,2,16,128]{4,3,1,2,0:T(8,128)(2,1)}, bf16[2,32,2,16,128]{4,3,1,2,0:T(8,128)(2,1)}, u32[]{:S(2)}, u32[]{:S(2)}) collective-permute-start(bf16[2,32,2,16,128]{4,3,1,2,0:T(8,128)(2,1)} %fusion.5), channel_id=1, source_target_pairs={{0,8},{4,12},{8,0},{12,4},{16,24},{20,28},{24,16},{28,20},{1,9},{5... | collective-permute-start | bytes 1572872 | tf_op jit(solution)/shard_map/ppermute | solution.py:144
  256.9 26.2 %collective-permute-start.37 = (bf16[32,128,128]{2,1,0:T(8,128)(2,1)S(1)}, bf16[32,128,128]{2,1,0:T(8,128)(2,1)}, u32[]{:S(2)}, u32[]{:S(2)}) collective-permute-start(bf16[32,128,128]{2,1,0:T(8,128)(2,1)S(1)} %copy-done.19), channel_id=1, source_target_pairs={{0,1},{1,0},{2,3},{3,2},{4,5},{5,4},{6,7},{7,6},{8,9},{9,8},{10,11... | collective-permute-start | bytes 3145736 | tf_op jit(solution)/shard_map/ppermute | solution.py:144
  256.9 26.2 %collective-permute-start.38 = (bf16[32,128,128]{2,1,0:T(8,128)(2,1)S(1)}, bf16[32,128,128]{2,1,0:T(8,128)(2,1)}, u32[]{:S(2)}, u32[]{:S(2)}) collective-permute-start(bf16[32,128,128]{2,1,0:T(8,128)(2,1)S(1)} %copy-done.18), channel_id=1, source_target_pairs={{0,2},{1,3},{2,0},{3,1},{4,6},{5,7},{6,4},{7,5},{8,10},{9,11},{10,... | collective-permute-start | bytes 3145736 | tf_op jit(solution)/shard_map/ppermute | solution.py:144
  (45 other events, 595.8 us)
